TPU v7x, 32 devices: a whole 2x2x4 slice. The times are simulated.
32 devices in a mesh: view: 8 (over z, y), plane: 4 (over x, core).
Axes of the slice: x: 2, y: 2, z: 4, core: 2. Of those that a mesh axis runs over, the one named last changes fastest.
Arguments:
- features: bfloat16 [32, 32, 512], P('view'), may hold values from -6 to 6
- sources: int32 [32, 10], replicated, may hold values from 0 to 31, as said below
- warp_weights: bfloat16 [48, 512, 512], P('plane'), may hold values from -0.25 to 0.25
- view_gate: float32 [8], replicated, may hold values from -6 to 6
- depth_kernel: float32 [3, 8, 8], replicated, may hold values from -4 to 4
- cotangent: bfloat16 [32, 48, 8, 512], P('view', 'plane'), may hold values from -6 to 6
Outputs:
- regular: bfloat16 [32, 48, 8, 512], P('view', 'plane')
- feature_grads: float32 [32, 32, 512], P('view')
Inputs may be any that keep to these rules, and one draw needn't show every extreme that they name: `sources`: view v is owned by the device at index v // 4 of view. Among the 40 entries of the rows of one device (rows i * 4 to i * 4 + 3), at most 10 name views of any one owner, and for each device some owner is named exactly 10 times.
All inputs are finite; a program needn't handle non-finite values.
Results may differ from a plain program's by a relative error of at most 0.0038.
Values may be sent and summed in bfloat16 or wider, within the bound.
No kernel may reach another device: no remote copies, remote signals or barrier semaphores. Data moves between devices by JAX's collectives and lax.ppermute only.
A program may use at most 128 MiB of HBM per device.

v0:
```python
import functools

import jax
import jax.numpy as jnp
from jax import lax
from jax.experimental import pallas as pl
from jax.experimental.pallas import tpu as pltpu
from jax.sharding import PartitionSpec as P

G = 8
GC = 4
SUB = 8
LANE = 128
VMEM_LIMIT = 48 * 1024 * 1024
NT = (((1,), (1,)), ((), ()))


def params(**extra):
    return pltpu.CompilerParams(vmem_limit_bytes=VMEM_LIMIT, **extra)


def low_half():
    return lax.broadcasted_iota(jnp.int32, (SUB, LANE), 0) < SUB // 2


def swap_halves(tile):
    return pltpu.roll(tile, SUB // 2, 0)


def spread(tile, half, low):
    other = swap_halves(tile)
    return jnp.where(low, tile, other) if half == 0 else jnp.where(low, other, tile)


def assemble_kernel(src_ref, all_ref, own_ref, rows_ref, refx_ref, scratch):
    local_views, per_view = src_ref.shape
    channels = own_ref.shape[1]
    pairs = local_views * per_view
    for pair in range(pairs):
        view = src_ref[pair % local_views, pair // local_views]
        for tile in range(scratch.shape[0]):
            scratch[tile, pl.ds(pair, channels, stride=pairs), :] = all_ref[
                view, :, pl.ds(tile * LANE, LANE)
            ].astype(jnp.float32)
    for tile in range(scratch.shape[0]):
        lanes = pl.ds(tile * LANE, LANE)
        rows_ref[:, lanes] = scratch[tile].astype(jnp.bfloat16)
        for view in range(local_views):
            own = own_ref[view, :, lanes].astype(jnp.float32)
            for copy in range(SUB // local_views):
                refx_ref[tile, pl.ds(copy * local_views + view, channels, stride=SUB), :] = own


def forward_kernel(
    gate_ref, rows_ref, refx_ref, w_ref, warped_ref, corr_ref, sig_ref, rden_ref, cost_ref, *chunks
):
    pairs = corr_ref.shape[2]
    groups = corr_ref.shape[1]
    tiles = pairs // SUB
    low = low_half()
    width = 2 * LANE
    for index, chunk in enumerate(chunks):
        chunk[...] = lax.dot_general(
            rows_ref[...],
            w_ref[0, index * width : (index + 1) * width, :],
            NT,
            preferred_element_type=jnp.float32,
        )
    for index, chunk in enumerate(chunks):
        warped_ref[0, :, index * width : (index + 1) * width] = chunk[...].astype(jnp.bfloat16)
        cost_pair = []
        for half in range(2):
            inner = pl.ds(half * LANE, LANE)
            lanes = pl.ds(index * width + half * LANE, LANE)
            logits = jnp.zeros((tiles, SUB, LANE), jnp.float32)
            for g in range(groups):
                total = None
                for j in range(GC):
                    c = g * GC + j
                    part = (
                        chunk[pl.ds(c * pairs, pairs), inner].reshape(tiles, SUB, LANE)
                        * refx_ref[2 * index + half, pl.ds(c * SUB, SUB), :][None]
                    )
                    total = part if total is None else total + part
                corr = total * (1.0 / GC)
                corr_ref[0, g, :, lanes] = corr.reshape(pairs, LANE)
                logits = logits + corr * gate_ref[g]
            sig = jax.nn.sigmoid(logits)
            sig_ref[0, :, lanes] = sig.reshape(pairs, LANE)
            visible = 0.5 + sig
            den = jnp.sum(visible, axis=0)
            rden = 1.0 / (den + swap_halves(den))
            rden_ref[0, :, lanes] = rden
            costs = []
            for g in range(groups):
                num = jnp.sum(
                    visible * corr_ref[0, g, :, lanes].reshape(tiles, SUB, LANE), axis=0
                )
                costs.append((num + swap_halves(num)) * rden)
            cost_pair.append(costs)
        for g in range(groups):
            cost_ref[0, pl.ds(g * SUB, SUB), pl.ds(index * LANE, LANE)] = jnp.where(
                low, cost_pair[0][g], cost_pair[1][g]
            )


def conv_kernel(taps_ref, cost_ref, cot_ref, regular_ref, grad_ref, slope):
    planes = regular_ref.shape[0]
    width = cost_ref.shape[2]

    def forward_plane(plane, carry):
        for lane in range(0, width, LANE):
            lanes = pl.ds(lane, LANE)
            inputs = [
                [cost_ref[plane + k, pl.ds(g * SUB, SUB), lanes] for g in range(G)]
                for k in range(3)
            ]
            pres = []
            for o in range(G):
                total = None
                for k in range(3):
                    for g in range(G):
                        part = inputs[k][g] * taps_ref[k, o, g]
                        total = part if total is None else total + part
                pres.append(total)
            pre = jnp.concatenate(pres, axis=0)
            sig = jax.nn.sigmoid(pre)
            cot = cot_ref[plane, :, lanes].astype(jnp.float32)
            slope[plane, :, lanes] = cot * (sig * (1.0 + pre * (1.0 - sig)))

            @pl.when((plane >= 1) & (plane <= planes))
            def _():
                regular_ref[plane - 1, :, lanes] = (pre * sig).astype(jnp.bfloat16)

        return carry

    lax.fori_loop(0, planes + 2, forward_plane, 0)

    def backward_plane(plane, carry):
        for lane in range(0, width, LANE):
            lanes = pl.ds(lane, LANE)
            inputs = [
                [slope[plane + 2 - k, pl.ds(o * SUB, SUB), lanes] for o in range(G)]
                for k in range(3)
            ]
            for g in range(G):
                total = None
                for k in range(3):
                    for o in range(G):
                        part = inputs[k][o] * taps_ref[k, o, g]
                        total = part if total is None else total + part
                grad_ref[plane, pl.ds(g * SUB, SUB), lanes] = total
        return carry

    lax.fori_loop(0, planes, backward_plane, 0)


def backward_kernel(
    gate_ref,
    src_ref,
    place_ref,
    refx_ref,
    w_ref,
    warped_ref,
    corr_ref,
    sig_ref,
    rden_ref,
    cost_ref,
    grad_ref,
    keep_ref,
    send_ref,
    rows,
    acc,
    dref,
    dense,
):
    step = pl.program_id(0)
    pairs = corr_ref.shape[2]
    groups = corr_ref.shape[1]
    tiles = pairs // SUB
    pixels = corr_ref.shape[3]
    local_views, per_view = src_ref.shape
    channels = groups * GC
    low = low_half()

    @pl.when(step == 0)
    def _():
        acc[...] = jnp.zeros_like(acc)
        dref[...] = jnp.zeros_like(dref)

    for tile in range(pixels // LANE):
        lanes = pl.ds(tile * LANE, LANE)
        packed = pl.ds((tile // 2) * LANE, LANE)
        half = tile % 2
        rden = rden_ref[0, :, lanes]
        mixed = None
        num_grads = []
        for g in range(groups):
            grad = grad_ref[0, pl.ds(g * SUB, SUB), packed]
            part = grad * cost_ref[0, pl.ds(g * SUB, SUB), packed]
            mixed = part if mixed is None else mixed + part
            num_grads.append(spread(grad, half, low) * rden)
        den_grad = spread(mixed, half, low) * rden
        vis_grad = -den_grad[None]
        for g in range(groups):
            vis_grad = vis_grad + num_grads[g][None] * corr_ref[0, g, :, lanes].reshape(
                tiles, SUB, LANE
            )
        sig = sig_ref[0, :, lanes].reshape(tiles, SUB, LANE)
        logit_grad = vis_grad * (sig * (1.0 - sig)) * (1.0 / GC)
        visible = (0.5 + sig) * (1.0 / GC)
        for g in range(groups):
            corr_grad = visible * num_grads[g][None] + logit_grad * gate_ref[g]
            for j in range(0, GC, 2):
                c = g * GC + j
                span = pl.ds(c * pairs, 2 * pairs)
                both = jnp.concatenate(
                    [
                        (corr_grad * refx_ref[tile, pl.ds((c + i) * SUB, SUB), :][None]).reshape(
                            pairs, LANE
                        )
                        for i in range(2)
                    ],
                    axis=0,
                )
                rows[span, lanes] = both.astype(jnp.bfloat16)
                warped = (
                    warped_ref[0, span, lanes].astype(jnp.float32).reshape(2, tiles, SUB, LANE)
                )
                for i in range(2):
                    dref[tile, pl.ds((c + i) * SUB, SUB), :] += jnp.sum(
                        corr_grad * warped[i], axis=0
                    )
    for index in range(pixels // (2 * LANE)):
        product = jnp.dot(
            rows[...],
            w_ref[0, :, pl.ds(index * 2 * LANE, 2 * LANE)],
            preferred_element_type=jnp.float32,
        )
        for half in range(2):
            acc[2 * index + half] += product[:, half * LANE : (half + 1) * LANE]

    @pl.when(step == pl.num_programs(0) - 1)
    def _():
        own_index = place_ref[0]
        parity = place_ref[1]
        dense[...] = jnp.zeros_like(dense)
        for tile in range(pixels // LANE):
            lanes = pl.ds(tile * LANE, LANE)
            for view in range(local_views):
                total = dref[tile, pl.ds(view, channels, stride=SUB), :]
                for copy in range(1, SUB // local_views):
                    first = copy * local_views + view
                    total = total + dref[tile, pl.ds(first, channels, stride=SUB), :]
                dense[own_index * local_views + view, :, lanes] = total
        for pair in range(pairs):
            view = src_ref[pair % local_views, pair // local_views]
            for tile in range(pixels // LANE):
                dense[view, :, pl.ds(tile * LANE, LANE)] += acc[
                    tile, pl.ds(pair, channels, stride=pairs), :
                ]
        blocks = keep_ref.shape[1]
        share = keep_ref.shape[2]

        def one_view(view, carry):
            kept = []
            sent = []
            for block in range(blocks):
                mine = pl.multiple_of((2 * block + parity) * share, share)
                theirs = pl.multiple_of((2 * block + 1 - parity) * share, share)
                keep_ref[view, block] = dense[view, pl.ds(mine, share), :]
                sent.append(dense[view, pl.ds(theirs, share), :])
            send_ref[view] = jnp.concatenate(sent, axis=0).astype(jnp.bfloat16)
            return carry

        lax.fori_loop(0, dense.shape[0], one_view, 0)


def whole(array):
    rank = len(array.shape)
    return pl.BlockSpec(array.shape, lambda d: (0,) * rank)


def per_plane(shape):
    rank = len(shape)
    return pl.BlockSpec((1,) + tuple(shape[1:]), lambda d: (d,) + (0,) * (rank - 1))


SMEM = functools.partial(pl.BlockSpec, memory_space=pltpu.SMEM)


def shards(features, sources, warp_weights, view_gate, depth_kernel, cotangent):
    view_count = lax.axis_size("view")
    plane_count = lax.axis_size("plane")
    own_index = lax.axis_index("view")
    plane_index = lax.axis_index("plane")
    local_views, channels, pixels = features.shape
    all_views, per_view = sources.shape
    pairs = local_views * per_view
    planes = warp_weights.shape[0]
    share = channels // plane_count
    blocks = plane_count // 2
    parity = plane_index % 2
    packed_rows = G * SUB
    packed_width = pixels // 2
    f32 = jnp.float32
    bf16 = jnp.bfloat16
    swap = [(i, i ^ 1) for i in range(plane_count)]
    up = [(i, i + 1) for i in range(plane_count - 1)]
    down = [(i + 1, i) for i in range(plane_count - 1)]

    halves = features.reshape(local_views, blocks, 2, share, pixels)
    mine = lax.dynamic_index_in_dim(halves, parity, 2, keepdims=False).reshape(
        local_views, channels // 2, pixels
    )
    gathered = lax.all_gather(mine, "view", axis=0, tiled=True)
    other = lax.ppermute(gathered, "plane", swap)
    shape5 = (all_views, blocks, 1, share, pixels)
    first = jnp.where(parity == 0, gathered, other).reshape(shape5)
    second = jnp.where(parity == 0, other, gathered).reshape(shape5)
    all_maps = jnp.concatenate([first, second], axis=2).reshape(all_views, channels, pixels)

    cot = cotangent.reshape(local_views, planes, G, pixels // (2 * LANE), 2, LANE)
    cot = cot.transpose(1, 2, 4, 0, 3, 5).reshape(planes, packed_rows, packed_width)
    cot_ext = jnp.concatenate(
        [
            lax.ppermute(cot[planes - 1 :], "plane", up),
            cot,
            lax.ppermute(cot[:1], "plane", down),
        ],
        axis=0,
    )

    src_own = lax.dynamic_slice_in_dim(sources, own_index * local_views, local_views, 0)
    rows, refx = pl.pallas_call(
        assemble_kernel,
        out_shape=(
            jax.ShapeDtypeStruct((channels * pairs, pixels), bf16),
            jax.ShapeDtypeStruct((pixels // LANE, channels * SUB, LANE), f32),
        ),
        in_specs=[SMEM(), pl.BlockSpec(), pl.BlockSpec()],
        scratch_shapes=[pltpu.VMEM((pixels // LANE, channels * pairs, LANE), f32)],
        compiler_params=params(),
        name="assemble",
    )(src_own, all_maps, features)

    warped_s = jax.ShapeDtypeStruct((planes, channels * pairs, pixels), bf16)
    corr_s = jax.ShapeDtypeStruct((planes, G, pairs, pixels), f32)
    sig_s = jax.ShapeDtypeStruct((planes, pairs, pixels), f32)
    rden_s = jax.ShapeDtypeStruct((planes, SUB, pixels), f32)
    cost_s = jax.ShapeDtypeStruct((planes, packed_rows, packed_width), f32)
    saved = (warped_s, corr_s, sig_s, rden_s, cost_s)
    warped, corr, sig, rden, cost = pl.pallas_call(
        forward_kernel,
        out_shape=saved,
        grid=(planes,),
        in_specs=[SMEM(), whole(rows), whole(refx), per_plane(warp_weights.shape)],
        out_specs=tuple(per_plane(s.shape) for s in saved),
        scratch_shapes=[
            pltpu.VMEM((channels * pairs, 2 * LANE), f32) for _ in range(pixels // (2 * LANE))
        ],
        compiler_params=params(),
        name="forward",
    )(view_gate, rows, refx, warp_weights)

    cost_ext = jnp.concatenate(
        [
            lax.ppermute(cost[planes - 2 :], "plane", up),
            cost,
            lax.ppermute(cost[:2], "plane", down),
        ],
        axis=0,
    )
    regular, cost_grad = pl.pallas_call(
        conv_kernel,
        out_shape=(
            jax.ShapeDtypeStruct((planes, packed_rows, packed_width), bf16),
            jax.ShapeDtypeStruct((planes, packed_rows, packed_width), f32),
        ),
        in_specs=[SMEM(), pl.BlockSpec(), pl.BlockSpec()],
        scratch_shapes=[pltpu.VMEM((planes + 2, packed_rows, packed_width), f32)],
        compiler_params=params(),
        name="depth_conv",
    )(depth_kernel, cost_ext, cot_ext)
    regular = (
        regular.reshape(planes, G, 2, local_views, pixels // (2 * LANE), LANE)
        .transpose(3, 0, 1, 4, 2, 5)
        .reshape(local_views, planes, G, pixels)
    )

    place = jnp.stack([own_index, parity]).astype(jnp.int32)
    keep, send = pl.pallas_call(
        backward_kernel,
        out_shape=(
            jax.ShapeDtypeStruct((all_views, blocks, share, pixels), f32),
            jax.ShapeDtypeStruct((all_views, blocks * share, pixels), bf16),
        ),
        grid=(planes,),
        in_specs=[SMEM(), SMEM(), SMEM(), whole(refx), per_plane(warp_weights.shape)]
        + [per_plane(s.shape) for s in saved]
        + [per_plane(cost_grad.shape)],
        out_specs=(
            pl.BlockSpec((all_views, blocks, share, pixels), lambda d: (0, 0, 0, 0)),
            pl.BlockSpec((all_views, blocks * share, pixels), lambda d: (0, 0, 0)),
        ),
        scratch_shapes=[
            pltpu.VMEM((channels * pairs, pixels), bf16),
            pltpu.VMEM((pixels // LANE, channels * pairs, LANE), f32),
            pltpu.VMEM((pixels // LANE, channels * SUB, LANE), f32),
            pltpu.VMEM((all_views, channels, pixels), f32),
        ],
        compiler_params=params(),
        name="backward",
    )(view_gate, src_own, place, refx, warp_weights, warped, corr, sig, rden, cost, cost_grad)

    received = lax.ppermute(send, "plane", swap)
    paired = keep + received.reshape(keep.shape).astype(f32)
    outbound = (
        paired.reshape(view_count, local_views, blocks, share, pixels)
        .transpose(0, 2, 1, 3, 4)
        .reshape(view_count * blocks, local_views, share, pixels)
        .astype(bf16)
    )
    fellows = [
        [v * plane_count + 2 * b + side for v in range(view_count) for b in range(blocks)]
        for side in range(2)
    ]
    inbound = lax.all_to_all(
        outbound, ("view", "plane"), 0, 0, axis_index_groups=fellows, tiled=True
    )
    own_share = jnp.sum(inbound.astype(f32), axis=0)
    return (regular, lax.all_gather(own_share, "plane", axis=1, tiled=True))


def solution(mesh):
    in_specs = (
        P("view", None, None),
        P(),
        P("plane", None, None),
        P(),
        P(),
        P("view", "plane", None, None),
    )
    out_specs = (P("view", "plane", None, None), P("view", None, None))
    return jax.shard_map(shards, mesh=mesh, in_specs=in_specs, out_specs=out_specs, check_vma=False)
```

profile of v0, /device:TPU:0, one launch (start us, length us, event | category | flops | bytes accessed | tf_op | source)
XLA Modules:
  0.0 129.7 jit_solution(12458515063538321863)
XLA Ops:
  0.6 0.0 copy-start
  0.7 0.8 dynamic-slice_bitcast_fusion
  1.5 33.0 %all_gather.6 = bf16[32,16,512]{2,1,0:T(8,128)(2,1)S(1)} all-gather(bf16[4,16,512]{2,1,0:T(8,128)(2,1)S(1)} %dynamic-slice_bitcast_fusion), channel_id=1, replica_groups=mesh['view'=8,'plane'=4] {'view'}, dimensions={0}, use_global_device_ids=true | all-gather | bytes 589824 | tf_op jit(solution)/shard_map/all_gather | solution.py:316
  34.5 0.0 collective-permute-start
  34.5 1.4 %copy.25 = bf16[4,12,8,2,2,128]{5,3,0,4,2,1:T(2,128)(2,1)S(1)} copy(bf16[4,12,8,2,2,128]{5,2,4,3,1,0:T(8,128)(2,1)} %bitcast.35) | data formatting | bytes 786432 | tf_op jit(solution)/shard_map/reshape | solution.py:323
  36.0 1.3 collective-permute-start.4
  37.3 0.6 slice.21
  37.9 3.0 %collective-permute-start.3 = (bf16[1,64,256]{2,1,0:T(8,128)(2,1)}, bf16[1,64,256]{2,1,0:T(8,128)(2,1)S(1)}, u32[]{:S(2)}, u32[]{:S(2)}) collective-permute-start(bf16[1,64,256]{2,1,0:T(8,128)(2,1)} %slice.21), channel_id=1, source_target_pairs={{0,1},{1,2},{2,3},{4,5},{5,6},{6,7},{8,9},{9,10},{10,11},{12,13},{... | collective-permute-start | bytes 98312 | tf_op jit(solution)/shard_map/ppermute | solution.py:327
  40.9 0.0 copy-done
  40.9 0.1 constant_dynamic-slice_fusion
  41.0 0.1 copy.22.src_ref
  41.1 0.0 collective-permute-done
  41.1 0.1 select_bitcast_fusion.1
  41.2 0.0 copy-start.2
  41.2 0.1 pad_maximum_fusion
  41.3 0.0 copy-start.4
  41.3 0.0 copy-start.1
  41.3 0.9 copy-done.1
  42.2 1.5 %assemble.1 = (bf16[1280,512]{1,0:T(8,128)(2,1)S(1)}, f32[4,256,128]{2,1,0:T(8,128)S(1)}) custom-call(s32[4,10]{1,0:T(4,128)S(1)} %copy.22.src_ref, bf16[32,32,512]{2,1,0:T(8,128)(2,1)S(1)} %bitcast.29, bf16[4,32,512]{2,1,0:T(8,128)(2,1)S(1)} %copy-done.1), custom_call_target="tpu_custom_call" | custom-call | tf_op jit(solution)/shard_map/assemble/pallas_call | solution.py:335
  43.7 0.0 copy-start.3
  43.8 0.6 copy-done.3
  44.4 16.9 %forward.1 = (bf16[12,1280,512]{2,1,0:T(8,128)(2,1)}, f32[12,8,40,512]{3,2,1,0:T(8,128)}, f32[12,40,512]{2,1,0:T(8,128)S(1)}, f32[12,8,512]{2,1,0:T(8,128)S(1)}, f32[12,64,256]{2,1,0:T(8,128)S(1)}) custom-call(f32[8]{0:T(128)S(1)} %copy-done.3, bf16[1280,512]{1,0:T(8,128)(2,1)S(1)} %get-tuple-element.13.rows_ref, ...), custom_call_target="tpu_custom_call" | custom-call | tf_op jit(solution)/shard_map/forward/pallas_call | solution.py:353
  61.3 0.7 fusion.1
  62.0 1.3 collective-permute-start.2
  63.3 4.9 %collective-permute-start.1 = (f32[2,64,256]{2,1,0:T(8,128)}, f32[2,64,256]{2,1,0:T(8,128)}, u32[]{:S(2)}, u32[]{:S(2)}) collective-permute-start(f32[2,64,256]{2,1,0:T(8,128)} %get-tuple-element.26), channel_id=1, source_target_pairs={{0,1},{1,2},{2,3},{4,5},{5,6},{6,7},{8,9},{9,10},{10,11},{12,13},{... | collective-permute-start | bytes 393224 | tf_op jit(solution)/shard_map/ppermute | solution.py:368
  68.3 0.1 pad_add_fusion.place_ref
  68.3 0.3 reshape.47
  68.6 0.0 collective-permute-done.4
  68.6 0.0 collective-permute-done.3
  68.6 0.1 pad_maximum_fusion.2.cot_ref
  68.7 0.0 collective-permute-done.2
  68.7 0.2 collective-permute-done.1
  68.9 1.0 pad_maximum_fusion.1.cost_ref
  69.9 0.0 copy-done.2
  69.9 5.7 %depth_conv.1 = (bf16[12,64,256]{2,1,0:T(8,128)(2,1)S(1)}, f32[12,64,256]{2,1,0:T(8,128)S(1)}) custom-call(f32[3,8,8]{2,1,0:T(8,128)S(1)} %copy-done.2, f32[16,64,256]{2,1,0:T(8,128)S(1)} %pad_maximum_fusion.1.cost_ref, bf16[14,64,256]{2,1,0:T(8,128)(2,1)S(1)} %pad_maximum_fusion.2.cot_ref), custom_call_target="tpu_custom_call" | custom-call | tf_op jit(solution)/shard_map/depth_conv/pallas_call | solution.py:374
  75.6 0.0 copy-done.4
  75.6 18.9 %backward.1 = (f32[32,2,8,512]{3,2,1,0:T(8,128)S(1)}, bf16[32,16,512]{2,1,0:T(8,128)(2,1)S(1)}) custom-call(f32[8]{0:T(128)S(1)} %copy-done.4, s32[4,10]{1,0:T(4,128)S(1)} %copy.22.src_ref, s32[2]{0:T(128)S(1)} %pad_add_fusion.place_ref, f32[4,256,128]{2,1,0:T(8,128)S(1)} %get-tuple-element.14.refx_ref, bf16[12,512,512]{2,1,0:T(8,128)(2,1)} %w_ref.3, ...), custom_call_target="tpu_custom_call" | custom-call | tf_op jit(solution)/shard_map/backward/pallas_call | solution.py:392
  94.5 2.7 %collective-permute-start.5 = (bf16[32,16,512]{2,1,0:T(8,128)(2,1)S(1)}, bf16[32,16,512]{2,1,0:T(8,128)(2,1)S(1)}, u32[]{:S(2)}, u32[]{:S(2)}) collective-permute-start(bf16[32,16,512]{2,1,0:T(8,128)(2,1)S(1)} %get-tuple-element.23), channel_id=1, source_target_pairs={{0,1},{1,0},{2,3},{3,2},{4,5},{5,4},{6,7},{7,6},{8,9},{9,8},{10,11... | collective-permute-start | bytes 1572872 | tf_op jit(solution)/shard_map/ppermute | solution.py:416
  97.2 1.5 %collective-permute-done.5 = bf16[32,16,512]{2,1,0:T(8,128)(2,1)S(1)} collective-permute-done((bf16[32,16,512]{2,1,0:T(8,128)(2,1)S(1)}, bf16[32,16,512]{2,1,0:T(8,128)(2,1)S(1)}, u32[]{:S(2)}, u32[]{:S(2)}) %collective-permute-start.5) | collective-permute-done | bytes 524320 | tf_op jit(solution)/shard_map/ppermute | solution.py:416
  98.8 0.2 fusion
  99.0 0.8 copy.21
  99.8 7.9 %all-to-all-start = ((bf16[16,4,8,512]{3,2,1,0:T(8,128)(2,1)}), bf16[16,4,8,512]{3,2,1,0:T(8,128)(2,1)S(1)}, u32[]{:S(2)}, u32[]{:S(2)}) async-start(bf16[16,4,8,512]{3,2,1,0:T(8,128)(2,1)} %bitcast.16), calls=%async_computation | async-start | bytes 1048576 | tf_op jit(solution)/shard_map/all_to_all | solution.py:428
  107.8 0.1 reshape.48
  107.9 0.8 copy.20
  108.7 14.4 %all-to-all-done = bf16[16,4,8,512]{3,2,1,0:T(8,128)(2,1)S(1)} async-done(((bf16[16,4,8,512]{3,2,1,0:T(8,128)(2,1)}), bf16[16,4,8,512]{3,2,1,0:T(8,128)(2,1)S(1)}, u32[]{:S(2)}, u32[]{:S(2)}) %all-to-all-start) | async-done | bytes 524320 | tf_op jit(solution)/shard_map/all_to_all | solution.py:428
  123.2 0.1 convert_reduce_fusion
  123.2 5.8 %all_gather.7 = f32[4,32,512]{2,1,0:T(8,128)S(1)} all-gather(f32[4,8,512]{2,1,0:T(8,128)S(1)} %convert_reduce_fusion), channel_id=1, replica_groups=mesh['view'=8,'plane'=4] {'plane'}, dimensions={1}, use_global_device_ids=true | all-gather | bytes 327680 | tf_op jit(solution)/shard_map/all_gather | solution.py:432
  129.0 0.7 copy.27
  (2 shorter events, 0.1 us)
Async XLA Ops:
  0.6 40.3 %copy-start = (s32[32,10]{0,1:T(8,128)S(1)}, s32[32,10]{0,1:T(8,128)}, u32[]{:S(2)}) copy-start(s32[32,10]{0,1:T(8,128)} %param.7) | copy-start | bytes 3844
  34.5 6.6 %collective-permute-start = (bf16[32,16,512]{2,1,0:T(8,128)(2,1)S(1)}, bf16[32,16,512]{2,1,0:T(8,128)(2,1)S(1)}, u32[]{:S(2)}, u32[]{:S(2)}) collective-permute-start(bf16[32,16,512]{2,1,0:T(8,128)(2,1)S(1)} %all_gather.6), channel_id=1, source_target_pairs={{0,1},{1,0},{2,3},{3,2},{4,5},{5,4},{6,7},{7,6},{8,9},{9,8},{10,11... | collective-permute-start | bytes 1572872 | tf_op jit(solution)/shard_map/ppermute | solution.py:317
  36.0 32.6 %collective-permute-start.4 = (bf16[1,64,256]{2,1,0:T(8,128)(2,1)S(1)}, bf16[1,64,256]{2,1,0:T(8,128)(2,1)S(1)}, u32[]{:S(2)}, u32[]{:S(2)}) collective-permute-start(bf16[1,64,256]{2,1,0:T(8,128)(2,1)S(1)} %slice.23), channel_id=1, source_target_pairs={{1,0},{2,1},{3,2},{5,4},{6,5},{7,6},{9,8},{10,9},{11,10},{13,12},{... | collective-permute-start | bytes 98312 | tf_op jit(solution)/shard_map/ppermute | solution.py:329
  37.9 30.7 %collective-permute-start.3 = (bf16[1,64,256]{2,1,0:T(8,128)(2,1)}, bf16[1,64,256]{2,1,0:T(8,128)(2,1)S(1)}, u32[]{:S(2)}, u32[]{:S(2)}) collective-permute-start(bf16[1,64,256]{2,1,0:T(8,128)(2,1)} %slice.21), channel_id=1, source_target_pairs={{0,1},{1,2},{2,3},{4,5},{5,6},{6,7},{8,9},{9,10},{10,11},{12,13},{... | collective-permute-start | bytes 98312 | tf_op jit(solution)/shard_map/ppermute | solution.py:327
  41.2 28.7 %copy-start.2 = (f32[3,8,8]{2,1,0:T(8,128)S(1)}, f32[3,8,8]{2,1,0:T(8,128)}, u32[]{:S(2)}) copy-start(f32[3,8,8]{2,1,0:T(8,128)} %taps_ref.1) | copy-start | bytes 2308
  41.3 34.3 %copy-start.4 = (f32[8]{0:T(128)S(1)}, f32[8]{0:T(128)}, u32[]{:S(2)}) copy-start(f32[8]{0:T(128)} %gate_ref.3) | copy-start | bytes 100
  41.3 0.9 copy-start.1
  43.7 0.7 copy-start.3
  62.0 6.6 %collective-permute-start.2 = (f32[2,64,256]{2,1,0:T(8,128)}, f32[2,64,256]{2,1,0:T(8,128)S(1)}, u32[]{:S(2)}, u32[]{:S(2)}) collective-permute-start(f32[2,64,256]{2,1,0:T(8,128)} %get-tuple-element.27), channel_id=1, source_target_pairs={{1,0},{2,1},{3,2},{5,4},{6,5},{7,6},{9,8},{10,9},{11,10},{13,12},{... | collective-permute-start | bytes 393224 | tf_op jit(solution)/shard_map/ppermute | solution.py:370
  63.3 5.6 %collective-permute-start.1 = (f32[2,64,256]{2,1,0:T(8,128)}, f32[2,64,256]{2,1,0:T(8,128)}, u32[]{:S(2)}, u32[]{:S(2)}) collective-permute-start(f32[2,64,256]{2,1,0:T(8,128)} %get-tuple-element.26), channel_id=1, source_target_pairs={{0,1},{1,2},{2,3},{4,5},{5,6},{6,7},{8,9},{9,10},{10,11},{12,13},{... | collective-permute-start | bytes 393224 | tf_op jit(solution)/shard_map/ppermute | solution.py:368
  94.5 4.3 %collective-permute-start.5 = (bf16[32,16,512]{2,1,0:T(8,128)(2,1)S(1)}, bf16[32,16,512]{2,1,0:T(8,128)(2,1)S(1)}, u32[]{:S(2)}, u32[]{:S(2)}) collective-permute-start(bf16[32,16,512]{2,1,0:T(8,128)(2,1)S(1)} %get-tuple-element.23), channel_id=1, source_target_pairs={{0,1},{1,0},{2,3},{3,2},{4,5},{5,4},{6,7},{7,6},{8,9},{9,8},{10,11... | collective-permute-start | bytes 1572872 | tf_op jit(solution)/shard_map/ppermute | solution.py:416
  99.8 23.3 %all-to-all-start = ((bf16[16,4,8,512]{3,2,1,0:T(8,128)(2,1)}), bf16[16,4,8,512]{3,2,1,0:T(8,128)(2,1)S(1)}, u32[]{:S(2)}, u32[]{:S(2)}) async-start(bf16[16,4,8,512]{3,2,1,0:T(8,128)(2,1)} %bitcast.16), calls=%async_computation | async-start | bytes 1048576 | tf_op jit(solution)/shard_map/all_to_all | solution.py:428
where the time goes:
time: 131 us; the launch traced here: 130 us
  Pallas kernels  43 us (33%)
  blocking collectives  38.8 us (30%)
  starting transfers between devices  21.2 us (16%)
  waiting for transfers between devices  16.2 us (12%)
  local copies, waits for them, and re-layouts  8.12 us (6%)
  other arithmetic  1.56 us (1%)
    all_gather x1, blocking collectives, shards(): gathered = lax.all_gather(mine, 'view', axis=0, tiled=True)  33 us
    pallas_call x1, Pallas kernels, shards(): pl.pallas_call(backward_kernel, out_shape=(jax.ShapeDtypeStruct((all_view...  18.9 us
    pallas_call x1, Pallas kernels, shards(): pl.pallas_call(forward_kernel, out_shape=saved, grid=(planes,), in_specs=...  16.9 us
    all_to_all x1, waiting for transfers between devices, shards(): lax.all_to_all(outbound, ('view', 'plane'), 0, 0, axis_index_groups=fello...  14.4 us
    all_to_all x1, starting transfers between devices, shards(): lax.all_to_all(outbound, ('view', 'plane'), 0, 0, axis_index_groups=fello...  7.93 us
    all_gather x1, blocking collectives, shards(): return (regular, lax.all_gather(own_share, 'plane', axis=1, tiled=True))  5.79 us
    pallas_call x1, Pallas kernels, shards(): pl.pallas_call(conv_kernel, out_shape=(jax.ShapeDtypeStruct((planes, pack...  5.7 us
    ppermute x1, starting transfers between devices, shards(): lax.ppermute(cost[planes - 2:], 'plane', up)  4.93 us
  transfers between devices with their start and end apart: 7, of which 3 were waited for; matrix products, arithmetic and copies ran while one was open for 3% of the time, Pallas kernels for 14%

commit v1 on v0

v1 whole, which is shorter than its diff:
```python
import functools

import jax
import jax.numpy as jnp
from jax import lax
from jax.experimental import pallas as pl
from jax.experimental.pallas import tpu as pltpu
from jax.sharding import PartitionSpec as P

G = 8
GC = 4
SUB = 8
LANE = 128
VMEM_LIMIT = 48 * 1024 * 1024
NT = (((1,), (1,)), ((), ()))


def params(**extra):
    return pltpu.CompilerParams(vmem_limit_bytes=VMEM_LIMIT, **extra)


def low_half():
    return lax.broadcasted_iota(jnp.int32, (SUB, LANE), 0) < SUB // 2


def swap_halves(tile):
    return pltpu.roll(tile, SUB // 2, 0)


def spread(tile, half, low):
    other = swap_halves(tile)
    return jnp.where(low, tile, other) if half == 0 else jnp.where(low, other, tile)


def assemble_kernel(src_ref, place_ref, mine_ref, other_ref, own_ref, rows_ref, refx_ref, scratch):
    local_views, per_view = src_ref.shape
    channels = own_ref.shape[1]
    tiles, _, _ = scratch.shape
    pairs = local_views * per_view
    share = SUB
    blocks = mine_ref.shape[1] // share
    own_index = place_ref[0]
    parity = place_ref[1]
    for pair in range(pairs):
        view = src_ref[pair % local_views, pair // local_views]
        slot = ((view // local_views) ^ own_index) * local_views + view % local_views
        for tile in range(tiles):
            lanes = pl.ds(tile * LANE, LANE)
            for side, ref in ((parity, mine_ref), (1 - parity, other_ref)):
                maps = ref[slot, :, lanes].astype(jnp.float32)
                for block in range(blocks):
                    first = (2 * block + side) * (share * pairs) + pair
                    scratch[tile, pl.ds(first, share, stride=pairs), :] = maps[
                        block * share : (block + 1) * share
                    ]
    for tile in range(tiles):
        lanes = pl.ds(tile * LANE, LANE)
        rows_ref[:, lanes] = scratch[tile].astype(jnp.bfloat16)
        for view in range(local_views):
            own = own_ref[view, :, lanes].astype(jnp.float32)
            for copy in range(SUB // local_views):
                refx_ref[tile, pl.ds(copy * local_views + view, channels, stride=SUB), :] = own


def forward_body(
    gate_ref, rows_ref, refx_ref, w_ref, warped_ref, corr_ref, sig_ref, rden_ref, cost_ref, chunks
):
    pairs = corr_ref.shape[2]
    groups = corr_ref.shape[1]
    tiles = pairs // SUB
    low = low_half()
    width = 2 * LANE
    for index, chunk in enumerate(chunks):
        chunk[...] = lax.dot_general(
            rows_ref[...],
            w_ref[0, index * width : (index + 1) * width, :],
            NT,
            preferred_element_type=jnp.float32,
        )
    for index, chunk in enumerate(chunks):
        warped_ref[0, :, index * width : (index + 1) * width] = chunk[...].astype(jnp.bfloat16)
        cost_pair = []
        for half in range(2):
            inner = pl.ds(half * LANE, LANE)
            lanes = pl.ds(index * width + half * LANE, LANE)
            logits = jnp.zeros((tiles, SUB, LANE), jnp.float32)
            for g in range(groups):
                total = None
                for j in range(GC):
                    c = g * GC + j
                    part = (
                        chunk[pl.ds(c * pairs, pairs), inner].reshape(tiles, SUB, LANE)
                        * refx_ref[2 * index + half, pl.ds(c * SUB, SUB), :][None]
                    )
                    total = part if total is None else total + part
                corr = total * (1.0 / GC)
                corr_ref[0, g, :, lanes] = corr.reshape(pairs, LANE)
                logits = logits + corr * gate_ref[g]
            sig = jax.nn.sigmoid(logits)
            sig_ref[0, :, lanes] = sig.reshape(pairs, LANE)
            visible = 0.5 + sig
            den = jnp.sum(visible, axis=0)
            rden = 1.0 / (den + swap_halves(den))
            rden_ref[0, :, lanes] = rden
            costs = []
            for g in range(groups):
                num = jnp.sum(
                    visible * corr_ref[0, g, :, lanes].reshape(tiles, SUB, LANE), axis=0
                )
                costs.append((num + swap_halves(num)) * rden)
            cost_pair.append(costs)
        for g in range(groups):
            cost_ref[0, index, pl.ds(g * SUB, SUB), :] = jnp.where(
                low, cost_pair[0][g], cost_pair[1][g]
            )


def pack_planes(array_ref, plane, out_ref, slot):
    local_views, _, groups, pixels = array_ref.shape
    for view in range(local_views):
        for tile in range(pixels // LANE):
            first = (tile % 2) * local_views + view
            out_ref[slot, tile // 2, pl.ds(first, groups, stride=SUB), :] = array_ref[
                view, plane, :, pl.ds(tile * LANE, LANE)
            ].astype(jnp.float32)


def edge_kernel(
    gate_ref,
    rows_ref,
    refx_ref,
    w_ref,
    cot_ref,
    warped_ref,
    corr_ref,
    sig_ref,
    rden_ref,
    up_ref,
    down_ref,
    *scratch,
):
    cost, *chunks = scratch
    step = pl.program_id(0)
    last = cot_ref.shape[1] - 1
    forward_body(
        gate_ref, rows_ref, refx_ref, w_ref, warped_ref, corr_ref, sig_ref, rden_ref, cost, chunks
    )

    @pl.when(step < 2)
    def _():
        down_ref[step] = cost[0]

    @pl.when(step >= 2)
    def _():
        up_ref[step - 2] = cost[0]

    @pl.when(step == 0)
    def _():
        pack_planes(cot_ref, 0, down_ref, 2)
        pack_planes(cot_ref, last, up_ref, 2)


def inner_kernel(
    gate_ref,
    rows_ref,
    refx_ref,
    w_ref,
    warped_in,
    corr_in,
    sig_in,
    rden_in,
    warped_ref,
    corr_ref,
    sig_ref,
    rden_ref,
    cost_ref,
    *chunks,
):
    forward_body(
        gate_ref,
        rows_ref,
        refx_ref,
        w_ref,
        warped_ref,
        corr_ref,
        sig_ref,
        rden_ref,
        cost_ref,
        chunks,
    )


def conv_kernel(
    taps_ref,
    below_ref,
    down_ref,
    inner_ref,
    up_ref,
    above_ref,
    cot_ref,
    regular_ref,
    cost_ref,
    grad_ref,
    cost,
    cot,
    slope,
    smooth,
):
    planes = grad_ref.shape[0]
    local_views, _, groups, pixels = cot_ref.shape
    cost[0:2] = below_ref[0:2]
    cost[2:4] = down_ref[0:2]
    cost[4:planes] = inner_ref[...]
    cost[planes : planes + 2] = up_ref[0:2]
    cost[planes + 2 : planes + 4] = above_ref[0:2]
    cost_ref[...] = cost[2 : planes + 2]
    cot[0] = below_ref[2]
    cot[planes + 1] = above_ref[2]

    def pack_one(plane, carry):
        pack_planes(cot_ref, plane, cot, plane + 1)
        return carry

    lax.fori_loop(0, planes, pack_one, 0)

    def mix(source, tap):
        results = []
        for a in range(G):
            total = None
            for k in range(3):
                for b in range(G):
                    part = source(k, b) * tap(k, a, b)
                    total = part if total is None else total + part
            results.append(total)
        return jnp.concatenate(results, axis=1)

    def forward_plane(plane, carry):
        pre = mix(
            lambda k, g: cost[plane + k, :, pl.ds(g * SUB, SUB), :],
            lambda k, o, g: taps_ref[k, o, g],
        )
        sig = jax.nn.sigmoid(pre)
        slope[plane] = cot[plane] * (sig * (1.0 + pre * (1.0 - sig)))
        smooth[plane] = pre * sig
        return carry

    lax.fori_loop(0, planes + 2, forward_plane, 0)

    def backward_plane(plane, carry):
        grad_ref[plane] = mix(
            lambda k, o: slope[plane + 2 - k, :, pl.ds(o * SUB, SUB), :],
            lambda k, g, o: taps_ref[k, o, g],
        )
        for view in range(local_views):
            for tile in range(pixels // LANE):
                first = (tile % 2) * local_views + view
                regular_ref[view, plane, :, pl.ds(tile * LANE, LANE)] = smooth[
                    plane + 1, tile // 2, pl.ds(first, groups, stride=SUB), :
                ].astype(jnp.bfloat16)
        return carry

    lax.fori_loop(0, planes, backward_plane, 0)


def backward_kernel(
    gate_ref,
    src_ref,
    place_ref,
    refx_ref,
    w_ref,
    warped_ref,
    corr_ref,
    sig_ref,
    rden_ref,
    cost_ref,
    grad_ref,
    keep_ref,
    send_ref,
    rows,
    acc,
    dref,
    dense,
):
    step = pl.program_id(0)
    pairs = corr_ref.shape[2]
    groups = corr_ref.shape[1]
    tiles = pairs // SUB
    pixels = corr_ref.shape[3]
    local_views, per_view = src_ref.shape
    channels = groups * GC
    low = low_half()

    @pl.when(step == 0)
    def _():
        acc[...] = jnp.zeros_like(acc)
        dref[...] = jnp.zeros_like(dref)

    for tile in range(pixels // LANE):
        lanes = pl.ds(tile * LANE, LANE)
        pack = tile // 2
        half = tile % 2
        rden = rden_ref[0, :, lanes]
        mixed = None
        num_grads = []
        for g in range(groups):
            grad = grad_ref[0, pack, pl.ds(g * SUB, SUB), :]
            part = grad * cost_ref[0, pack, pl.ds(g * SUB, SUB), :]
            mixed = part if mixed is None else mixed + part
            num_grads.append(spread(grad, half, low) * rden)
        den_grad = spread(mixed, half, low) * rden
        vis_grad = -den_grad[None]
        for g in range(groups):
            vis_grad = vis_grad + num_grads[g][None] * corr_ref[0, g, :, lanes].reshape(
                tiles, SUB, LANE
            )
        sig = sig_ref[0, :, lanes].reshape(tiles, SUB, LANE)
        logit_grad = vis_grad * (sig * (1.0 - sig)) * (1.0 / GC)
        visible = (0.5 + sig) * (1.0 / GC)
        for g in range(groups):
            corr_grad = visible * num_grads[g][None] + logit_grad * gate_ref[g]
            for j in range(0, GC, 2):
                c = g * GC + j
                span = pl.ds(c * pairs, 2 * pairs)
                both = jnp.concatenate(
                    [
                        (corr_grad * refx_ref[tile, pl.ds((c + i) * SUB, SUB), :][None]).reshape(
                            pairs, LANE
                        )
                        for i in range(2)
                    ],
                    axis=0,
                )
                rows[span, lanes] = both.astype(jnp.bfloat16)
                warped = (
                    warped_ref[0, span, lanes].astype(jnp.float32).reshape(2, tiles, SUB, LANE)
                )
                for i in range(2):
                    dref[tile, pl.ds((c + i) * SUB, SUB), :] += jnp.sum(
                        corr_grad * warped[i], axis=0
                    )
    for index in range(pixels // (2 * LANE)):
        product = jnp.dot(
            rows[...],
            w_ref[0, :, pl.ds(index * 2 * LANE, 2 * LANE)],
            preferred_element_type=jnp.float32,
        )
        for half in range(2):
            acc[2 * index + half] += product[:, half * LANE : (half + 1) * LANE]

    @pl.when(step == pl.num_programs(0) - 1)
    def _():
        own_index = place_ref[0]
        parity = place_ref[1]
        dense[...] = jnp.zeros_like(dense)
        for tile in range(pixels // LANE):
            lanes = pl.ds(tile * LANE, LANE)
            for view in range(local_views):
                total = dref[tile, pl.ds(view, channels, stride=SUB), :]
                for copy in range(1, SUB // local_views):
                    first = copy * local_views + view
                    total = total + dref[tile, pl.ds(first, channels, stride=SUB), :]
                dense[view, :, lanes] = total
        for pair in range(pairs):
            view = src_ref[pair % local_views, pair // local_views]
            slot = ((view // local_views) ^ own_index) * local_views + view % local_views
            for tile in range(pixels // LANE):
                dense[slot, :, pl.ds(tile * LANE, LANE)] += acc[
                    tile, pl.ds(pair, channels, stride=pairs), :
                ]
        share = SUB
        blocks = keep_ref.shape[1] // share

        def one_view(view, carry):
            kept = []
            sent = []
            for block in range(blocks):
                mine = pl.multiple_of((2 * block + parity) * share, share)
                theirs = pl.multiple_of((2 * block + 1 - parity) * share, share)
                kept.append(dense[view, pl.ds(mine, share), :])
                sent.append(dense[view, pl.ds(theirs, share), :])
            keep_ref[view] = jnp.concatenate(kept, axis=0)
            send_ref[view] = jnp.concatenate(sent, axis=0).astype(jnp.bfloat16)
            return carry

        lax.fori_loop(0, dense.shape[0], one_view, 0)


def combine_kernel(keep_ref, received_ref, own_ref, *out_refs):
    local_views = own_ref.shape[0]
    own_ref[...] = keep_ref[0:local_views] + received_ref[0:local_views].astype(jnp.float32)
    for index, out_ref in enumerate(out_refs):
        span = pl.ds((index + 1) * local_views, local_views)
        out_ref[...] = (keep_ref[span] + received_ref[span].astype(jnp.float32)).astype(
            jnp.bfloat16
        )


def per_plane(shape, plane):
    rank = len(shape)
    return pl.BlockSpec((1,) + tuple(shape[1:]), lambda d: (plane(d),) + (0,) * (rank - 1))


def fixed(shape):
    rank = len(shape)
    return pl.BlockSpec(tuple(shape), lambda d: (0,) * rank)


SMEM = functools.partial(pl.BlockSpec, memory_space=pltpu.SMEM)


def shards(features, sources, warp_weights, view_gate, depth_kernel, cotangent):
    view_count = lax.axis_size("view")
    plane_count = lax.axis_size("plane")
    own_index = lax.axis_index("view")
    plane_index = lax.axis_index("plane")
    local_views, channels, pixels = features.shape
    all_views, per_view = sources.shape
    pairs = local_views * per_view
    planes = warp_weights.shape[0]
    share = channels // plane_count
    blocks = plane_count // 2
    parity = plane_index % 2
    f32 = jnp.float32
    bf16 = jnp.bfloat16
    near = [(i, i ^ 1) for i in range(plane_count)]
    far = [(i, i ^ 2) for i in range(plane_count)]
    up = [(i, i + 1) for i in range(plane_count - 1)]
    down = [(i + 1, i) for i in range(plane_count - 1)]
    shape = jax.ShapeDtypeStruct

    halves = features.reshape(local_views, blocks, 2, share, pixels)
    mine = lax.dynamic_index_in_dim(halves, parity, 2, keepdims=False).reshape(
        local_views, channels // 2, pixels
    )

    def over_view(array, k):
        return lax.ppermute(array, "view", [(i, i ^ k) for i in range(view_count)])

    mine_all = jnp.concatenate(
        [mine] + [over_view(mine, k) for k in range(1, view_count)], axis=0
    )
    other_all = lax.ppermute(mine_all, "plane", near)

    src_own = lax.dynamic_slice_in_dim(sources, own_index * local_views, local_views, 0)
    place = jnp.stack([own_index, parity]).astype(jnp.int32)
    rows, refx = pl.pallas_call(
        assemble_kernel,
        out_shape=(
            shape((channels * pairs, pixels), bf16),
            shape((pixels // LANE, channels * SUB, LANE), f32),
        ),
        in_specs=[SMEM(), SMEM(), pl.BlockSpec(), pl.BlockSpec(), pl.BlockSpec()],
        scratch_shapes=[pltpu.VMEM((pixels // LANE, channels * pairs, LANE), f32)],
        compiler_params=params(),
        name="assemble",
    )(src_own, place, mine_all, other_all, features)

    packed = (pixels // (2 * LANE), G * SUB, LANE)
    saved = (
        shape((planes, channels * pairs, pixels), bf16),
        shape((planes, G, pairs, pixels), f32),
        shape((planes, pairs, pixels), f32),
        shape((planes, SUB, pixels), f32),
    )
    chunks = [
        pltpu.VMEM((channels * pairs, 2 * LANE), f32) for _ in range(pixels // (2 * LANE))
    ]

    def edge(d):
        return jnp.where(d < 2, d, planes - 4 + d)

    def inner(d):
        return d + 2

    fixed_specs = [SMEM(), fixed(rows.shape), fixed(refx.shape)]
    *edge_saved, up_load, down_load = pl.pallas_call(
        edge_kernel,
        out_shape=saved + (shape((3,) + packed, f32),) * 2,
        grid=(4,),
        in_specs=fixed_specs + [per_plane(warp_weights.shape, edge), fixed(cotangent.shape)],
        out_specs=tuple(per_plane(s.shape, edge) for s in saved) + (fixed((3,) + packed),) * 2,
        scratch_shapes=[pltpu.VMEM((1,) + packed, f32)] + chunks,
        compiler_params=params(),
        name="forward_edge",
    )(view_gate, rows, refx, warp_weights, cotangent)
    below = lax.ppermute(up_load, "plane", up)
    above = lax.ppermute(down_load, "plane", down)
    *saved_values, inner_cost = pl.pallas_call(
        inner_kernel,
        out_shape=saved + (shape((planes - 4,) + packed, f32),),
        grid=(planes - 4,),
        in_specs=fixed_specs
        + [per_plane(warp_weights.shape, inner)]
        + [pl.BlockSpec(memory_space=pl.ANY)] * 4,
        out_specs=tuple(per_plane(s.shape, inner) for s in saved)
        + (per_plane((planes - 4,) + packed, lambda d: d),),
        scratch_shapes=chunks,
        input_output_aliases={4: 0, 5: 1, 6: 2, 7: 3},
        compiler_params=params(),
        cost_estimate=pl.CostEstimate(
            flops=2 * channels * pairs * pixels * pixels * (planes - 4),
            bytes_accessed=40 * 1024 * 1024,
            transcendentals=0,
        ),
        name="forward_inner",
    )(view_gate, rows, refx, warp_weights, *edge_saved)

    regular, cost, cost_grad = pl.pallas_call(
        conv_kernel,
        out_shape=(
            shape(cotangent.shape, bf16),
            shape((planes,) + packed, f32),
            shape((planes,) + packed, f32),
        ),
        in_specs=[SMEM()] + [pl.BlockSpec()] * 6,
        scratch_shapes=[
            pltpu.VMEM((planes + 4,) + packed, f32),
            pltpu.VMEM((planes + 2,) + packed, f32),
            pltpu.VMEM((planes + 2,) + packed, f32),
            pltpu.VMEM((planes + 2,) + packed, f32),
        ],
        compiler_params=params(),
        name="depth_conv",
    )(depth_kernel, below, down_load, inner_cost, up_load, above, cotangent)

    def same(d):
        return d

    returned = (all_views, channels // 2, pixels)
    keep, send = pl.pallas_call(
        backward_kernel,
        out_shape=(shape(returned, f32), shape(returned, bf16)),
        grid=(planes,),
        in_specs=[SMEM(), SMEM(), SMEM(), fixed(refx.shape), per_plane(warp_weights.shape, same)]
        + [per_plane(s.shape, same) for s in saved]
        + [per_plane(cost.shape, same), per_plane(cost_grad.shape, same)],
        out_specs=(fixed(returned), fixed(returned)),
        scratch_shapes=[
            pltpu.VMEM((channels * pairs, pixels), bf16),
            pltpu.VMEM((pixels // LANE, channels * pairs, LANE), f32),
            pltpu.VMEM((pixels // LANE, channels * SUB, LANE), f32),
            pltpu.VMEM((all_views, channels, pixels), f32),
        ],
        compiler_params=params(),
        name="backward",
    )(view_gate, src_own, place, refx, warp_weights, *saved_values, cost, cost_grad)

    received = lax.ppermute(send, "plane", near)
    piece = (local_views, channels // 2, pixels)
    total, *pieces = pl.pallas_call(
        combine_kernel,
        out_shape=(shape(piece, f32),) + (shape(piece, bf16),) * (view_count - 1),
        compiler_params=params(),
        name="combine",
    )(keep, received)
    for k, part in enumerate(pieces):
        total = total + over_view(part, k + 1).astype(f32)
    total = total + lax.ppermute(total, "plane", far)
    other = lax.ppermute(total, "plane", near)
    cut = (local_views, blocks, 1, share, pixels)
    first = jnp.where(parity == 0, total, other).reshape(cut)
    second = jnp.where(parity == 0, other, total).reshape(cut)
    feature_grads = jnp.concatenate([first, second], axis=2).reshape(features.shape)
    return (regular, feature_grads)


def solution(mesh):
    in_specs = (
        P("view", None, None),
        P(),
        P("plane", None, None),
        P(),
        P(),
        P("view", "plane", None, None),
    )
    out_specs = (P("view", "plane", None, None), P("view", None, None))
    return jax.shard_map(shards, mesh=mesh, in_specs=in_specs, out_specs=out_specs, check_vma=False)
```

time: 131 us -> 108 us (0.82)
  blocking collectives: 38.8 us -> 0 us
  starting transfers between devices: 21.2 us -> 30.8 us
  waiting for transfers between devices: 16.2 us -> 24.1 us
  local copies, waits for them, and re-layouts: 8.12 us -> 4.36 us
  Pallas kernels: 43 us -> 46.5 us
  other arithmetic: 1.56 us -> 0.2 us
    all_gather x2 -> x0, blocking collectives: 38.8 us -> none  [the longest x1 33 us: shards(): gathered = lax.all_gather(mine, 'view', axis=0, tiled=True)]
    ppermute x6 -> x20, waiting for transfers between devices: 1.77 us -> 24.1 us  [the longest x14 16.6 us: over_view(): return lax.ppermute(array, 'view', [(i, i ^ k) for i in range(view_count)])]
    ppermute x6 -> x20, starting transfers between devices: 13.3 us -> 30.8 us  [the longest x14 23.1 us: over_view(): return lax.ppermute(array, 'view', [(i, i ^ k) for i in range(view_count)])]
    all_to_all x1 -> x0, waiting for transfers between devices: 14.4 us -> none  [shards(): lax.all_to_all(outbound, ('view', 'plane'), 0, 0, axis_index_groups=fello...]
    all_to_all x1 -> x0, starting transfers between devices: 7.93 us -> none  [shards(): lax.all_to_all(outbound, ('view', 'plane'), 0, 0, axis_index_groups=fello...]
    pallas_call x4 -> x6, Pallas kernels: 43 us -> 46.5 us  [the longest x1 18.8 us: shards(): pl.pallas_call(backward_kernel, out_shape=(shape(returned, f32), shape(re...]
    reshape x4 -> x0, local copies, waits for them, and re-layouts: 2.55 us -> none  [the longest x1 1.36 us: shards(): cotangent.reshape(local_views, planes, G, pixels // (2 * LANE), 2, LANE)]
    slice x4 -> x0, local copies, waits for them, and re-layouts: 1.42 us -> none  [the longest x1 0.71 us: shards(): cost[planes - 2:]]
  transfers between devices with their start and end apart: 7 -> 20, of which waited for: 3 -> 9; matrix products, arithmetic and copies ran while one was open for 3% -> 0% of each run, Pallas kernels for 14% -> 11%
where the time goes in v1:
time: 108 us; the launch traced here: 107 us
  Pallas kernels  46.5 us (43%)
  starting transfers between devices  30.8 us (29%)
  waiting for transfers between devices  24.1 us (22%)
  local copies, waits for them, and re-layouts  4.36 us (4%)
    ppermute x14, starting transfers between devices, over_view(): return lax.ppermute(array, 'view', [(i, i ^ k) for i in range(view_count)])  23.1 us
    pallas_call x1, Pallas kernels, shards(): pl.pallas_call(backward_kernel, out_shape=(shape(returned, f32), shape(re...  18.8 us
    ppermute x14, waiting for transfers between devices, over_view(): return lax.ppermute(array, 'view', [(i, i ^ k) for i in range(view_count)])  16.6 us
    pallas_call x1, Pallas kernels, shards(): pl.pallas_call(inner_kernel, out_shape=saved + (shape((planes - 4,) + pac...  12.1 us
    pallas_call x1, Pallas kernels, shards(): pl.pallas_call(edge_kernel, out_shape=saved + (shape((3,) + packed, f32),...  7.09 us
    pallas_call x1, Pallas kernels, shards(): pl.pallas_call(conv_kernel, out_shape=(shape(cotangent.shape, bf16), shap...  6.83 us
    unnamed x22, local copies, waits for them, and re-layouts  3.56 us
    ppermute x1, waiting for transfers between devices, shards(): total = total + lax.ppermute(total, 'plane', far)  2.99 us
  transfers between devices with their start and end apart: 20, of which 9 were waited for; matrix products, arithmetic and copies ran while one was open for 0% of the time, Pallas kernels for 11%

profile of v1, /device:TPU:0, one launch (start us, length us, event | category | flops | bytes accessed | tf_op | source)
XLA Modules:
  0.0 106.9 jit_solution(5126754684729079078)
XLA Ops:
  0.6 0.0 copy-start
  0.7 0.9 constant_dynamic-update-slice_fusion.7
  1.5 3.0 %collective-permute-start = (bf16[4,16,512]{2,1,0:T(8,128)(2,1)S(1)}, bf16[4,16,512]{2,1,0:T(8,128)(2,1)S(1)}, u32[]{:S(2)}, u32[]{:S(2)}) collective-permute-start(bf16[4,16,512]{2,1,0:T(8,128)(2,1)S(1)} %get-tuple-element.55), channel_id=1, source_target_pairs={{0,4},{4,0},{8,12},{12,8},{16,20},{20,16},{24,28},{28,24},{1,5},{5... | collective-permute-start | bytes 196616 | tf_op jit(solution)/shard_map/ppermute | solution.py:437
  4.5 3.5 %collective-permute-start.6 = (bf16[4,16,512]{2,1,0:T(8,128)(2,1)S(1)}, bf16[4,16,512]{2,1,0:T(8,128)(2,1)S(1)}, u32[]{:S(2)}, u32[]{:S(2)}) collective-permute-start(bf16[4,16,512]{2,1,0:T(8,128)(2,1)S(1)} %get-tuple-element.55), channel_id=1, source_target_pairs={{0,28},{4,24},{8,20},{12,16},{16,12},{20,8},{24,4},{28,0},{1,29},{... | collective-permute-start | bytes 196616 | tf_op jit(solution)/shard_map/ppermute | solution.py:437
  8.1 0.1 collective-permute-start.5
  8.2 1.9 %collective-permute-start.4 = (bf16[4,16,512]{2,1,0:T(8,128)(2,1)S(1)}, bf16[4,16,512]{2,1,0:T(8,128)(2,1)S(1)}, u32[]{:S(2)}, u32[]{:S(2)}) collective-permute-start(bf16[4,16,512]{2,1,0:T(8,128)(2,1)S(1)} %get-tuple-element.55), channel_id=1, source_target_pairs={{0,20},{4,16},{8,28},{12,24},{16,4},{20,0},{24,12},{28,8},{1,21},{... | collective-permute-start | bytes 196616 | tf_op jit(solution)/shard_map/ppermute | solution.py:437
  10.1 2.1 %collective-permute-start.3 = (bf16[4,16,512]{2,1,0:T(8,128)(2,1)S(1)}, bf16[4,16,512]{2,1,0:T(8,128)(2,1)S(1)}, u32[]{:S(2)}, u32[]{:S(2)}) collective-permute-start(bf16[4,16,512]{2,1,0:T(8,128)(2,1)S(1)} %get-tuple-element.55), channel_id=1, source_target_pairs={{0,16},{4,20},{8,24},{12,28},{16,0},{20,4},{24,8},{28,12},{1,17},{... | collective-permute-start | bytes 196616 | tf_op jit(solution)/shard_map/ppermute | solution.py:437
  12.2 1.2 %collective-permute-start.1 = (bf16[4,16,512]{2,1,0:T(8,128)(2,1)S(1)}, bf16[4,16,512]{2,1,0:T(8,128)(2,1)S(1)}, u32[]{:S(2)}, u32[]{:S(2)}) collective-permute-start(bf16[4,16,512]{2,1,0:T(8,128)(2,1)S(1)} %get-tuple-element.55), channel_id=1, source_target_pairs={{0,8},{4,12},{8,0},{12,4},{16,24},{20,28},{24,16},{28,20},{1,9},{5... | collective-permute-start | bytes 196616 | tf_op jit(solution)/shard_map/ppermute | solution.py:437
  13.5 6.2 %collective-permute-done.1 = bf16[4,16,512]{2,1,0:T(8,128)(2,1)S(1)} collective-permute-done((bf16[4,16,512]{2,1,0:T(8,128)(2,1)S(1)}, bf16[4,16,512]{2,1,0:T(8,128)(2,1)S(1)}, u32[]{:S(2)}, u32[]{:S(2)}) %collective-permute-start.1) | collective-permute-done | bytes 65568 | tf_op jit(solution)/shard_map/ppermute | solution.py:437
  19.7 5.2 %collective-permute-done.2 = bf16[4,16,512]{2,1,0:T(8,128)(2,1)S(1)} collective-permute-done((bf16[4,16,512]{2,1,0:T(8,128)(2,1)S(1)}, bf16[4,16,512]{2,1,0:T(8,128)(2,1)S(1)}, u32[]{:S(2)}, u32[]{:S(2)}) %collective-permute-start.2) | collective-permute-done | bytes 65568 | tf_op jit(solution)/shard_map/ppermute | solution.py:437
  24.9 0.1 collective-permute-start.7
  25.0 0.1 constant_dynamic-slice_fusion
  25.1 0.1 copy.15.src_ref
  25.2 0.1 pad_add_fusion.place_ref
  25.3 1.6 %collective-permute-done.7.other_ref = bf16[32,16,512]{2,1,0:T(8,128)(2,1)S(1)} collective-permute-done((bf16[32,16,512]{2,1,0:T(8,128)(2,1)S(1)}, bf16[32,16,512]{2,1,0:T(8,128)(2,1)S(1)}, u32[]{:S(2)}, u32[]{:S(2)}) %collective-permute-start.7) | collective-permute-done | bytes 524320 | tf_op jit(solution)/shard_map/ppermute | solution.py:442
  26.9 0.9 copy-done.3
  27.8 1.6 %assemble.1 = (bf16[1280,512]{1,0:T(8,128)(2,1)S(1)}, f32[4,256,128]{2,1,0:T(8,128)S(1)}) custom-call(s32[4,10]{1,0:T(4,128)S(1)} %copy.15.src_ref, s32[2]{0:T(128)S(1)} %pad_add_fusion.place_ref, bf16[32,16,512]{2,1,0:T(8,128)(2,1)S(1)} %constant_dynamic-update-slice_fusion.mine_ref, bf16[32,16,512]{2,1,0:T(8,128)(2,1)S(1)} %collective-permute-done.7.other_ref, ...), custom_call_target="tpu_custom_call" | custom-call | tf_op jit(solution)/shard_map/assemble/pallas_call | solution.py:446
  29.4 0.0 copy-start.1
  29.4 1.0 copy-done.1
  30.4 0.7 copy-done.5
  31.0 7.1 %forward_edge.1 = (bf16[12,1280,512]{2,1,0:T(8,128)(2,1)}, f32[12,8,40,512]{3,2,1,0:T(8,128)}, f32[12,40,512]{2,1,0:T(8,128)S(1)}, f32[12,8,512]{2,1,0:T(8,128)S...) custom-call(f32[8]{0:T(128)S(1)} %copy-done.5, bf16[1280,512]{1,0:T(8,128)(2,1)S(1)} %get-tuple-element.28.rows_ref, ...), custom_call_target="tpu_custom_call" | custom-call | tf_op jit(solution)/shard_map/forward_edge/pallas_call | solution.py:476
  38.1 2.0 %collective-permute-start.8 = (f32[3,2,64,128]{3,2,1,0:T(8,128)S(1)}, f32[3,2,64,128]{3,2,1,0:T(8,128)S(1)}, u32[]{:S(2)}, u32[]{:S(2)}) collective-permute-start(f32[3,2,64,128]{3,2,1,0:T(8,128)S(1)} %get-tuple-element.30.up_ref), channel_id=1, source_target_pairs={{0,1},{1,2},{2,3},{4,5},{5,6},{6,7},{8,9},{9,10},{10,11},{12,13},{... | collective-permute-start | bytes 589832 | tf_op jit(solution)/shard_map/ppermute | solution.py:486
  40.2 1.3 %collective-permute-start.9 = (f32[3,2,64,128]{3,2,1,0:T(8,128)S(1)}, f32[3,2,64,128]{3,2,1,0:T(8,128)S(1)}, u32[]{:S(2)}, u32[]{:S(2)}) collective-permute-start(f32[3,2,64,128]{3,2,1,0:T(8,128)S(1)} %get-tuple-element.31.down_ref), channel_id=1, source_target_pairs={{1,0},{2,1},{3,2},{5,4},{6,5},{7,6},{9,8},{10,9},{11,10},{13,12},{... | collective-permute-start | bytes 589832 | tf_op jit(solution)/shard_map/ppermute | solution.py:487
  41.5 0.0 copy-start.2
  41.5 0.0 copy-start.4
  41.5 0.0 copy-start.6
  41.5 12.1 %forward_inner.1 = (bf16[12,1280,512]{2,1,0:T(8,128)(2,1)}, f32[12,8,40,512]{3,2,1,0:T(8,128)}, f32[12,40,512]{2,1,0:T(8,128)S(1)}, f32[12,8,512]{2,1,0:T(8,128)S(1)}, f32[8,2,64,128]{3,2,1,0:T(8,128)S(1)}) custom-call(f32[8]{0:T(128)S(1)} %copy-done.5, ...), custom_call_target="tpu_custom_call", output_to_operand_aliasing={{0}: (4, {}), {1}: (5, {}), {2}: (6, {}), {3}: (7, {})} | custom-call | flops 5368709120 | bytes 41943040 | tf_op jit(solution)/shard_map/forward_inner/pallas_call | solution.py:488
  53.6 6.8 %depth_conv.1 = (bf16[4,12,8,512]{3,2,1,0:T(8,128)(2,1)}, f32[12,2,64,128]{3,2,1,0:T(8,128)S(1)}, f32[12,2,64,128]{3,2,1,0:T(8,128)S(1)}) custom-call(f32[3,8,8]{2,1,0:T(8,128)S(1)} %copy-done.4, f32[3,2,64,128]{3,2,1,0:T(8,128)S(1)} %collective-permute-done.8.below_ref, f32[3,2,64,128]{3,2,1,0:T(8,128)S(1)} %get-tuple-element.31.down_ref, ...), custom_call_target="tpu_custom_call" | custom-call | tf_op jit(solution)/shard_map/depth_conv/pallas_call | solution.py:508
  60.4 18.8 %backward.1 = (f32[32,16,512]{2,1,0:T(8,128)S(1)}, bf16[32,16,512]{2,1,0:T(8,128)(2,1)S(1)}) custom-call(f32[8]{0:T(128)S(1)} %copy-done.6, s32[4,10]{1,0:T(4,128)S(1)} %copy.15.src_ref, s32[2]{0:T(128)S(1)} %pad_add_fusion.place_ref, f32[4,256,128]{2,1,0:T(8,128)S(1)} %get-tuple-element.29.refx_ref, bf16[12,512,512]{2,1,0:T(8,128)(2,1)} %w_ref.5, ...), custom_call_target="tpu_custom_call" | custom-call | tf_op jit(solution)/shard_map/backward/pallas_call | solution.py:530
  79.3 2.1 %collective-permute-start.10 = (bf16[32,16,512]{2,1,0:T(8,128)(2,1)S(1)}, bf16[32,16,512]{2,1,0:T(8,128)(2,1)S(1)}, u32[]{:S(2)}, u32[]{:S(2)}) collective-permute-start(bf16[32,16,512]{2,1,0:T(8,128)(2,1)S(1)} %get-tuple-element.45), channel_id=1, source_target_pairs={{0,1},{1,0},{2,3},{3,2},{4,5},{5,4},{6,7},{7,6},{8,9},{9,8},{10,11... | collective-permute-start | bytes 1572872 | tf_op jit(solution)/shard_map/ppermute | solution.py:548
  81.4 1.5 %collective-permute-done.10.received_ref = bf16[32,16,512]{2,1,0:T(8,128)(2,1)S(1)} collective-permute-done((bf16[32,16,512]{2,1,0:T(8,128)(2,1)S(1)}, bf16[32,16,512]{2,1,0:T(8,128)(2,1)S(1)}, u32[]{:S(2)}, u32[]{:S(2)}) %collective-permute-start.10) | collective-permute-done | bytes 524320 | tf_op jit(solution)/shard_map/ppermute | solution.py:548
  83.0 0.1 combine.1
  83.1 0.1 collective-permute-start.11
  83.2 0.6 collective-permute-start.12
  83.7 2.9 %collective-permute-start.13 = (bf16[4,16,512]{2,1,0:T(8,128)(2,1)S(1)}, bf16[4,16,512]{2,1,0:T(8,128)(2,1)S(1)}, u32[]{:S(2)}, u32[]{:S(2)}) collective-permute-start(bf16[4,16,512]{2,1,0:T(8,128)(2,1)S(1)} %get-tuple-element.49), channel_id=1, source_target_pairs={{0,12},{4,8},{8,4},{12,0},{16,28},{20,24},{24,20},{28,16},{1,13},{... | collective-permute-start | bytes 196616 | tf_op jit(solution)/shard_map/ppermute | solution.py:437
  86.7 1.6 %collective-permute-start.14 = (bf16[4,16,512]{2,1,0:T(8,128)(2,1)S(1)}, bf16[4,16,512]{2,1,0:T(8,128)(2,1)S(1)}, u32[]{:S(2)}, u32[]{:S(2)}) collective-permute-start(bf16[4,16,512]{2,1,0:T(8,128)(2,1)S(1)} %get-tuple-element.50), channel_id=1, source_target_pairs={{0,16},{4,20},{8,24},{12,28},{16,0},{20,4},{24,8},{28,12},{1,17},{... | collective-permute-start | bytes 196616 | tf_op jit(solution)/shard_map/ppermute | solution.py:437
  88.2 0.9 collective-permute-start.15
  89.1 3.4 %collective-permute-start.16 = (bf16[4,16,512]{2,1,0:T(8,128)(2,1)S(1)}, bf16[4,16,512]{2,1,0:T(8,128)(2,1)S(1)}, u32[]{:S(2)}, u32[]{:S(2)}) collective-permute-start(bf16[4,16,512]{2,1,0:T(8,128)(2,1)S(1)} %get-tuple-element.52), channel_id=1, source_target_pairs={{0,24},{4,28},{8,16},{12,20},{16,8},{20,12},{24,0},{28,4},{1,25},{... | collective-permute-start | bytes 196616 | tf_op jit(solution)/shard_map/ppermute | solution.py:437
  92.5 1.8 %collective-permute-start.17 = (bf16[4,16,512]{2,1,0:T(8,128)(2,1)S(1)}, bf16[4,16,512]{2,1,0:T(8,128)(2,1)S(1)}, u32[]{:S(2)}, u32[]{:S(2)}) collective-permute-start(bf16[4,16,512]{2,1,0:T(8,128)(2,1)S(1)} %get-tuple-element.53), channel_id=1, source_target_pairs={{0,28},{4,24},{8,20},{12,16},{16,12},{20,8},{24,4},{28,0},{1,29},{... | collective-permute-start | bytes 196616 | tf_op jit(solution)/shard_map/ppermute | solution.py:437
  94.3 2.1 %collective-permute-done.14 = bf16[4,16,512]{2,1,0:T(8,128)(2,1)S(1)} collective-permute-done((bf16[4,16,512]{2,1,0:T(8,128)(2,1)S(1)}, bf16[4,16,512]{2,1,0:T(8,128)(2,1)S(1)}, u32[]{:S(2)}, u32[]{:S(2)}) %collective-permute-start.14) | collective-permute-done | bytes 65568 | tf_op jit(solution)/shard_map/ppermute | solution.py:437
  96.4 2.0 %collective-permute-done.15 = bf16[4,16,512]{2,1,0:T(8,128)(2,1)S(1)} collective-permute-done((bf16[4,16,512]{2,1,0:T(8,128)(2,1)S(1)}, bf16[4,16,512]{2,1,0:T(8,128)(2,1)S(1)}, u32[]{:S(2)}, u32[]{:S(2)}) %collective-permute-start.15) | collective-permute-done | bytes 65568 | tf_op jit(solution)/shard_map/ppermute | solution.py:437
  98.4 1.2 %collective-permute-done.17 = bf16[4,16,512]{2,1,0:T(8,128)(2,1)S(1)} collective-permute-done((bf16[4,16,512]{2,1,0:T(8,128)(2,1)S(1)}, bf16[4,16,512]{2,1,0:T(8,128)(2,1)S(1)}, u32[]{:S(2)}, u32[]{:S(2)}) %collective-permute-start.17) | collective-permute-done | bytes 65568 | tf_op jit(solution)/shard_map/ppermute | solution.py:437
  99.6 0.1 convert_add_fusion
  99.7 2.0 %collective-permute-start.18 = (f32[4,16,512]{2,1,0:T(8,128)S(1)}, f32[4,16,512]{2,1,0:T(8,128)S(1)}, u32[]{:S(2)}, u32[]{:S(2)}) collective-permute-start(f32[4,16,512]{2,1,0:T(8,128)S(1)} %convert_add_fusion), channel_id=1, source_target_pairs={{0,2},{1,3},{2,0},{3,1},{4,6},{5,7},{6,4},{7,5},{8,10},{9,11},{10,... | collective-permute-start | bytes 393224 | tf_op jit(solution)/shard_map/ppermute | solution.py:558
  101.7 3.0 %collective-permute-done.18 = f32[4,16,512]{2,1,0:T(8,128)S(1)} collective-permute-done((f32[4,16,512]{2,1,0:T(8,128)S(1)}, f32[4,16,512]{2,1,0:T(8,128)S(1)}, u32[]{:S(2)}, u32[]{:S(2)}) %collective-permute-start.18) | collective-permute-done | bytes 131104 | tf_op jit(solution)/shard_map/ppermute | solution.py:558
  104.7 0.1 collective-permute-start.19
  104.8 1.3 %collective-permute-done.19 = f32[4,16,512]{2,1,0:T(8,128)S(1)} collective-permute-done((f32[4,16,512]{2,1,0:T(8,128)S(1)}, f32[4,16,512]{2,1,0:T(8,128)S(1)}, u32[]{:S(2)}, u32[]{:S(2)}) %collective-permute-start.19) | collective-permute-done | bytes 131104 | tf_op jit(solution)/shard_map/ppermute | solution.py:559
  106.2 0.7 copy.14
  (28 shorter events, 0.1 us)
Async XLA Ops:
  0.6 24.4 %copy-start = (s32[32,10]{0,1:T(8,128)S(1)}, s32[32,10]{0,1:T(8,128)}, u32[]{:S(2)}) copy-start(s32[32,10]{0,1:T(8,128)} %param.7) | copy-start | bytes 3844
  1.5 10.7 %collective-permute-start = (bf16[4,16,512]{2,1,0:T(8,128)(2,1)S(1)}, bf16[4,16,512]{2,1,0:T(8,128)(2,1)S(1)}, u32[]{:S(2)}, u32[]{:S(2)}) collective-permute-start(bf16[4,16,512]{2,1,0:T(8,128)(2,1)S(1)} %get-tuple-element.55), channel_id=1, source_target_pairs={{0,4},{4,0},{8,12},{12,8},{16,20},{20,16},{24,28},{28,24},{1,5},{5... | collective-permute-start | bytes 196616 | tf_op jit(solution)/shard_map/ppermute | solution.py:437
  4.5 20.3 %collective-permute-start.6 = (bf16[4,16,512]{2,1,0:T(8,128)(2,1)S(1)}, bf16[4,16,512]{2,1,0:T(8,128)(2,1)S(1)}, u32[]{:S(2)}, u32[]{:S(2)}) collective-permute-start(bf16[4,16,512]{2,1,0:T(8,128)(2,1)S(1)} %get-tuple-element.55), channel_id=1, source_target_pairs={{0,28},{4,24},{8,20},{12,16},{16,12},{20,8},{24,4},{28,0},{1,29},{... | collective-permute-start | bytes 196616 | tf_op jit(solution)/shard_map/ppermute | solution.py:437
  8.1 16.8 %collective-permute-start.5 = (bf16[4,16,512]{2,1,0:T(8,128)(2,1)S(1)}, bf16[4,16,512]{2,1,0:T(8,128)(2,1)S(1)}, u32[]{:S(2)}, u32[]{:S(2)}) collective-permute-start(bf16[4,16,512]{2,1,0:T(8,128)(2,1)S(1)} %get-tuple-element.55), channel_id=1, source_target_pairs={{0,24},{4,28},{8,16},{12,20},{16,8},{20,12},{24,0},{28,4},{1,25},{... | collective-permute-start | bytes 196616 | tf_op jit(solution)/shard_map/ppermute | solution.py:437
  8.2 16.7 %collective-permute-start.4 = (bf16[4,16,512]{2,1,0:T(8,128)(2,1)S(1)}, bf16[4,16,512]{2,1,0:T(8,128)(2,1)S(1)}, u32[]{:S(2)}, u32[]{:S(2)}) collective-permute-start(bf16[4,16,512]{2,1,0:T(8,128)(2,1)S(1)} %get-tuple-element.55), channel_id=1, source_target_pairs={{0,20},{4,16},{8,28},{12,24},{16,4},{20,0},{24,12},{28,8},{1,21},{... | collective-permute-start | bytes 196616 | tf_op jit(solution)/shard_map/ppermute | solution.py:437
  10.1 14.8 %collective-permute-start.3 = (bf16[4,16,512]{2,1,0:T(8,128)(2,1)S(1)}, bf16[4,16,512]{2,1,0:T(8,128)(2,1)S(1)}, u32[]{:S(2)}, u32[]{:S(2)}) collective-permute-start(bf16[4,16,512]{2,1,0:T(8,128)(2,1)S(1)} %get-tuple-element.55), channel_id=1, source_target_pairs={{0,16},{4,20},{8,24},{12,28},{16,0},{20,4},{24,8},{28,12},{1,17},{... | collective-permute-start | bytes 196616 | tf_op jit(solution)/shard_map/ppermute | solution.py:437
  12.2 7.4 %collective-permute-start.1 = (bf16[4,16,512]{2,1,0:T(8,128)(2,1)S(1)}, bf16[4,16,512]{2,1,0:T(8,128)(2,1)S(1)}, u32[]{:S(2)}, u32[]{:S(2)}) collective-permute-start(bf16[4,16,512]{2,1,0:T(8,128)(2,1)S(1)} %get-tuple-element.55), channel_id=1, source_target_pairs={{0,8},{4,12},{8,0},{12,4},{16,24},{20,28},{24,16},{28,20},{1,9},{5... | collective-permute-start | bytes 196616 | tf_op jit(solution)/shard_map/ppermute | solution.py:437
  19.7 5.2 %collective-permute-start.2 = (bf16[4,16,512]{2,1,0:T(8,128)(2,1)S(1)}, bf16[4,16,512]{2,1,0:T(8,128)(2,1)S(1)}, u32[]{:S(2)}, u32[]{:S(2)}) collective-permute-start(bf16[4,16,512]{2,1,0:T(8,128)(2,1)S(1)} %get-tuple-element.55), channel_id=1, source_target_pairs={{0,12},{4,8},{8,4},{12,0},{16,28},{20,24},{24,20},{28,16},{1,13},{... | collective-permute-start | bytes 196616 | tf_op jit(solution)/shard_map/ppermute | solution.py:437
  24.9 2.0 %collective-permute-start.7 = (bf16[32,16,512]{2,1,0:T(8,128)(2,1)S(1)}, bf16[32,16,512]{2,1,0:T(8,128)(2,1)S(1)}, u32[]{:S(2)}, u32[]{:S(2)}) collective-permute-start(bf16[32,16,512]{2,1,0:T(8,128)(2,1)S(1)} %constant_dynamic-update-slice_fusion.mine_ref), channel_id=1, source_target_pairs={{0,1},{1,0},{2,3},{3,2},{4,5},{5,4},{6,7},{7,6},{8,9},{9,8},{10,11... | collective-permute-start | bytes 1572872 | tf_op jit(solution)/shard_map/ppermute | solution.py:442
  26.9 0.9 copy-start.3
  29.4 1.0 copy-start.1
  30.4 0.7 copy-start.5
  38.1 15.4 %collective-permute-start.8 = (f32[3,2,64,128]{3,2,1,0:T(8,128)S(1)}, f32[3,2,64,128]{3,2,1,0:T(8,128)S(1)}, u32[]{:S(2)}, u32[]{:S(2)}) collective-permute-start(f32[3,2,64,128]{3,2,1,0:T(8,128)S(1)} %get-tuple-element.30.up_ref), channel_id=1, source_target_pairs={{0,1},{1,2},{2,3},{4,5},{5,6},{6,7},{8,9},{9,10},{10,11},{12,13},{... | collective-permute-start | bytes 589832 | tf_op jit(solution)/shard_map/ppermute | solution.py:486
  40.2 13.4 %collective-permute-start.9 = (f32[3,2,64,128]{3,2,1,0:T(8,128)S(1)}, f32[3,2,64,128]{3,2,1,0:T(8,128)S(1)}, u32[]{:S(2)}, u32[]{:S(2)}) collective-permute-start(f32[3,2,64,128]{3,2,1,0:T(8,128)S(1)} %get-tuple-element.31.down_ref), channel_id=1, source_target_pairs={{1,0},{2,1},{3,2},{5,4},{6,5},{7,6},{9,8},{10,9},{11,10},{13,12},{... | collective-permute-start | bytes 589832 | tf_op jit(solution)/shard_map/ppermute | solution.py:487
  41.5 12.1 %copy-start.2 = (bf16[4,12,8,512]{3,2,1,0:T(8,128)(2,1)S(1)}, bf16[4,12,8,512]{3,2,1,0:T(8,128)(2,1)}, u32[]{:S(2)}) copy-start(bf16[4,12,8,512]{3,2,1,0:T(8,128)(2,1)} %cot_ref.3) | copy-start | bytes 1179652
  41.5 12.1 %copy-start.4 = (f32[3,8,8]{2,1,0:T(8,128)S(1)}, f32[3,8,8]{2,1,0:T(8,128)}, u32[]{:S(2)}) copy-start(f32[3,8,8]{2,1,0:T(8,128)} %taps_ref.1) | copy-start | bytes 2308
  41.5 18.9 %copy-start.6 = (f32[8]{0:T(128)S(1)}, f32[8]{0:T(128)}, u32[]{:S(2)}) copy-start(f32[8]{0:T(128)} %gate_ref.5) | copy-start | bytes 100
  79.3 3.7 %collective-permute-start.10 = (bf16[32,16,512]{2,1,0:T(8,128)(2,1)S(1)}, bf16[32,16,512]{2,1,0:T(8,128)(2,1)S(1)}, u32[]{:S(2)}, u32[]{:S(2)}) collective-permute-start(bf16[32,16,512]{2,1,0:T(8,128)(2,1)S(1)} %get-tuple-element.45), channel_id=1, source_target_pairs={{0,1},{1,0},{2,3},{3,2},{4,5},{5,4},{6,7},{7,6},{8,9},{9,8},{10,11... | collective-permute-start | bytes 1572872 | tf_op jit(solution)/shard_map/ppermute | solution.py:548
  83.1 6.0 %collective-permute-start.11 = (bf16[4,16,512]{2,1,0:T(8,128)(2,1)S(1)}, bf16[4,16,512]{2,1,0:T(8,128)(2,1)S(1)}, u32[]{:S(2)}, u32[]{:S(2)}) collective-permute-start(bf16[4,16,512]{2,1,0:T(8,128)(2,1)S(1)} %get-tuple-element.47), channel_id=1, source_target_pairs={{0,4},{4,0},{8,12},{12,8},{16,20},{20,16},{24,28},{28,24},{1,5},{5... | collective-permute-start | bytes 196616 | tf_op jit(solution)/shard_map/ppermute | solution.py:437
  83.2 9.3 %collective-permute-start.12 = (bf16[4,16,512]{2,1,0:T(8,128)(2,1)S(1)}, bf16[4,16,512]{2,1,0:T(8,128)(2,1)S(1)}, u32[]{:S(2)}, u32[]{:S(2)}) collective-permute-start(bf16[4,16,512]{2,1,0:T(8,128)(2,1)S(1)} %get-tuple-element.48), channel_id=1, source_target_pairs={{0,8},{4,12},{8,0},{12,4},{16,24},{20,28},{24,16},{28,20},{1,9},{5... | collective-permute-start | bytes 196616 | tf_op jit(solution)/shard_map/ppermute | solution.py:437
  83.7 10.6 %collective-permute-start.13 = (bf16[4,16,512]{2,1,0:T(8,128)(2,1)S(1)}, bf16[4,16,512]{2,1,0:T(8,128)(2,1)S(1)}, u32[]{:S(2)}, u32[]{:S(2)}) collective-permute-start(bf16[4,16,512]{2,1,0:T(8,128)(2,1)S(1)} %get-tuple-element.49), channel_id=1, source_target_pairs={{0,12},{4,8},{8,4},{12,0},{16,28},{20,24},{24,20},{28,16},{1,13},{... | collective-permute-start | bytes 196616 | tf_op jit(solution)/shard_map/ppermute | solution.py:437
  86.7 9.7 %collective-permute-start.14 = (bf16[4,16,512]{2,1,0:T(8,128)(2,1)S(1)}, bf16[4,16,512]{2,1,0:T(8,128)(2,1)S(1)}, u32[]{:S(2)}, u32[]{:S(2)}) collective-permute-start(bf16[4,16,512]{2,1,0:T(8,128)(2,1)S(1)} %get-tuple-element.50), channel_id=1, source_target_pairs={{0,16},{4,20},{8,24},{12,28},{16,0},{20,4},{24,8},{28,12},{1,17},{... | collective-permute-start | bytes 196616 | tf_op jit(solution)/shard_map/ppermute | solution.py:437
  88.2 10.2 %collective-permute-start.15 = (bf16[4,16,512]{2,1,0:T(8,128)(2,1)S(1)}, bf16[4,16,512]{2,1,0:T(8,128)(2,1)S(1)}, u32[]{:S(2)}, u32[]{:S(2)}) collective-permute-start(bf16[4,16,512]{2,1,0:T(8,128)(2,1)S(1)} %get-tuple-element.51), channel_id=1, source_target_pairs={{0,20},{4,16},{8,28},{12,24},{16,4},{20,0},{24,12},{28,8},{1,21},{... | collective-permute-start | bytes 196616 | tf_op jit(solution)/shard_map/ppermute | solution.py:437
  89.1 9.3 %collective-permute-start.16 = (bf16[4,16,512]{2,1,0:T(8,128)(2,1)S(1)}, bf16[4,16,512]{2,1,0:T(8,128)(2,1)S(1)}, u32[]{:S(2)}, u32[]{:S(2)}) collective-permute-start(bf16[4,16,512]{2,1,0:T(8,128)(2,1)S(1)} %get-tuple-element.52), channel_id=1, source_target_pairs={{0,24},{4,28},{8,16},{12,20},{16,8},{20,12},{24,0},{28,4},{1,25},{... | collective-permute-start | bytes 196616 | tf_op jit(solution)/shard_map/ppermute | solution.py:437
  92.5 7.1 %collective-permute-start.17 = (bf16[4,16,512]{2,1,0:T(8,128)(2,1)S(1)}, bf16[4,16,512]{2,1,0:T(8,128)(2,1)S(1)}, u32[]{:S(2)}, u32[]{:S(2)}) collective-permute-start(bf16[4,16,512]{2,1,0:T(8,128)(2,1)S(1)} %get-tuple-element.53), channel_id=1, source_target_pairs={{0,28},{4,24},{8,20},{12,16},{16,12},{20,8},{24,4},{28,0},{1,29},{... | collective-permute-start | bytes 196616 | tf_op jit(solution)/shard_map/ppermute | solution.py:437
  99.7 5.0 %collective-permute-start.18 = (f32[4,16,512]{2,1,0:T(8,128)S(1)}, f32[4,16,512]{2,1,0:T(8,128)S(1)}, u32[]{:S(2)}, u32[]{:S(2)}) collective-permute-start(f32[4,16,512]{2,1,0:T(8,128)S(1)} %convert_add_fusion), channel_id=1, source_target_pairs={{0,2},{1,3},{2,0},{3,1},{4,6},{5,7},{6,4},{7,5},{8,10},{9,11},{10,... | collective-permute-start | bytes 393224 | tf_op jit(solution)/shard_map/ppermute | solution.py:558
  104.7 1.4 %collective-permute-start.19 = (f32[4,16,512]{2,1,0:T(8,128)S(1)}, f32[4,16,512]{2,1,0:T(8,128)S(1)}, u32[]{:S(2)}, u32[]{:S(2)}) collective-permute-start(f32[4,16,512]{2,1,0:T(8,128)S(1)} %add.45), channel_id=1, source_target_pairs={{0,1},{1,0},{2,3},{3,2},{4,5},{5,4},{6,7},{7,6},{8,9},{9,8},{10,11... | collective-permute-start | bytes 393224 | tf_op jit(solution)/shard_map/ppermute | solution.py:559

commit v2 on v1

v2 whole, which is shorter than its diff:
```python
import functools

import jax
import jax.numpy as jnp
from jax import lax
from jax.experimental import pallas as pl
from jax.experimental.pallas import tpu as pltpu
from jax.sharding import PartitionSpec as P

G = 8
GC = 4
SUB = 8
LANE = 128
VMEM_LIMIT = 48 * 1024 * 1024
NT = (((1,), (1,)), ((), ()))


def params():
    return pltpu.CompilerParams(vmem_limit_bytes=VMEM_LIMIT)


def low_half():
    return lax.broadcasted_iota(jnp.int32, (SUB, LANE), 0) < SUB // 2


def swap_halves(tile):
    return pltpu.roll(tile, SUB // 2, 0)


def spread(tile, half, low):
    other = swap_halves(tile)
    return jnp.where(low, tile, other) if half == 0 else jnp.where(low, other, tile)


def pack_planes(array_ref, plane, out_ref, slot):
    local_views, _, groups, pixels = array_ref.shape
    for view in range(local_views):
        for tile in range(pixels // LANE):
            first = (tile % 2) * local_views + view
            out_ref[slot, tile // 2, pl.ds(first, groups, stride=SUB), :] = array_ref[
                view, plane, :, pl.ds(tile * LANE, LANE)
            ].astype(jnp.float32)


def prep_kernel(gate_ref, own_ref, cot_ref, refx_ref, gates_ref, cot_out):
    local_views, channels, pixels = own_ref.shape
    for tile in range(pixels // LANE):
        for view in range(local_views):
            own = own_ref[view, :, pl.ds(tile * LANE, LANE)].astype(jnp.float32)
            for copy in range(SUB // local_views):
                refx_ref[tile, pl.ds(copy * local_views + view, channels, stride=SUB), :] = own
    for g in range(gates_ref.shape[0]):
        gates_ref[g] = jnp.full((SUB, LANE), gate_ref[g], jnp.float32)

    def pack_one(plane, carry):
        pack_planes(cot_ref, plane, cot_out, plane)
        return carry

    lax.fori_loop(0, cot_out.shape[0], pack_one, 0)


def position(view, own_index, local_views, view_count):
    distance = (view // local_views) ^ own_index
    place = distance // 2 + (distance % 2) * (view_count // 2)
    return place * local_views + view % local_views


def assemble_kernel(src_ref, place_ref, even_ref, odd_ref, even_far, odd_far, rows_ref, scratch):
    local_views, per_view = src_ref.shape
    tiles = scratch.shape[0]
    pairs = local_views * per_view
    half_views = even_ref.shape[0]
    blocks = even_ref.shape[1] // SUB
    own_index = place_ref[0]
    parity = place_ref[1]
    for pair in range(pairs):
        view = src_ref[pair % local_views, pair // local_views]
        slot = position(view, own_index, local_views, 2 * half_views // local_views)
        odd = slot >= half_views
        index = jnp.where(odd, slot - half_views, slot)
        for tile in range(tiles):
            lanes = pl.ds(tile * LANE, LANE)
            for side, even, other in ((parity, even_ref, odd_ref), (1 - parity, even_far, odd_far)):
                maps = jnp.where(odd, other[index, :, lanes], even[index, :, lanes]).astype(
                    jnp.float32
                )
                for block in range(blocks):
                    first = (2 * block + side) * (SUB * pairs) + pair
                    scratch[tile, pl.ds(first, SUB, stride=pairs), :] = maps[
                        block * SUB : (block + 1) * SUB
                    ]
    for tile in range(tiles):
        rows_ref[:, pl.ds(tile * LANE, LANE)] = scratch[tile].astype(jnp.bfloat16)


def forward_vector(gates_ref, refx_ref, chunk, first_tile, half, outs):
    warped_ref, corr_ref, sig_ref, rden_ref = outs
    groups, pairs = corr_ref.shape[1:3]
    tiles = pairs // SUB
    lanes = pl.ds(half * LANE, LANE)
    logits = None
    for g in range(groups):
        total = None
        for j in range(0, GC, 2):
            c = g * GC + j
            span = pl.ds(c * pairs, 2 * pairs)
            both = chunk[span, lanes]
            warped_ref[0, span, lanes] = both.astype(jnp.bfloat16)
            both = both.reshape(2, tiles, SUB, LANE)
            for i in range(2):
                part = both[i] * refx_ref[first_tile + half, pl.ds((c + i) * SUB, SUB), :][None]
                total = part if total is None else total + part
        corr = total * (1.0 / GC)
        corr_ref[0, g, :, lanes] = corr.reshape(pairs, LANE)
        part = corr * gates_ref[g][None]
        logits = part if logits is None else logits + part
    sig = jax.nn.sigmoid(logits)
    sig_ref[0, :, lanes] = sig.reshape(pairs, LANE)
    visible = 0.5 + sig
    den = jnp.sum(visible, axis=0)
    rden = 1.0 / (den + swap_halves(den))
    rden_ref[0, :, lanes] = rden
    costs = []
    for g in range(groups):
        num = jnp.sum(visible * corr_ref[0, g, :, lanes].reshape(tiles, SUB, LANE), axis=0)
        costs.append((num + swap_halves(num)) * rden)
    return costs


def forward_dot(rows_ref, w_ref, chunk, part, parts):
    count = rows_ref.shape[0] // parts
    span = pl.ds(part * count, count)
    chunk[span, :] = lax.dot_general(
        rows_ref[span, :], w_ref[0], NT, preferred_element_type=jnp.float32
    )


def forward_body(gates_ref, rows_ref, refx_ref, w0_ref, w1_ref, outs, cost_ref, chunks):
    step = pl.program_id(0)
    count = pl.num_programs(0) - 1
    low = low_half()

    def vector(index, plane, matmul):
        costs = []
        for half in range(2):
            if matmul is not None:
                matmul(half)
            costs.append(
                forward_vector(
                    gates_ref, refx_ref, chunks[index], 2 * index, half, outs[4 * index : 4 * index + 4]
                )
            )
        for g in range(G):
            cost_ref[plane, index, pl.ds(g * SUB, SUB), :] = jnp.where(
                low, costs[0][g], costs[1][g]
            )

    @pl.when(step < count)
    def _():
        vector(
            1,
            jnp.maximum(step - 1, 0),
            lambda part: forward_dot(rows_ref, w0_ref, chunks[0], part, 2),
        )
        vector(0, step, lambda part: forward_dot(rows_ref, w1_ref, chunks[1], part, 2))

    @pl.when(step == count)
    def _():
        vector(1, step - 1, None)


def edge_kernel(gates_ref, rows_ref, refx_ref, w0_ref, w1_ref, cot_ref, *rest):
    outs = rest[:8]
    up_ref, down_ref, cost, *chunks = rest[8:]
    forward_body(gates_ref, rows_ref, refx_ref, w0_ref, w1_ref, outs, cost, chunks)

    @pl.when(pl.program_id(0) == pl.num_programs(0) - 1)
    def _():
        down_ref[0:2] = cost[0:2]
        up_ref[0:2] = cost[2:4]
        down_ref[2] = cot_ref[0]
        up_ref[2] = cot_ref[cot_ref.shape[0] - 1]


def inner_kernel(gates_ref, rows_ref, refx_ref, w0_ref, w1_ref, *rest):
    outs = rest[8:16]
    cost_ref, *chunks = rest[16:]
    forward_body(gates_ref, rows_ref, refx_ref, w0_ref, w1_ref, outs, cost_ref, chunks)


def conv_kernel(
    taps_ref,
    below_ref,
    down_ref,
    inner_ref,
    up_ref,
    above_ref,
    cot_ref,
    regular_ref,
    cost_ref,
    grad_ref,
    cost,
    slope,
    smooth,
):
    planes = grad_ref.shape[0]
    local_views, _, groups, pixels = regular_ref.shape
    cost[0:2] = below_ref[0:2]
    cost[2:4] = down_ref[0:2]
    cost[4:planes] = inner_ref[...]
    cost[planes : planes + 2] = up_ref[0:2]
    cost[planes + 2 : planes + 4] = above_ref[0:2]
    cost_ref[...] = cost[2 : planes + 2]
    slope[0] = below_ref[2]
    slope[1 : planes + 1] = cot_ref[...]
    slope[planes + 1] = above_ref[2]

    def mix(source, tap):
        totals = [None] * G
        for k in range(3):
            for b in range(G):
                value = source(k, b)
                for a in range(G):
                    part = value * tap(k, a, b)
                    totals[a] = part if totals[a] is None else totals[a] + part
        return totals

    def forward_planes(index, carry):
        plane = 2 * index
        pres = mix(
            lambda k, g: cost[pl.ds(plane + k, 2), :, pl.ds(g * SUB, SUB), :],
            lambda k, o, g: taps_ref[k, o, g],
        )
        for o in range(G):
            pre = pres[o]
            rows = pl.ds(o * SUB, SUB)
            sig = jax.nn.sigmoid(pre)
            both = pl.ds(plane, 2)
            slope[both, :, rows, :] = slope[both, :, rows, :] * (sig * (1.0 + pre * (1.0 - sig)))
            smooth[both, :, rows, :] = pre * sig
        return carry

    lax.fori_loop(0, (planes + 2) // 2, forward_planes, 0)

    def backward_planes(index, carry):
        plane = 2 * index
        grads = mix(
            lambda k, o: slope[pl.ds(plane + 2 - k, 2), :, pl.ds(o * SUB, SUB), :],
            lambda k, g, o: taps_ref[k, o, g],
        )
        for g in range(G):
            grad_ref[pl.ds(plane, 2), :, pl.ds(g * SUB, SUB), :] = grads[g]
        for view in range(local_views):
            for tile in range(pixels // LANE):
                first = (tile % 2) * local_views + view
                for i in range(2):
                    regular_ref[view, plane + i, :, pl.ds(tile * LANE, LANE)] = smooth[
                        plane + i + 1, tile // 2, pl.ds(first, groups, stride=SUB), :
                    ].astype(jnp.bfloat16)
        return carry

    lax.fori_loop(0, planes // 2, backward_planes, 0)


def backward_kernel(src_ref, place_ref, gates_ref, refx_ref, w_ref, *rest):
    saved = (rest[0:4], rest[4:8])
    cost_ref, grad_ref, keep_ref, send_ref = rest[8:12]
    rows_lo, rows_hi, acc, dref, logit, w_prev, dense = rest[12:]
    step = pl.program_id(0)
    count = pl.num_programs(0) - 1
    groups, pairs = saved[0][1].shape[1:3]
    tiles = pairs // SUB
    lane_tiles = dref.shape[0]
    local_views = src_ref.shape[0]
    channels = groups * GC
    half_rows = rows_lo.shape[0]
    low = low_half()

    def vector(tile, upper, target):
        _, corr_ref, sig_ref, rden_ref = saved[tile // 2]
        warped_ref = saved[tile // 2][0]
        lanes = pl.ds((tile % 2) * LANE, LANE)
        full = pl.ds(tile * LANE, LANE)
        pack = tile // 2
        half = tile % 2
        rden = rden_ref[0, :, lanes]
        sig = sig_ref[0, :, lanes].reshape(tiles, SUB, LANE)
        wanted = range(groups // 2, groups) if upper else range(groups)
        num_grads = {}
        for g in wanted:
            grad = grad_ref[0, pack, pl.ds(g * SUB, SUB), :]
            num_grads[g] = spread(grad, half, low) * rden
        if upper:
            logit_grad = logit[:, full].reshape(tiles, SUB, LANE)
        else:
            mixed = None
            for g in range(groups):
                rows = pl.ds(g * SUB, SUB)
                part = grad_ref[0, pack, rows, :] * cost_ref[0, pack, rows, :]
                mixed = part if mixed is None else mixed + part
            vis_grad = -(spread(mixed, half, low) * rden)[None]
            for g in range(groups):
                vis_grad = vis_grad + num_grads[g][None] * corr_ref[0, g, :, lanes].reshape(
                    tiles, SUB, LANE
                )
            logit_grad = vis_grad * (sig * (1.0 - sig)) * (1.0 / GC)
            logit[:, full] = logit_grad.reshape(pairs, LANE)
        visible = (0.5 + sig) * (1.0 / GC)
        base = groups // 2 if upper else 0
        for g in range(base, base + groups // 2):
            corr_grad = visible * num_grads[g][None] + logit_grad * gates_ref[g][None]
            for j in range(0, GC, 2):
                c = g * GC + j
                local = (c - base * GC) * pairs
                both = jnp.concatenate(
                    [
                        (corr_grad * refx_ref[tile, pl.ds((c + i) * SUB, SUB), :][None]).reshape(
                            pairs, LANE
                        )
                        for i in range(2)
                    ],
                    axis=0,
                )
                target[pl.ds(local, 2 * pairs), full] = both.astype(jnp.bfloat16)
                warped = (
                    warped_ref[0, pl.ds(c * pairs, 2 * pairs), lanes]
                    .astype(jnp.float32)
                    .reshape(2, tiles, SUB, LANE)
                )
                for i in range(2):
                    dref[tile, pl.ds((c + i) * SUB, SUB), :] += jnp.sum(
                        corr_grad * warped[i], axis=0
                    )

    def matmul(rows, weights, base, index):
        product = jnp.dot(
            rows[...],
            weights(pl.ds(index * 2 * LANE, 2 * LANE)),
            preferred_element_type=jnp.float32,
        )
        for half in range(2):
            acc[2 * index + half, pl.ds(base, half_rows), :] += product[
                :, half * LANE : (half + 1) * LANE
            ]

    @pl.when(step == 0)
    def _():
        acc[...] = jnp.zeros_like(acc)
        dref[...] = jnp.zeros_like(dref)
        rows_hi[...] = jnp.zeros_like(rows_hi)
        w_prev[...] = jnp.zeros_like(w_prev)

    @pl.when(step < count)
    def _():
        for tile in range(lane_tiles):
            if tile % 2 == 0:
                matmul(rows_hi, lambda lanes: w_prev[:, lanes], half_rows, tile // 2)
            vector(tile, False, rows_lo)
        w_prev[...] = w_ref[0]
        for tile in range(lane_tiles):
            if tile % 2 == 0:
                matmul(rows_lo, lambda lanes: w_ref[0, :, lanes], 0, tile // 2)
            vector(tile, True, rows_hi)

    @pl.when(step == count)
    def _():
        for index in range(lane_tiles // 2):
            matmul(rows_hi, lambda lanes: w_prev[:, lanes], half_rows, index)
        own_index = place_ref[0]
        parity = place_ref[1]
        dense[...] = jnp.zeros_like(dense)
        for tile in range(lane_tiles):
            lanes = pl.ds(tile * LANE, LANE)
            for view in range(local_views):
                total = dref[tile, pl.ds(view, channels, stride=SUB), :]
                for copy in range(1, SUB // local_views):
                    first = copy * local_views + view
                    total = total + dref[tile, pl.ds(first, channels, stride=SUB), :]
                dense[view, :, lanes] = total
        for pair in range(pairs):
            view = src_ref[pair % local_views, pair // local_views]
            slot = position(view, own_index, local_views, dense.shape[0] // local_views)
            for tile in range(lane_tiles):
                dense[slot, :, pl.ds(tile * LANE, LANE)] += acc[
                    tile, pl.ds(pair, channels, stride=pairs), :
                ]
        blocks = keep_ref.shape[1] // SUB

        def one_view(view, carry):
            kept = []
            sent = []
            for block in range(blocks):
                mine = pl.multiple_of((2 * block + parity) * SUB, SUB)
                theirs = pl.multiple_of((2 * block + 1 - parity) * SUB, SUB)
                kept.append(dense[view, pl.ds(mine, SUB), :])
                sent.append(dense[view, pl.ds(theirs, SUB), :])
            keep_ref[view] = jnp.concatenate(kept, axis=0)
            send_ref[view] = jnp.concatenate(sent, axis=0).astype(jnp.bfloat16)
            return carry

        lax.fori_loop(0, dense.shape[0], one_view, 0)


def split_kernel(keep_ref, received_ref, even_ref, near_ref, far_ref):
    near = near_ref.shape[0]
    half = even_ref.shape[0]
    even_ref[...] = keep_ref[0:half] + received_ref[0:half].astype(jnp.float32)
    for out_ref, first, count in ((near_ref, half, near), (far_ref, half + near, half - near)):
        span = pl.ds(first, count)
        out_ref[...] = (keep_ref[span] + received_ref[span].astype(jnp.float32)).astype(
            jnp.bfloat16
        )


def spread_kernel(first, even_ref, received_ref, *out_refs):
    size = out_refs[0].shape[0]
    for index, out_ref in enumerate(out_refs):
        span = pl.ds(first + index * size, size)
        out_ref[...] = (
            even_ref[span] + received_ref[pl.ds(index * size, size)].astype(jnp.float32)
        ).astype(out_ref.dtype)


def per_plane(shape, plane):
    rank = len(shape)
    return pl.BlockSpec((1,) + tuple(shape[1:]), lambda d: (plane(d),) + (0,) * (rank - 1))


def fixed(shape):
    rank = len(shape)
    return pl.BlockSpec(tuple(shape), lambda d: (0,) * rank)


SMEM = functools.partial(pl.BlockSpec, memory_space=pltpu.SMEM)


def shards(features, sources, warp_weights, view_gate, depth_kernel, cotangent):
    view_count = lax.axis_size("view")
    plane_count = lax.axis_size("plane")
    own_index = lax.axis_index("view")
    plane_index = lax.axis_index("plane")
    local_views, channels, pixels = features.shape
    all_views, per_view = sources.shape
    pairs = local_views * per_view
    planes = warp_weights.shape[0]
    share = channels // plane_count
    blocks = plane_count // 2
    parity = plane_index % 2
    f32 = jnp.float32
    bf16 = jnp.bfloat16
    near = [(i, i ^ 1) for i in range(plane_count)]
    far = [(i, i ^ 2) for i in range(plane_count)]
    up = [(i, i + 1) for i in range(plane_count - 1)]
    down = [(i + 1, i) for i in range(plane_count - 1)]
    shape = jax.ShapeDtypeStruct

    halves = features.reshape(local_views, blocks, 2, share, pixels)
    mine = lax.dynamic_index_in_dim(halves, parity, 2, keepdims=False).reshape(
        local_views, channels // 2, pixels
    )

    def over_view(array, k):
        return lax.ppermute(array, "view", [(i, i ^ k) for i in range(view_count)])

    evens = range(2, view_count, 2)
    even = jnp.concatenate([mine] + [over_view(mine, k) for k in evens], axis=0)
    odd = over_view(even, 1)
    even_far = lax.ppermute(even, "plane", near)
    odd_far = lax.ppermute(odd, "plane", near)

    packed = (pixels // (2 * LANE), G * SUB, LANE)
    refx, gates, cot = pl.pallas_call(
        prep_kernel,
        out_shape=(
            shape((pixels // LANE, channels * SUB, LANE), f32),
            shape((G, SUB, LANE), f32),
            shape((planes,) + packed, f32),
        ),
        in_specs=[SMEM(), pl.BlockSpec(), pl.BlockSpec()],
        compiler_params=params(),
        name="prep",
    )(view_gate, features, cotangent)

    src_own = lax.dynamic_slice_in_dim(sources, own_index * local_views, local_views, 0)
    place = jnp.stack([own_index, parity]).astype(jnp.int32)
    rows = pl.pallas_call(
        assemble_kernel,
        out_shape=shape((channels * pairs, pixels), bf16),
        in_specs=[SMEM(), SMEM()] + [pl.BlockSpec()] * 4,
        scratch_shapes=[pltpu.VMEM((pixels // LANE, channels * pairs, LANE), f32)],
        compiler_params=params(),
        name="assemble",
    )(src_own, place, even, odd, even_far, odd_far)

    width = 2 * LANE
    saved = (
        shape((planes, channels * pairs, width), bf16),
        shape((planes, G, pairs, width), f32),
        shape((planes, pairs, width), f32),
        shape((planes, SUB, width), f32),
    )
    chunks = [pltpu.VMEM((channels * pairs, width), f32)] * 2

    def edge(d):
        return jnp.where(d < 2, d, planes - 4 + d)

    def inner(d):
        return d + 2

    def lane_half(index, plane, count):
        if index == 0:
            return lambda d: plane(jnp.minimum(d, count - 1))
        return lambda d: plane(jnp.maximum(d - 1, 0))

    def forward_specs(plane, count):
        ins = [fixed(gates.shape), fixed(rows.shape), fixed(refx.shape)] + [
            pl.BlockSpec(
                (1, width, pixels),
                lambda d, index=index: (plane(jnp.minimum(d, count - 1)), index, 0),
            )
            for index in range(2)
        ]
        outs = [
            per_plane(s.shape, lane_half(index, plane, count)) for index in range(2) for s in saved
        ]
        return ins, outs

    edge_ins, edge_outs = forward_specs(edge, 4)
    *edge_saved, up_load, down_load = pl.pallas_call(
        edge_kernel,
        out_shape=saved * 2 + (shape((3,) + packed, f32),) * 2,
        grid=(5,),
        in_specs=edge_ins + [fixed(cot.shape)],
        out_specs=tuple(edge_outs) + (fixed((3,) + packed),) * 2,
        scratch_shapes=[pltpu.VMEM((4,) + packed, f32)] + chunks,
        compiler_params=params(),
        name="forward_edge",
    )(gates, rows, refx, warp_weights, warp_weights, cot)
    below = lax.ppermute(up_load, "plane", up)
    above = lax.ppermute(down_load, "plane", down)
    inner_ins, inner_outs = forward_specs(inner, planes - 4)
    *saved_values, inner_cost = pl.pallas_call(
        inner_kernel,
        out_shape=saved * 2 + (shape((planes - 4,) + packed, f32),),
        grid=(planes - 3,),
        in_specs=inner_ins + [pl.BlockSpec(memory_space=pl.ANY)] * 8,
        out_specs=tuple(inner_outs) + (fixed((planes - 4,) + packed),),
        scratch_shapes=chunks,
        input_output_aliases={5 + i: i for i in range(8)},
        compiler_params=params(),
        cost_estimate=pl.CostEstimate(
            flops=2 * channels * pairs * pixels * pixels * (planes - 4),
            bytes_accessed=40 * 1024 * 1024,
            transcendentals=0,
        ),
        name="forward_inner",
    )(gates, rows, refx, warp_weights, warp_weights, *edge_saved)

    regular, cost, cost_grad = pl.pallas_call(
        conv_kernel,
        out_shape=(
            shape(cotangent.shape, bf16),
            shape((planes,) + packed, f32),
            shape((planes,) + packed, f32),
        ),
        in_specs=[SMEM()] + [pl.BlockSpec()] * 6,
        scratch_shapes=[
            pltpu.VMEM((planes + 4,) + packed, f32),
            pltpu.VMEM((planes + 2,) + packed, f32),
            pltpu.VMEM((planes + 2,) + packed, f32),
        ],
        compiler_params=params(),
        name="depth_conv",
    )(depth_kernel, below, down_load, inner_cost, up_load, above, cot)

    def clamped(d):
        return jnp.minimum(d, planes - 1)

    returned = (all_views, channels // 2, pixels)
    keep, send = pl.pallas_call(
        backward_kernel,
        out_shape=(shape(returned, f32), shape(returned, bf16)),
        grid=(planes + 1,),
        in_specs=[SMEM(), SMEM(), fixed(gates.shape), fixed(refx.shape)]
        + [per_plane(warp_weights.shape, clamped)]
        + [per_plane(s.shape, clamped) for s in saved * 2]
        + [per_plane(cost.shape, clamped), per_plane(cost_grad.shape, clamped)],
        out_specs=(fixed(returned), fixed(returned)),
        scratch_shapes=[
            pltpu.VMEM((channels * pairs // 2, pixels), bf16),
            pltpu.VMEM((channels * pairs // 2, pixels), bf16),
            pltpu.VMEM((pixels // LANE, channels * pairs, LANE), f32),
            pltpu.VMEM((pixels // LANE, channels * SUB, LANE), f32),
            pltpu.VMEM((pairs, pixels), f32),
            pltpu.VMEM((pixels, pixels), bf16),
            pltpu.VMEM((all_views, channels, pixels), f32),
        ],
        compiler_params=params(),
        name="backward",
    )(src_own, place, gates, refx, warp_weights, *saved_values, cost, cost_grad)

    received = lax.ppermute(send, "plane", near)
    half_views = all_views // 2
    close = half_views // 2
    piece = (local_views, channels // 2, pixels)
    even_sum, send_close, send_away = pl.pallas_call(
        split_kernel,
        out_shape=(
            shape((half_views,) + piece[1:], f32),
            shape((close,) + piece[1:], bf16),
            shape((half_views - close,) + piece[1:], bf16),
        ),
        compiler_params=params(),
        name="split",
    )(keep, received)
    away = over_view(send_away, 1)
    closer = over_view(send_close, 1)
    count = close // local_views
    away_parts = pl.pallas_call(
        functools.partial(spread_kernel, close),
        out_shape=(shape(piece, bf16),) * (view_count // 2 - count),
        compiler_params=params(),
        name="spread_away",
    )(even_sum, away)
    total, *close_parts = pl.pallas_call(
        functools.partial(spread_kernel, 0),
        out_shape=(shape(piece, f32),) + (shape(piece, bf16),) * (count - 1),
        compiler_params=params(),
        name="spread_close",
    )(even_sum, closer)
    for index, part in enumerate(away_parts):
        total = total + over_view(part, 2 * (count + index)).astype(f32)
    for index, part in enumerate(close_parts):
        total = total + over_view(part, 2 * (index + 1)).astype(f32)
    total = total + lax.ppermute(total, "plane", far)
    other = lax.ppermute(total, "plane", near)
    cut = (local_views, blocks, 1, share, pixels)
    first = jnp.where(parity == 0, total, other).reshape(cut)
    second = jnp.where(parity == 0, other, total).reshape(cut)
    feature_grads = jnp.concatenate([first, second], axis=2).reshape(features.shape)
    return (regular, feature_grads)


def solution(mesh):
    in_specs = (
        P("view", None, None),
        P(),
        P("plane", None, None),
        P(),
        P(),
        P("view", "plane", None, None),
    )
    out_specs = (P("view", "plane", None, None), P("view", None, None))
    return jax.shard_map(shards, mesh=mesh, in_specs=in_specs, out_specs=out_specs, check_vma=False)
```

time: 108 us -> 101 us (0.935)
  starting transfers between devices: 30.8 us -> 19 us
  waiting for transfers between devices: 24.1 us -> 29.2 us
    ppermute x14 -> x9, starting transfers between devices: 23.1 us -> 11.7 us  [over_view(): return lax.ppermute(array, 'view', [(i, i ^ k) for i in range(view_count)])]
    ppermute x14 -> x9, waiting for transfers between devices: 16.6 us -> 22.9 us  [over_view(): return lax.ppermute(array, 'view', [(i, i ^ k) for i in range(view_count)])]
    ppermute x1 -> x2, waiting for transfers between devices: 1.64 us -> 0.01 us  [the longest x1 0.01 us: shards(): even_far = lax.ppermute(even, 'plane', near)]
    pallas_call x1, Pallas kernels: 6.83 us -> 5.24 us  [shards(): pl.pallas_call(conv_kernel, out_shape=(shape(cotangent.shape, bf16), shap...]
    pallas_call x4 -> x7, Pallas kernels: 20.9 us -> 21.9 us  [the longest x1 12 us: shards(): pl.pallas_call(inner_kernel, out_shape=saved * 2 + (shape((planes - 4,) +...]
    unnamed x22 -> x11, local copies, waits for them, and re-layouts: 3.56 us -> 2.67 us
  transfers between devices with their start and end apart: 20 -> 16, of which waited for: 9 -> 9; matrix products, arithmetic and copies ran while one was open for 0% -> 0% of each run, Pallas kernels for 11% -> 13%
where the time goes in v2:
time: 101 us; the launch traced here: 100 us
  Pallas kernels  46.9 us (46%)
  waiting for transfers between devices  29.2 us (29%)
  starting transfers between devices  19 us (19%)
  local copies, waits for them, and re-layouts  4.31 us (4%)
    ppermute x9, waiting for transfers between devices, over_view(): return lax.ppermute(array, 'view', [(i, i ^ k) for i in range(view_count)])  22.9 us
    pallas_call x1, Pallas kernels, shards(): pl.pallas_call(backward_kernel, out_shape=(shape(returned, f32), shape(re...  19.7 us
    pallas_call x1, Pallas kernels, shards(): pl.pallas_call(inner_kernel, out_shape=saved * 2 + (shape((planes - 4,) +...  12 us
    ppermute x9, starting transfers between devices, over_view(): return lax.ppermute(array, 'view', [(i, i ^ k) for i in range(view_count)])  11.7 us
    pallas_call x1, Pallas kernels, shards(): pl.pallas_call(edge_kernel, out_shape=saved * 2 + (shape((3,) + packed, f...  7.19 us
    pallas_call x1, Pallas kernels, shards(): pl.pallas_call(conv_kernel, out_shape=(shape(cotangent.shape, bf16), shap...  5.24 us
    ppermute x1, waiting for transfers between devices, shards(): total = total + lax.ppermute(total, 'plane', far)  3.47 us
    unnamed x11, local copies, waits for them, and re-layouts  2.67 us
  transfers between devices with their start and end apart: 16, of which 9 were waited for; matrix products, arithmetic and copies ran while one was open for 0% of the time, Pallas kernels for 13%

profile of v2, /device:TPU:0, one launch (start us, length us, event | category | flops | bytes accessed | tf_op | source)
XLA Modules:
  0.0 100.4 jit_solution(1471133852360919437)
XLA Ops:
  0.6 0.0 copy-start
  0.7 0.8 dynamic-slice_bitcast_fusion
  1.5 5.0 %collective-permute-start.2 = (bf16[4,16,512]{2,1,0:T(8,128)(2,1)S(1)}, bf16[4,16,512]{2,1,0:T(8,128)(2,1)S(1)}, u32[]{:S(2)}, u32[]{:S(2)}) collective-permute-start(bf16[4,16,512]{2,1,0:T(8,128)(2,1)S(1)} %dynamic-slice_bitcast_fusion), channel_id=1, source_target_pairs={{0,24},{4,28},{8,16},{12,20},{16,8},{20,12},{24,0},{28,4},{1,25},{... | collective-permute-start | bytes 196616 | tf_op jit(solution)/shard_map/ppermute | solution.py:463
  6.6 0.0 collective-permute-start.1
  6.6 0.6 collective-permute-start
  7.1 2.0 %collective-permute-done.2 = bf16[4,16,512]{2,1,0:T(8,128)(2,1)S(1)} collective-permute-done((bf16[4,16,512]{2,1,0:T(8,128)(2,1)S(1)}, bf16[4,16,512]{2,1,0:T(8,128)(2,1)S(1)}, u32[]{:S(2)}, u32[]{:S(2)}) %collective-permute-start.2) | collective-permute-done | bytes 65568 | tf_op jit(solution)/shard_map/ppermute | solution.py:463
  9.1 3.0 %collective-permute-done.1 = bf16[4,16,512]{2,1,0:T(8,128)(2,1)S(1)} collective-permute-done((bf16[4,16,512]{2,1,0:T(8,128)(2,1)S(1)}, bf16[4,16,512]{2,1,0:T(8,128)(2,1)S(1)}, u32[]{:S(2)}, u32[]{:S(2)}) %collective-permute-start.1) | collective-permute-done | bytes 65568 | tf_op jit(solution)/shard_map/ppermute | solution.py:463
  12.2 0.0 collective-permute-done
  12.2 1.6 %collective-permute-start.3 = (bf16[16,16,512]{2,1,0:T(8,128)(2,1)S(1)}, bf16[16,16,512]{2,1,0:T(8,128)(2,1)S(1)}, u32[]{:S(2)}, u32[]{:S(2)}) collective-permute-start(bf16[16,16,512]{2,1,0:T(8,128)(2,1)S(1)} %pad_maximum_fusion.even_ref), channel_id=1, source_target_pairs={{0,4},{4,0},{8,12},{12,8},{16,20},{20,16},{24,28},{28,24},{1,5},{5... | collective-permute-start | bytes 786440 | tf_op jit(solution)/shard_map/ppermute | solution.py:463
  13.8 0.0 collective-permute-start.4
  13.8 6.4 %collective-permute-done.3.odd_ref = bf16[16,16,512]{2,1,0:T(8,128)(2,1)S(1)} collective-permute-done((bf16[16,16,512]{2,1,0:T(8,128)(2,1)S(1)}, bf16[16,16,512]{2,1,0:T(8,128)(2,1)S(1)}, u32[]{:S(2)}, u32[]{:S(2)}) %collective-permute-start.3) | collective-permute-done | bytes 262176 | tf_op jit(solution)/shard_map/ppermute | solution.py:463
  20.2 0.1 constant_dynamic-slice_fusion
  20.2 0.1 copy.19.src_ref
  20.3 1.0 copy-done.1
  21.3 0.9 copy-done.2
  22.2 0.7 copy-done.4
  22.9 0.8 prep.1
  23.7 0.1 pad_add_fusion.place_ref
  23.8 0.0 collective-permute-done.4.even_far
  23.8 0.0 collective-permute-done.5.odd_far
  23.8 1.7 %assemble.1.rows_ref = bf16[1280,512]{1,0:T(8,128)(2,1)S(1)} custom-call(s32[4,10]{1,0:T(4,128)S(1)} %copy.19.src_ref, s32[2]{0:T(128)S(1)} %pad_add_fusion.place_ref, bf16[16,16,512]{2,1,0:T(8,128)(2,1)S(1)} %pad_maximum_fusion.even_ref, bf16[16,16,512]{2,1,0:T(8,128)(2,1)S(1)} %collective-permute-done.3.odd_ref, ...), custom_call_target="tpu_custom_call" | custom-call | tf_op jit(solution)/shard_map/assemble/pallas_call | solution.py:486
  25.5 7.2 %forward_edge.1 = (bf16[12,1280,256]{2,1,0:T(8,128)(2,1)}, f32[12,8,40,256]{3,2,1,0:T(8,128)}, f32[12,40,256]{2,1,0:T(8,128)S(1)}, f32[12,8,256]{2,1,0:T(8,128)S...) custom-call(f32[8,8,128]{2,1,0:T(8,128)S(1)} %get-tuple-element.36.g, ...), custom_call_target="tpu_custom_call" | custom-call | tf_op jit(solution)/shard_map/forward_edge/pallas_call | solution.py:529
  32.7 2.4 %collective-permute-start.6 = (f32[3,2,64,128]{3,2,1,0:T(8,128)S(1)}, f32[3,2,64,128]{3,2,1,0:T(8,128)S(1)}, u32[]{:S(2)}, u32[]{:S(2)}) collective-permute-start(f32[3,2,64,128]{3,2,1,0:T(8,128)S(1)} %get-tuple-element.39.up_ref), channel_id=1, source_target_pairs={{0,1},{1,2},{2,3},{4,5},{5,6},{6,7},{8,9},{9,10},{10,11},{12,13},{... | collective-permute-start | bytes 589832 | tf_op jit(solution)/shard_map/ppermute | solution.py:539
  35.1 1.3 %collective-permute-start.7 = (f32[3,2,64,128]{3,2,1,0:T(8,128)S(1)}, f32[3,2,64,128]{3,2,1,0:T(8,128)S(1)}, u32[]{:S(2)}, u32[]{:S(2)}) collective-permute-start(f32[3,2,64,128]{3,2,1,0:T(8,128)S(1)} %get-tuple-element.40.down_ref), channel_id=1, source_target_pairs={{1,0},{2,1},{3,2},{5,4},{6,5},{7,6},{9,8},{10,9},{11,10},{13,12},{... | collective-permute-start | bytes 589832 | tf_op jit(solution)/shard_map/ppermute | solution.py:540
  36.4 0.0 copy-start.3
  36.4 12.0 %forward_inner.1 = (bf16[12,1280,256]{2,1,0:T(8,128)(2,1)}, f32[12,8,40,256]{3,2,1,0:T(8,128)}, f32[12,40,256]{2,1,0:T(8,128)S(1)}, f32[12,8,256]{2,1,0:T(8,128)...) custom-call(f32[8,8,128]{2,1,0:T(8,128)S(1)} %get-tuple-element.36.g, ...), custom_call_target="tpu_custom_call", output_to_operand_aliasing={{0}: (5, {}), {1}: (6, {}), {2}: (7, {}), {3}: (8, {}), {4}... | custom-call | flops 5368709120 | bytes 41943040 | tf_op jit(solution)/shard_map/forward_inner/pallas_call | solution.py:542
  48.5 0.0 collective-permute-done.6.below_ref
  48.5 0.0 collective-permute-done.7.above_ref
  48.5 5.2 %depth_conv.1 = (bf16[4,12,8,512]{3,2,1,0:T(8,128)(2,1)}, f32[12,2,64,128]{3,2,1,0:T(8,128)S(1)}, f32[12,2,64,128]{3,2,1,0:T(8,128)S(1)}) custom-call(f32[3,8,8]{2,1,0:T(8,128)S(1)} %copy-done.3, f32[3,2,64,128]{3,2,1,0:T(8,128)S(1)} %collective-permute-done.6.below_ref, f32[3,2,64,128]{3,2,1,0:T(8,128)S(1)} %get-tuple-element.40.down_ref, ...), custom_call_target="tpu_custom_call" | custom-call | tf_op jit(solution)/shard_map/depth_conv/pallas_call | solution.py:559
  53.7 19.7 %backward.1 = (f32[32,16,512]{2,1,0:T(8,128)S(1)}, bf16[32,16,512]{2,1,0:T(8,128)(2,1)S(1)}) custom-call(s32[4,10]{1,0:T(4,128)S(1)} %copy.19.src_ref, s32[2]{0:T(128)S(1)} %pad_add_fusion.place_ref, f32[8,8,128]{2,1,0:T(8,128)S(1)} %get-tuple-element.36.gates_ref, f32[4,256,128]{2,1,0:T(8,128)S(1)} %get-tuple-element.37.refx_ref, ...), custom_call_target="tpu_custom_call" | custom-call | tf_op jit(solution)/shard_map/backward/pallas_call | solution.py:580
  73.4 2.0 %collective-permute-start.8 = (bf16[32,16,512]{2,1,0:T(8,128)(2,1)S(1)}, bf16[32,16,512]{2,1,0:T(8,128)(2,1)S(1)}, u32[]{:S(2)}, u32[]{:S(2)}) collective-permute-start(bf16[32,16,512]{2,1,0:T(8,128)(2,1)S(1)} %get-tuple-element.62), channel_id=1, source_target_pairs={{0,1},{1,0},{2,3},{3,2},{4,5},{5,4},{6,7},{7,6},{8,9},{9,8},{10,11... | collective-permute-start | bytes 1572872 | tf_op jit(solution)/shard_map/ppermute | solution.py:602
  75.4 1.5 %collective-permute-done.8.received_ref = bf16[32,16,512]{2,1,0:T(8,128)(2,1)S(1)} collective-permute-done((bf16[32,16,512]{2,1,0:T(8,128)(2,1)S(1)}, bf16[32,16,512]{2,1,0:T(8,128)(2,1)S(1)}, u32[]{:S(2)}, u32[]{:S(2)}) %collective-permute-start.8) | collective-permute-done | bytes 524320 | tf_op jit(solution)/shard_map/ppermute | solution.py:602
  76.9 0.1 split.1
  77.1 1.6 %collective-permute-start.9 = (bf16[8,16,512]{2,1,0:T(8,128)(2,1)S(1)}, bf16[8,16,512]{2,1,0:T(8,128)(2,1)S(1)}, u32[]{:S(2)}, u32[]{:S(2)}) collective-permute-start(bf16[8,16,512]{2,1,0:T(8,128)(2,1)S(1)} %get-tuple-element.64), channel_id=1, source_target_pairs={{0,4},{4,0},{8,12},{12,8},{16,20},{20,16},{24,28},{28,24},{1,5},{5... | collective-permute-start | bytes 393224 | tf_op jit(solution)/shard_map/ppermute | solution.py:463
  78.7 0.5 collective-permute-start.10
  79.2 4.3 %collective-permute-done.9.received_ref = bf16[8,16,512]{2,1,0:T(8,128)(2,1)S(1)} collective-permute-done((bf16[8,16,512]{2,1,0:T(8,128)(2,1)S(1)}, bf16[8,16,512]{2,1,0:T(8,128)(2,1)S(1)}, u32[]{:S(2)}, u32[]{:S(2)}) %collective-permute-start.9) | collective-permute-done | bytes 131104 | tf_op jit(solution)/shard_map/ppermute | solution.py:463
  83.5 0.1 collective-permute-start.13
  83.6 2.1 %collective-permute-done.10.received_ref = bf16[8,16,512]{2,1,0:T(8,128)(2,1)S(1)} collective-permute-done((bf16[8,16,512]{2,1,0:T(8,128)(2,1)S(1)}, bf16[8,16,512]{2,1,0:T(8,128)(2,1)S(1)}, u32[]{:S(2)}, u32[]{:S(2)}) %collective-permute-start.10) | collective-permute-done | bytes 131104 | tf_op jit(solution)/shard_map/ppermute | solution.py:463
  85.7 0.2 collective-permute-start.11
  86.0 2.1 %collective-permute-start.12 = (bf16[4,16,512]{2,1,0:T(8,128)(2,1)S(1)}, bf16[4,16,512]{2,1,0:T(8,128)(2,1)S(1)}, u32[]{:S(2)}, u32[]{:S(2)}) collective-permute-start(bf16[4,16,512]{2,1,0:T(8,128)(2,1)S(1)} %get-tuple-element.68), channel_id=1, source_target_pairs={{0,24},{4,28},{8,16},{12,20},{16,8},{20,12},{24,0},{28,4},{1,25},{... | collective-permute-start | bytes 196616 | tf_op jit(solution)/shard_map/ppermute | solution.py:463
  88.1 0.0 collective-permute-done.13
  88.1 5.0 %collective-permute-done.11 = bf16[4,16,512]{2,1,0:T(8,128)(2,1)S(1)} collective-permute-done((bf16[4,16,512]{2,1,0:T(8,128)(2,1)S(1)}, bf16[4,16,512]{2,1,0:T(8,128)(2,1)S(1)}, u32[]{:S(2)}, u32[]{:S(2)}) %collective-permute-start.11) | collective-permute-done | bytes 65568 | tf_op jit(solution)/shard_map/ppermute | solution.py:463
  93.1 0.0 collective-permute-done.12
  93.2 1.6 %collective-permute-start.14 = (f32[4,16,512]{2,1,0:T(8,128)S(1)}, f32[4,16,512]{2,1,0:T(8,128)S(1)}, u32[]{:S(2)}, u32[]{:S(2)}) collective-permute-start(f32[4,16,512]{2,1,0:T(8,128)S(1)} %convert_add_fusion), channel_id=1, source_target_pairs={{0,2},{1,3},{2,0},{3,1},{4,6},{5,7},{6,4},{7,5},{8,10},{9,11},{10,... | collective-permute-start | bytes 393224 | tf_op jit(solution)/shard_map/ppermute | solution.py:635
  94.7 3.5 %collective-permute-done.14 = f32[4,16,512]{2,1,0:T(8,128)S(1)} collective-permute-done((f32[4,16,512]{2,1,0:T(8,128)S(1)}, f32[4,16,512]{2,1,0:T(8,128)S(1)}, u32[]{:S(2)}, u32[]{:S(2)}) %collective-permute-start.14) | collective-permute-done | bytes 131104 | tf_op jit(solution)/shard_map/ppermute | solution.py:635
  98.2 0.1 collective-permute-start.15
  98.3 1.3 %collective-permute-done.15 = f32[4,16,512]{2,1,0:T(8,128)S(1)} collective-permute-done((f32[4,16,512]{2,1,0:T(8,128)S(1)}, f32[4,16,512]{2,1,0:T(8,128)S(1)}, u32[]{:S(2)}, u32[]{:S(2)}) %collective-permute-start.15) | collective-permute-done | bytes 131104 | tf_op jit(solution)/shard_map/ppermute | solution.py:636
  99.7 0.7 copy.18
  (13 shorter events, 0.2 us)
Async XLA Ops:
  0.6 19.5 %copy-start = (s32[32,10]{0,1:T(8,128)S(1)}, s32[32,10]{0,1:T(8,128)}, u32[]{:S(2)}) copy-start(s32[32,10]{0,1:T(8,128)} %param.7) | copy-start | bytes 3844
  1.5 7.6 %collective-permute-start.2 = (bf16[4,16,512]{2,1,0:T(8,128)(2,1)S(1)}, bf16[4,16,512]{2,1,0:T(8,128)(2,1)S(1)}, u32[]{:S(2)}, u32[]{:S(2)}) collective-permute-start(bf16[4,16,512]{2,1,0:T(8,128)(2,1)S(1)} %dynamic-slice_bitcast_fusion), channel_id=1, source_target_pairs={{0,24},{4,28},{8,16},{12,20},{16,8},{20,12},{24,0},{28,4},{1,25},{... | collective-permute-start | bytes 196616 | tf_op jit(solution)/shard_map/ppermute | solution.py:463
  6.6 5.6 %collective-permute-start.1 = (bf16[4,16,512]{2,1,0:T(8,128)(2,1)S(1)}, bf16[4,16,512]{2,1,0:T(8,128)(2,1)S(1)}, u32[]{:S(2)}, u32[]{:S(2)}) collective-permute-start(bf16[4,16,512]{2,1,0:T(8,128)(2,1)S(1)} %dynamic-slice_bitcast_fusion), channel_id=1, source_target_pairs={{0,16},{4,20},{8,24},{12,28},{16,0},{20,4},{24,8},{28,12},{1,17},{... | collective-permute-start | bytes 196616 | tf_op jit(solution)/shard_map/ppermute | solution.py:463
  6.6 5.6 %collective-permute-start = (bf16[4,16,512]{2,1,0:T(8,128)(2,1)S(1)}, bf16[4,16,512]{2,1,0:T(8,128)(2,1)S(1)}, u32[]{:S(2)}, u32[]{:S(2)}) collective-permute-start(bf16[4,16,512]{2,1,0:T(8,128)(2,1)S(1)} %dynamic-slice_bitcast_fusion), channel_id=1, source_target_pairs={{0,8},{4,12},{8,0},{12,4},{16,24},{20,28},{24,16},{28,20},{1,9},{5... | collective-permute-start | bytes 196616 | tf_op jit(solution)/shard_map/ppermute | solution.py:463
  12.2 7.9 %collective-permute-start.3 = (bf16[16,16,512]{2,1,0:T(8,128)(2,1)S(1)}, bf16[16,16,512]{2,1,0:T(8,128)(2,1)S(1)}, u32[]{:S(2)}, u32[]{:S(2)}) collective-permute-start(bf16[16,16,512]{2,1,0:T(8,128)(2,1)S(1)} %pad_maximum_fusion.even_ref), channel_id=1, source_target_pairs={{0,4},{4,0},{8,12},{12,8},{16,20},{20,16},{24,28},{28,24},{1,5},{5... | collective-permute-start | bytes 786440 | tf_op jit(solution)/shard_map/ppermute | solution.py:463
  13.8 10.0 %collective-permute-start.4 = (bf16[16,16,512]{2,1,0:T(8,128)(2,1)S(1)}, bf16[16,16,512]{2,1,0:T(8,128)(2,1)S(1)}, u32[]{:S(2)}, u32[]{:S(2)}) collective-permute-start(bf16[16,16,512]{2,1,0:T(8,128)(2,1)S(1)} %pad_maximum_fusion.even_ref), channel_id=1, source_target_pairs={{0,1},{1,0},{2,3},{3,2},{4,5},{5,4},{6,7},{7,6},{8,9},{9,8},{10,11... | collective-permute-start | bytes 786440 | tf_op jit(solution)/shard_map/ppermute | solution.py:468
  20.1 3.6 %collective-permute-start.5 = (bf16[16,16,512]{2,1,0:T(8,128)(2,1)S(1)}, bf16[16,16,512]{2,1,0:T(8,128)(2,1)S(1)}, u32[]{:S(2)}, u32[]{:S(2)}) collective-permute-start(bf16[16,16,512]{2,1,0:T(8,128)(2,1)S(1)} %collective-permute-done.3.odd_ref), channel_id=1, source_target_pairs={{0,1},{1,0},{2,3},{3,2},{4,5},{5,4},{6,7},{7,6},{8,9},{9,8},{10,11... | collective-permute-start | bytes 786440 | tf_op jit(solution)/shard_map/ppermute | solution.py:469
  20.3 1.0 copy-start.1
  21.3 0.9 copy-start.2
  22.2 0.7 copy-start.4
  32.7 15.8 %collective-permute-start.6 = (f32[3,2,64,128]{3,2,1,0:T(8,128)S(1)}, f32[3,2,64,128]{3,2,1,0:T(8,128)S(1)}, u32[]{:S(2)}, u32[]{:S(2)}) collective-permute-start(f32[3,2,64,128]{3,2,1,0:T(8,128)S(1)} %get-tuple-element.39.up_ref), channel_id=1, source_target_pairs={{0,1},{1,2},{2,3},{4,5},{5,6},{6,7},{8,9},{9,10},{10,11},{12,13},{... | collective-permute-start | bytes 589832 | tf_op jit(solution)/shard_map/ppermute | solution.py:539
  35.1 13.4 %collective-permute-start.7 = (f32[3,2,64,128]{3,2,1,0:T(8,128)S(1)}, f32[3,2,64,128]{3,2,1,0:T(8,128)S(1)}, u32[]{:S(2)}, u32[]{:S(2)}) collective-permute-start(f32[3,2,64,128]{3,2,1,0:T(8,128)S(1)} %get-tuple-element.40.down_ref), channel_id=1, source_target_pairs={{1,0},{2,1},{3,2},{5,4},{6,5},{7,6},{9,8},{10,9},{11,10},{13,12},{... | collective-permute-start | bytes 589832 | tf_op jit(solution)/shard_map/ppermute | solution.py:540
  36.4 12.1 %copy-start.3 = (f32[3,8,8]{2,1,0:T(8,128)S(1)}, f32[3,8,8]{2,1,0:T(8,128)}, u32[]{:S(2)}) copy-start(f32[3,8,8]{2,1,0:T(8,128)} %taps_ref.1) | copy-start | bytes 2308
  73.4 3.5 %collective-permute-start.8 = (bf16[32,16,512]{2,1,0:T(8,128)(2,1)S(1)}, bf16[32,16,512]{2,1,0:T(8,128)(2,1)S(1)}, u32[]{:S(2)}, u32[]{:S(2)}) collective-permute-start(bf16[32,16,512]{2,1,0:T(8,128)(2,1)S(1)} %get-tuple-element.62), channel_id=1, source_target_pairs={{0,1},{1,0},{2,3},{3,2},{4,5},{5,4},{6,7},{7,6},{8,9},{9,8},{10,11... | collective-permute-start | bytes 1572872 | tf_op jit(solution)/shard_map/ppermute | solution.py:602
  77.1 6.4 %collective-permute-start.9 = (bf16[8,16,512]{2,1,0:T(8,128)(2,1)S(1)}, bf16[8,16,512]{2,1,0:T(8,128)(2,1)S(1)}, u32[]{:S(2)}, u32[]{:S(2)}) collective-permute-start(bf16[8,16,512]{2,1,0:T(8,128)(2,1)S(1)} %get-tuple-element.64), channel_id=1, source_target_pairs={{0,4},{4,0},{8,12},{12,8},{16,20},{20,16},{24,28},{28,24},{1,5},{5... | collective-permute-start | bytes 393224 | tf_op jit(solution)/shard_map/ppermute | solution.py:463
  78.7 7.1 %collective-permute-start.10 = (bf16[8,16,512]{2,1,0:T(8,128)(2,1)S(1)}, bf16[8,16,512]{2,1,0:T(8,128)(2,1)S(1)}, u32[]{:S(2)}, u32[]{:S(2)}) collective-permute-start(bf16[8,16,512]{2,1,0:T(8,128)(2,1)S(1)} %get-tuple-element.66), channel_id=1, source_target_pairs={{0,4},{4,0},{8,12},{12,8},{16,20},{20,16},{24,28},{28,24},{1,5},{5... | collective-permute-start | bytes 393224 | tf_op jit(solution)/shard_map/ppermute | solution.py:463
  83.5 4.6 %collective-permute-start.13 = (bf16[4,16,512]{2,1,0:T(8,128)(2,1)S(1)}, bf16[4,16,512]{2,1,0:T(8,128)(2,1)S(1)}, u32[]{:S(2)}, u32[]{:S(2)}) collective-permute-start(bf16[4,16,512]{2,1,0:T(8,128)(2,1)S(1)} %get-tuple-element.69), channel_id=1, source_target_pairs={{0,8},{4,12},{8,0},{12,4},{16,24},{20,28},{24,16},{28,20},{1,9},{5... | collective-permute-start | bytes 196616 | tf_op jit(solution)/shard_map/ppermute | solution.py:463
  85.7 7.4 %collective-permute-start.11 = (bf16[4,16,512]{2,1,0:T(8,128)(2,1)S(1)}, bf16[4,16,512]{2,1,0:T(8,128)(2,1)S(1)}, u32[]{:S(2)}, u32[]{:S(2)}) collective-permute-start(bf16[4,16,512]{2,1,0:T(8,128)(2,1)S(1)} %get-tuple-element.67), channel_id=1, source_target_pairs={{0,16},{4,20},{8,24},{12,28},{16,0},{20,4},{24,8},{28,12},{1,17},{... | collective-permute-start | bytes 196616 | tf_op jit(solution)/shard_map/ppermute | solution.py:463
  86.0 7.2 %collective-permute-start.12 = (bf16[4,16,512]{2,1,0:T(8,128)(2,1)S(1)}, bf16[4,16,512]{2,1,0:T(8,128)(2,1)S(1)}, u32[]{:S(2)}, u32[]{:S(2)}) collective-permute-start(bf16[4,16,512]{2,1,0:T(8,128)(2,1)S(1)} %get-tuple-element.68), channel_id=1, source_target_pairs={{0,24},{4,28},{8,16},{12,20},{16,8},{20,12},{24,0},{28,4},{1,25},{... | collective-permute-start | bytes 196616 | tf_op jit(solution)/shard_map/ppermute | solution.py:463
  93.2 5.0 %collective-permute-start.14 = (f32[4,16,512]{2,1,0:T(8,128)S(1)}, f32[4,16,512]{2,1,0:T(8,128)S(1)}, u32[]{:S(2)}, u32[]{:S(2)}) collective-permute-start(f32[4,16,512]{2,1,0:T(8,128)S(1)} %convert_add_fusion), channel_id=1, source_target_pairs={{0,2},{1,3},{2,0},{3,1},{4,6},{5,7},{6,4},{7,5},{8,10},{9,11},{10,... | collective-permute-start | bytes 393224 | tf_op jit(solution)/shard_map/ppermute | solution.py:635
  98.2 1.4 %collective-permute-start.15 = (f32[4,16,512]{2,1,0:T(8,128)S(1)}, f32[4,16,512]{2,1,0:T(8,128)S(1)}, u32[]{:S(2)}, u32[]{:S(2)}) collective-permute-start(f32[4,16,512]{2,1,0:T(8,128)S(1)} %add.29), channel_id=1, source_target_pairs={{0,1},{1,0},{2,3},{3,2},{4,5},{5,4},{6,7},{7,6},{8,9},{9,8},{10,11... | collective-permute-start | bytes 393224 | tf_op jit(solution)/shard_map/ppermute | solution.py:636

commit v3 on v2

--- a/solution.py
+++ b/solution.py
@@ -11,12 +11,12 @@
 GC = 4
 SUB = 8
 LANE = 128
-VMEM_LIMIT = 48 * 1024 * 1024
+MIB = 1024 * 1024
 NT = (((1,), (1,)), ((), ()))
 
 
-def params():
-    return pltpu.CompilerParams(vmem_limit_bytes=VMEM_LIMIT)
+def params(mib=16):
+    return pltpu.CompilerParams(vmem_limit_bytes=mib * MIB)
 
 
 def low_half():
@@ -65,28 +65,31 @@
     return place * local_views + view % local_views
 
 
-def assemble_kernel(src_ref, place_ref, even_ref, odd_ref, even_far, odd_far, rows_ref, scratch):
+def assemble_kernel(src_ref, place_ref, *rest):
+    *map_refs, rows_ref, maps, scratch = rest
     local_views, per_view = src_ref.shape
     tiles = scratch.shape[0]
     pairs = local_views * per_view
-    half_views = even_ref.shape[0]
-    blocks = even_ref.shape[1] // SUB
+    view_count = maps.shape[1] // local_views
+    blocks = maps.shape[2] // SUB
     own_index = place_ref[0]
     parity = place_ref[1]
+    half = len(map_refs) // 2
+    for side in range(2):
+        first = 0
+        for ref in map_refs[side * half : (side + 1) * half]:
+            maps[side, first : first + ref.shape[0]] = ref[...]
+            first += ref.shape[0]
     for pair in range(pairs):
         view = src_ref[pair % local_views, pair // local_views]
-        slot = position(view, own_index, local_views, 2 * half_views // local_views)
-        odd = slot >= half_views
-        index = jnp.where(odd, slot - half_views, slot)
+        slot = position(view, own_index, local_views, view_count)
         for tile in range(tiles):
-            lanes = pl.ds(tile * LANE, LANE)
-            for side, even, other in ((parity, even_ref, odd_ref), (1 - parity, even_far, odd_far)):
-                maps = jnp.where(odd, other[index, :, lanes], even[index, :, lanes]).astype(
-                    jnp.float32
-                )
+            for side in range(2):
+                values = maps[side, slot, :, pl.ds(tile * LANE, LANE)].astype(jnp.float32)
+                held = parity if side == 0 else 1 - parity
                 for block in range(blocks):
-                    first = (2 * block + side) * (SUB * pairs) + pair
-                    scratch[tile, pl.ds(first, SUB, stride=pairs), :] = maps[
+                    first = (2 * block + held) * (SUB * pairs) + pair
+                    scratch[tile, pl.ds(first, SUB, stride=pairs), :] = values[
                         block * SUB : (block + 1) * SUB
                     ]
     for tile in range(tiles):
@@ -412,7 +415,7 @@
         )
 
 
-def spread_kernel(first, even_ref, received_ref, *out_refs):
+def spread_kernel(first, even_ref, received_ref, after_ref, *out_refs):
     size = out_refs[0].shape[0]
     for index, out_ref in enumerate(out_refs):
         span = pl.ds(first + index * size, size)
@@ -462,11 +465,12 @@
     def over_view(array, k):
         return lax.ppermute(array, "view", [(i, i ^ k) for i in range(view_count)])
 
-    evens = range(2, view_count, 2)
-    even = jnp.concatenate([mine] + [over_view(mine, k) for k in evens], axis=0)
-    odd = over_view(even, 1)
-    even_far = lax.ppermute(even, "plane", near)
-    odd_far = lax.ppermute(odd, "plane", near)
+    quarter = max(view_count // 4, 1)
+    even = [mine] + [over_view(mine, k) for k in range(2, view_count, 2)]
+    near_even = jnp.concatenate(even[:quarter], axis=0)
+    far_even = jnp.concatenate(even[quarter:], axis=0)
+    maps = [near_even, far_even, over_view(near_even, 1), over_view(far_even, 1)]
+    maps = maps + [lax.ppermute(part, "plane", near) for part in maps]
 
     packed = (pixels // (2 * LANE), G * SUB, LANE)
     refx, gates, cot = pl.pallas_call(
@@ -478,6 +482,7 @@
         ),
         in_specs=[SMEM(), pl.BlockSpec(), pl.BlockSpec()],
         compiler_params=params(),
+        cost_estimate=pl.CostEstimate(flops=10**9, bytes_accessed=4 * MIB, transcendentals=0),
         name="prep",
     )(view_gate, features, cotangent)
 
@@ -486,11 +491,14 @@
     rows = pl.pallas_call(
         assemble_kernel,
         out_shape=shape((channels * pairs, pixels), bf16),
-        in_specs=[SMEM(), SMEM()] + [pl.BlockSpec()] * 4,
-        scratch_shapes=[pltpu.VMEM((pixels // LANE, channels * pairs, LANE), f32)],
-        compiler_params=params(),
+        in_specs=[SMEM(), SMEM()] + [pl.BlockSpec()] * len(maps),
+        scratch_shapes=[
+            pltpu.VMEM((2, all_views, channels // 2, pixels), bf16),
+            pltpu.VMEM((pixels // LANE, channels * pairs, LANE), f32),
+        ],
+        compiler_params=params(24),
         name="assemble",
-    )(src_own, place, even, odd, even_far, odd_far)
+    )(src_own, place, *maps)
 
     width = 2 * LANE
     saved = (
@@ -533,7 +541,7 @@
         in_specs=edge_ins + [fixed(cot.shape)],
         out_specs=tuple(edge_outs) + (fixed((3,) + packed),) * 2,
         scratch_shapes=[pltpu.VMEM((4,) + packed, f32)] + chunks,
-        compiler_params=params(),
+        compiler_params=params(20),
         name="forward_edge",
     )(gates, rows, refx, warp_weights, warp_weights, cot)
     below = lax.ppermute(up_load, "plane", up)
@@ -547,7 +555,7 @@
         out_specs=tuple(inner_outs) + (fixed((planes - 4,) + packed),),
         scratch_shapes=chunks,
         input_output_aliases={5 + i: i for i in range(8)},
-        compiler_params=params(),
+        compiler_params=params(20),
         cost_estimate=pl.CostEstimate(
             flops=2 * channels * pairs * pixels * pixels * (planes - 4),
             bytes_accessed=40 * 1024 * 1024,
@@ -595,7 +603,7 @@
             pltpu.VMEM((pixels, pixels), bf16),
             pltpu.VMEM((all_views, channels, pixels), f32),
         ],
-        compiler_params=params(),
+        compiler_params=params(16 + 14 * all_views * channels * pixels // MIB),
         name="backward",
     )(src_own, place, gates, refx, warp_weights, *saved_values, cost, cost_grad)
 
@@ -610,7 +618,7 @@
             shape((close,) + piece[1:], bf16),
             shape((half_views - close,) + piece[1:], bf16),
         ),
-        compiler_params=params(),
+        compiler_params=params(32),
         name="split",
     )(keep, received)
     away = over_view(send_away, 1)
@@ -619,15 +627,17 @@
     away_parts = pl.pallas_call(
         functools.partial(spread_kernel, close),
         out_shape=(shape(piece, bf16),) * (view_count // 2 - count),
-        compiler_params=params(),
+        in_specs=[pl.BlockSpec(), pl.BlockSpec(), pl.BlockSpec(memory_space=pl.ANY)],
+        compiler_params=params(32),
         name="spread_away",
-    )(even_sum, away)
+    )(even_sum, away, away)
     total, *close_parts = pl.pallas_call(
         functools.partial(spread_kernel, 0),
         out_shape=(shape(piece, f32),) + (shape(piece, bf16),) * (count - 1),
-        compiler_params=params(),
+        in_specs=[pl.BlockSpec(), pl.BlockSpec(), pl.BlockSpec(memory_space=pl.ANY)],
+        compiler_params=params(32),
         name="spread_close",
-    )(even_sum, closer)
+    )(even_sum, closer, away_parts[0])
     for index, part in enumerate(away_parts):
         total = total + over_view(part, 2 * (count + index)).astype(f32)
     for index, part in enumerate(close_parts):

time: 101 us -> 124 us (1.23)
  local copies, waits for them, and re-layouts: 4.31 us -> 37.5 us
  Pallas kernels: 46.9 us -> 35.8 us
  starting transfers between devices: 19 us -> 22.4 us
  waiting for transfers between devices: 29.2 us -> 26.2 us
    unnamed x11 -> x42, local copies, waits for them, and re-layouts: 2.67 us -> 35.9 us
    pallas_call x1, Pallas kernels: 12 us -> 7.9 us  [shards(): pl.pallas_call(inner_kernel, out_shape=saved * 2 + (shape((planes - 4,) +...]
    pallas_call x1, Pallas kernels: 19.7 us -> 16.1 us  [shards(): pl.pallas_call(backward_kernel, out_shape=(shape(returned, f32), shape(re...]
    pallas_call x1, Pallas kernels: 7.19 us -> 4.1 us  [shards(): pl.pallas_call(edge_kernel, out_shape=saved * 2 + (shape((3,) + packed, f...]
    ppermute x9 -> x10, waiting for transfers between devices: 22.9 us -> 20 us  [over_view(): return lax.ppermute(array, 'view', [(i, i ^ k) for i in range(view_count)])]
    ppermute x9 -> x10, starting transfers between devices: 11.7 us -> 14.5 us  [over_view(): return lax.ppermute(array, 'view', [(i, i ^ k) for i in range(view_count)])]
  transfers between devices with their start and end apart: 16 -> 19, of which waited for: 9 -> 10; matrix products, arithmetic and copies ran while one was open for 0% -> 0% of each run, Pallas kernels for 13% -> 7%
where the time goes in v3:
time: 124 us; the launch traced here: 123 us
  local copies, waits for them, and re-layouts  37.5 us (30%)
  Pallas kernels  35.8 us (29%)
  waiting for transfers between devices  26.2 us (21%)
  starting transfers between devices  22.4 us (18%)
    unnamed x42, local copies, waits for them, and re-layouts  35.9 us
    ppermute x10, waiting for transfers between devices, over_view(): return lax.ppermute(array, 'view', [(i, i ^ k) for i in range(view_count)])  20 us
    pallas_call x1, Pallas kernels, shards(): pl.pallas_call(backward_kernel, out_shape=(shape(returned, f32), shape(re...  16.1 us
    ppermute x10, starting transfers between devices, over_view(): return lax.ppermute(array, 'view', [(i, i ^ k) for i in range(view_count)])  14.5 us
    pallas_call x1, Pallas kernels, shards(): pl.pallas_call(inner_kernel, out_shape=saved * 2 + (shape((planes - 4,) +...  7.9 us
    pallas_call x1, Pallas kernels, shards(): pl.pallas_call(conv_kernel, out_shape=(shape(cotangent.shape, bf16), shap...  5.24 us
    pallas_call x1, Pallas kernels, shards(): pl.pallas_call(edge_kernel, out_shape=saved * 2 + (shape((3,) + packed, f...  4.1 us
    ppermute x1, waiting for transfers between devices, shards(): total = total + lax.ppermute(total, 'plane', far)  3.27 us
  transfers between devices with their start and end apart: 19, of which 10 were waited for; matrix products, arithmetic and copies ran while one was open for 0% of the time, Pallas kernels for 7%

profile of v3, /device:TPU:0, one launch (start us, length us, event | category | flops | bytes accessed | tf_op | source)
XLA Modules:
  0.0 123.0 jit_solution(2963535824284451138)
XLA Ops:
  0.7 0.8 dynamic-slice_bitcast_fusion
  1.5 3.0 %collective-permute-start = (bf16[4,16,512]{2,1,0:T(8,128)(2,1)S(1)}, bf16[4,16,512]{2,1,0:T(8,128)(2,1)S(1)}, u32[]{:S(2)}, u32[]{:S(2)}) collective-permute-start(bf16[4,16,512]{2,1,0:T(8,128)(2,1)S(1)} %dynamic-slice_bitcast_fusion), channel_id=1, source_target_pairs={{0,8},{4,12},{8,0},{12,4},{16,24},{20,28},{24,16},{28,20},{1,9},{5... | collective-permute-start | bytes 196616 | tf_op jit(solution)/shard_map/ppermute | solution.py:466
  4.5 2.5 %collective-permute-start.2 = (bf16[4,16,512]{2,1,0:T(8,128)(2,1)S(1)}, bf16[4,16,512]{2,1,0:T(8,128)(2,1)S(1)}, u32[]{:S(2)}, u32[]{:S(2)}) collective-permute-start(bf16[4,16,512]{2,1,0:T(8,128)(2,1)S(1)} %dynamic-slice_bitcast_fusion), channel_id=1, source_target_pairs={{0,24},{4,28},{8,16},{12,20},{16,8},{20,12},{24,0},{28,4},{1,25},{... | collective-permute-start | bytes 196616 | tf_op jit(solution)/shard_map/ppermute | solution.py:466
  7.1 1.7 %collective-permute-start.3 = (bf16[8,16,512]{2,1,0:T(8,128)(2,1)S(1)}, bf16[8,16,512]{2,1,0:T(8,128)(2,1)S(1)}, u32[]{:S(2)}, u32[]{:S(2)}) collective-permute-start(bf16[8,16,512]{2,1,0:T(8,128)(2,1)S(1)} %pad_maximum_fusion.1.rest_0_), channel_id=1, source_target_pairs={{0,4},{4,0},{8,12},{12,8},{16,20},{20,16},{24,28},{28,24},{1,5},{5... | collective-permute-start | bytes 393224 | tf_op jit(solution)/shard_map/ppermute | solution.py:466
  8.8 4.6 %collective-permute-done.1 = bf16[4,16,512]{2,1,0:T(8,128)(2,1)S(1)} collective-permute-done((bf16[4,16,512]{2,1,0:T(8,128)(2,1)S(1)}, bf16[4,16,512]{2,1,0:T(8,128)(2,1)S(1)}, u32[]{:S(2)}, u32[]{:S(2)}) %collective-permute-start.1) | collective-permute-done | bytes 65568 | tf_op jit(solution)/shard_map/ppermute | solution.py:466
  13.5 1.6 %collective-permute-start.4 = (bf16[8,16,512]{2,1,0:T(8,128)(2,1)S(1)}, bf16[8,16,512]{2,1,0:T(8,128)(2,1)S(1)}, u32[]{:S(2)}, u32[]{:S(2)}) collective-permute-start(bf16[8,16,512]{2,1,0:T(8,128)(2,1)S(1)} %constant_dynamic-update-slice_fusion.rest_1_), channel_id=1, source_target_pairs={{0,4},{4,0},{8,12},{12,8},{16,20},{20,16},{24,28},{28,24},{1,5},{5... | collective-permute-start | bytes 393224 | tf_op jit(solution)/shard_map/ppermute | solution.py:466
  15.2 0.5 collective-permute-start.6
  15.7 3.2 %collective-permute-done.4.rest_3_ = bf16[8,16,512]{2,1,0:T(8,128)(2,1)S(1)} collective-permute-done((bf16[8,16,512]{2,1,0:T(8,128)(2,1)S(1)}, bf16[8,16,512]{2,1,0:T(8,128)(2,1)S(1)}, u32[]{:S(2)}, u32[]{:S(2)}) %collective-permute-start.4) | collective-permute-done | bytes 131104 | tf_op jit(solution)/shard_map/ppermute | solution.py:466
  18.9 0.9 copy-done.14
  19.8 1.0 copy-done.16
  20.8 0.7 copy-done.17
  21.5 0.8 prep.1
  22.5 1.6 %assemble.1.rows_ref = bf16[1280,512]{1,0:T(8,128)(2,1)S(1)} custom-call(s32[4,10]{1,0:T(4,128)S(1)} %copy.19.src_ref, s32[2]{0:T(128)S(1)} %pad_add_fusion.place_ref, bf16[8,16,512]{2,1,0:T(8,128)(2,1)S(1)} %pad_maximum_fusion.1.rest_0_, bf16[8,16,512]{2,1,0:T(8,128)(2,1)S(1)} %constant_dynamic-update-slice_fusion.rest_1_, ...), custom_call_target="tpu_custom_call" | custom-call | tf_op jit(solution)/shard_map/assemble/pallas_call | solution.py:491
  24.1 2.8 %copy-done.1 = bf16[12,512,512]{2,1,0:T(8,128)(2,1)S(1)} copy-done((bf16[12,512,512]{2,1,0:T(8,128)(2,1)S(1)}, bf16[12,512,512]{2,1,0:T(8,128)(2,1)}, u32[]{:S(2)}) %copy-start.1) | copy-done | bytes 6291480
  26.8 4.1 %forward_edge.1 = (bf16[12,1280,256]{2,1,0:T(8,128)(2,1)S(1)}, f32[12,8,40,256]{3,2,1,0:T(8,128)S(1)}, f32[12,40,256]{2,1,0:T(8,128)S(1)}, f32[12,8,256]{2,1,0:T...) custom-call(f32[8,8,128]{2,1,0:T(8,128)S(1)} %get-tuple-element.36.g, ...), custom_call_target="tpu_custom_call" | custom-call | tf_op jit(solution)/shard_map/forward_edge/pallas_call | solution.py:537
  31.0 3.1 %copy-done.3 = bf16[12,1280,256]{2,1,0:T(8,128)(2,1)} copy-done((bf16[12,1280,256]{2,1,0:T(8,128)(2,1)}, bf16[12,1280,256]{2,1,0:T(8,128)(2,1)S(1)}, u32[]{:S(2)}) %copy-start.3) | copy-done | bytes 7864344
  34.0 3.1 %copy-done.5 = bf16[12,1280,256]{2,1,0:T(8,128)(2,1)} copy-done((bf16[12,1280,256]{2,1,0:T(8,128)(2,1)}, bf16[12,1280,256]{2,1,0:T(8,128)(2,1)S(1)}, u32[]{:S(2)}) %copy-start.5) | copy-done | bytes 7864344
  37.1 1.9 %copy-done.8 = f32[12,8,40,256]{3,2,1,0:T(8,128)} copy-done((f32[12,8,40,256]{3,2,1,0:T(8,128)}, f32[12,8,40,256]{3,2,1,0:T(8,128)S(1)}, u32[]{:S(2)}) %copy-start.8) | copy-done | bytes 3932184
  39.0 1.9 %copy-done.10 = f32[12,8,40,256]{3,2,1,0:T(8,128)} copy-done((f32[12,8,40,256]{3,2,1,0:T(8,128)}, f32[12,8,40,256]{3,2,1,0:T(8,128)S(1)}, u32[]{:S(2)}) %copy-start.10) | copy-done | bytes 3932184
  40.9 2.4 %collective-permute-start.9 = (f32[3,2,64,128]{3,2,1,0:T(8,128)S(1)}, f32[3,2,64,128]{3,2,1,0:T(8,128)S(1)}, u32[]{:S(2)}, u32[]{:S(2)}) collective-permute-start(f32[3,2,64,128]{3,2,1,0:T(8,128)S(1)} %get-tuple-element.39.up_ref), channel_id=1, source_target_pairs={{0,1},{1,2},{2,3},{4,5},{5,6},{6,7},{8,9},{9,10},{10,11},{12,13},{... | collective-permute-start | bytes 589832 | tf_op jit(solution)/shard_map/ppermute | solution.py:547
  43.3 1.3 %collective-permute-start.10 = (f32[3,2,64,128]{3,2,1,0:T(8,128)S(1)}, f32[3,2,64,128]{3,2,1,0:T(8,128)S(1)}, u32[]{:S(2)}, u32[]{:S(2)}) collective-permute-start(f32[3,2,64,128]{3,2,1,0:T(8,128)S(1)} %get-tuple-element.40.down_ref), channel_id=1, source_target_pairs={{1,0},{2,1},{3,2},{5,4},{6,5},{7,6},{9,8},{10,9},{11,10},{13,12},{... | collective-permute-start | bytes 589832 | tf_op jit(solution)/shard_map/ppermute | solution.py:548
  44.6 2.8 %copy-done.2 = bf16[12,512,512]{2,1,0:T(8,128)(2,1)S(1)} copy-done((bf16[12,512,512]{2,1,0:T(8,128)(2,1)S(1)}, bf16[12,512,512]{2,1,0:T(8,128)(2,1)}, u32[]{:S(2)}) %copy-start.2) | copy-done | bytes 6291480
  47.4 3.2 %copy-done.4 = bf16[12,1280,256]{2,1,0:T(8,128)(2,1)S(1)} copy-done((bf16[12,1280,256]{2,1,0:T(8,128)(2,1)S(1)}, bf16[12,1280,256]{2,1,0:T(8,128)(2,1)}, u32[]{:S(2)}) %copy-start.4) | copy-done | bytes 7864344
  50.6 3.2 %copy-done.6 = bf16[12,1280,256]{2,1,0:T(8,128)(2,1)S(1)} copy-done((bf16[12,1280,256]{2,1,0:T(8,128)(2,1)S(1)}, bf16[12,1280,256]{2,1,0:T(8,128)(2,1)}, u32[]{:S(2)}) %copy-start.6) | copy-done | bytes 7864344
  53.9 2.1 %copy-done.9 = f32[12,8,40,256]{3,2,1,0:T(8,128)S(1)} copy-done((f32[12,8,40,256]{3,2,1,0:T(8,128)S(1)}, f32[12,8,40,256]{3,2,1,0:T(8,128)}, u32[]{:S(2)}) %copy-start.9) | copy-done | bytes 3932184
  56.0 2.1 %copy-done.11 = f32[12,8,40,256]{3,2,1,0:T(8,128)S(1)} copy-done((f32[12,8,40,256]{3,2,1,0:T(8,128)S(1)}, f32[12,8,40,256]{3,2,1,0:T(8,128)}, u32[]{:S(2)}) %copy-start.11) | copy-done | bytes 3932184
  58.1 7.9 %forward_inner.1 = (bf16[12,1280,256]{2,1,0:T(8,128)(2,1)S(1)}, f32[12,8,40,256]{3,2,1,0:T(8,128)S(1)}, f32[12,40,256]{2,1,0:T(8,128)S(1)}, f32[12,8,256]{2,1,0:...) custom-call(f32[8,8,128]{2,1,0:T(8,128)S(1)} %get-tuple-element.36.g, ...), custom_call_target="tpu_custom_call", output_to_operand_aliasing={{0}: (5, {}), {1}: (6, {}), {2}: (7, {}), {3}: (8, {}), {4}... | custom-call | flops 5368709120 | bytes 41943040 | tf_op jit(solution)/shard_map/forward_inner/pallas_call | solution.py:550
  66.0 3.1 %copy-done.7 = bf16[12,1280,256]{2,1,0:T(8,128)(2,1)} copy-done((bf16[12,1280,256]{2,1,0:T(8,128)(2,1)}, bf16[12,1280,256]{2,1,0:T(8,128)(2,1)S(1)}, u32[]{:S(2)}) %copy-start.7) | copy-done | bytes 7864344
  69.1 1.9 %copy-done.12 = f32[12,8,40,256]{3,2,1,0:T(8,128)} copy-done((f32[12,8,40,256]{3,2,1,0:T(8,128)}, f32[12,8,40,256]{3,2,1,0:T(8,128)S(1)}, u32[]{:S(2)}) %copy-start.12) | copy-done | bytes 3932184
  71.0 5.2 %depth_conv.1 = (bf16[4,12,8,512]{3,2,1,0:T(8,128)(2,1)}, f32[12,2,64,128]{3,2,1,0:T(8,128)S(1)}, f32[12,2,64,128]{3,2,1,0:T(8,128)S(1)}) custom-call(f32[3,8,8]{2,1,0:T(8,128)S(1)} %copy-done.15, f32[3,2,64,128]{3,2,1,0:T(8,128)S(1)} %collective-permute-done.9.below_ref, f32[3,2,64,128]{3,2,1,0:T(8,128)S(1)} %get-tuple-element.40.down_ref, ...), custom_call_target="tpu_custom_call" | custom-call | tf_op jit(solution)/shard_map/depth_conv/pallas_call | solution.py:567
  76.2 2.1 %copy-done.13 = f32[12,8,40,256]{3,2,1,0:T(8,128)S(1)} copy-done((f32[12,8,40,256]{3,2,1,0:T(8,128)S(1)}, f32[12,8,40,256]{3,2,1,0:T(8,128)}, u32[]{:S(2)}) %copy-start.13) | copy-done | bytes 3932184
  78.3 16.1 %backward.1 = (f32[32,16,512]{2,1,0:T(8,128)S(1)}, bf16[32,16,512]{2,1,0:T(8,128)(2,1)S(1)}) custom-call(s32[4,10]{1,0:T(4,128)S(1)} %copy.19.src_ref, s32[2]{0:T(128)S(1)} %pad_add_fusion.place_ref, f32[8,8,128]{2,1,0:T(8,128)S(1)} %get-tuple-element.36.gates_ref, f32[4,256,128]{2,1,0:T(8,128)S(1)} %get-tuple-element.37.refx_ref, ...), custom_call_target="tpu_custom_call" | custom-call | tf_op jit(solution)/shard_map/backward/pallas_call | solution.py:588
  94.4 1.8 %collective-permute-start.11 = (bf16[32,16,512]{2,1,0:T(8,128)(2,1)S(1)}, bf16[32,16,512]{2,1,0:T(8,128)(2,1)S(1)}, u32[]{:S(2)}, u32[]{:S(2)}) collective-permute-start(bf16[32,16,512]{2,1,0:T(8,128)(2,1)S(1)} %get-tuple-element.62), channel_id=1, source_target_pairs={{0,1},{1,0},{2,3},{3,2},{4,5},{5,4},{6,7},{7,6},{8,9},{9,8},{10,11... | collective-permute-start | bytes 1572872 | tf_op jit(solution)/shard_map/ppermute | solution.py:610
  96.2 1.5 %collective-permute-done.11.received_ref = bf16[32,16,512]{2,1,0:T(8,128)(2,1)S(1)} collective-permute-done((bf16[32,16,512]{2,1,0:T(8,128)(2,1)S(1)}, bf16[32,16,512]{2,1,0:T(8,128)(2,1)S(1)}, u32[]{:S(2)}, u32[]{:S(2)}) %collective-permute-start.11) | collective-permute-done | bytes 524320 | tf_op jit(solution)/shard_map/ppermute | solution.py:610
  97.7 0.1 split.1
  97.8 1.6 %collective-permute-start.13 = (bf16[8,16,512]{2,1,0:T(8,128)(2,1)S(1)}, bf16[8,16,512]{2,1,0:T(8,128)(2,1)S(1)}, u32[]{:S(2)}, u32[]{:S(2)}) collective-permute-start(bf16[8,16,512]{2,1,0:T(8,128)(2,1)S(1)} %get-tuple-element.65), channel_id=1, source_target_pairs={{0,4},{4,0},{8,12},{12,8},{16,20},{20,16},{24,28},{28,24},{1,5},{5... | collective-permute-start | bytes 393224 | tf_op jit(solution)/shard_map/ppermute | solution.py:466
  99.5 0.5 collective-permute-start.12
  99.9 4.3 %collective-permute-done.13.received_ref.after_ref = bf16[8,16,512]{2,1,0:T(8,128)(2,1)S(1)} collective-permute-done((bf16[8,16,512]{2,1,0:T(8,128)(2,1)S(1)}, bf16[8,16,512]{2,1,0:T(8,128)(2,1)S(1)}, u32[]{:S(2)}, u32[]{:S(2)}) %collective-permute-start.13) | collective-permute-done | bytes 131104 | tf_op jit(solution)/shard_map/ppermute | solution.py:466
  104.3 2.2 %collective-permute-done.12.received_ref = bf16[8,16,512]{2,1,0:T(8,128)(2,1)S(1)} collective-permute-done((bf16[8,16,512]{2,1,0:T(8,128)(2,1)S(1)}, bf16[8,16,512]{2,1,0:T(8,128)(2,1)S(1)}, u32[]{:S(2)}, u32[]{:S(2)}) %collective-permute-start.12) | collective-permute-done | bytes 131104 | tf_op jit(solution)/shard_map/ppermute | solution.py:466
  106.6 2.1 %collective-permute-start.15 = (bf16[4,16,512]{2,1,0:T(8,128)(2,1)S(1)}, bf16[4,16,512]{2,1,0:T(8,128)(2,1)S(1)}, u32[]{:S(2)}, u32[]{:S(2)}) collective-permute-start(bf16[4,16,512]{2,1,0:T(8,128)(2,1)S(1)} %get-tuple-element.68), channel_id=1, source_target_pairs={{0,24},{4,28},{8,16},{12,20},{16,8},{20,12},{24,0},{28,4},{1,25},{... | collective-permute-start | bytes 196616 | tf_op jit(solution)/shard_map/ppermute | solution.py:466
  108.7 1.4 %collective-permute-start.14 = (bf16[4,16,512]{2,1,0:T(8,128)(2,1)S(1)}, bf16[4,16,512]{2,1,0:T(8,128)(2,1)S(1)}, u32[]{:S(2)}, u32[]{:S(2)}) collective-permute-start(bf16[4,16,512]{2,1,0:T(8,128)(2,1)S(1)} %get-tuple-element.66.after_ref), channel_id=1, source_target_pairs={{0,16},{4,20},{8,24},{12,28},{16,0},{20,4},{24,8},{28,12},{1,17},{... | collective-permute-start | bytes 196616 | tf_op jit(solution)/shard_map/ppermute | solution.py:466
  110.1 1.1 collective-permute-done.16
  111.2 1.9 %collective-permute-done.15 = bf16[4,16,512]{2,1,0:T(8,128)(2,1)S(1)} collective-permute-done((bf16[4,16,512]{2,1,0:T(8,128)(2,1)S(1)}, bf16[4,16,512]{2,1,0:T(8,128)(2,1)S(1)}, u32[]{:S(2)}, u32[]{:S(2)}) %collective-permute-start.15) | collective-permute-done | bytes 65568 | tf_op jit(solution)/shard_map/ppermute | solution.py:466
  113.1 2.7 %collective-permute-done.14 = bf16[4,16,512]{2,1,0:T(8,128)(2,1)S(1)} collective-permute-done((bf16[4,16,512]{2,1,0:T(8,128)(2,1)S(1)}, bf16[4,16,512]{2,1,0:T(8,128)(2,1)S(1)}, u32[]{:S(2)}, u32[]{:S(2)}) %collective-permute-start.14) | collective-permute-done | bytes 65568 | tf_op jit(solution)/shard_map/ppermute | solution.py:466
  115.8 1.8 %collective-permute-start.17 = (f32[4,16,512]{2,1,0:T(8,128)S(1)}, f32[4,16,512]{2,1,0:T(8,128)S(1)}, u32[]{:S(2)}, u32[]{:S(2)}) collective-permute-start(f32[4,16,512]{2,1,0:T(8,128)S(1)} %convert_add_fusion), channel_id=1, source_target_pairs={{0,2},{1,3},{2,0},{3,1},{4,6},{5,7},{6,4},{7,5},{8,10},{9,11},{10,... | collective-permute-start | bytes 393224 | tf_op jit(solution)/shard_map/ppermute | solution.py:645
  117.6 3.3 %collective-permute-done.17 = f32[4,16,512]{2,1,0:T(8,128)S(1)} collective-permute-done((f32[4,16,512]{2,1,0:T(8,128)S(1)}, f32[4,16,512]{2,1,0:T(8,128)S(1)}, u32[]{:S(2)}, u32[]{:S(2)}) %collective-permute-start.17) | collective-permute-done | bytes 131104 | tf_op jit(solution)/shard_map/ppermute | solution.py:645
  120.9 1.3 %collective-permute-done.18 = f32[4,16,512]{2,1,0:T(8,128)S(1)} collective-permute-done((f32[4,16,512]{2,1,0:T(8,128)S(1)}, f32[4,16,512]{2,1,0:T(8,128)S(1)}, u32[]{:S(2)}, u32[]{:S(2)}) %collective-permute-start.18) | collective-permute-done | bytes 131104 | tf_op jit(solution)/shard_map/ppermute | solution.py:646
  122.3 0.7 copy.18
  (52 shorter events, 0.8 us)
Async XLA Ops:
  0.6 14.4 %copy-start = (s32[32,10]{0,1:T(8,128)S(1)}, s32[32,10]{0,1:T(8,128)}, u32[]{:S(2)}) copy-start(s32[32,10]{0,1:T(8,128)} %param.7) | copy-start | bytes 3844
  1.5 5.6 %collective-permute-start = (bf16[4,16,512]{2,1,0:T(8,128)(2,1)S(1)}, bf16[4,16,512]{2,1,0:T(8,128)(2,1)S(1)}, u32[]{:S(2)}, u32[]{:S(2)}) collective-permute-start(bf16[4,16,512]{2,1,0:T(8,128)(2,1)S(1)} %dynamic-slice_bitcast_fusion), channel_id=1, source_target_pairs={{0,8},{4,12},{8,0},{12,4},{16,24},{20,28},{24,16},{28,20},{1,9},{5... | collective-permute-start | bytes 196616 | tf_op jit(solution)/shard_map/ppermute | solution.py:466
  4.5 8.9 %collective-permute-start.2 = (bf16[4,16,512]{2,1,0:T(8,128)(2,1)S(1)}, bf16[4,16,512]{2,1,0:T(8,128)(2,1)S(1)}, u32[]{:S(2)}, u32[]{:S(2)}) collective-permute-start(bf16[4,16,512]{2,1,0:T(8,128)(2,1)S(1)} %dynamic-slice_bitcast_fusion), channel_id=1, source_target_pairs={{0,24},{4,28},{8,16},{12,20},{16,8},{20,12},{24,0},{28,4},{1,25},{... | collective-permute-start | bytes 196616 | tf_op jit(solution)/shard_map/ppermute | solution.py:466
  7.0 6.4 %collective-permute-start.1 = (bf16[4,16,512]{2,1,0:T(8,128)(2,1)S(1)}, bf16[4,16,512]{2,1,0:T(8,128)(2,1)S(1)}, u32[]{:S(2)}, u32[]{:S(2)}) collective-permute-start(bf16[4,16,512]{2,1,0:T(8,128)(2,1)S(1)} %dynamic-slice_bitcast_fusion), channel_id=1, source_target_pairs={{0,16},{4,20},{8,24},{12,28},{16,0},{20,4},{24,8},{28,12},{1,17},{... | collective-permute-start | bytes 196616 | tf_op jit(solution)/shard_map/ppermute | solution.py:466
  7.1 8.5 %collective-permute-start.3 = (bf16[8,16,512]{2,1,0:T(8,128)(2,1)S(1)}, bf16[8,16,512]{2,1,0:T(8,128)(2,1)S(1)}, u32[]{:S(2)}, u32[]{:S(2)}) collective-permute-start(bf16[8,16,512]{2,1,0:T(8,128)(2,1)S(1)} %pad_maximum_fusion.1.rest_0_), channel_id=1, source_target_pairs={{0,4},{4,0},{8,12},{12,8},{16,20},{20,16},{24,28},{28,24},{1,5},{5... | collective-permute-start | bytes 393224 | tf_op jit(solution)/shard_map/ppermute | solution.py:466
  13.5 5.4 %collective-permute-start.4 = (bf16[8,16,512]{2,1,0:T(8,128)(2,1)S(1)}, bf16[8,16,512]{2,1,0:T(8,128)(2,1)S(1)}, u32[]{:S(2)}, u32[]{:S(2)}) collective-permute-start(bf16[8,16,512]{2,1,0:T(8,128)(2,1)S(1)} %constant_dynamic-update-slice_fusion.rest_1_), channel_id=1, source_target_pairs={{0,4},{4,0},{8,12},{12,8},{16,20},{20,16},{24,28},{28,24},{1,5},{5... | collective-permute-start | bytes 393224 | tf_op jit(solution)/shard_map/ppermute | solution.py:466
  15.1 7.3 %collective-permute-start.5 = (bf16[8,16,512]{2,1,0:T(8,128)(2,1)S(1)}, bf16[8,16,512]{2,1,0:T(8,128)(2,1)S(1)}, u32[]{:S(2)}, u32[]{:S(2)}) collective-permute-start(bf16[8,16,512]{2,1,0:T(8,128)(2,1)S(1)} %pad_maximum_fusion.1.rest_0_), channel_id=1, source_target_pairs={{0,1},{1,0},{2,3},{3,2},{4,5},{5,4},{6,7},{7,6},{8,9},{9,8},{10,11... | collective-permute-start | bytes 393224 | tf_op jit(solution)/shard_map/ppermute | solution.py:473
  15.2 7.3 %collective-permute-start.6 = (bf16[8,16,512]{2,1,0:T(8,128)(2,1)S(1)}, bf16[8,16,512]{2,1,0:T(8,128)(2,1)S(1)}, u32[]{:S(2)}, u32[]{:S(2)}) collective-permute-start(bf16[8,16,512]{2,1,0:T(8,128)(2,1)S(1)} %constant_dynamic-update-slice_fusion.rest_1_), channel_id=1, source_target_pairs={{0,1},{1,0},{2,3},{3,2},{4,5},{5,4},{6,7},{7,6},{8,9},{9,8},{10,11... | collective-permute-start | bytes 393224 | tf_op jit(solution)/shard_map/ppermute | solution.py:473
  15.7 6.8 %collective-permute-start.7 = (bf16[8,16,512]{2,1,0:T(8,128)(2,1)S(1)}, bf16[8,16,512]{2,1,0:T(8,128)(2,1)S(1)}, u32[]{:S(2)}, u32[]{:S(2)}) collective-permute-start(bf16[8,16,512]{2,1,0:T(8,128)(2,1)S(1)} %collective-permute-done.3.rest_2_), channel_id=1, source_target_pairs={{0,1},{1,0},{2,3},{3,2},{4,5},{5,4},{6,7},{7,6},{8,9},{9,8},{10,11... | collective-permute-start | bytes 393224 | tf_op jit(solution)/shard_map/ppermute | solution.py:473
  18.9 3.5 %collective-permute-start.8 = (bf16[8,16,512]{2,1,0:T(8,128)(2,1)S(1)}, bf16[8,16,512]{2,1,0:T(8,128)(2,1)S(1)}, u32[]{:S(2)}, u32[]{:S(2)}) collective-permute-start(bf16[8,16,512]{2,1,0:T(8,128)(2,1)S(1)} %collective-permute-done.4.rest_3_), channel_id=1, source_target_pairs={{0,1},{1,0},{2,3},{3,2},{4,5},{5,4},{6,7},{7,6},{8,9},{9,8},{10,11... | collective-permute-start | bytes 393224 | tf_op jit(solution)/shard_map/ppermute | solution.py:473
  18.9 0.9 copy-start.14
  19.8 1.0 copy-start.16
  20.8 0.7 copy-start.17
  24.1 2.8 %copy-start.1 = (bf16[12,512,512]{2,1,0:T(8,128)(2,1)S(1)}, bf16[12,512,512]{2,1,0:T(8,128)(2,1)}, u32[]{:S(2)}) copy-start(bf16[12,512,512]{2,1,0:T(8,128)(2,1)} %w_ref.1) | copy-start | bytes 18874372
  26.8 49.4 %slice-start = ((s8[6291456]{0:T(1024)(128)(4,1)}), s8[2097152]{0:T(1024)(128)(4,1)S(1)}, s32[]{:S(2)}) async-start(s8[6291456]{0:T(1024)(128)(4,1)} %bitcast.12), calls=%async_computation | async-start | bytes 4194304
  31.0 3.1 %copy-start.3 = (bf16[12,1280,256]{2,1,0:T(8,128)(2,1)}, bf16[12,1280,256]{2,1,0:T(8,128)(2,1)S(1)}, u32[]{:S(2)}) copy-start(bf16[12,1280,256]{2,1,0:T(8,128)(2,1)S(1)} %get-tuple-element.41.rest_0_) | copy-start | bytes 23592964
  34.0 3.1 %copy-start.5 = (bf16[12,1280,256]{2,1,0:T(8,128)(2,1)}, bf16[12,1280,256]{2,1,0:T(8,128)(2,1)S(1)}, u32[]{:S(2)}) copy-start(bf16[12,1280,256]{2,1,0:T(8,128)(2,1)S(1)} %get-tuple-element.45.rest_4_) | copy-start | bytes 23592964
  37.1 1.9 %copy-start.8 = (f32[12,8,40,256]{3,2,1,0:T(8,128)}, f32[12,8,40,256]{3,2,1,0:T(8,128)S(1)}, u32[]{:S(2)}) copy-start(f32[12,8,40,256]{3,2,1,0:T(8,128)S(1)} %get-tuple-element.42.rest_1_) | copy-start | bytes 11796484
  39.0 1.9 %copy-start.10 = (f32[12,8,40,256]{3,2,1,0:T(8,128)}, f32[12,8,40,256]{3,2,1,0:T(8,128)S(1)}, u32[]{:S(2)}) copy-start(f32[12,8,40,256]{3,2,1,0:T(8,128)S(1)} %get-tuple-element.46.rest_5_) | copy-start | bytes 11796484
  40.9 30.1 %collective-permute-start.9 = (f32[3,2,64,128]{3,2,1,0:T(8,128)S(1)}, f32[3,2,64,128]{3,2,1,0:T(8,128)S(1)}, u32[]{:S(2)}, u32[]{:S(2)}) collective-permute-start(f32[3,2,64,128]{3,2,1,0:T(8,128)S(1)} %get-tuple-element.39.up_ref), channel_id=1, source_target_pairs={{0,1},{1,2},{2,3},{4,5},{5,6},{6,7},{8,9},{9,10},{10,11},{12,13},{... | collective-permute-start | bytes 589832 | tf_op jit(solution)/shard_map/ppermute | solution.py:547
  43.3 27.6 %collective-permute-start.10 = (f32[3,2,64,128]{3,2,1,0:T(8,128)S(1)}, f32[3,2,64,128]{3,2,1,0:T(8,128)S(1)}, u32[]{:S(2)}, u32[]{:S(2)}) collective-permute-start(f32[3,2,64,128]{3,2,1,0:T(8,128)S(1)} %get-tuple-element.40.down_ref), channel_id=1, source_target_pairs={{1,0},{2,1},{3,2},{5,4},{6,5},{7,6},{9,8},{10,9},{11,10},{13,12},{... | collective-permute-start | bytes 589832 | tf_op jit(solution)/shard_map/ppermute | solution.py:548
  44.6 2.8 %copy-start.2 = (bf16[12,512,512]{2,1,0:T(8,128)(2,1)S(1)}, bf16[12,512,512]{2,1,0:T(8,128)(2,1)}, u32[]{:S(2)}) copy-start(bf16[12,512,512]{2,1,0:T(8,128)(2,1)} %w_ref.1) | copy-start | bytes 18874372
  47.4 3.2 %copy-start.4 = (bf16[12,1280,256]{2,1,0:T(8,128)(2,1)S(1)}, bf16[12,1280,256]{2,1,0:T(8,128)(2,1)}, u32[]{:S(2)}) copy-start(bf16[12,1280,256]{2,1,0:T(8,128)(2,1)} %copy-done.3) | copy-start | bytes 23592964
  50.6 3.2 %copy-start.6 = (bf16[12,1280,256]{2,1,0:T(8,128)(2,1)S(1)}, bf16[12,1280,256]{2,1,0:T(8,128)(2,1)}, u32[]{:S(2)}) copy-start(bf16[12,1280,256]{2,1,0:T(8,128)(2,1)} %copy-done.5) | copy-start | bytes 23592964
  53.9 2.1 %copy-start.9 = (f32[12,8,40,256]{3,2,1,0:T(8,128)S(1)}, f32[12,8,40,256]{3,2,1,0:T(8,128)}, u32[]{:S(2)}) copy-start(f32[12,8,40,256]{3,2,1,0:T(8,128)} %copy-done.8) | copy-start | bytes 11796484
  56.0 2.1 %copy-start.11 = (f32[12,8,40,256]{3,2,1,0:T(8,128)S(1)}, f32[12,8,40,256]{3,2,1,0:T(8,128)}, u32[]{:S(2)}) copy-start(f32[12,8,40,256]{3,2,1,0:T(8,128)} %copy-done.10) | copy-start | bytes 11796484
  58.1 12.9 %copy-start.15 = (f32[3,8,8]{2,1,0:T(8,128)S(1)}, f32[3,8,8]{2,1,0:T(8,128)}, u32[]{:S(2)}) copy-start(f32[3,8,8]{2,1,0:T(8,128)} %taps_ref.1) | copy-start | bytes 2308
  58.1 18.1 %slice-start.1 = ((s8[6291456]{0:T(1024)(128)(4,1)}), s8[4194304]{0:T(1024)(128)(4,1)S(1)}, s32[]{:S(2)}) async-start(s8[6291456]{0:T(1024)(128)(4,1)} %bitcast.12), calls=%async_computation.1 | async-start | bytes 8388608
  66.0 3.1 %copy-start.7 = (bf16[12,1280,256]{2,1,0:T(8,128)(2,1)}, bf16[12,1280,256]{2,1,0:T(8,128)(2,1)S(1)}, u32[]{:S(2)}) copy-start(bf16[12,1280,256]{2,1,0:T(8,128)(2,1)S(1)} %get-tuple-element.55.rest_4_) | copy-start | bytes 23592964
  69.1 1.9 %copy-start.12 = (f32[12,8,40,256]{3,2,1,0:T(8,128)}, f32[12,8,40,256]{3,2,1,0:T(8,128)S(1)}, u32[]{:S(2)}) copy-start(f32[12,8,40,256]{3,2,1,0:T(8,128)S(1)} %get-tuple-element.56.rest_5_) | copy-start | bytes 11796484
  76.2 2.1 %copy-start.13 = (f32[12,8,40,256]{3,2,1,0:T(8,128)S(1)}, f32[12,8,40,256]{3,2,1,0:T(8,128)}, u32[]{:S(2)}) copy-start(f32[12,8,40,256]{3,2,1,0:T(8,128)} %copy-done.12) | copy-start | bytes 11796484
  94.4 3.3 %collective-permute-start.11 = (bf16[32,16,512]{2,1,0:T(8,128)(2,1)S(1)}, bf16[32,16,512]{2,1,0:T(8,128)(2,1)S(1)}, u32[]{:S(2)}, u32[]{:S(2)}) collective-permute-start(bf16[32,16,512]{2,1,0:T(8,128)(2,1)S(1)} %get-tuple-element.62), channel_id=1, source_target_pairs={{0,1},{1,0},{2,3},{3,2},{4,5},{5,4},{6,7},{7,6},{8,9},{9,8},{10,11... | collective-permute-start | bytes 1572872 | tf_op jit(solution)/shard_map/ppermute | solution.py:610
  97.8 6.4 %collective-permute-start.13 = (bf16[8,16,512]{2,1,0:T(8,128)(2,1)S(1)}, bf16[8,16,512]{2,1,0:T(8,128)(2,1)S(1)}, u32[]{:S(2)}, u32[]{:S(2)}) collective-permute-start(bf16[8,16,512]{2,1,0:T(8,128)(2,1)S(1)} %get-tuple-element.65), channel_id=1, source_target_pairs={{0,4},{4,0},{8,12},{12,8},{16,20},{20,16},{24,28},{28,24},{1,5},{5... | collective-permute-start | bytes 393224 | tf_op jit(solution)/shard_map/ppermute | solution.py:466
  99.5 7.0 %collective-permute-start.12 = (bf16[8,16,512]{2,1,0:T(8,128)(2,1)S(1)}, bf16[8,16,512]{2,1,0:T(8,128)(2,1)S(1)}, u32[]{:S(2)}, u32[]{:S(2)}) collective-permute-start(bf16[8,16,512]{2,1,0:T(8,128)(2,1)S(1)} %get-tuple-element.64), channel_id=1, source_target_pairs={{0,4},{4,0},{8,12},{12,8},{16,20},{20,16},{24,28},{28,24},{1,5},{5... | collective-permute-start | bytes 393224 | tf_op jit(solution)/shard_map/ppermute | solution.py:466
  106.5 4.7 %collective-permute-start.16 = (bf16[4,16,512]{2,1,0:T(8,128)(2,1)S(1)}, bf16[4,16,512]{2,1,0:T(8,128)(2,1)S(1)}, u32[]{:S(2)}, u32[]{:S(2)}) collective-permute-start(bf16[4,16,512]{2,1,0:T(8,128)(2,1)S(1)} %get-tuple-element.69), channel_id=1, source_target_pairs={{0,8},{4,12},{8,0},{12,4},{16,24},{20,28},{24,16},{28,20},{1,9},{5... | collective-permute-start | bytes 196616 | tf_op jit(solution)/shard_map/ppermute | solution.py:466
  106.6 6.5 %collective-permute-start.15 = (bf16[4,16,512]{2,1,0:T(8,128)(2,1)S(1)}, bf16[4,16,512]{2,1,0:T(8,128)(2,1)S(1)}, u32[]{:S(2)}, u32[]{:S(2)}) collective-permute-start(bf16[4,16,512]{2,1,0:T(8,128)(2,1)S(1)} %get-tuple-element.68), channel_id=1, source_target_pairs={{0,24},{4,28},{8,16},{12,20},{16,8},{20,12},{24,0},{28,4},{1,25},{... | collective-permute-start | bytes 196616 | tf_op jit(solution)/shard_map/ppermute | solution.py:466
  108.7 7.1 %collective-permute-start.14 = (bf16[4,16,512]{2,1,0:T(8,128)(2,1)S(1)}, bf16[4,16,512]{2,1,0:T(8,128)(2,1)S(1)}, u32[]{:S(2)}, u32[]{:S(2)}) collective-permute-start(bf16[4,16,512]{2,1,0:T(8,128)(2,1)S(1)} %get-tuple-element.66.after_ref), channel_id=1, source_target_pairs={{0,16},{4,20},{8,24},{12,28},{16,0},{20,4},{24,8},{28,12},{1,17},{... | collective-permute-start | bytes 196616 | tf_op jit(solution)/shard_map/ppermute | solution.py:466
  115.8 5.0 %collective-permute-start.17 = (f32[4,16,512]{2,1,0:T(8,128)S(1)}, f32[4,16,512]{2,1,0:T(8,128)S(1)}, u32[]{:S(2)}, u32[]{:S(2)}) collective-permute-start(f32[4,16,512]{2,1,0:T(8,128)S(1)} %convert_add_fusion), channel_id=1, source_target_pairs={{0,2},{1,3},{2,0},{3,1},{4,6},{5,7},{6,4},{7,5},{8,10},{9,11},{10,... | collective-permute-start | bytes 393224 | tf_op jit(solution)/shard_map/ppermute | solution.py:645
  120.8 1.4 %collective-permute-start.18 = (f32[4,16,512]{2,1,0:T(8,128)S(1)}, f32[4,16,512]{2,1,0:T(8,128)S(1)}, u32[]{:S(2)}, u32[]{:S(2)}) collective-permute-start(f32[4,16,512]{2,1,0:T(8,128)S(1)} %add.29), channel_id=1, source_target_pairs={{0,1},{1,0},{2,3},{3,2},{4,5},{5,4},{6,7},{7,6},{8,9},{9,8},{10,11... | collective-permute-start | bytes 393224 | tf_op jit(solution)/shard_map/ppermute | solution.py:646

commit v4 on v3

--- a/solution.py
+++ b/solution.py
@@ -96,13 +96,14 @@
         rows_ref[:, pl.ds(tile * LANE, LANE)] = scratch[tile].astype(jnp.bfloat16)
 
 
-def forward_vector(gates_ref, refx_ref, chunk, first_tile, half, outs):
+def forward_vector(gates_ref, refx_ref, chunk, tile, outs):
     warped_ref, corr_ref, sig_ref, rden_ref = outs
-    groups, pairs = corr_ref.shape[1:3]
+    pairs = sig_ref.shape[1]
     tiles = pairs // SUB
-    lanes = pl.ds(half * LANE, LANE)
+    lanes = pl.ds((tile % 2) * LANE, LANE)
     logits = None
-    for g in range(groups):
+    corrs = []
+    for g in range(G):
         total = None
         for j in range(0, GC, 2):
             c = g * GC + j
@@ -111,12 +112,15 @@
             warped_ref[0, span, lanes] = both.astype(jnp.bfloat16)
             both = both.reshape(2, tiles, SUB, LANE)
             for i in range(2):
-                part = both[i] * refx_ref[first_tile + half, pl.ds((c + i) * SUB, SUB), :][None]
+                part = both[i] * refx_ref[tile, pl.ds((c + i) * SUB, SUB), :][None]
                 total = part if total is None else total + part
         corr = total * (1.0 / GC)
-        corr_ref[0, g, :, lanes] = corr.reshape(pairs, LANE)
+        corrs.append(corr)
         part = corr * gates_ref[g][None]
         logits = part if logits is None else logits + part
+        if g % 2 == 1:
+            both = jnp.concatenate([item.reshape(pairs, LANE) for item in corrs[-2:]], axis=0)
+            corr_ref[0, pl.ds((g - 1) * pairs, 2 * pairs), lanes] = both.astype(jnp.bfloat16)
     sig = jax.nn.sigmoid(logits)
     sig_ref[0, :, lanes] = sig.reshape(pairs, LANE)
     visible = 0.5 + sig
@@ -124,33 +128,44 @@
     rden = 1.0 / (den + swap_halves(den))
     rden_ref[0, :, lanes] = rden
     costs = []
-    for g in range(groups):
-        num = jnp.sum(visible * corr_ref[0, g, :, lanes].reshape(tiles, SUB, LANE), axis=0)
+    for g in range(G):
+        num = jnp.sum(visible * corrs[g], axis=0)
         costs.append((num + swap_halves(num)) * rden)
     return costs
 
 
-def forward_dot(rows_ref, w_ref, chunk, part, parts):
-    count = rows_ref.shape[0] // parts
-    span = pl.ds(part * count, count)
-    chunk[span, :] = lax.dot_general(
-        rows_ref[span, :], w_ref[0], NT, preferred_element_type=jnp.float32
-    )
-
-
-def forward_body(gates_ref, rows_ref, refx_ref, w0_ref, w1_ref, outs, cost_ref, chunks):
+def weight_copy(w_ref, held, sems, plane, slot):
+    return pltpu.make_async_copy(w_ref.at[plane], held.at[slot], sems.at[slot])
+
+
+def forward_body(plane_of, gates_ref, rows_ref, refx_ref, w_ref, outs, cost_ref, scratch):
+    held, sems, *chunks = scratch
     step = pl.program_id(0)
     count = pl.num_programs(0) - 1
+    slot = lax.rem(step, 2)
     low = low_half()
 
-    def vector(index, plane, matmul):
+    def matmul(index, part):
+        rows = pl.ds(part * (rows_ref.shape[0] // 2), rows_ref.shape[0] // 2)
+        chunks[index][rows, :] = lax.dot_general(
+            rows_ref[rows, :],
+            held[slot, pl.ds(index * 2 * LANE, 2 * LANE), :],
+            NT,
+            preferred_element_type=jnp.float32,
+        )
+
+    def vector(index, plane, beside):
         costs = []
         for half in range(2):
-            if matmul is not None:
-                matmul(half)
+            if beside is not None:
+                matmul(beside, half)
             costs.append(
                 forward_vector(
-                    gates_ref, refx_ref, chunks[index], 2 * index, half, outs[4 * index : 4 * index + 4]
+                    gates_ref,
+                    refx_ref,
+                    chunks[index],
+                    2 * index + half,
+                    outs[4 * index : 4 * index + 4],
                 )
             )
         for g in range(G):
@@ -158,40 +173,59 @@
                 low, costs[0][g], costs[1][g]
             )
 
+    @pl.when(step == 0)
+    def _():
+        weight_copy(w_ref, held, sems, plane_of(0), 0).start()
+
+    @pl.when(step + 1 < count)
+    def _():
+        weight_copy(w_ref, held, sems, plane_of(step + 1), 1 - slot).start()
+
     @pl.when(step < count)
     def _():
-        vector(
-            1,
-            jnp.maximum(step - 1, 0),
-            lambda part: forward_dot(rows_ref, w0_ref, chunks[0], part, 2),
-        )
-        vector(0, step, lambda part: forward_dot(rows_ref, w1_ref, chunks[1], part, 2))
+        weight_copy(w_ref, held, sems, plane_of(step), slot).wait()
+        vector(1, jnp.maximum(step - 1, 0), 0)
+        vector(0, step, 1)
 
     @pl.when(step == count)
     def _():
         vector(1, step - 1, None)
 
 
-def edge_kernel(gates_ref, rows_ref, refx_ref, w0_ref, w1_ref, cot_ref, *rest):
-    outs = rest[:8]
-    up_ref, down_ref, cost, *chunks = rest[8:]
-    forward_body(gates_ref, rows_ref, refx_ref, w0_ref, w1_ref, outs, cost, chunks)
+def edge_plane(planes, index):
+    return jnp.where(index < 2, index, planes - 4 + index)
+
+
+def edge_kernel(gates_ref, rows_ref, refx_ref, w_ref, cot_ref, *rest):
+    up_ref, down_ref, cost, *scratch = rest[8:]
+    planes = w_ref.shape[0]
+    forward_body(
+        functools.partial(edge_plane, planes),
+        gates_ref,
+        rows_ref,
+        refx_ref,
+        w_ref,
+        rest[:8],
+        cost,
+        scratch,
+    )
 
     @pl.when(pl.program_id(0) == pl.num_programs(0) - 1)
     def _():
         down_ref[0:2] = cost[0:2]
         up_ref[0:2] = cost[2:4]
         down_ref[2] = cot_ref[0]
-        up_ref[2] = cot_ref[cot_ref.shape[0] - 1]
-
-
-def inner_kernel(gates_ref, rows_ref, refx_ref, w0_ref, w1_ref, *rest):
-    outs = rest[8:16]
-    cost_ref, *chunks = rest[16:]
-    forward_body(gates_ref, rows_ref, refx_ref, w0_ref, w1_ref, outs, cost_ref, chunks)
-
-
-def conv_kernel(
+        up_ref[2] = cot_ref[planes - 1]
+
+
+def inner_kernel(gates_ref, rows_ref, refx_ref, w_ref, *rest):
+    cost_ref, *scratch = rest[8:]
+    forward_body(
+        lambda index: index + 2, gates_ref, rows_ref, refx_ref, w_ref, rest[:8], cost_ref, scratch
+    )
+
+
+def depth_conv(
     taps_ref,
     below_ref,
     down_ref,
@@ -200,9 +234,8 @@
     above_ref,
     cot_ref,
     regular_ref,
-    cost_ref,
+    cost,
     grad_ref,
-    cost,
     slope,
     smooth,
 ):
@@ -213,7 +246,6 @@
     cost[4:planes] = inner_ref[...]
     cost[planes : planes + 2] = up_ref[0:2]
     cost[planes + 2 : planes + 4] = above_ref[0:2]
-    cost_ref[...] = cost[2 : planes + 2]
     slope[0] = below_ref[2]
     slope[1 : planes + 1] = cot_ref[...]
     slope[planes + 1] = above_ref[2]
@@ -265,52 +297,65 @@
     lax.fori_loop(0, planes // 2, backward_planes, 0)
 
 
-def backward_kernel(src_ref, place_ref, gates_ref, refx_ref, w_ref, *rest):
-    saved = (rest[0:4], rest[4:8])
-    cost_ref, grad_ref, keep_ref, send_ref = rest[8:12]
-    rows_lo, rows_hi, acc, dref, logit, w_prev, dense = rest[12:]
+def backward_kernel(src_ref, place_ref, taps_ref, gates_ref, refx_ref, w_ref, *rest):
+    halo_refs = rest[:6]
+    inner_saved = (rest[6:10], rest[10:14])
+    edge_saved = (rest[14:18], rest[18:22])
+    regular_ref, keep_ref, send_ref = rest[22:25]
+    cost, grad_ref, slope, smooth, rows_lo, rows_hi, acc, dref, logit, held, sems, dense = rest[25:]
     step = pl.program_id(0)
     count = pl.num_programs(0) - 1
-    groups, pairs = saved[0][1].shape[1:3]
+    pairs = logit.shape[0]
     tiles = pairs // SUB
     lane_tiles = dref.shape[0]
     local_views = src_ref.shape[0]
-    channels = groups * GC
+    channels = G * GC
     half_rows = rows_lo.shape[0]
     low = low_half()
-
-    def vector(tile, upper, target):
-        _, corr_ref, sig_ref, rden_ref = saved[tile // 2]
-        warped_ref = saved[tile // 2][0]
+    inner_count = count - 4
+
+    def plane_of(index):
+        return jnp.where(index < inner_count, index + 2, edge_plane(count, index - inner_count))
+
+    plane = plane_of(step)
+    slot = lax.rem(step, 3)
+    slot_before = lax.rem(step + 2, 3)
+
+    def vector(saved, tile, upper, target):
+        warped_ref, corr_ref, sig_ref, rden_ref = saved[tile // 2]
         lanes = pl.ds((tile % 2) * LANE, LANE)
         full = pl.ds(tile * LANE, LANE)
         pack = tile // 2
         half = tile % 2
         rden = rden_ref[0, :, lanes]
         sig = sig_ref[0, :, lanes].reshape(tiles, SUB, LANE)
-        wanted = range(groups // 2, groups) if upper else range(groups)
+        wanted = range(G // 2, G) if upper else range(G)
         num_grads = {}
         for g in wanted:
-            grad = grad_ref[0, pack, pl.ds(g * SUB, SUB), :]
+            grad = grad_ref[plane, pack, pl.ds(g * SUB, SUB), :]
             num_grads[g] = spread(grad, half, low) * rden
         if upper:
             logit_grad = logit[:, full].reshape(tiles, SUB, LANE)
         else:
             mixed = None
-            for g in range(groups):
+            for g in range(G):
                 rows = pl.ds(g * SUB, SUB)
-                part = grad_ref[0, pack, rows, :] * cost_ref[0, pack, rows, :]
+                part = grad_ref[plane, pack, rows, :] * cost[plane + 2, pack, rows, :]
                 mixed = part if mixed is None else mixed + part
             vis_grad = -(spread(mixed, half, low) * rden)[None]
-            for g in range(groups):
-                vis_grad = vis_grad + num_grads[g][None] * corr_ref[0, g, :, lanes].reshape(
-                    tiles, SUB, LANE
+            for g in range(0, G, 2):
+                corr = (
+                    corr_ref[0, pl.ds(g * pairs, 2 * pairs), lanes]
+                    .astype(jnp.float32)
+                    .reshape(2, tiles, SUB, LANE)
                 )
+                vis_grad = vis_grad + num_grads[g][None] * corr[0]
+                vis_grad = vis_grad + num_grads[g + 1][None] * corr[1]
             logit_grad = vis_grad * (sig * (1.0 - sig)) * (1.0 / GC)
             logit[:, full] = logit_grad.reshape(pairs, LANE)
         visible = (0.5 + sig) * (1.0 / GC)
-        base = groups // 2 if upper else 0
-        for g in range(base, base + groups // 2):
+        base = G // 2 if upper else 0
+        for g in range(base, base + G // 2):
             corr_grad = visible * num_grads[g][None] + logit_grad * gates_ref[g][None]
             for j in range(0, GC, 2):
                 c = g * GC + j
@@ -335,10 +380,10 @@
                         corr_grad * warped[i], axis=0
                     )
 
-    def matmul(rows, weights, base, index):
+    def matmul(rows, where, base, index):
         product = jnp.dot(
             rows[...],
-            weights(pl.ds(index * 2 * LANE, 2 * LANE)),
+            held[where, :, pl.ds(index * 2 * LANE, 2 * LANE)],
             preferred_element_type=jnp.float32,
         )
         for half in range(2):
@@ -346,29 +391,42 @@
                 :, half * LANE : (half + 1) * LANE
             ]
 
+    def one_plane(saved):
+        weight_copy(w_ref, held, sems, plane, slot).wait()
+        for tile in range(lane_tiles):
+            if tile % 2 == 0:
+                matmul(rows_hi, slot_before, half_rows, tile // 2)
+            vector(saved, tile, False, rows_lo)
+        for tile in range(lane_tiles):
+            if tile % 2 == 0:
+                matmul(rows_lo, slot, 0, tile // 2)
+            vector(saved, tile, True, rows_hi)
+
     @pl.when(step == 0)
     def _():
+        weight_copy(w_ref, held, sems, plane_of(0), 0).start()
         acc[...] = jnp.zeros_like(acc)
         dref[...] = jnp.zeros_like(dref)
         rows_hi[...] = jnp.zeros_like(rows_hi)
-        w_prev[...] = jnp.zeros_like(w_prev)
-
-    @pl.when(step < count)
-    def _():
-        for tile in range(lane_tiles):
-            if tile % 2 == 0:
-                matmul(rows_hi, lambda lanes: w_prev[:, lanes], half_rows, tile // 2)
-            vector(tile, False, rows_lo)
-        w_prev[...] = w_ref[0]
-        for tile in range(lane_tiles):
-            if tile % 2 == 0:
-                matmul(rows_lo, lambda lanes: w_ref[0, :, lanes], 0, tile // 2)
-            vector(tile, True, rows_hi)
+        held[2] = jnp.zeros_like(held[2])
+        depth_conv(taps_ref, *halo_refs, regular_ref, cost, grad_ref, slope, smooth)
+
+    @pl.when(step + 1 < count)
+    def _():
+        weight_copy(w_ref, held, sems, plane_of(step + 1), lax.rem(step + 1, 3)).start()
+
+    @pl.when(step < inner_count)
+    def _():
+        one_plane(inner_saved)
+
+    @pl.when((step >= inner_count) & (step < count))
+    def _():
+        one_plane(edge_saved)
 
     @pl.when(step == count)
     def _():
         for index in range(lane_tiles // 2):
-            matmul(rows_hi, lambda lanes: w_prev[:, lanes], half_rows, index)
+            matmul(rows_hi, slot_before, half_rows, index)
         own_index = place_ref[0]
         parity = place_ref[1]
         dense[...] = jnp.zeros_like(dense)
@@ -404,24 +462,23 @@
         lax.fori_loop(0, dense.shape[0], one_view, 0)
 
 
-def split_kernel(keep_ref, received_ref, even_ref, near_ref, far_ref):
-    near = near_ref.shape[0]
-    half = even_ref.shape[0]
-    even_ref[...] = keep_ref[0:half] + received_ref[0:half].astype(jnp.float32)
-    for out_ref, first, count in ((near_ref, half, near), (far_ref, half + near, half - near)):
-        span = pl.ds(first, count)
+def split_kernel(first, keep_ref, received_ref, after_ref, even_ref, send_ref):
+    count = even_ref.shape[0]
+    half = keep_ref.shape[0] // 2
+    for out_ref, start in ((even_ref, first), (send_ref, half + first)):
+        span = pl.ds(start, count)
         out_ref[...] = (keep_ref[span] + received_ref[span].astype(jnp.float32)).astype(
-            jnp.bfloat16
+            out_ref.dtype
         )
 
 
-def spread_kernel(first, even_ref, received_ref, after_ref, *out_refs):
+def spread_kernel(even_ref, received_ref, *out_refs):
     size = out_refs[0].shape[0]
     for index, out_ref in enumerate(out_refs):
-        span = pl.ds(first + index * size, size)
-        out_ref[...] = (
-            even_ref[span] + received_ref[pl.ds(index * size, size)].astype(jnp.float32)
-        ).astype(out_ref.dtype)
+        span = pl.ds(index * size, size)
+        out_ref[...] = (even_ref[span] + received_ref[span].astype(jnp.float32)).astype(
+            out_ref.dtype
+        )
 
 
 def per_plane(shape, plane):
@@ -431,7 +488,7 @@
 
 def fixed(shape):
     rank = len(shape)
-    return pl.BlockSpec(tuple(shape), lambda d: (0,) * rank)
+    return pl.BlockSpec(tuple(shape), lambda d: (0,) * rank, pipeline_mode=pl.Buffered(1))
 
 
 SMEM = functools.partial(pl.BlockSpec, memory_space=pltpu.SMEM)
@@ -469,9 +526,6 @@
     even = [mine] + [over_view(mine, k) for k in range(2, view_count, 2)]
     near_even = jnp.concatenate(even[:quarter], axis=0)
     far_even = jnp.concatenate(even[quarter:], axis=0)
-    maps = [near_even, far_even, over_view(near_even, 1), over_view(far_even, 1)]
-    maps = maps + [lax.ppermute(part, "plane", near) for part in maps]
-
     packed = (pixels // (2 * LANE), G * SUB, LANE)
     refx, gates, cot = pl.pallas_call(
         prep_kernel,
@@ -485,6 +539,9 @@
         cost_estimate=pl.CostEstimate(flops=10**9, bytes_accessed=4 * MIB, transcendentals=0),
         name="prep",
     )(view_gate, features, cotangent)
+    near_even, refx, gates, cot = lax.optimization_barrier((near_even, refx, gates, cot))
+    maps = [near_even, far_even, over_view(near_even, 1), over_view(far_even, 1)]
+    maps = maps + [lax.ppermute(part, "plane", near) for part in maps]
 
     src_own = lax.dynamic_slice_in_dim(sources, own_index * local_views, local_views, 0)
     place = jnp.stack([own_index, parity]).astype(jnp.int32)
@@ -501,145 +558,134 @@
     )(src_own, place, *maps)
 
     width = 2 * LANE
-    saved = (
-        shape((planes, channels * pairs, width), bf16),
-        shape((planes, G, pairs, width), f32),
-        shape((planes, pairs, width), f32),
-        shape((planes, SUB, width), f32),
-    )
-    chunks = [pltpu.VMEM((channels * pairs, width), f32)] * 2
-
-    def edge(d):
-        return jnp.where(d < 2, d, planes - 4 + d)
-
-    def inner(d):
-        return d + 2
-
-    def lane_half(index, plane, count):
-        if index == 0:
-            return lambda d: plane(jnp.minimum(d, count - 1))
-        return lambda d: plane(jnp.maximum(d - 1, 0))
-
-    def forward_specs(plane, count):
-        ins = [fixed(gates.shape), fixed(rows.shape), fixed(refx.shape)] + [
-            pl.BlockSpec(
-                (1, width, pixels),
-                lambda d, index=index: (plane(jnp.minimum(d, count - 1)), index, 0),
-            )
-            for index in range(2)
-        ]
-        outs = [
-            per_plane(s.shape, lane_half(index, plane, count)) for index in range(2) for s in saved
-        ]
-        return ins, outs
-
-    edge_ins, edge_outs = forward_specs(edge, 4)
+
+    def saved_shapes(count):
+        one = (
+            shape((count, channels * pairs, width), bf16),
+            shape((count, G * pairs, width), bf16),
+            shape((count, pairs, width), f32),
+            shape((count, SUB, width), f32),
+        )
+        return one * 2
+
+    def saved_specs(count):
+        specs = []
+        for index, item in enumerate(saved_shapes(count)):
+            if index < 4:
+                specs.append(per_plane(item.shape, lambda d: jnp.minimum(d, count - 1)))
+            else:
+                specs.append(per_plane(item.shape, lambda d: jnp.maximum(d - 1, 0)))
+        return specs
+
+    hbm = pl.BlockSpec(memory_space=pltpu.HBM)
+    fixed_specs = [fixed(gates.shape), fixed(rows.shape), fixed(refx.shape), hbm]
+    scratch = [
+        pltpu.VMEM((2, pixels, pixels), bf16),
+        pltpu.SemaphoreType.DMA((2,)),
+        pltpu.VMEM((channels * pairs, width), f32),
+        pltpu.VMEM((channels * pairs, width), f32),
+    ]
+    inner_count = planes - 4
+    load = (3,) + packed
     *edge_saved, up_load, down_load = pl.pallas_call(
         edge_kernel,
-        out_shape=saved * 2 + (shape((3,) + packed, f32),) * 2,
+        out_shape=saved_shapes(4) + (shape(load, f32),) * 2,
         grid=(5,),
-        in_specs=edge_ins + [fixed(cot.shape)],
-        out_specs=tuple(edge_outs) + (fixed((3,) + packed),) * 2,
-        scratch_shapes=[pltpu.VMEM((4,) + packed, f32)] + chunks,
-        compiler_params=params(20),
+        in_specs=fixed_specs + [fixed(cot.shape)],
+        out_specs=tuple(saved_specs(4)) + (fixed(load),) * 2,
+        scratch_shapes=[pltpu.VMEM((4,) + packed, f32)] + scratch,
+        compiler_params=params(14),
         name="forward_edge",
-    )(gates, rows, refx, warp_weights, warp_weights, cot)
+    )(gates, rows, refx, warp_weights, cot)
     below = lax.ppermute(up_load, "plane", up)
     above = lax.ppermute(down_load, "plane", down)
-    inner_ins, inner_outs = forward_specs(inner, planes - 4)
-    *saved_values, inner_cost = pl.pallas_call(
+    *inner_saved, inner_cost = pl.pallas_call(
         inner_kernel,
-        out_shape=saved * 2 + (shape((planes - 4,) + packed, f32),),
-        grid=(planes - 3,),
-        in_specs=inner_ins + [pl.BlockSpec(memory_space=pl.ANY)] * 8,
-        out_specs=tuple(inner_outs) + (fixed((planes - 4,) + packed),),
-        scratch_shapes=chunks,
-        input_output_aliases={5 + i: i for i in range(8)},
-        compiler_params=params(20),
+        out_shape=saved_shapes(inner_count) + (shape((inner_count,) + packed, f32),),
+        grid=(inner_count + 1,),
+        in_specs=fixed_specs,
+        out_specs=tuple(saved_specs(inner_count)) + (fixed((inner_count,) + packed),),
+        scratch_shapes=scratch,
+        compiler_params=params(14),
         cost_estimate=pl.CostEstimate(
-            flops=2 * channels * pairs * pixels * pixels * (planes - 4),
-            bytes_accessed=40 * 1024 * 1024,
+            flops=2 * channels * pairs * pixels * pixels * inner_count,
+            bytes_accessed=40 * MIB,
             transcendentals=0,
         ),
         name="forward_inner",
-    )(gates, rows, refx, warp_weights, warp_weights, *edge_saved)
-
-    regular, cost, cost_grad = pl.pallas_call(
-        conv_kernel,
-        out_shape=(
-            shape(cotangent.shape, bf16),
-            shape((planes,) + packed, f32),
-            shape((planes,) + packed, f32),
-        ),
-        in_specs=[SMEM()] + [pl.BlockSpec()] * 6,
+    )(gates, rows, refx, warp_weights)
+
+    halo = (below, down_load, inner_cost, up_load, above, cot)
+    returned = (all_views, channels // 2, pixels)
+    regular, keep, send = pl.pallas_call(
+        backward_kernel,
+        out_shape=(shape(cotangent.shape, bf16), shape(returned, f32), shape(returned, bf16)),
+        grid=(planes + 1,),
+        in_specs=[SMEM()] * 3
+        + [fixed(gates.shape), fixed(refx.shape), hbm]
+        + [fixed(item.shape) for item in halo]
+        + [
+            per_plane(item.shape, lambda d: jnp.minimum(d, inner_count - 1))
+            for item in inner_saved
+        ]
+        + [
+            per_plane(item.shape, lambda d: jnp.clip(d - inner_count, 0, 3))
+            for item in edge_saved
+        ],
+        out_specs=(fixed(cotangent.shape), fixed(returned), fixed(returned)),
         scratch_shapes=[
             pltpu.VMEM((planes + 4,) + packed, f32),
+            pltpu.VMEM((planes,) + packed, f32),
             pltpu.VMEM((planes + 2,) + packed, f32),
             pltpu.VMEM((planes + 2,) + packed, f32),
-        ],
-        compiler_params=params(),
-        name="depth_conv",
-    )(depth_kernel, below, down_load, inner_cost, up_load, above, cot)
-
-    def clamped(d):
-        return jnp.minimum(d, planes - 1)
-
-    returned = (all_views, channels // 2, pixels)
-    keep, send = pl.pallas_call(
-        backward_kernel,
-        out_shape=(shape(returned, f32), shape(returned, bf16)),
-        grid=(planes + 1,),
-        in_specs=[SMEM(), SMEM(), fixed(gates.shape), fixed(refx.shape)]
-        + [per_plane(warp_weights.shape, clamped)]
-        + [per_plane(s.shape, clamped) for s in saved * 2]
-        + [per_plane(cost.shape, clamped), per_plane(cost_grad.shape, clamped)],
-        out_specs=(fixed(returned), fixed(returned)),
-        scratch_shapes=[
             pltpu.VMEM((channels * pairs // 2, pixels), bf16),
             pltpu.VMEM((channels * pairs // 2, pixels), bf16),
             pltpu.VMEM((pixels // LANE, channels * pairs, LANE), f32),
             pltpu.VMEM((pixels // LANE, channels * SUB, LANE), f32),
             pltpu.VMEM((pairs, pixels), f32),
-            pltpu.VMEM((pixels, pixels), bf16),
+            pltpu.VMEM((3, pixels, pixels), bf16),
+            pltpu.SemaphoreType.DMA((3,)),
             pltpu.VMEM((all_views, channels, pixels), f32),
         ],
-        compiler_params=params(16 + 14 * all_views * channels * pixels // MIB),
+        compiler_params=params(15 + 14 * all_views * channels * pixels // MIB),
         name="backward",
-    )(src_own, place, gates, refx, warp_weights, *saved_values, cost, cost_grad)
+    )(
+        src_own,
+        place,
+        depth_kernel,
+        gates,
+        refx,
+        warp_weights,
+        *halo,
+        *inner_saved,
+        *edge_saved,
+    )
 
     received = lax.ppermute(send, "plane", near)
-    half_views = all_views // 2
-    close = half_views // 2
+    close = quarter * local_views
     piece = (local_views, channels // 2, pixels)
-    even_sum, send_close, send_away = pl.pallas_call(
-        split_kernel,
-        out_shape=(
-            shape((half_views,) + piece[1:], f32),
-            shape((close,) + piece[1:], bf16),
-            shape((half_views - close,) + piece[1:], bf16),
-        ),
-        compiler_params=params(32),
-        name="split",
-    )(keep, received)
-    away = over_view(send_away, 1)
-    closer = over_view(send_close, 1)
-    count = close // local_views
-    away_parts = pl.pallas_call(
-        functools.partial(spread_kernel, close),
-        out_shape=(shape(piece, bf16),) * (view_count // 2 - count),
-        in_specs=[pl.BlockSpec(), pl.BlockSpec(), pl.BlockSpec(memory_space=pl.ANY)],
-        compiler_params=params(32),
-        name="spread_away",
-    )(even_sum, away, away)
-    total, *close_parts = pl.pallas_call(
-        functools.partial(spread_kernel, 0),
-        out_shape=(shape(piece, f32),) + (shape(piece, bf16),) * (count - 1),
-        in_specs=[pl.BlockSpec(), pl.BlockSpec(), pl.BlockSpec(memory_space=pl.ANY)],
-        compiler_params=params(32),
-        name="spread_close",
-    )(even_sum, closer, away_parts[0])
+    anywhere = pl.BlockSpec(memory_space=pl.ANY)
+
+    def stage(first, count, after, kind):
+        even_sum, outgoing = pl.pallas_call(
+            functools.partial(split_kernel, first),
+            out_shape=(shape((count,) + piece[1:], f32), shape((count,) + piece[1:], bf16)),
+            in_specs=[pl.BlockSpec(), pl.BlockSpec(), anywhere],
+            compiler_params=params(32),
+            name="split",
+        )(keep, received, after)
+        incoming = over_view(outgoing, 1)
+        return pl.pallas_call(
+            spread_kernel,
+            out_shape=(shape(piece, kind),) + (shape(piece, bf16),) * (count // local_views - 1),
+            compiler_params=params(32),
+            name="spread",
+        )(even_sum, incoming)
+
+    away_parts = stage(close, all_views // 2 - close, received, bf16)
+    total, *close_parts = stage(0, close, away_parts[0], f32)
     for index, part in enumerate(away_parts):
-        total = total + over_view(part, 2 * (count + index)).astype(f32)
+        total = total + over_view(part, 2 * (quarter + index)).astype(f32)
     for index, part in enumerate(close_parts):
         total = total + over_view(part, 2 * (index + 1)).astype(f32)
     total = total + lax.ppermute(total, "plane", far)

time: 124 us -> 95.2 us (0.77)
  local copies, waits for them, and re-layouts: 37.5 us -> 12.4 us
  waiting for transfers between devices: 26.2 us -> 23.1 us
    unnamed x42 -> x26, local copies, waits for them, and re-layouts: 35.9 us -> 10.8 us
    ppermute x10, waiting for transfers between devices: 20 us -> 15.8 us  [over_view(): return lax.ppermute(array, 'view', [(i, i ^ k) for i in range(view_count)])]
  transfers between devices with their start and end apart: 19 -> 19, of which waited for: 10 -> 12; matrix products, arithmetic and copies ran while one was open for 0% -> 0% of each run, Pallas kernels for 7% -> 10%
where the time goes in v4:
time: 95.2 us; the launch traced here: 94.8 us
  Pallas kernels  36.9 us (39%)
  waiting for transfers between devices  23.1 us (24%)
  starting transfers between devices  21.4 us (22%)
  local copies, waits for them, and re-layouts  12.4 us (13%)
    pallas_call x1, Pallas kernels, shards(): pl.pallas_call(backward_kernel, out_shape=(shape(cotangent.shape, bf16),...  20.8 us
    ppermute x10, waiting for transfers between devices, over_view(): return lax.ppermute(array, 'view', [(i, i ^ k) for i in range(view_count)])  15.8 us
    ppermute x10, starting transfers between devices, over_view(): return lax.ppermute(array, 'view', [(i, i ^ k) for i in range(view_count)])  13.5 us
    unnamed x26, local copies, waits for them, and re-layouts  10.8 us
    pallas_call x1, Pallas kernels, shards(): pl.pallas_call(inner_kernel, out_shape=saved_shapes(inner_count) + (shape...  8.93 us
    pallas_call x1, Pallas kernels, shards(): pl.pallas_call(edge_kernel, out_shape=saved_shapes(4) + (shape(load, f32)...  4.64 us
    ppermute x1, waiting for transfers between devices, shards(): total = total + lax.ppermute(total, 'plane', far)  3.36 us
    ppermute x1, starting transfers between devices, shards(): received = lax.ppermute(send, 'plane', near)  2.32 us
  transfers between devices with their start and end apart: 19, of which 12 were waited for; matrix products, arithmetic and copies ran while one was open for 0% of the time, Pallas kernels for 10%

profile of v4, /device:TPU:0, one launch (start us, length us, event | category | flops | bytes accessed | tf_op | source)
XLA Modules:
  0.0 94.8 jit_solution(7788290930863340849)
XLA Ops:
  0.6 0.0 copy-start
  0.7 0.8 dynamic-slice_bitcast_fusion
  1.5 5.0 %collective-permute-start.2 = (bf16[4,16,512]{2,1,0:T(8,128)(2,1)S(1)}, bf16[4,16,512]{2,1,0:T(8,128)(2,1)S(1)}, u32[]{:S(2)}, u32[]{:S(2)}) collective-permute-start(bf16[4,16,512]{2,1,0:T(8,128)(2,1)S(1)} %dynamic-slice_bitcast_fusion), channel_id=1, source_target_pairs={{0,24},{4,28},{8,16},{12,20},{16,8},{20,12},{24,0},{28,4},{1,25},{... | collective-permute-start | bytes 196616 | tf_op jit(solution)/shard_map/ppermute | solution.py:523
  6.6 0.6 collective-permute-start
  7.1 0.9 copy-done.8
  8.0 1.0 %copy-done.10 = bf16[4,12,8,512]{3,2,1,0:T(8,128)(2,1)S(1)} copy-done((bf16[4,12,8,512]{3,2,1,0:T(8,128)(2,1)S(1)}, bf16[4,12,8,512]{3,2,1,0:T(8,128)(2,1)}, u32[]{:S(2)}) %copy-start.10) | copy-done | bytes 393240
  9.0 0.7 copy-done.11
  9.7 0.8 prep.1
  10.5 0.8 copy-done.6
  11.3 0.9 collective-permute-done.1
  12.2 1.6 %collective-permute-start.4 = (bf16[8,16,512]{2,1,0:T(8,128)(2,1)S(1)}, bf16[8,16,512]{2,1,0:T(8,128)(2,1)S(1)}, u32[]{:S(2)}, u32[]{:S(2)}) collective-permute-start(bf16[8,16,512]{2,1,0:T(8,128)(2,1)S(1)} %constant_dynamic-update-slice_fusion.rest_1_), channel_id=1, source_target_pairs={{0,4},{4,0},{8,12},{12,8},{16,20},{20,16},{24,28},{28,24},{1,5},{5... | collective-permute-start | bytes 393224 | tf_op jit(solution)/shard_map/ppermute | solution.py:523
  13.8 0.6 collective-permute-start.3
  14.4 0.5 collective-permute-start.5
  14.9 3.7 %collective-permute-done.4.rest_3_ = bf16[8,16,512]{2,1,0:T(8,128)(2,1)S(1)} collective-permute-done((bf16[8,16,512]{2,1,0:T(8,128)(2,1)S(1)}, bf16[8,16,512]{2,1,0:T(8,128)(2,1)S(1)}, u32[]{:S(2)}, u32[]{:S(2)}) %collective-permute-start.4) | collective-permute-done | bytes 131104 | tf_op jit(solution)/shard_map/ppermute | solution.py:523
  18.6 1.5 %collective-permute-done.3.rest_2_ = bf16[8,16,512]{2,1,0:T(8,128)(2,1)S(1)} collective-permute-done((bf16[8,16,512]{2,1,0:T(8,128)(2,1)S(1)}, bf16[8,16,512]{2,1,0:T(8,128)(2,1)S(1)}, u32[]{:S(2)}, u32[]{:S(2)}) %collective-permute-start.3) | collective-permute-done | bytes 131104 | tf_op jit(solution)/shard_map/ppermute | solution.py:523
  20.1 0.1 constant_dynamic-slice_fusion
  20.2 0.1 copy.11.src_ref
  20.3 0.1 pad_add_fusion.place_ref
  20.4 1.1 %collective-permute-done.7.rest_6_ = bf16[8,16,512]{2,1,0:T(8,128)(2,1)S(1)} collective-permute-done((bf16[8,16,512]{2,1,0:T(8,128)(2,1)S(1)}, bf16[8,16,512]{2,1,0:T(8,128)(2,1)S(1)}, u32[]{:S(2)}, u32[]{:S(2)}) %collective-permute-start.7) | collective-permute-done | bytes 131104 | tf_op jit(solution)/shard_map/ppermute | solution.py:544
  21.5 1.6 %assemble.1.rows_ref = bf16[1280,512]{1,0:T(8,128)(2,1)S(1)} custom-call(s32[4,10]{1,0:T(4,128)S(1)} %copy.11.src_ref, s32[2]{0:T(128)S(1)} %pad_add_fusion.place_ref, bf16[8,16,512]{2,1,0:T(8,128)(2,1)S(1)} %pad_maximum_fusion.1.rest_0_, bf16[8,16,512]{2,1,0:T(8,128)(2,1)S(1)} %constant_dynamic-update-slice_fusion.rest_1_, ...), custom_call_target="tpu_custom_call" | custom-call | tf_op jit(solution)/shard_map/assemble/pallas_call | solution.py:548
  23.1 0.0 copy-start.1
  23.1 2.8 %copy-done.1 = bf16[12,512,512]{2,1,0:T(8,128)(2,1)S(1)} copy-done((bf16[12,512,512]{2,1,0:T(8,128)(2,1)S(1)}, bf16[12,512,512]{2,1,0:T(8,128)(2,1)}, u32[]{:S(2)}) %copy-start.1) | copy-done | bytes 6291480
  25.9 4.6 %forward_edge.1 = (bf16[4,1280,256]{2,1,0:T(8,128)(2,1)S(1)}, bf16[4,320,256]{2,1,0:T(8,128)(2,1)S(1)}, f32[4,40,256]{2,1,0:T(8,128)S(1)}, f32[4,8,256]{2,1,0:T(...) custom-call(f32[8,8,128]{2,1,0:T(8,128)S(1)} %get-tuple-element.42.g, ...), custom_call_target="tpu_custom_call" | custom-call | tf_op jit(solution)/shard_map/forward_edge/pallas_call | solution.py:590
  30.5 2.1 %collective-permute-start.9 = (f32[3,2,64,128]{3,2,1,0:T(8,128)S(1)}, f32[3,2,64,128]{3,2,1,0:T(8,128)S(1)}, u32[]{:S(2)}, u32[]{:S(2)}) collective-permute-start(f32[3,2,64,128]{3,2,1,0:T(8,128)S(1)} %get-tuple-element.46.rest_3_), channel_id=1, source_target_pairs={{0,1},{1,2},{2,3},{4,5},{5,6},{6,7},{8,9},{9,10},{10,11},{12,13},{... | collective-permute-start | bytes 589832 | tf_op jit(solution)/shard_map/ppermute | solution.py:600
  32.6 1.3 %collective-permute-start.10 = (f32[3,2,64,128]{3,2,1,0:T(8,128)S(1)}, f32[3,2,64,128]{3,2,1,0:T(8,128)S(1)}, u32[]{:S(2)}, u32[]{:S(2)}) collective-permute-start(f32[3,2,64,128]{3,2,1,0:T(8,128)S(1)} %get-tuple-element.47.rest_1_), channel_id=1, source_target_pairs={{1,0},{2,1},{3,2},{5,4},{6,5},{7,6},{9,8},{10,9},{11,10},{13,12},{... | collective-permute-start | bytes 589832 | tf_op jit(solution)/shard_map/ppermute | solution.py:601
  33.9 2.8 %copy-done.2 = bf16[12,512,512]{2,1,0:T(8,128)(2,1)S(1)} copy-done((bf16[12,512,512]{2,1,0:T(8,128)(2,1)S(1)}, bf16[12,512,512]{2,1,0:T(8,128)(2,1)}, u32[]{:S(2)}) %copy-start.2) | copy-done | bytes 6291480
  36.7 8.9 %forward_inner.1 = (bf16[8,1280,256]{2,1,0:T(8,128)(2,1)S(1)}, bf16[8,320,256]{2,1,0:T(8,128)(2,1)S(1)}, f32[8,40,256]{2,1,0:T(8,128)S(1)}, f32[8,8,256]{2,1,0:T...) custom-call(f32[8,8,128]{2,1,0:T(8,128)S(1)} %get-tuple-element.42.g, ...), custom_call_target="tpu_custom_call" | custom-call | flops 5368709120 | bytes 41943040 | tf_op jit(solution)/shard_map/forward_inner/pallas_call | solution.py:602
  45.7 1.7 %copy-done.5 = bf16[4,1280,256]{2,1,0:T(8,128)(2,1)S(1)} copy-done((bf16[4,1280,256]{2,1,0:T(8,128)(2,1)S(1)}, bf16[4,1280,256]{2,1,0:T(8,128)(2,1)}, u32[]{:S(2)}) %copy-start.5) | copy-done | bytes 2621464
  47.4 20.8 %backward.1 = (bf16[4,12,8,512]{3,2,1,0:T(8,128)(2,1)}, f32[32,16,512]{2,1,0:T(8,128)S(1)}, bf16[32,16,512]{2,1,0:T(8,128)(2,1)S(1)}) custom-call(s32[4,10]{1,0:T(4,128)S(1)} %copy.11.src_ref, s32[2]{0:T(128)S(1)} %pad_add_fusion.place_ref, f32[3,8,8]{2,1,0:T(8,128)S(1)} %copy-done.9, f32[8,8,128]{2,1,0:T(8,128)S(1)} %get-tuple-element.42.gates_ref, ...), custom_call_target="tpu_custom_call" | custom-call | tf_op jit(solution)/shard_map/backward/pallas_call | solution.py:620
  68.2 2.3 %collective-permute-start.11 = (bf16[32,16,512]{2,1,0:T(8,128)(2,1)S(1)}, bf16[32,16,512]{2,1,0:T(8,128)(2,1)S(1)}, u32[]{:S(2)}, u32[]{:S(2)}) collective-permute-start(bf16[32,16,512]{2,1,0:T(8,128)(2,1)S(1)} %get-tuple-element.67), channel_id=1, source_target_pairs={{0,1},{1,0},{2,3},{3,2},{4,5},{5,4},{6,7},{7,6},{8,9},{9,8},{10,11... | collective-permute-start | bytes 1572872 | tf_op jit(solution)/shard_map/ppermute | solution.py:664
  70.5 1.5 %collective-permute-done.11.received_ref.after_ref = bf16[32,16,512]{2,1,0:T(8,128)(2,1)S(1)} collective-permute-done((bf16[32,16,512]{2,1,0:T(8,128)(2,1)S(1)}, bf16[32,16,512]{2,1,0:T(8,128)(2,1)S(1)}, u32[]{:S(2)}, u32[]{:S(2)}) %collective-permute-start.11) | collective-permute-done | bytes 524320 | tf_op jit(solution)/shard_map/ppermute | solution.py:664
  72.0 0.1 split.2
  72.1 1.6 %collective-permute-start.12 = (bf16[8,16,512]{2,1,0:T(8,128)(2,1)S(1)}, bf16[8,16,512]{2,1,0:T(8,128)(2,1)S(1)}, u32[]{:S(2)}, u32[]{:S(2)}) collective-permute-start(bf16[8,16,512]{2,1,0:T(8,128)(2,1)S(1)} %get-tuple-element.69), channel_id=1, source_target_pairs={{0,4},{4,0},{8,12},{12,8},{16,20},{20,16},{24,28},{28,24},{1,5},{5... | collective-permute-start | bytes 393224 | tf_op jit(solution)/shard_map/ppermute | solution.py:523
  73.7 4.2 %collective-permute-done.12.received_ref = bf16[8,16,512]{2,1,0:T(8,128)(2,1)S(1)} collective-permute-done((bf16[8,16,512]{2,1,0:T(8,128)(2,1)S(1)}, bf16[8,16,512]{2,1,0:T(8,128)(2,1)S(1)}, u32[]{:S(2)}, u32[]{:S(2)}) %collective-permute-start.12) | collective-permute-done | bytes 131104 | tf_op jit(solution)/shard_map/ppermute | solution.py:523
  78.0 0.1 split.3
  78.0 1.6 %collective-permute-start.13 = (bf16[8,16,512]{2,1,0:T(8,128)(2,1)S(1)}, bf16[8,16,512]{2,1,0:T(8,128)(2,1)S(1)}, u32[]{:S(2)}, u32[]{:S(2)}) collective-permute-start(bf16[8,16,512]{2,1,0:T(8,128)(2,1)S(1)} %get-tuple-element.72), channel_id=1, source_target_pairs={{0,4},{4,0},{8,12},{12,8},{16,20},{20,16},{24,28},{28,24},{1,5},{5... | collective-permute-start | bytes 393224 | tf_op jit(solution)/shard_map/ppermute | solution.py:523
  79.6 0.9 collective-permute-start.14
  80.5 1.5 %collective-permute-start.15 = (bf16[4,16,512]{2,1,0:T(8,128)(2,1)S(1)}, bf16[4,16,512]{2,1,0:T(8,128)(2,1)S(1)}, u32[]{:S(2)}, u32[]{:S(2)}) collective-permute-start(bf16[4,16,512]{2,1,0:T(8,128)(2,1)S(1)} %get-tuple-element.74), channel_id=1, source_target_pairs={{0,24},{4,28},{8,16},{12,20},{16,8},{20,12},{24,0},{28,4},{1,25},{... | collective-permute-start | bytes 196616 | tf_op jit(solution)/shard_map/ppermute | solution.py:523
  82.0 1.1 %collective-permute-done.13.received_ref = bf16[8,16,512]{2,1,0:T(8,128)(2,1)S(1)} collective-permute-done((bf16[8,16,512]{2,1,0:T(8,128)(2,1)S(1)}, bf16[8,16,512]{2,1,0:T(8,128)(2,1)S(1)}, u32[]{:S(2)}, u32[]{:S(2)}) %collective-permute-start.13) | collective-permute-done | bytes 131104 | tf_op jit(solution)/shard_map/ppermute | solution.py:523
  83.1 0.1 collective-permute-start.16
  83.2 3.5 %collective-permute-done.15 = bf16[4,16,512]{2,1,0:T(8,128)(2,1)S(1)} collective-permute-done((bf16[4,16,512]{2,1,0:T(8,128)(2,1)S(1)}, bf16[4,16,512]{2,1,0:T(8,128)(2,1)S(1)}, u32[]{:S(2)}, u32[]{:S(2)}) %collective-permute-start.15) | collective-permute-done | bytes 65568 | tf_op jit(solution)/shard_map/ppermute | solution.py:523
  86.8 0.1 collective-permute-done.14
  86.9 0.7 collective-permute-done.16
  87.6 1.7 %collective-permute-start.17 = (f32[4,16,512]{2,1,0:T(8,128)S(1)}, f32[4,16,512]{2,1,0:T(8,128)S(1)}, u32[]{:S(2)}, u32[]{:S(2)}) collective-permute-start(f32[4,16,512]{2,1,0:T(8,128)S(1)} %convert_add_fusion), channel_id=1, source_target_pairs={{0,2},{1,3},{2,0},{3,1},{4,6},{5,7},{6,4},{7,5},{8,10},{9,11},{10,... | collective-permute-start | bytes 393224 | tf_op jit(solution)/shard_map/ppermute | solution.py:691
  89.3 3.4 %collective-permute-done.17 = f32[4,16,512]{2,1,0:T(8,128)S(1)} collective-permute-done((f32[4,16,512]{2,1,0:T(8,128)S(1)}, f32[4,16,512]{2,1,0:T(8,128)S(1)}, u32[]{:S(2)}, u32[]{:S(2)}) %collective-permute-start.17) | collective-permute-done | bytes 131104 | tf_op jit(solution)/shard_map/ppermute | solution.py:691
  92.7 0.1 collective-permute-start.18
  92.7 1.3 %collective-permute-done.18 = f32[4,16,512]{2,1,0:T(8,128)S(1)} collective-permute-done((f32[4,16,512]{2,1,0:T(8,128)S(1)}, f32[4,16,512]{2,1,0:T(8,128)S(1)}, u32[]{:S(2)}, u32[]{:S(2)}) %collective-permute-start.18) | collective-permute-done | bytes 131104 | tf_op jit(solution)/shard_map/ppermute | solution.py:692
  94.1 0.7 copy.10
  (35 shorter events, 0.2 us)
Async XLA Ops:
  0.6 19.5 %copy-start = (s32[32,10]{0,1:T(8,128)S(1)}, s32[32,10]{0,1:T(8,128)}, u32[]{:S(2)}) copy-start(s32[32,10]{0,1:T(8,128)} %param.7) | copy-start | bytes 3844
  1.5 10.7 %collective-permute-start.2 = (bf16[4,16,512]{2,1,0:T(8,128)(2,1)S(1)}, bf16[4,16,512]{2,1,0:T(8,128)(2,1)S(1)}, u32[]{:S(2)}, u32[]{:S(2)}) collective-permute-start(bf16[4,16,512]{2,1,0:T(8,128)(2,1)S(1)} %dynamic-slice_bitcast_fusion), channel_id=1, source_target_pairs={{0,24},{4,28},{8,16},{12,20},{16,8},{20,12},{24,0},{28,4},{1,25},{... | collective-permute-start | bytes 196616 | tf_op jit(solution)/shard_map/ppermute | solution.py:523
  6.6 5.6 %collective-permute-start.1 = (bf16[4,16,512]{2,1,0:T(8,128)(2,1)S(1)}, bf16[4,16,512]{2,1,0:T(8,128)(2,1)S(1)}, u32[]{:S(2)}, u32[]{:S(2)}) collective-permute-start(bf16[4,16,512]{2,1,0:T(8,128)(2,1)S(1)} %dynamic-slice_bitcast_fusion), channel_id=1, source_target_pairs={{0,16},{4,20},{8,24},{12,28},{16,0},{20,4},{24,8},{28,12},{1,17},{... | collective-permute-start | bytes 196616 | tf_op jit(solution)/shard_map/ppermute | solution.py:523
  6.6 7.2 %collective-permute-start = (bf16[4,16,512]{2,1,0:T(8,128)(2,1)S(1)}, bf16[4,16,512]{2,1,0:T(8,128)(2,1)S(1)}, u32[]{:S(2)}, u32[]{:S(2)}) collective-permute-start(bf16[4,16,512]{2,1,0:T(8,128)(2,1)S(1)} %dynamic-slice_bitcast_fusion), channel_id=1, source_target_pairs={{0,8},{4,12},{8,0},{12,4},{16,24},{20,28},{24,16},{28,20},{1,9},{5... | collective-permute-start | bytes 196616 | tf_op jit(solution)/shard_map/ppermute | solution.py:523
  7.1 0.9 copy-start.8
  8.0 1.0 %copy-start.10 = (bf16[4,12,8,512]{3,2,1,0:T(8,128)(2,1)S(1)}, bf16[4,12,8,512]{3,2,1,0:T(8,128)(2,1)}, u32[]{:S(2)}) copy-start(bf16[4,12,8,512]{3,2,1,0:T(8,128)(2,1)} %cot_ref.1) | copy-start | bytes 1179652
  9.0 0.7 copy-start.11
  10.5 0.8 copy-start.6
  12.2 6.4 %collective-permute-start.4 = (bf16[8,16,512]{2,1,0:T(8,128)(2,1)S(1)}, bf16[8,16,512]{2,1,0:T(8,128)(2,1)S(1)}, u32[]{:S(2)}, u32[]{:S(2)}) collective-permute-start(bf16[8,16,512]{2,1,0:T(8,128)(2,1)S(1)} %constant_dynamic-update-slice_fusion.rest_1_), channel_id=1, source_target_pairs={{0,4},{4,0},{8,12},{12,8},{16,20},{20,16},{24,28},{28,24},{1,5},{5... | collective-permute-start | bytes 393224 | tf_op jit(solution)/shard_map/ppermute | solution.py:523
  13.8 6.3 %collective-permute-start.3 = (bf16[8,16,512]{2,1,0:T(8,128)(2,1)S(1)}, bf16[8,16,512]{2,1,0:T(8,128)(2,1)S(1)}, u32[]{:S(2)}, u32[]{:S(2)}) collective-permute-start(bf16[8,16,512]{2,1,0:T(8,128)(2,1)S(1)} %pad_maximum_fusion.1.rest_0_), channel_id=1, source_target_pairs={{0,4},{4,0},{8,12},{12,8},{16,20},{20,16},{24,28},{28,24},{1,5},{5... | collective-permute-start | bytes 393224 | tf_op jit(solution)/shard_map/ppermute | solution.py:523
  14.4 6.0 %collective-permute-start.6 = (bf16[8,16,512]{2,1,0:T(8,128)(2,1)S(1)}, bf16[8,16,512]{2,1,0:T(8,128)(2,1)S(1)}, u32[]{:S(2)}, u32[]{:S(2)}) collective-permute-start(bf16[8,16,512]{2,1,0:T(8,128)(2,1)S(1)} %constant_dynamic-update-slice_fusion.rest_1_), channel_id=1, source_target_pairs={{0,1},{1,0},{2,3},{3,2},{4,5},{5,4},{6,7},{7,6},{8,9},{9,8},{10,11... | collective-permute-start | bytes 393224 | tf_op jit(solution)/shard_map/ppermute | solution.py:544
  14.4 6.0 %collective-permute-start.5 = (bf16[8,16,512]{2,1,0:T(8,128)(2,1)S(1)}, bf16[8,16,512]{2,1,0:T(8,128)(2,1)S(1)}, u32[]{:S(2)}, u32[]{:S(2)}) collective-permute-start(bf16[8,16,512]{2,1,0:T(8,128)(2,1)S(1)} %pad_maximum_fusion.1.rest_0_), channel_id=1, source_target_pairs={{0,1},{1,0},{2,3},{3,2},{4,5},{5,4},{6,7},{7,6},{8,9},{9,8},{10,11... | collective-permute-start | bytes 393224 | tf_op jit(solution)/shard_map/ppermute | solution.py:544
  18.6 1.8 %collective-permute-start.8 = (bf16[8,16,512]{2,1,0:T(8,128)(2,1)S(1)}, bf16[8,16,512]{2,1,0:T(8,128)(2,1)S(1)}, u32[]{:S(2)}, u32[]{:S(2)}) collective-permute-start(bf16[8,16,512]{2,1,0:T(8,128)(2,1)S(1)} %collective-permute-done.4.rest_3_), channel_id=1, source_target_pairs={{0,1},{1,0},{2,3},{3,2},{4,5},{5,4},{6,7},{7,6},{8,9},{9,8},{10,11... | collective-permute-start | bytes 393224 | tf_op jit(solution)/shard_map/ppermute | solution.py:544
  20.1 1.3 %collective-permute-start.7 = (bf16[8,16,512]{2,1,0:T(8,128)(2,1)S(1)}, bf16[8,16,512]{2,1,0:T(8,128)(2,1)S(1)}, u32[]{:S(2)}, u32[]{:S(2)}) collective-permute-start(bf16[8,16,512]{2,1,0:T(8,128)(2,1)S(1)} %collective-permute-done.3.rest_2_), channel_id=1, source_target_pairs={{0,1},{1,0},{2,3},{3,2},{4,5},{5,4},{6,7},{7,6},{8,9},{9,8},{10,11... | collective-permute-start | bytes 393224 | tf_op jit(solution)/shard_map/ppermute | solution.py:544
  20.3 2.8 %copy-start.7 = (f32[4,256,128]{2,1,0:T(8,128)S(1)}, f32[4,256,128]{2,1,0:T(8,128)}, u32[]{:S(2)}) copy-start(f32[4,256,128]{2,1,0:T(8,128)} %copy-done.6) | copy-start | bytes 1572868
  23.1 2.8 %copy-start.1 = (bf16[12,512,512]{2,1,0:T(8,128)(2,1)S(1)}, bf16[12,512,512]{2,1,0:T(8,128)(2,1)}, u32[]{:S(2)}) copy-start(bf16[12,512,512]{2,1,0:T(8,128)(2,1)} %w_ref.5) | copy-start | bytes 18874372
  30.5 15.1 %copy-start.4 = (bf16[4,1280,256]{2,1,0:T(8,128)(2,1)}, bf16[4,1280,256]{2,1,0:T(8,128)(2,1)S(1)}, u32[]{:S(2)}) copy-start(bf16[4,1280,256]{2,1,0:T(8,128)(2,1)S(1)} %get-tuple-element.61.rest_18_) | copy-start | bytes 7864324
  30.5 15.1 %collective-permute-start.9 = (f32[3,2,64,128]{3,2,1,0:T(8,128)S(1)}, f32[3,2,64,128]{3,2,1,0:T(8,128)S(1)}, u32[]{:S(2)}, u32[]{:S(2)}) collective-permute-start(f32[3,2,64,128]{3,2,1,0:T(8,128)S(1)} %get-tuple-element.46.rest_3_), channel_id=1, source_target_pairs={{0,1},{1,2},{2,3},{4,5},{5,6},{6,7},{8,9},{9,10},{10,11},{12,13},{... | collective-permute-start | bytes 589832 | tf_op jit(solution)/shard_map/ppermute | solution.py:600
  32.6 13.1 %collective-permute-start.10 = (f32[3,2,64,128]{3,2,1,0:T(8,128)S(1)}, f32[3,2,64,128]{3,2,1,0:T(8,128)S(1)}, u32[]{:S(2)}, u32[]{:S(2)}) collective-permute-start(f32[3,2,64,128]{3,2,1,0:T(8,128)S(1)} %get-tuple-element.47.rest_1_), channel_id=1, source_target_pairs={{1,0},{2,1},{3,2},{5,4},{6,5},{7,6},{9,8},{10,9},{11,10},{13,12},{... | collective-permute-start | bytes 589832 | tf_op jit(solution)/shard_map/ppermute | solution.py:601
  33.9 2.8 %copy-start.2 = (bf16[12,512,512]{2,1,0:T(8,128)(2,1)S(1)}, bf16[12,512,512]{2,1,0:T(8,128)(2,1)}, u32[]{:S(2)}) copy-start(bf16[12,512,512]{2,1,0:T(8,128)(2,1)} %w_ref.5) | copy-start | bytes 18874372
  36.7 9.0 %copy-start.3 = (bf16[12,512,512]{2,1,0:T(8,128)(2,1)S(1)}, bf16[12,512,512]{2,1,0:T(8,128)(2,1)}, u32[]{:S(2)}) copy-start(bf16[12,512,512]{2,1,0:T(8,128)(2,1)} %w_ref.5) | copy-start | bytes 18874372
  36.7 9.0 %copy-start.9 = (f32[3,8,8]{2,1,0:T(8,128)S(1)}, f32[3,8,8]{2,1,0:T(8,128)}, u32[]{:S(2)}) copy-start(f32[3,8,8]{2,1,0:T(8,128)} %taps_ref.1) | copy-start | bytes 2308
  45.7 1.7 %copy-start.5 = (bf16[4,1280,256]{2,1,0:T(8,128)(2,1)S(1)}, bf16[4,1280,256]{2,1,0:T(8,128)(2,1)}, u32[]{:S(2)}) copy-start(bf16[4,1280,256]{2,1,0:T(8,128)(2,1)} %copy-done.4) | copy-start | bytes 7864324
  68.2 3.9 %collective-permute-start.11 = (bf16[32,16,512]{2,1,0:T(8,128)(2,1)S(1)}, bf16[32,16,512]{2,1,0:T(8,128)(2,1)S(1)}, u32[]{:S(2)}, u32[]{:S(2)}) collective-permute-start(bf16[32,16,512]{2,1,0:T(8,128)(2,1)S(1)} %get-tuple-element.67), channel_id=1, source_target_pairs={{0,1},{1,0},{2,3},{3,2},{4,5},{5,4},{6,7},{7,6},{8,9},{9,8},{10,11... | collective-permute-start | bytes 1572872 | tf_op jit(solution)/shard_map/ppermute | solution.py:664
  72.1 5.8 %collective-permute-start.12 = (bf16[8,16,512]{2,1,0:T(8,128)(2,1)S(1)}, bf16[8,16,512]{2,1,0:T(8,128)(2,1)S(1)}, u32[]{:S(2)}, u32[]{:S(2)}) collective-permute-start(bf16[8,16,512]{2,1,0:T(8,128)(2,1)S(1)} %get-tuple-element.69), channel_id=1, source_target_pairs={{0,4},{4,0},{8,12},{12,8},{16,20},{20,16},{24,28},{28,24},{1,5},{5... | collective-permute-start | bytes 393224 | tf_op jit(solution)/shard_map/ppermute | solution.py:523
  78.0 5.0 %collective-permute-start.13 = (bf16[8,16,512]{2,1,0:T(8,128)(2,1)S(1)}, bf16[8,16,512]{2,1,0:T(8,128)(2,1)S(1)}, u32[]{:S(2)}, u32[]{:S(2)}) collective-permute-start(bf16[8,16,512]{2,1,0:T(8,128)(2,1)S(1)} %get-tuple-element.72), channel_id=1, source_target_pairs={{0,4},{4,0},{8,12},{12,8},{16,20},{20,16},{24,28},{28,24},{1,5},{5... | collective-permute-start | bytes 393224 | tf_op jit(solution)/shard_map/ppermute | solution.py:523
  79.6 7.2 %collective-permute-start.14 = (bf16[4,16,512]{2,1,0:T(8,128)(2,1)S(1)}, bf16[4,16,512]{2,1,0:T(8,128)(2,1)S(1)}, u32[]{:S(2)}, u32[]{:S(2)}) collective-permute-start(bf16[4,16,512]{2,1,0:T(8,128)(2,1)S(1)} %get-tuple-element.70.after_ref), channel_id=1, source_target_pairs={{0,16},{4,20},{8,24},{12,28},{16,0},{20,4},{24,8},{28,12},{1,17},{... | collective-permute-start | bytes 196616 | tf_op jit(solution)/shard_map/ppermute | solution.py:523
  80.5 6.2 %collective-permute-start.15 = (bf16[4,16,512]{2,1,0:T(8,128)(2,1)S(1)}, bf16[4,16,512]{2,1,0:T(8,128)(2,1)S(1)}, u32[]{:S(2)}, u32[]{:S(2)}) collective-permute-start(bf16[4,16,512]{2,1,0:T(8,128)(2,1)S(1)} %get-tuple-element.74), channel_id=1, source_target_pairs={{0,24},{4,28},{8,16},{12,20},{16,8},{20,12},{24,0},{28,4},{1,25},{... | collective-permute-start | bytes 196616 | tf_op jit(solution)/shard_map/ppermute | solution.py:523
  83.1 4.5 %collective-permute-start.16 = (bf16[4,16,512]{2,1,0:T(8,128)(2,1)S(1)}, bf16[4,16,512]{2,1,0:T(8,128)(2,1)S(1)}, u32[]{:S(2)}, u32[]{:S(2)}) collective-permute-start(bf16[4,16,512]{2,1,0:T(8,128)(2,1)S(1)} %get-tuple-element.75), channel_id=1, source_target_pairs={{0,8},{4,12},{8,0},{12,4},{16,24},{20,28},{24,16},{28,20},{1,9},{5... | collective-permute-start | bytes 196616 | tf_op jit(solution)/shard_map/ppermute | solution.py:523
  87.6 5.0 %collective-permute-start.17 = (f32[4,16,512]{2,1,0:T(8,128)S(1)}, f32[4,16,512]{2,1,0:T(8,128)S(1)}, u32[]{:S(2)}, u32[]{:S(2)}) collective-permute-start(f32[4,16,512]{2,1,0:T(8,128)S(1)} %convert_add_fusion), channel_id=1, source_target_pairs={{0,2},{1,3},{2,0},{3,1},{4,6},{5,7},{6,4},{7,5},{8,10},{9,11},{10,... | collective-permute-start | bytes 393224 | tf_op jit(solution)/shard_map/ppermute | solution.py:691
  92.7 1.4 %collective-permute-start.18 = (f32[4,16,512]{2,1,0:T(8,128)S(1)}, f32[4,16,512]{2,1,0:T(8,128)S(1)}, u32[]{:S(2)}, u32[]{:S(2)}) collective-permute-start(f32[4,16,512]{2,1,0:T(8,128)S(1)} %add.29), channel_id=1, source_target_pairs={{0,1},{1,0},{2,3},{3,2},{4,5},{5,4},{6,7},{7,6},{8,9},{9,8},{10,11... | collective-permute-start | bytes 393224 | tf_op jit(solution)/shard_map/ppermute | solution.py:692

commit v5 on v4

--- a/solution.py
+++ b/solution.py
@@ -12,6 +12,8 @@
 SUB = 8
 LANE = 128
 MIB = 1024 * 1024
+PARTS = 4
+BACK_PARTS = 2
 NT = (((1,), (1,)), ((), ()))
 
 
@@ -42,13 +44,24 @@
             ].astype(jnp.float32)
 
 
-def prep_kernel(gate_ref, own_ref, cot_ref, refx_ref, gates_ref, cot_out):
+def prep_kernel(
+    gate_ref, own_hbm, cot_hbm, refx_ref, gates_ref, cot_out, own_ref, cot_ref, sems
+):
+    copies = [
+        pltpu.make_async_copy(own_hbm, own_ref, sems.at[0]),
+        pltpu.make_async_copy(cot_hbm, cot_ref, sems.at[1]),
+    ]
+    for copy in copies:
+        copy.start()
+    for copy in copies:
+        copy.wait()
     local_views, channels, pixels = own_ref.shape
     for tile in range(pixels // LANE):
         for view in range(local_views):
             own = own_ref[view, :, pl.ds(tile * LANE, LANE)].astype(jnp.float32)
-            for copy in range(SUB // local_views):
-                refx_ref[tile, pl.ds(copy * local_views + view, channels, stride=SUB), :] = own
+            for copied in range(SUB // local_views):
+                first = copied * local_views + view
+                refx_ref[tile, pl.ds(first, channels, stride=SUB), :] = own
     for g in range(gates_ref.shape[0]):
         gates_ref[g] = jnp.full((SUB, LANE), gate_ref[g], jnp.float32)
 
@@ -96,7 +109,7 @@
         rows_ref[:, pl.ds(tile * LANE, LANE)] = scratch[tile].astype(jnp.bfloat16)
 
 
-def forward_vector(gates_ref, refx_ref, chunk, tile, outs):
+def forward_vector(gates_ref, refx_ref, chunk, tile, outs, held_corr, tick):
     warped_ref, corr_ref, sig_ref, rden_ref = outs
     pairs = sig_ref.shape[1]
     tiles = pairs // SUB
@@ -104,6 +117,7 @@
     logits = None
     corrs = []
     for g in range(G):
+        tick()
         total = None
         for j in range(0, GC, 2):
             c = g * GC + j
@@ -116,6 +130,7 @@
                 total = part if total is None else total + part
         corr = total * (1.0 / GC)
         corrs.append(corr)
+        held_corr[pl.ds(g * pairs, pairs), :] = corr.reshape(pairs, LANE)
         part = corr * gates_ref[g][None]
         logits = part if logits is None else logits + part
         if g % 2 == 1:
@@ -129,24 +144,37 @@
     rden_ref[0, :, lanes] = rden
     costs = []
     for g in range(G):
-        num = jnp.sum(visible * corrs[g], axis=0)
+        corr = held_corr[pl.ds(g * pairs, pairs), :].reshape(tiles, SUB, LANE)
+        num = jnp.sum(visible * corr, axis=0)
         costs.append((num + swap_halves(num)) * rden)
     return costs
 
 
+def ticker(thunks, ticks):
+    state = [0, 0]
+
+    def tick():
+        state[0] += 1
+        while state[1] * ticks < state[0] * len(thunks) and state[1] < len(thunks):
+            thunks[state[1]]()
+            state[1] += 1
+
+    return tick
+
+
 def weight_copy(w_ref, held, sems, plane, slot):
     return pltpu.make_async_copy(w_ref.at[plane], held.at[slot], sems.at[slot])
 
 
 def forward_body(plane_of, gates_ref, rows_ref, refx_ref, w_ref, outs, cost_ref, scratch):
-    held, sems, *chunks = scratch
+    held, sems, held_corr, *chunks = scratch
     step = pl.program_id(0)
     count = pl.num_programs(0) - 1
     slot = lax.rem(step, 2)
     low = low_half()
 
     def matmul(index, part):
-        rows = pl.ds(part * (rows_ref.shape[0] // 2), rows_ref.shape[0] // 2)
+        rows = pl.ds(part * (rows_ref.shape[0] // PARTS), rows_ref.shape[0] // PARTS)
         chunks[index][rows, :] = lax.dot_general(
             rows_ref[rows, :],
             held[slot, pl.ds(index * 2 * LANE, 2 * LANE), :],
@@ -156,9 +184,11 @@
 
     def vector(index, plane, beside):
         costs = []
+        thunks = []
+        if beside is not None:
+            thunks = [functools.partial(matmul, beside, part) for part in range(PARTS)]
+        tick = ticker(thunks, 2 * G)
         for half in range(2):
-            if beside is not None:
-                matmul(beside, half)
             costs.append(
                 forward_vector(
                     gates_ref,
@@ -166,6 +196,8 @@
                     chunks[index],
                     2 * index + half,
                     outs[4 * index : 4 * index + 4],
+                    held_corr,
+                    tick,
                 )
             )
         for g in range(G):
@@ -321,7 +353,7 @@
     slot = lax.rem(step, 3)
     slot_before = lax.rem(step + 2, 3)
 
-    def vector(saved, tile, upper, target):
+    def vector(saved, tile, upper, target, tick):
         warped_ref, corr_ref, sig_ref, rden_ref = saved[tile // 2]
         lanes = pl.ds((tile % 2) * LANE, LANE)
         full = pl.ds(tile * LANE, LANE)
@@ -356,6 +388,7 @@
         visible = (0.5 + sig) * (1.0 / GC)
         base = G // 2 if upper else 0
         for g in range(base, base + G // 2):
+            tick()
             corr_grad = visible * num_grads[g][None] + logit_grad * gates_ref[g][None]
             for j in range(0, GC, 2):
                 c = g * GC + j
@@ -380,27 +413,33 @@
                         corr_grad * warped[i], axis=0
                     )
 
-    def matmul(rows, where, base, index):
+    def matmul(rows, where, base, index, part):
+        size = half_rows // BACK_PARTS
         product = jnp.dot(
-            rows[...],
+            rows[pl.ds(part * size, size), :],
             held[where, :, pl.ds(index * 2 * LANE, 2 * LANE)],
             preferred_element_type=jnp.float32,
         )
         for half in range(2):
-            acc[2 * index + half, pl.ds(base, half_rows), :] += product[
+            acc[2 * index + half, pl.ds(base + part * size, size), :] += product[
                 :, half * LANE : (half + 1) * LANE
             ]
 
+    def matmuls(rows, where, base):
+        return [
+            functools.partial(matmul, rows, where, base, index, part)
+            for index in range(lane_tiles // 2)
+            for part in range(BACK_PARTS)
+        ]
+
     def one_plane(saved):
         weight_copy(w_ref, held, sems, plane, slot).wait()
+        tick = ticker(matmuls(rows_hi, slot_before, half_rows), lane_tiles * G // 2)
         for tile in range(lane_tiles):
-            if tile % 2 == 0:
-                matmul(rows_hi, slot_before, half_rows, tile // 2)
-            vector(saved, tile, False, rows_lo)
+            vector(saved, tile, False, rows_lo, tick)
+        tick = ticker(matmuls(rows_lo, slot, 0), lane_tiles * G // 2)
         for tile in range(lane_tiles):
-            if tile % 2 == 0:
-                matmul(rows_lo, slot, 0, tile // 2)
-            vector(saved, tile, True, rows_hi)
+            vector(saved, tile, True, rows_hi, tick)
 
     @pl.when(step == 0)
     def _():
@@ -425,8 +464,8 @@
 
     @pl.when(step == count)
     def _():
-        for index in range(lane_tiles // 2):
-            matmul(rows_hi, slot_before, half_rows, index)
+        for thunk in matmuls(rows_hi, slot_before, half_rows):
+            thunk()
         own_index = place_ref[0]
         parity = place_ref[1]
         dense[...] = jnp.zeros_like(dense)
@@ -527,6 +566,9 @@
     near_even = jnp.concatenate(even[:quarter], axis=0)
     far_even = jnp.concatenate(even[quarter:], axis=0)
     packed = (pixels // (2 * LANE), G * SUB, LANE)
+    hbm = pl.BlockSpec(memory_space=pltpu.HBM)
+    anywhere = pl.BlockSpec(memory_space=pl.ANY)
+    weights = pltpu.with_memory_space_constraint(warp_weights, pltpu.HBM)
     refx, gates, cot = pl.pallas_call(
         prep_kernel,
         out_shape=(
@@ -534,12 +576,21 @@
             shape((G, SUB, LANE), f32),
             shape((planes,) + packed, f32),
         ),
-        in_specs=[SMEM(), pl.BlockSpec(), pl.BlockSpec()],
+        in_specs=[SMEM(), hbm, hbm],
+        scratch_shapes=[
+            pltpu.VMEM(features.shape, bf16),
+            pltpu.VMEM(cotangent.shape, bf16),
+            pltpu.SemaphoreType.DMA((2,)),
+        ],
         compiler_params=params(),
         cost_estimate=pl.CostEstimate(flops=10**9, bytes_accessed=4 * MIB, transcendentals=0),
         name="prep",
-    )(view_gate, features, cotangent)
-    near_even, refx, gates, cot = lax.optimization_barrier((near_even, refx, gates, cot))
+    )(
+        pltpu.with_memory_space_constraint(view_gate, pltpu.HBM),
+        pltpu.with_memory_space_constraint(features, pltpu.HBM),
+        pltpu.with_memory_space_constraint(cotangent, pltpu.HBM),
+    )
+    far_even, refx, gates, cot = lax.optimization_barrier((far_even, refx, gates, cot))
     maps = [near_even, far_even, over_view(near_even, 1), over_view(far_even, 1)]
     maps = maps + [lax.ppermute(part, "plane", near) for part in maps]
 
@@ -561,10 +612,10 @@
 
     def saved_shapes(count):
         one = (
-            shape((count, channels * pairs, width), bf16),
-            shape((count, G * pairs, width), bf16),
-            shape((count, pairs, width), f32),
-            shape((count, SUB, width), f32),
+            pltpu.VMEM((count, channels * pairs, width), bf16),
+            pltpu.VMEM((count, G * pairs, width), bf16),
+            pltpu.VMEM((count, pairs, width), f32),
+            pltpu.VMEM((count, SUB, width), f32),
         )
         return one * 2
 
@@ -577,11 +628,11 @@
                 specs.append(per_plane(item.shape, lambda d: jnp.maximum(d - 1, 0)))
         return specs
 
-    hbm = pl.BlockSpec(memory_space=pltpu.HBM)
     fixed_specs = [fixed(gates.shape), fixed(rows.shape), fixed(refx.shape), hbm]
     scratch = [
         pltpu.VMEM((2, pixels, pixels), bf16),
         pltpu.SemaphoreType.DMA((2,)),
+        pltpu.VMEM((G * pairs, LANE), f32),
         pltpu.VMEM((channels * pairs, width), f32),
         pltpu.VMEM((channels * pairs, width), f32),
     ]
@@ -594,9 +645,9 @@
         in_specs=fixed_specs + [fixed(cot.shape)],
         out_specs=tuple(saved_specs(4)) + (fixed(load),) * 2,
         scratch_shapes=[pltpu.VMEM((4,) + packed, f32)] + scratch,
-        compiler_params=params(14),
+        compiler_params=params(11),
         name="forward_edge",
-    )(gates, rows, refx, warp_weights, cot)
+    )(gates, rows, refx, weights, cot)
     below = lax.ppermute(up_load, "plane", up)
     above = lax.ppermute(down_load, "plane", down)
     *inner_saved, inner_cost = pl.pallas_call(
@@ -606,16 +657,20 @@
         in_specs=fixed_specs,
         out_specs=tuple(saved_specs(inner_count)) + (fixed((inner_count,) + packed),),
         scratch_shapes=scratch,
-        compiler_params=params(14),
+        compiler_params=params(11),
         cost_estimate=pl.CostEstimate(
             flops=2 * channels * pairs * pixels * pixels * inner_count,
             bytes_accessed=40 * MIB,
             transcendentals=0,
         ),
         name="forward_inner",
-    )(gates, rows, refx, warp_weights)
+    )(gates, rows, refx, weights)
 
     halo = (below, down_load, inner_cost, up_load, above, cot)
+    inner_saved, edge_saved = [
+        [pltpu.with_memory_space_constraint(item, pltpu.VMEM) for item in group]
+        for group in (inner_saved, edge_saved)
+    ]
     returned = (all_views, channels // 2, pixels)
     regular, keep, send = pl.pallas_call(
         backward_kernel,
@@ -647,7 +702,7 @@
             pltpu.SemaphoreType.DMA((3,)),
             pltpu.VMEM((all_views, channels, pixels), f32),
         ],
-        compiler_params=params(15 + 14 * all_views * channels * pixels // MIB),
+        compiler_params=params(12 + 14 * all_views * channels * pixels // MIB),
         name="backward",
     )(
         src_own,
@@ -655,7 +710,7 @@
         depth_kernel,
         gates,
         refx,
-        warp_weights,
+        weights,
         *halo,
         *inner_saved,
         *edge_saved,
@@ -664,7 +719,6 @@
     received = lax.ppermute(send, "plane", near)
     close = quarter * local_views
     piece = (local_views, channels // 2, pixels)
-    anywhere = pl.BlockSpec(memory_space=pl.ANY)
 
     def stage(first, count, after, kind):
         even_sum, outgoing = pl.pallas_call(
@@ -688,7 +742,8 @@
         total = total + over_view(part, 2 * (quarter + index)).astype(f32)
     for index, part in enumerate(close_parts):
         total = total + over_view(part, 2 * (index + 1)).astype(f32)
-    total = total + lax.ppermute(total, "plane", far)
+    rounded = total.astype(bf16)
+    total = rounded.astype(f32) + lax.ppermute(rounded, "plane", far).astype(f32)
     other = lax.ppermute(total, "plane", near)
     cut = (local_views, blocks, 1, share, pixels)
     first = jnp.where(parity == 0, total, other).reshape(cut)

time: 95.2 us -> 90.5 us (0.951)
  local copies, waits for them, and re-layouts: 12.4 us -> 1.75 us
  Pallas kernels: 36.9 us -> 42.7 us
    unnamed x26 -> x5, local copies, waits for them, and re-layouts: 10.8 us -> 0.11 us
    pallas_call x1, Pallas kernels: 20.8 us -> 24.2 us  [shards(): pl.pallas_call(backward_kernel, out_shape=(shape(cotangent.shape, bf16),...]
    pallas_call x1, Pallas kernels: 0.79 us -> 1.99 us  [shards(): pl.pallas_call(prep_kernel, out_shape=(shape((pixels // LANE, channels *...]
  transfers between devices with their start and end apart: 19 -> 19, of which waited for: 12 -> 12; matrix products, arithmetic and copies ran while one was open for 0% -> 0% of each run, Pallas kernels for 10% -> 13%
where the time goes in v5:
time: 90.5 us; the launch traced here: 90 us
  Pallas kernels  42.7 us (47%)
  waiting for transfers between devices  22.4 us (25%)
  starting transfers between devices  22.1 us (24%)
  local copies, waits for them, and re-layouts  1.75 us (2%)
    pallas_call x1, Pallas kernels, shards(): pl.pallas_call(backward_kernel, out_shape=(shape(cotangent.shape, bf16),...  24.2 us
    ppermute x10, waiting for transfers between devices, over_view(): return lax.ppermute(array, 'view', [(i, i ^ k) for i in range(view_count)])  15.8 us
    ppermute x10, starting transfers between devices, over_view(): return lax.ppermute(array, 'view', [(i, i ^ k) for i in range(view_count)])  14.3 us
    pallas_call x1, Pallas kernels, shards(): pl.pallas_call(inner_kernel, out_shape=saved_shapes(inner_count) + (shape...  9.44 us
    pallas_call x1, Pallas kernels, shards(): pl.pallas_call(edge_kernel, out_shape=saved_shapes(4) + (shape(load, f32)...  5.39 us
    ppermute x1, waiting for transfers between devices, shards(): lax.ppermute(rounded, 'plane', far).astype(f32)  2.62 us
    ppermute x1, starting transfers between devices, shards(): received = lax.ppermute(send, 'plane', near)  2.14 us
    ppermute x1, starting transfers between devices, shards(): below = lax.ppermute(up_load, 'plane', up)  2.06 us
  transfers between devices with their start and end apart: 19, of which 12 were waited for; matrix products, arithmetic and copies ran while one was open for 0% of the time, Pallas kernels for 13%

profile of v5, /device:TPU:0, one launch (start us, length us, event | category | flops | bytes accessed | tf_op | source)
XLA Modules:
  0.0 90.0 jit_solution(12638867738435411350)
XLA Ops:
  0.6 0.0 copy-start
  0.7 0.8 dynamic-slice_bitcast_fusion
  1.5 3.0 %collective-permute-start.2 = (bf16[4,16,512]{2,1,0:T(8,128)(2,1)S(1)}, bf16[4,16,512]{2,1,0:T(8,128)(2,1)S(1)}, u32[]{:S(2)}, u32[]{:S(2)}) collective-permute-start(bf16[4,16,512]{2,1,0:T(8,128)(2,1)S(1)} %dynamic-slice_bitcast_fusion), channel_id=1, source_target_pairs={{0,8},{4,12},{8,0},{12,4},{16,24},{20,28},{24,16},{28,20},{1,9},{5... | collective-permute-start | bytes 196616 | tf_op jit(solution)/shard_map/ppermute | solution.py:562
  4.5 2.5 %collective-permute-start.1 = (bf16[4,16,512]{2,1,0:T(8,128)(2,1)S(1)}, bf16[4,16,512]{2,1,0:T(8,128)(2,1)S(1)}, u32[]{:S(2)}, u32[]{:S(2)}) collective-permute-start(bf16[4,16,512]{2,1,0:T(8,128)(2,1)S(1)} %dynamic-slice_bitcast_fusion), channel_id=1, source_target_pairs={{0,24},{4,28},{8,16},{12,20},{16,8},{20,12},{24,0},{28,4},{1,25},{... | collective-permute-start | bytes 196616 | tf_op jit(solution)/shard_map/ppermute | solution.py:562
  7.0 0.1 collective-permute-start
  7.1 2.0 %prep.1 = (f32[4,256,128]{2,1,0:T(8,128)S(1)}, f32[8,8,128]{2,1,0:T(8,128)S(1)}, f32[12,2,64,128]{3,2,1,0:T(8,128)S(1)}) custom-call(f32[8]{0:T(128)} %gate_ref.1, bf16[4,32,512]{2,1,0:T(8,128)(2,1)} %own_hbm.1, bf16[4,12,8,512]{3,2,1,0:T(8,128)(2,1)} %cot_hbm.1), custom_call_target="tpu_custom_call" | custom-call | flops 1000000000 | bytes 4194304 | tf_op jit(solution)/shard_map/prep/pallas_call | solution.py:572
  9.2 1.6 %collective-permute-start.3 = (bf16[8,16,512]{2,1,0:T(8,128)(2,1)S(1)}, bf16[8,16,512]{2,1,0:T(8,128)(2,1)S(1)}, u32[]{:S(2)}, u32[]{:S(2)}) collective-permute-start(bf16[8,16,512]{2,1,0:T(8,128)(2,1)S(1)} %pad_maximum_fusion.2.rest_0_), channel_id=1, source_target_pairs={{0,4},{4,0},{8,12},{12,8},{16,20},{20,16},{24,28},{28,24},{1,5},{5... | collective-permute-start | bytes 393224 | tf_op jit(solution)/shard_map/ppermute | solution.py:562
  10.7 0.7 collective-permute-done.1
  11.4 2.1 %collective-permute-done = bf16[4,16,512]{2,1,0:T(8,128)(2,1)S(1)} collective-permute-done((bf16[4,16,512]{2,1,0:T(8,128)(2,1)S(1)}, bf16[4,16,512]{2,1,0:T(8,128)(2,1)S(1)}, u32[]{:S(2)}, u32[]{:S(2)}) %collective-permute-start) | collective-permute-done | bytes 65568 | tf_op jit(solution)/shard_map/ppermute | solution.py:562
  13.5 1.6 %collective-permute-start.4 = (bf16[8,16,512]{2,1,0:T(8,128)(2,1)S(1)}, bf16[8,16,512]{2,1,0:T(8,128)(2,1)S(1)}, u32[]{:S(2)}, u32[]{:S(2)}) collective-permute-start(bf16[8,16,512]{2,1,0:T(8,128)(2,1)S(1)} %pad_maximum_fusion.1.rest_1_), channel_id=1, source_target_pairs={{0,4},{4,0},{8,12},{12,8},{16,20},{20,16},{24,28},{28,24},{1,5},{5... | collective-permute-start | bytes 393224 | tf_op jit(solution)/shard_map/ppermute | solution.py:562
  15.1 0.0 collective-permute-start.5
  15.1 0.5 collective-permute-start.6
  15.6 0.0 collective-permute-start.7
  15.6 3.3 %collective-permute-done.4.rest_3_ = bf16[8,16,512]{2,1,0:T(8,128)(2,1)S(1)} collective-permute-done((bf16[8,16,512]{2,1,0:T(8,128)(2,1)S(1)}, bf16[8,16,512]{2,1,0:T(8,128)(2,1)S(1)}, u32[]{:S(2)}, u32[]{:S(2)}) %collective-permute-start.4) | collective-permute-done | bytes 131104 | tf_op jit(solution)/shard_map/ppermute | solution.py:562
  18.9 0.0 collective-permute-start.8
  18.9 0.1 constant_dynamic-slice_fusion
  19.0 0.1 copy.11.src_ref
  19.1 0.1 pad_add_fusion.place_ref
  19.2 0.0 collective-permute-done.5.rest_4_
  19.2 0.0 collective-permute-done.6.rest_5_
  19.2 0.0 collective-permute-done.7.rest_6_
  19.2 1.1 %collective-permute-done.8.rest_7_ = bf16[8,16,512]{2,1,0:T(8,128)(2,1)S(1)} collective-permute-done((bf16[8,16,512]{2,1,0:T(8,128)(2,1)S(1)}, bf16[8,16,512]{2,1,0:T(8,128)(2,1)S(1)}, u32[]{:S(2)}, u32[]{:S(2)}) %collective-permute-start.8) | collective-permute-done | bytes 131104 | tf_op jit(solution)/shard_map/ppermute | solution.py:595
  20.3 1.6 %assemble.1.rows_ref = bf16[1280,512]{1,0:T(8,128)(2,1)S(1)} custom-call(s32[4,10]{1,0:T(4,128)S(1)} %copy.11.src_ref, s32[2]{0:T(128)S(1)} %pad_add_fusion.place_ref, bf16[8,16,512]{2,1,0:T(8,128)(2,1)S(1)} %pad_maximum_fusion.2.rest_0_, bf16[8,16,512]{2,1,0:T(8,128)(2,1)S(1)} %pad_maximum_fusion.1.rest_1_, ...), custom_call_target="tpu_custom_call" | custom-call | tf_op jit(solution)/shard_map/assemble/pallas_call | solution.py:599
  21.8 5.4 %forward_edge.1 = (bf16[4,1280,256]{2,1,0:T(8,128)(2,1)S(1)}, bf16[4,320,256]{2,1,0:T(8,128)(2,1)S(1)}, f32[4,40,256]{2,1,0:T(8,128)S(1)}, f32[4,8,256]{2,1,0:T(...) custom-call(f32[8,8,128]{2,1,0:T(8,128)S(1)} %get-tuple-element.42.g, ...), custom_call_target="tpu_custom_call" | custom-call | tf_op jit(solution)/shard_map/forward_edge/pallas_call | solution.py:641
  27.2 2.1 %collective-permute-start.9 = (f32[3,2,64,128]{3,2,1,0:T(8,128)S(1)}, f32[3,2,64,128]{3,2,1,0:T(8,128)S(1)}, u32[]{:S(2)}, u32[]{:S(2)}) collective-permute-start(f32[3,2,64,128]{3,2,1,0:T(8,128)S(1)} %get-tuple-element.46.rest_3_), channel_id=1, source_target_pairs={{0,1},{1,2},{2,3},{4,5},{5,6},{6,7},{8,9},{9,10},{10,11},{12,13},{... | collective-permute-start | bytes 589832 | tf_op jit(solution)/shard_map/ppermute | solution.py:651
  29.3 0.0 copy-start.1
  29.3 1.3 %collective-permute-start.10 = (f32[3,2,64,128]{3,2,1,0:T(8,128)S(1)}, f32[3,2,64,128]{3,2,1,0:T(8,128)S(1)}, u32[]{:S(2)}, u32[]{:S(2)}) collective-permute-start(f32[3,2,64,128]{3,2,1,0:T(8,128)S(1)} %get-tuple-element.47.rest_1_), channel_id=1, source_target_pairs={{1,0},{2,1},{3,2},{5,4},{6,5},{7,6},{9,8},{10,9},{11,10},{13,12},{... | collective-permute-start | bytes 589832 | tf_op jit(solution)/shard_map/ppermute | solution.py:652
  30.6 9.4 %forward_inner.1 = (bf16[8,1280,256]{2,1,0:T(8,128)(2,1)S(1)}, bf16[8,320,256]{2,1,0:T(8,128)(2,1)S(1)}, f32[8,40,256]{2,1,0:T(8,128)S(1)}, f32[8,8,256]{2,1,0:T...) custom-call(f32[8,8,128]{2,1,0:T(8,128)S(1)} %get-tuple-element.42.g, ...), custom_call_target="tpu_custom_call" | custom-call | flops 5368709120 | bytes 41943040 | tf_op jit(solution)/shard_map/forward_inner/pallas_call | solution.py:653
  40.1 24.2 %backward.1 = (bf16[4,12,8,512]{3,2,1,0:T(8,128)(2,1)}, f32[32,16,512]{2,1,0:T(8,128)S(1)}, bf16[32,16,512]{2,1,0:T(8,128)(2,1)S(1)}) custom-call(s32[4,10]{1,0:T(4,128)S(1)} %copy.11.src_ref, s32[2]{0:T(128)S(1)} %pad_add_fusion.place_ref, f32[3,8,8]{2,1,0:T(8,128)S(1)} %copy-done.1, f32[8,8,128]{2,1,0:T(8,128)S(1)} %get-tuple-element.42.gates_ref, ...), custom_call_target="tpu_custom_call" | custom-call | tf_op jit(solution)/shard_map/backward/pallas_call | solution.py:675
  64.3 2.1 %collective-permute-start.11 = (bf16[32,16,512]{2,1,0:T(8,128)(2,1)S(1)}, bf16[32,16,512]{2,1,0:T(8,128)(2,1)S(1)}, u32[]{:S(2)}, u32[]{:S(2)}) collective-permute-start(bf16[32,16,512]{2,1,0:T(8,128)(2,1)S(1)} %get-tuple-element.67), channel_id=1, source_target_pairs={{0,1},{1,0},{2,3},{3,2},{4,5},{5,4},{6,7},{7,6},{8,9},{9,8},{10,11... | collective-permute-start | bytes 1572872 | tf_op jit(solution)/shard_map/ppermute | solution.py:719
  66.4 1.5 %collective-permute-done.11.received_ref.after_ref = bf16[32,16,512]{2,1,0:T(8,128)(2,1)S(1)} collective-permute-done((bf16[32,16,512]{2,1,0:T(8,128)(2,1)S(1)}, bf16[32,16,512]{2,1,0:T(8,128)(2,1)S(1)}, u32[]{:S(2)}, u32[]{:S(2)}) %collective-permute-start.11) | collective-permute-done | bytes 524320 | tf_op jit(solution)/shard_map/ppermute | solution.py:719
  68.0 0.1 split.2
  68.0 1.6 %collective-permute-start.12 = (bf16[8,16,512]{2,1,0:T(8,128)(2,1)S(1)}, bf16[8,16,512]{2,1,0:T(8,128)(2,1)S(1)}, u32[]{:S(2)}, u32[]{:S(2)}) collective-permute-start(bf16[8,16,512]{2,1,0:T(8,128)(2,1)S(1)} %get-tuple-element.69), channel_id=1, source_target_pairs={{0,4},{4,0},{8,12},{12,8},{16,20},{20,16},{24,28},{28,24},{1,5},{5... | collective-permute-start | bytes 393224 | tf_op jit(solution)/shard_map/ppermute | solution.py:562
  69.6 4.2 %collective-permute-done.12.received_ref = bf16[8,16,512]{2,1,0:T(8,128)(2,1)S(1)} collective-permute-done((bf16[8,16,512]{2,1,0:T(8,128)(2,1)S(1)}, bf16[8,16,512]{2,1,0:T(8,128)(2,1)S(1)}, u32[]{:S(2)}, u32[]{:S(2)}) %collective-permute-start.12) | collective-permute-done | bytes 131104 | tf_op jit(solution)/shard_map/ppermute | solution.py:562
  73.9 0.1 split.3
  74.0 1.6 %collective-permute-start.13 = (bf16[8,16,512]{2,1,0:T(8,128)(2,1)S(1)}, bf16[8,16,512]{2,1,0:T(8,128)(2,1)S(1)}, u32[]{:S(2)}, u32[]{:S(2)}) collective-permute-start(bf16[8,16,512]{2,1,0:T(8,128)(2,1)S(1)} %get-tuple-element.72), channel_id=1, source_target_pairs={{0,4},{4,0},{8,12},{12,8},{16,20},{20,16},{24,28},{28,24},{1,5},{5... | collective-permute-start | bytes 393224 | tf_op jit(solution)/shard_map/ppermute | solution.py:562
  75.5 0.9 collective-permute-start.14
  76.4 1.4 %collective-permute-start.15 = (bf16[4,16,512]{2,1,0:T(8,128)(2,1)S(1)}, bf16[4,16,512]{2,1,0:T(8,128)(2,1)S(1)}, u32[]{:S(2)}, u32[]{:S(2)}) collective-permute-start(bf16[4,16,512]{2,1,0:T(8,128)(2,1)S(1)} %get-tuple-element.74), channel_id=1, source_target_pairs={{0,24},{4,28},{8,16},{12,20},{16,8},{20,12},{24,0},{28,4},{1,25},{... | collective-permute-start | bytes 196616 | tf_op jit(solution)/shard_map/ppermute | solution.py:562
  77.8 1.2 %collective-permute-done.13.received_ref = bf16[8,16,512]{2,1,0:T(8,128)(2,1)S(1)} collective-permute-done((bf16[8,16,512]{2,1,0:T(8,128)(2,1)S(1)}, bf16[8,16,512]{2,1,0:T(8,128)(2,1)S(1)}, u32[]{:S(2)}, u32[]{:S(2)}) %collective-permute-start.13) | collective-permute-done | bytes 131104 | tf_op jit(solution)/shard_map/ppermute | solution.py:562
  79.0 0.1 collective-permute-start.16
  79.1 3.5 %collective-permute-done.15 = bf16[4,16,512]{2,1,0:T(8,128)(2,1)S(1)} collective-permute-done((bf16[4,16,512]{2,1,0:T(8,128)(2,1)S(1)}, bf16[4,16,512]{2,1,0:T(8,128)(2,1)S(1)}, u32[]{:S(2)}, u32[]{:S(2)}) %collective-permute-start.15) | collective-permute-done | bytes 65568 | tf_op jit(solution)/shard_map/ppermute | solution.py:562
  82.6 0.1 collective-permute-done.14
  82.7 0.7 collective-permute-done.16
  83.5 1.7 %collective-permute-start.17 = (bf16[4,16,512]{2,1,0:T(8,128)(2,1)S(1)}, bf16[4,16,512]{2,1,0:T(8,128)(2,1)S(1)}, u32[]{:S(2)}, u32[]{:S(2)}) collective-permute-start(bf16[4,16,512]{2,1,0:T(8,128)(2,1)S(1)} %add_convert_fusion), channel_id=1, source_target_pairs={{0,2},{1,3},{2,0},{3,1},{4,6},{5,7},{6,4},{7,5},{8,10},{9,11},{10,... | collective-permute-start | bytes 196616 | tf_op jit(solution)/shard_map/ppermute | solution.py:746
  85.2 2.6 %collective-permute-done.17 = bf16[4,16,512]{2,1,0:T(8,128)(2,1)S(1)} collective-permute-done((bf16[4,16,512]{2,1,0:T(8,128)(2,1)S(1)}, bf16[4,16,512]{2,1,0:T(8,128)(2,1)S(1)}, u32[]{:S(2)}, u32[]{:S(2)}) %collective-permute-start.17) | collective-permute-done | bytes 65568 | tf_op jit(solution)/shard_map/ppermute | solution.py:746
  87.9 0.1 collective-permute-start.18
  87.9 1.3 %collective-permute-done.18 = f32[4,16,512]{2,1,0:T(8,128)S(1)} collective-permute-done((f32[4,16,512]{2,1,0:T(8,128)S(1)}, f32[4,16,512]{2,1,0:T(8,128)S(1)}, u32[]{:S(2)}, u32[]{:S(2)}) %collective-permute-start.18) | collective-permute-done | bytes 131104 | tf_op jit(solution)/shard_map/ppermute | solution.py:747
  89.3 0.7 copy.10
  (14 shorter events, 0.2 us)
Async XLA Ops:
  0.6 18.3 %copy-start = (s32[32,10]{0,1:T(8,128)S(1)}, s32[32,10]{0,1:T(8,128)}, u32[]{:S(2)}) copy-start(s32[32,10]{0,1:T(8,128)} %param.7) | copy-start | bytes 3844
  1.5 7.6 %collective-permute-start.2 = (bf16[4,16,512]{2,1,0:T(8,128)(2,1)S(1)}, bf16[4,16,512]{2,1,0:T(8,128)(2,1)S(1)}, u32[]{:S(2)}, u32[]{:S(2)}) collective-permute-start(bf16[4,16,512]{2,1,0:T(8,128)(2,1)S(1)} %dynamic-slice_bitcast_fusion), channel_id=1, source_target_pairs={{0,8},{4,12},{8,0},{12,4},{16,24},{20,28},{24,16},{28,20},{1,9},{5... | collective-permute-start | bytes 196616 | tf_op jit(solution)/shard_map/ppermute | solution.py:562
  4.5 6.9 %collective-permute-start.1 = (bf16[4,16,512]{2,1,0:T(8,128)(2,1)S(1)}, bf16[4,16,512]{2,1,0:T(8,128)(2,1)S(1)}, u32[]{:S(2)}, u32[]{:S(2)}) collective-permute-start(bf16[4,16,512]{2,1,0:T(8,128)(2,1)S(1)} %dynamic-slice_bitcast_fusion), channel_id=1, source_target_pairs={{0,24},{4,28},{8,16},{12,20},{16,8},{20,12},{24,0},{28,4},{1,25},{... | collective-permute-start | bytes 196616 | tf_op jit(solution)/shard_map/ppermute | solution.py:562
  7.0 6.4 %collective-permute-start = (bf16[4,16,512]{2,1,0:T(8,128)(2,1)S(1)}, bf16[4,16,512]{2,1,0:T(8,128)(2,1)S(1)}, u32[]{:S(2)}, u32[]{:S(2)}) collective-permute-start(bf16[4,16,512]{2,1,0:T(8,128)(2,1)S(1)} %dynamic-slice_bitcast_fusion), channel_id=1, source_target_pairs={{0,16},{4,20},{8,24},{12,28},{16,0},{20,4},{24,8},{28,12},{1,17},{... | collective-permute-start | bytes 196616 | tf_op jit(solution)/shard_map/ppermute | solution.py:562
  9.2 6.4 %collective-permute-start.3 = (bf16[8,16,512]{2,1,0:T(8,128)(2,1)S(1)}, bf16[8,16,512]{2,1,0:T(8,128)(2,1)S(1)}, u32[]{:S(2)}, u32[]{:S(2)}) collective-permute-start(bf16[8,16,512]{2,1,0:T(8,128)(2,1)S(1)} %pad_maximum_fusion.2.rest_0_), channel_id=1, source_target_pairs={{0,4},{4,0},{8,12},{12,8},{16,20},{20,16},{24,28},{28,24},{1,5},{5... | collective-permute-start | bytes 393224 | tf_op jit(solution)/shard_map/ppermute | solution.py:562
  13.5 5.4 %collective-permute-start.4 = (bf16[8,16,512]{2,1,0:T(8,128)(2,1)S(1)}, bf16[8,16,512]{2,1,0:T(8,128)(2,1)S(1)}, u32[]{:S(2)}, u32[]{:S(2)}) collective-permute-start(bf16[8,16,512]{2,1,0:T(8,128)(2,1)S(1)} %pad_maximum_fusion.1.rest_1_), channel_id=1, source_target_pairs={{0,4},{4,0},{8,12},{12,8},{16,20},{20,16},{24,28},{28,24},{1,5},{5... | collective-permute-start | bytes 393224 | tf_op jit(solution)/shard_map/ppermute | solution.py:562
  15.1 4.1 %collective-permute-start.5 = (bf16[8,16,512]{2,1,0:T(8,128)(2,1)S(1)}, bf16[8,16,512]{2,1,0:T(8,128)(2,1)S(1)}, u32[]{:S(2)}, u32[]{:S(2)}) collective-permute-start(bf16[8,16,512]{2,1,0:T(8,128)(2,1)S(1)} %pad_maximum_fusion.2.rest_0_), channel_id=1, source_target_pairs={{0,1},{1,0},{2,3},{3,2},{4,5},{5,4},{6,7},{7,6},{8,9},{9,8},{10,11... | collective-permute-start | bytes 393224 | tf_op jit(solution)/shard_map/ppermute | solution.py:595
  15.1 4.1 %collective-permute-start.6 = (bf16[8,16,512]{2,1,0:T(8,128)(2,1)S(1)}, bf16[8,16,512]{2,1,0:T(8,128)(2,1)S(1)}, u32[]{:S(2)}, u32[]{:S(2)}) collective-permute-start(bf16[8,16,512]{2,1,0:T(8,128)(2,1)S(1)} %pad_maximum_fusion.1.rest_1_), channel_id=1, source_target_pairs={{0,1},{1,0},{2,3},{3,2},{4,5},{5,4},{6,7},{7,6},{8,9},{9,8},{10,11... | collective-permute-start | bytes 393224 | tf_op jit(solution)/shard_map/ppermute | solution.py:595
  15.6 3.6 %collective-permute-start.7 = (bf16[8,16,512]{2,1,0:T(8,128)(2,1)S(1)}, bf16[8,16,512]{2,1,0:T(8,128)(2,1)S(1)}, u32[]{:S(2)}, u32[]{:S(2)}) collective-permute-start(bf16[8,16,512]{2,1,0:T(8,128)(2,1)S(1)} %collective-permute-done.3.rest_2_), channel_id=1, source_target_pairs={{0,1},{1,0},{2,3},{3,2},{4,5},{5,4},{6,7},{7,6},{8,9},{9,8},{10,11... | collective-permute-start | bytes 393224 | tf_op jit(solution)/shard_map/ppermute | solution.py:595
  18.9 1.3 %collective-permute-start.8 = (bf16[8,16,512]{2,1,0:T(8,128)(2,1)S(1)}, bf16[8,16,512]{2,1,0:T(8,128)(2,1)S(1)}, u32[]{:S(2)}, u32[]{:S(2)}) collective-permute-start(bf16[8,16,512]{2,1,0:T(8,128)(2,1)S(1)} %collective-permute-done.4.rest_3_), channel_id=1, source_target_pairs={{0,1},{1,0},{2,3},{3,2},{4,5},{5,4},{6,7},{7,6},{8,9},{9,8},{10,11... | collective-permute-start | bytes 393224 | tf_op jit(solution)/shard_map/ppermute | solution.py:595
  27.2 12.8 %collective-permute-start.9 = (f32[3,2,64,128]{3,2,1,0:T(8,128)S(1)}, f32[3,2,64,128]{3,2,1,0:T(8,128)S(1)}, u32[]{:S(2)}, u32[]{:S(2)}) collective-permute-start(f32[3,2,64,128]{3,2,1,0:T(8,128)S(1)} %get-tuple-element.46.rest_3_), channel_id=1, source_target_pairs={{0,1},{1,2},{2,3},{4,5},{5,6},{6,7},{8,9},{9,10},{10,11},{12,13},{... | collective-permute-start | bytes 589832 | tf_op jit(solution)/shard_map/ppermute | solution.py:651
  29.3 10.8 %copy-start.1 = (f32[3,8,8]{2,1,0:T(8,128)S(1)}, f32[3,8,8]{2,1,0:T(8,128)}, u32[]{:S(2)}) copy-start(f32[3,8,8]{2,1,0:T(8,128)} %taps_ref.1) | copy-start | bytes 2308
  29.3 10.8 %collective-permute-start.10 = (f32[3,2,64,128]{3,2,1,0:T(8,128)S(1)}, f32[3,2,64,128]{3,2,1,0:T(8,128)S(1)}, u32[]{:S(2)}, u32[]{:S(2)}) collective-permute-start(f32[3,2,64,128]{3,2,1,0:T(8,128)S(1)} %get-tuple-element.47.rest_1_), channel_id=1, source_target_pairs={{1,0},{2,1},{3,2},{5,4},{6,5},{7,6},{9,8},{10,9},{11,10},{13,12},{... | collective-permute-start | bytes 589832 | tf_op jit(solution)/shard_map/ppermute | solution.py:652
  64.3 3.7 %collective-permute-start.11 = (bf16[32,16,512]{2,1,0:T(8,128)(2,1)S(1)}, bf16[32,16,512]{2,1,0:T(8,128)(2,1)S(1)}, u32[]{:S(2)}, u32[]{:S(2)}) collective-permute-start(bf16[32,16,512]{2,1,0:T(8,128)(2,1)S(1)} %get-tuple-element.67), channel_id=1, source_target_pairs={{0,1},{1,0},{2,3},{3,2},{4,5},{5,4},{6,7},{7,6},{8,9},{9,8},{10,11... | collective-permute-start | bytes 1572872 | tf_op jit(solution)/shard_map/ppermute | solution.py:719
  68.0 5.8 %collective-permute-start.12 = (bf16[8,16,512]{2,1,0:T(8,128)(2,1)S(1)}, bf16[8,16,512]{2,1,0:T(8,128)(2,1)S(1)}, u32[]{:S(2)}, u32[]{:S(2)}) collective-permute-start(bf16[8,16,512]{2,1,0:T(8,128)(2,1)S(1)} %get-tuple-element.69), channel_id=1, source_target_pairs={{0,4},{4,0},{8,12},{12,8},{16,20},{20,16},{24,28},{28,24},{1,5},{5... | collective-permute-start | bytes 393224 | tf_op jit(solution)/shard_map/ppermute | solution.py:562
  74.0 5.0 %collective-permute-start.13 = (bf16[8,16,512]{2,1,0:T(8,128)(2,1)S(1)}, bf16[8,16,512]{2,1,0:T(8,128)(2,1)S(1)}, u32[]{:S(2)}, u32[]{:S(2)}) collective-permute-start(bf16[8,16,512]{2,1,0:T(8,128)(2,1)S(1)} %get-tuple-element.72), channel_id=1, source_target_pairs={{0,4},{4,0},{8,12},{12,8},{16,20},{20,16},{24,28},{28,24},{1,5},{5... | collective-permute-start | bytes 393224 | tf_op jit(solution)/shard_map/ppermute | solution.py:562
  75.5 7.2 %collective-permute-start.14 = (bf16[4,16,512]{2,1,0:T(8,128)(2,1)S(1)}, bf16[4,16,512]{2,1,0:T(8,128)(2,1)S(1)}, u32[]{:S(2)}, u32[]{:S(2)}) collective-permute-start(bf16[4,16,512]{2,1,0:T(8,128)(2,1)S(1)} %get-tuple-element.70.after_ref), channel_id=1, source_target_pairs={{0,16},{4,20},{8,24},{12,28},{16,0},{20,4},{24,8},{28,12},{1,17},{... | collective-permute-start | bytes 196616 | tf_op jit(solution)/shard_map/ppermute | solution.py:562
  76.4 6.2 %collective-permute-start.15 = (bf16[4,16,512]{2,1,0:T(8,128)(2,1)S(1)}, bf16[4,16,512]{2,1,0:T(8,128)(2,1)S(1)}, u32[]{:S(2)}, u32[]{:S(2)}) collective-permute-start(bf16[4,16,512]{2,1,0:T(8,128)(2,1)S(1)} %get-tuple-element.74), channel_id=1, source_target_pairs={{0,24},{4,28},{8,16},{12,20},{16,8},{20,12},{24,0},{28,4},{1,25},{... | collective-permute-start | bytes 196616 | tf_op jit(solution)/shard_map/ppermute | solution.py:562
  79.0 4.4 %collective-permute-start.16 = (bf16[4,16,512]{2,1,0:T(8,128)(2,1)S(1)}, bf16[4,16,512]{2,1,0:T(8,128)(2,1)S(1)}, u32[]{:S(2)}, u32[]{:S(2)}) collective-permute-start(bf16[4,16,512]{2,1,0:T(8,128)(2,1)S(1)} %get-tuple-element.75), channel_id=1, source_target_pairs={{0,8},{4,12},{8,0},{12,4},{16,24},{20,28},{24,16},{28,20},{1,9},{5... | collective-permute-start | bytes 196616 | tf_op jit(solution)/shard_map/ppermute | solution.py:562
  83.5 4.3 %collective-permute-start.17 = (bf16[4,16,512]{2,1,0:T(8,128)(2,1)S(1)}, bf16[4,16,512]{2,1,0:T(8,128)(2,1)S(1)}, u32[]{:S(2)}, u32[]{:S(2)}) collective-permute-start(bf16[4,16,512]{2,1,0:T(8,128)(2,1)S(1)} %add_convert_fusion), channel_id=1, source_target_pairs={{0,2},{1,3},{2,0},{3,1},{4,6},{5,7},{6,4},{7,5},{8,10},{9,11},{10,... | collective-permute-start | bytes 196616 | tf_op jit(solution)/shard_map/ppermute | solution.py:746
  87.9 1.4 %collective-permute-start.18 = (f32[4,16,512]{2,1,0:T(8,128)S(1)}, f32[4,16,512]{2,1,0:T(8,128)S(1)}, u32[]{:S(2)}, u32[]{:S(2)}) collective-permute-start(f32[4,16,512]{2,1,0:T(8,128)S(1)} %convert_add_fusion), channel_id=1, source_target_pairs={{0,1},{1,0},{2,3},{3,2},{4,5},{5,4},{6,7},{7,6},{8,9},{9,8},{10,11... | collective-permute-start | bytes 393224 | tf_op jit(solution)/shard_map/ppermute | solution.py:747

commit v6 on v5

v6 whole, which is shorter than its diff:
```python
import functools

import jax
import jax.numpy as jnp
from jax import lax
from jax.experimental import pallas as pl
from jax.experimental.pallas import tpu as pltpu
from jax.sharding import PartitionSpec as P

G = 8
GC = 4
SUB = 8
LANE = 128
MIB = 1024 * 1024
NT = (((1,), (1,)), ((), ()))


def params(mib=16):
    return pltpu.CompilerParams(vmem_limit_bytes=mib * MIB)


def low_half():
    return lax.broadcasted_iota(jnp.int32, (SUB, LANE), 0) < SUB // 2


def swap_halves(tile):
    return pltpu.roll(tile, SUB // 2, 0)


def spread(tile, half, low):
    other = swap_halves(tile)
    return jnp.where(low, tile, other) if half == 0 else jnp.where(low, other, tile)


def pack_planes(array_ref, plane, out_ref, slot):
    local_views, _, groups, pixels = array_ref.shape
    for view in range(local_views):
        for tile in range(pixels // LANE):
            first = (tile % 2) * local_views + view
            out_ref[slot, tile // 2, pl.ds(first, groups, stride=SUB), :] = array_ref[
                view, plane, :, pl.ds(tile * LANE, LANE)
            ].astype(jnp.float32)


def prep_kernel(
    gate_ref, own_hbm, cot_hbm, refx_ref, gates_ref, cot_out, own_ref, cot_ref, sems
):
    copies = [
        pltpu.make_async_copy(own_hbm, own_ref, sems.at[0]),
        pltpu.make_async_copy(cot_hbm, cot_ref, sems.at[1]),
    ]
    for copy in copies:
        copy.start()
    for copy in copies:
        copy.wait()
    local_views, channels, pixels = own_ref.shape
    for tile in range(pixels // LANE):
        for view in range(local_views):
            own = own_ref[view, :, pl.ds(tile * LANE, LANE)].astype(jnp.float32)
            for copied in range(SUB // local_views):
                first = copied * local_views + view
                refx_ref[tile, pl.ds(first, channels, stride=SUB), :] = own
    for g in range(gates_ref.shape[0]):
        gates_ref[g] = jnp.full((SUB, LANE), gate_ref[g], jnp.float32)

    def pack_one(plane, carry):
        pack_planes(cot_ref, plane, cot_out, plane)
        return carry

    lax.fori_loop(0, cot_out.shape[0], pack_one, 0)


def position(view, own_index, local_views, view_count):
    distance = (view // local_views) ^ own_index
    place = distance // 2 + (distance % 2) * (view_count // 2)
    return place * local_views + view % local_views


def assemble_kernel(src_ref, place_ref, *rest):
    *map_refs, rows_ref, maps, scratch = rest
    local_views, per_view = src_ref.shape
    tiles = scratch.shape[0]
    pairs = local_views * per_view
    view_count = maps.shape[1] // local_views
    blocks = maps.shape[2] // SUB
    own_index = place_ref[0]
    parity = place_ref[1]
    half = len(map_refs) // 2
    for side in range(2):
        first = 0
        for ref in map_refs[side * half : (side + 1) * half]:
            maps[side, first : first + ref.shape[0]] = ref[...]
            first += ref.shape[0]
    for pair in range(pairs):
        view = src_ref[pair % local_views, pair // local_views]
        slot = position(view, own_index, local_views, view_count)
        for tile in range(tiles):
            for side in range(2):
                values = maps[side, slot, :, pl.ds(tile * LANE, LANE)].astype(jnp.float32)
                held = parity if side == 0 else 1 - parity
                for block in range(blocks):
                    first = (2 * block + held) * (SUB * pairs) + pair
                    scratch[tile, pl.ds(first, SUB, stride=pairs), :] = values[
                        block * SUB : (block + 1) * SUB
                    ]
    for tile in range(tiles):
        rows_ref[:, pl.ds(tile * LANE, LANE)] = scratch[tile].astype(jnp.bfloat16)


def forward_vector(gates_ref, refx_ref, chunk, tile, plane, saved):
    warped_ref, corr_ref, sig_ref, rden_ref = saved
    pairs = sig_ref.shape[1]
    tiles = pairs // SUB
    inner = pl.ds((tile % 2) * LANE, LANE)
    lanes = pl.ds(tile * LANE, LANE)
    logits = None
    for g in range(G):
        total = None
        for j in range(0, GC, 2):
            c = g * GC + j
            span = pl.ds(c * pairs, 2 * pairs)
            both = chunk[span, inner]
            warped_ref[plane, span, lanes] = both.astype(jnp.bfloat16)
            both = both.reshape(2, tiles, SUB, LANE)
            for i in range(2):
                part = both[i] * refx_ref[tile, pl.ds((c + i) * SUB, SUB), :][None]
                total = part if total is None else total + part
        corr = total * (1.0 / GC)
        corr_ref[plane, pl.ds(g * pairs, pairs), lanes] = corr.reshape(pairs, LANE)
        part = corr * gates_ref[g][None]
        logits = part if logits is None else logits + part
    sig = jax.nn.sigmoid(logits)
    sig_ref[plane, :, lanes] = sig.reshape(pairs, LANE)
    visible = 0.5 + sig
    den = jnp.sum(visible, axis=0)
    rden = 1.0 / (den + swap_halves(den))
    rden_ref[plane, :, lanes] = rden
    costs = []
    for g in range(G):
        corr = corr_ref[plane, pl.ds(g * pairs, pairs), lanes].reshape(tiles, SUB, LANE)
        num = jnp.sum(visible * corr, axis=0)
        costs.append((num + swap_halves(num)) * rden)
    return costs


def weight_copy(w_ref, held, sems, plane, slot):
    return pltpu.make_async_copy(w_ref.at[plane], held.at[slot], sems.at[slot])


def forward_body(count, plane_of, gates_ref, rows_ref, refx_ref, w_ref, saved, cost_ref, scratch):
    held, sems, *chunks = scratch
    low = low_half()

    def matmul(index, slot):
        chunks[index][...] = lax.dot_general(
            rows_ref[...],
            held[slot, pl.ds(index * 2 * LANE, 2 * LANE), :],
            NT,
            preferred_element_type=jnp.float32,
        )

    def vector(index, at):
        costs = [
            forward_vector(
                gates_ref, refx_ref, chunks[index], 2 * index + half, plane_of(at), saved
            )
            for half in range(2)
        ]
        for g in range(G):
            cost_ref[at, index, pl.ds(g * SUB, SUB), :] = jnp.where(low, costs[0][g], costs[1][g])

    weight_copy(w_ref, held, sems, plane_of(0), 0).start()

    def one(step, carry):
        slot = lax.rem(step, 2)

        @pl.when(step + 1 < count)
        def _():
            weight_copy(w_ref, held, sems, plane_of(step + 1), 1 - slot).start()

        weight_copy(w_ref, held, sems, plane_of(step), slot).wait()
        matmul(0, slot)
        vector(1, jnp.maximum(step - 1, 0))
        matmul(1, slot)
        vector(0, step)
        return carry

    lax.fori_loop(0, count, one, 0)
    vector(1, count - 1)


def edge_plane(planes, index):
    return jnp.where(index < 2, index, planes - 4 + index)


def edge_kernel(gates_ref, rows_ref, refx_ref, w_ref, cot_ref, *rest):
    up_ref, down_ref, cost, *scratch = rest[4:]
    planes = w_ref.shape[0]
    forward_body(
        4,
        functools.partial(edge_plane, planes),
        gates_ref,
        rows_ref,
        refx_ref,
        w_ref,
        rest[:4],
        cost,
        scratch,
    )
    down_ref[0:2] = cost[0:2]
    up_ref[0:2] = cost[2:4]
    down_ref[2] = cot_ref[0]
    up_ref[2] = cot_ref[planes - 1]


def inner_kernel(gates_ref, rows_ref, refx_ref, w_ref, *rest):
    cost_ref, *scratch = rest[8:]
    forward_body(
        cost_ref.shape[0],
        lambda index: index + 2,
        gates_ref,
        rows_ref,
        refx_ref,
        w_ref,
        rest[4:8],
        cost_ref,
        scratch,
    )


def depth_conv(
    taps_ref,
    below_ref,
    down_ref,
    inner_ref,
    up_ref,
    above_ref,
    cot_ref,
    regular_ref,
    cost,
    grad_ref,
    slope,
    smooth,
):
    planes = grad_ref.shape[0]
    local_views, _, groups, pixels = regular_ref.shape
    cost[0:2] = below_ref[0:2]
    cost[2:4] = down_ref[0:2]
    cost[4:planes] = inner_ref[...]
    cost[planes : planes + 2] = up_ref[0:2]
    cost[planes + 2 : planes + 4] = above_ref[0:2]
    slope[0] = below_ref[2]
    slope[1 : planes + 1] = cot_ref[...]
    slope[planes + 1] = above_ref[2]

    def mix(source, tap):
        totals = [None] * G
        for k in range(3):
            for b in range(G):
                value = source(k, b)
                for a in range(G):
                    part = value * tap(k, a, b)
                    totals[a] = part if totals[a] is None else totals[a] + part
        return totals

    def forward_planes(index, carry):
        plane = 2 * index
        pres = mix(
            lambda k, g: cost[pl.ds(plane + k, 2), :, pl.ds(g * SUB, SUB), :],
            lambda k, o, g: taps_ref[k, o, g],
        )
        for o in range(G):
            pre = pres[o]
            rows = pl.ds(o * SUB, SUB)
            sig = jax.nn.sigmoid(pre)
            both = pl.ds(plane, 2)
            slope[both, :, rows, :] = slope[both, :, rows, :] * (sig * (1.0 + pre * (1.0 - sig)))
            smooth[both, :, rows, :] = pre * sig
        return carry

    lax.fori_loop(0, (planes + 2) // 2, forward_planes, 0)

    def backward_planes(index, carry):
        plane = 2 * index
        grads = mix(
            lambda k, o: slope[pl.ds(plane + 2 - k, 2), :, pl.ds(o * SUB, SUB), :],
            lambda k, g, o: taps_ref[k, o, g],
        )
        for g in range(G):
            grad_ref[pl.ds(plane, 2), :, pl.ds(g * SUB, SUB), :] = grads[g]
        for view in range(local_views):
            for tile in range(pixels // LANE):
                first = (tile % 2) * local_views + view
                for i in range(2):
                    regular_ref[view, plane + i, :, pl.ds(tile * LANE, LANE)] = smooth[
                        plane + i + 1, tile // 2, pl.ds(first, groups, stride=SUB), :
                    ].astype(jnp.bfloat16)
        return carry

    lax.fori_loop(0, planes // 2, backward_planes, 0)


def backward_kernel(src_ref, place_ref, taps_ref, gates_ref, refx_ref, w_ref, *rest):
    halo_refs = rest[:6]
    warped_ref, corr_ref, sig_ref, rden_ref = rest[6:10]
    regular_ref, keep_ref, send_ref = rest[10:13]
    cost, grad_ref, slope, smooth, rows_a, rows_b, acc, dref, held, sems, dense = rest[13:]
    count = w_ref.shape[0]
    pairs = sig_ref.shape[1]
    tiles = pairs // SUB
    lane_tiles = dref.shape[0]
    local_views = src_ref.shape[0]
    channels = G * GC
    low = low_half()

    def vector(plane, tile, target):
        lanes = pl.ds(tile * LANE, LANE)
        pack = tile // 2
        half = tile % 2
        rden = rden_ref[plane, :, lanes]
        sig = sig_ref[plane, :, lanes].reshape(tiles, SUB, LANE)
        num_grads = []
        mixed = None
        for g in range(G):
            rows = pl.ds(g * SUB, SUB)
            grad = grad_ref[plane, pack, rows, :]
            num_grads.append(spread(grad, half, low) * rden)
            part = grad * cost[plane + 2, pack, rows, :]
            mixed = part if mixed is None else mixed + part
        vis_grad = -(spread(mixed, half, low) * rden)[None]
        for g in range(G):
            corr = corr_ref[plane, pl.ds(g * pairs, pairs), lanes].reshape(tiles, SUB, LANE)
            vis_grad = vis_grad + num_grads[g][None] * corr
        logit_grad = vis_grad * (sig * (1.0 - sig)) * (1.0 / GC)
        visible = (0.5 + sig) * (1.0 / GC)
        for g in range(G):
            corr_grad = visible * num_grads[g][None] + logit_grad * gates_ref[g][None]
            for j in range(0, GC, 2):
                c = g * GC + j
                span = pl.ds(c * pairs, 2 * pairs)
                both = jnp.concatenate(
                    [
                        (corr_grad * refx_ref[tile, pl.ds((c + i) * SUB, SUB), :][None]).reshape(
                            pairs, LANE
                        )
                        for i in range(2)
                    ],
                    axis=0,
                )
                target[span, lanes] = both.astype(jnp.bfloat16)
                warped = (
                    warped_ref[plane, span, lanes]
                    .astype(jnp.float32)
                    .reshape(2, tiles, SUB, LANE)
                )
                for i in range(2):
                    dref[tile, pl.ds((c + i) * SUB, SUB), :] += jnp.sum(
                        corr_grad * warped[i], axis=0
                    )

    def matmul(rows, slot, index):
        product = jnp.dot(
            rows[...],
            held[slot, :, pl.ds(index * 2 * LANE, 2 * LANE)],
            preferred_element_type=jnp.float32,
        )
        for half in range(2):
            acc[2 * index + half] += product[:, half * LANE : (half + 1) * LANE]

    def fetch(plane):
        return weight_copy(w_ref, held, sems, plane, lax.rem(plane, 4))

    fetch(0).start()
    fetch(1).start()
    acc[...] = jnp.zeros_like(acc)
    dref[...] = jnp.zeros_like(dref)
    rows_b[...] = jnp.zeros_like(rows_b)
    held[3] = jnp.zeros_like(held[3])
    depth_conv(taps_ref, *halo_refs, regular_ref, cost, grad_ref, slope, smooth)

    def two_planes(turn, carry):
        first = 2 * turn
        for offset, rows, before in ((0, rows_a, rows_b), (1, rows_b, rows_a)):
            plane = first + offset
            fetch(plane).wait()

            @pl.when(plane + 2 < count)
            def _():
                fetch(plane + 2).start()

            slot = lax.rem(plane + 3, 4)
            for tile in range(lane_tiles):
                if tile % 2 == 0:
                    matmul(before, slot, tile // 2)
                vector(plane, tile, rows)
        return carry

    lax.fori_loop(0, count // 2, two_planes, 0)
    for index in range(lane_tiles // 2):
        matmul(rows_b, (count - 1) % 4, index)
    own_index = place_ref[0]
    parity = place_ref[1]
    blocks = keep_ref.shape[1] // SUB
    for target, held_side in ((dense, 1 - parity), (keep_ref, parity)):
        target[...] = jnp.zeros_like(target)
        for tile in range(lane_tiles):
            lanes = pl.ds(tile * LANE, LANE)
            for block in range(blocks):
                channel = (2 * block + held_side) * SUB
                part = pl.ds(block * SUB, SUB)
                for view in range(local_views):
                    total = None
                    for copy in range(SUB // local_views):
                        first = channel * SUB + copy * local_views + view
                        value = dref[tile, pl.ds(first, SUB, stride=SUB), :]
                        total = value if total is None else total + value
                    target[view, part, lanes] = total
        for pair in range(pairs):
            view = src_ref[pair % local_views, pair // local_views]
            slot = position(view, own_index, local_views, dense.shape[0] // local_views)
            for block in range(blocks):
                first = (2 * block + held_side) * (SUB * pairs) + pair
                part = pl.ds(block * SUB, SUB)
                for tile in range(lane_tiles):
                    target[slot, part, pl.ds(tile * LANE, LANE)] += acc[
                        tile, pl.ds(first, SUB, stride=pairs), :
                    ]
    send_ref[...] = dense[...].astype(jnp.bfloat16)


def split_kernel(first, keep_ref, received_ref, after_ref, even_ref, send_ref):
    count = even_ref.shape[0]
    half = keep_ref.shape[0] // 2
    for out_ref, start in ((even_ref, first), (send_ref, half + first)):
        span = pl.ds(start, count)
        out_ref[...] = (keep_ref[span] + received_ref[span].astype(jnp.float32)).astype(
            out_ref.dtype
        )


def spread_kernel(even_ref, received_ref, *out_refs):
    size = out_refs[0].shape[0]
    for index, out_ref in enumerate(out_refs):
        span = pl.ds(index * size, size)
        out_ref[...] = (even_ref[span] + received_ref[span].astype(jnp.float32)).astype(
            out_ref.dtype
        )


SMEM = functools.partial(pl.BlockSpec, memory_space=pltpu.SMEM)


def shards(features, sources, warp_weights, view_gate, depth_kernel, cotangent):
    view_count = lax.axis_size("view")
    plane_count = lax.axis_size("plane")
    own_index = lax.axis_index("view")
    plane_index = lax.axis_index("plane")
    local_views, channels, pixels = features.shape
    all_views, per_view = sources.shape
    pairs = local_views * per_view
    planes = warp_weights.shape[0]
    share = channels // plane_count
    blocks = plane_count // 2
    parity = plane_index % 2
    f32 = jnp.float32
    bf16 = jnp.bfloat16
    near = [(i, i ^ 1) for i in range(plane_count)]
    far = [(i, i ^ 2) for i in range(plane_count)]
    up = [(i, i + 1) for i in range(plane_count - 1)]
    down = [(i + 1, i) for i in range(plane_count - 1)]
    shape = jax.ShapeDtypeStruct

    halves = features.reshape(local_views, blocks, 2, share, pixels)
    mine = lax.dynamic_index_in_dim(halves, parity, 2, keepdims=False).reshape(
        local_views, channels // 2, pixels
    )

    def over_view(array, k):
        return lax.ppermute(array, "view", [(i, i ^ k) for i in range(view_count)])

    quarter = max(view_count // 4, 1)
    even = [mine] + [over_view(mine, k) for k in range(2, view_count, 2)]
    near_even = jnp.concatenate(even[:quarter], axis=0)
    far_even = jnp.concatenate(even[quarter:], axis=0)
    packed = (pixels // (2 * LANE), G * SUB, LANE)
    hbm = pl.BlockSpec(memory_space=pltpu.HBM)
    anywhere = pl.BlockSpec(memory_space=pl.ANY)
    weights = pltpu.with_memory_space_constraint(warp_weights, pltpu.HBM)
    refx, gates, cot = pl.pallas_call(
        prep_kernel,
        out_shape=(
            shape((pixels // LANE, channels * SUB, LANE), f32),
            shape((G, SUB, LANE), f32),
            shape((planes,) + packed, f32),
        ),
        in_specs=[SMEM(), hbm, hbm],
        scratch_shapes=[
            pltpu.VMEM(features.shape, bf16),
            pltpu.VMEM(cotangent.shape, bf16),
            pltpu.SemaphoreType.DMA((2,)),
        ],
        compiler_params=params(),
        cost_estimate=pl.CostEstimate(flops=10**9, bytes_accessed=4 * MIB, transcendentals=0),
        name="prep",
    )(
        pltpu.with_memory_space_constraint(view_gate, pltpu.HBM),
        pltpu.with_memory_space_constraint(features, pltpu.HBM),
        pltpu.with_memory_space_constraint(cotangent, pltpu.HBM),
    )
    far_even, refx, gates, cot = lax.optimization_barrier((far_even, refx, gates, cot))
    maps = [near_even, far_even, over_view(near_even, 1), over_view(far_even, 1)]
    maps = maps + [lax.ppermute(part, "plane", near) for part in maps]

    src_own = lax.dynamic_slice_in_dim(sources, own_index * local_views, local_views, 0)
    place = jnp.stack([own_index, parity]).astype(jnp.int32)
    rows = pl.pallas_call(
        assemble_kernel,
        out_shape=shape((channels * pairs, pixels), bf16),
        in_specs=[SMEM(), SMEM()] + [pl.BlockSpec()] * len(maps),
        scratch_shapes=[
            pltpu.VMEM((2, all_views, channels // 2, pixels), bf16),
            pltpu.VMEM((pixels // LANE, channels * pairs, LANE), f32),
        ],
        compiler_params=params(24),
        name="assemble",
    )(src_own, place, *maps)

    saved = (
        pltpu.VMEM((planes, channels * pairs, pixels), bf16),
        pltpu.VMEM((planes, G * pairs, pixels), f32),
        pltpu.VMEM((planes, pairs, pixels), f32),
        pltpu.VMEM((planes, SUB, pixels), f32),
    )
    on_chip = functools.partial(pltpu.with_memory_space_constraint, memory_space=pltpu.VMEM)
    vmem = pl.BlockSpec(memory_space=pltpu.VMEM)
    scratch = [
        pltpu.VMEM((2, pixels, pixels), bf16),
        pltpu.SemaphoreType.DMA((2,)),
        pltpu.VMEM((channels * pairs, 2 * LANE), f32),
        pltpu.VMEM((channels * pairs, 2 * LANE), f32),
    ]
    load = (3,) + packed
    rows, refx, gates, cot = [on_chip(item) for item in (rows, refx, gates, cot)]
    *edge_saved, up_load, down_load = pl.pallas_call(
        edge_kernel,
        out_shape=saved + (shape(load, f32),) * 2,
        in_specs=[vmem] * 3 + [hbm, vmem],
        out_specs=(vmem,) * 6,
        scratch_shapes=[pltpu.VMEM((4,) + packed, f32)] + scratch,
        compiler_params=params(8),
        name="forward_edge",
    )(gates, rows, refx, weights, cot)
    below = lax.ppermute(up_load, "plane", up)
    above = lax.ppermute(down_load, "plane", down)
    inner_count = planes - 4
    *all_saved, inner_cost = pl.pallas_call(
        inner_kernel,
        out_shape=saved + (pltpu.VMEM((inner_count,) + packed, f32),),
        in_specs=[vmem] * 3 + [hbm] + [anywhere] * 4,
        out_specs=(vmem,) * 5,
        scratch_shapes=scratch,
        input_output_aliases={4 + i: i for i in range(4)},
        compiler_params=params(8),
        cost_estimate=pl.CostEstimate(
            flops=2 * channels * pairs * pixels * pixels * inner_count,
            bytes_accessed=40 * MIB,
            transcendentals=0,
        ),
        name="forward_inner",
    )(gates, rows, refx, weights, *[on_chip(item) for item in edge_saved])

    halo = (below, down_load, inner_cost, up_load, above, cot)
    returned = (all_views, channels // 2, pixels)
    regular, keep, send = pl.pallas_call(
        backward_kernel,
        out_shape=(shape(cotangent.shape, bf16), shape(returned, f32), shape(returned, bf16)),
        in_specs=[SMEM()] * 3 + [vmem, vmem, hbm] + [vmem] * 10,
        out_specs=(vmem,) * 3,
        scratch_shapes=[
            pltpu.VMEM((planes + 4,) + packed, f32),
            pltpu.VMEM((planes,) + packed, f32),
            pltpu.VMEM((planes + 2,) + packed, f32),
            pltpu.VMEM((planes + 2,) + packed, f32),
            pltpu.VMEM((channels * pairs, pixels), bf16),
            pltpu.VMEM((channels * pairs, pixels), bf16),
            pltpu.VMEM((pixels // LANE, channels * pairs, LANE), f32),
            pltpu.VMEM((pixels // LANE, channels * SUB, LANE), f32),
            pltpu.VMEM((4, pixels, pixels), bf16),
            pltpu.SemaphoreType.DMA((4,)),
            pltpu.VMEM(returned, f32),
        ],
        compiler_params=params(14 + 5 * all_views * channels * pixels // MIB),
        name="backward",
    )(
        src_own,
        place,
        pltpu.with_memory_space_constraint(depth_kernel, pltpu.HBM),
        gates,
        refx,
        weights,
        *halo,
        *[on_chip(item) for item in all_saved],
    )

    received = lax.ppermute(send, "plane", near)
    close = quarter * local_views
    piece = (local_views, channels // 2, pixels)

    def stage(first, count, after, kind):
        even_sum, outgoing = pl.pallas_call(
            functools.partial(split_kernel, first),
            out_shape=(shape((count,) + piece[1:], f32), shape((count,) + piece[1:], bf16)),
            in_specs=[pl.BlockSpec(), pl.BlockSpec(), anywhere],
            compiler_params=params(32),
            name="split",
        )(keep, received, after)
        incoming = over_view(outgoing, 1)
        return pl.pallas_call(
            spread_kernel,
            out_shape=(shape(piece, kind),) + (shape(piece, bf16),) * (count // local_views - 1),
            compiler_params=params(32),
            name="spread",
        )(even_sum, incoming)

    away_parts = stage(close, all_views // 2 - close, received, bf16)
    total, *close_parts = stage(0, close, away_parts[0], f32)
    for index, part in enumerate(away_parts):
        total = total + over_view(part, 2 * (quarter + index)).astype(f32)
    for index, part in enumerate(close_parts):
        total = total + over_view(part, 2 * (index + 1)).astype(f32)
    rounded = total.astype(bf16)
    total = rounded.astype(f32) + lax.ppermute(rounded, "plane", far).astype(f32)
    other = lax.ppermute(total, "plane", near)
    cut = (local_views, blocks, 1, share, pixels)
    first = jnp.where(parity == 0, total, other).reshape(cut)
    second = jnp.where(parity == 0, other, total).reshape(cut)
    feature_grads = jnp.concatenate([first, second], axis=2).reshape(features.shape)
    return (regular, feature_grads)


def solution(mesh):
    in_specs = (
        P("view", None, None),
        P(),
        P("plane", None, None),
        P(),
        P(),
        P("view", "plane", None, None),
    )
    out_specs = (P("view", "plane", None, None), P("view", None, None))
    return jax.shard_map(shards, mesh=mesh, in_specs=in_specs, out_specs=out_specs, check_vma=False)
```

time: 90.5 us -> 89 us (0.983)
  Pallas kernels: 42.7 us -> 41 us
    pallas_call x1, Pallas kernels: 24.2 us -> 22.2 us  [shards(): pl.pallas_call(backward_kernel, out_shape=(shape(cotangent.shape, bf16),...]
where the time goes in v6:
time: 89 us; the launch traced here: 88.3 us
  Pallas kernels  41 us (46%)
  waiting for transfers between devices  22.4 us (25%)
  starting transfers between devices  22.1 us (25%)
  local copies, waits for them, and re-layouts  1.75 us (2%)
    pallas_call x1, Pallas kernels, shards(): pl.pallas_call(backward_kernel, out_shape=(shape(cotangent.shape, bf16),...  22.2 us
    ppermute x10, waiting for transfers between devices, over_view(): return lax.ppermute(array, 'view', [(i, i ^ k) for i in range(view_count)])  15.8 us
    ppermute x10, starting transfers between devices, over_view(): return lax.ppermute(array, 'view', [(i, i ^ k) for i in range(view_count)])  14.3 us
    pallas_call x1, Pallas kernels, shards(): pl.pallas_call(inner_kernel, out_shape=saved + (pltpu.VMEM((inner_count,)...  9.64 us
    pallas_call x1, Pallas kernels, shards(): pl.pallas_call(edge_kernel, out_shape=saved + (shape(load, f32),) * 2, in...  5.49 us
    ppermute x1, waiting for transfers between devices, shards(): lax.ppermute(rounded, 'plane', far).astype(f32)  2.63 us
    ppermute x1, starting transfers between devices, shards(): received = lax.ppermute(send, 'plane', near)  2.14 us
    ppermute x1, starting transfers between devices, shards(): below = lax.ppermute(up_load, 'plane', up)  2.06 us
  transfers between devices with their start and end apart: 19, of which 12 were waited for; matrix products, arithmetic and copies ran while one was open for 0% of the time, Pallas kernels for 13%

profile of v6, /device:TPU:0, one launch (start us, length us, event | category | flops | bytes accessed | tf_op | source)
XLA Modules:
  0.0 88.3 jit_solution(14525632297556354996)
XLA Ops:
  0.6 0.0 copy-start
  0.7 0.8 dynamic-slice_bitcast_fusion
  1.5 3.0 %collective-permute-start.2 = (bf16[4,16,512]{2,1,0:T(8,128)(2,1)S(1)}, bf16[4,16,512]{2,1,0:T(8,128)(2,1)S(1)}, u32[]{:S(2)}, u32[]{:S(2)}) collective-permute-start(bf16[4,16,512]{2,1,0:T(8,128)(2,1)S(1)} %dynamic-slice_bitcast_fusion), channel_id=1, source_target_pairs={{0,8},{4,12},{8,0},{12,4},{16,24},{20,28},{24,16},{28,20},{1,9},{5... | collective-permute-start | bytes 196616 | tf_op jit(solution)/shard_map/ppermute | solution.py:479
  4.5 2.5 %collective-permute-start.1 = (bf16[4,16,512]{2,1,0:T(8,128)(2,1)S(1)}, bf16[4,16,512]{2,1,0:T(8,128)(2,1)S(1)}, u32[]{:S(2)}, u32[]{:S(2)}) collective-permute-start(bf16[4,16,512]{2,1,0:T(8,128)(2,1)S(1)} %dynamic-slice_bitcast_fusion), channel_id=1, source_target_pairs={{0,24},{4,28},{8,16},{12,20},{16,8},{20,12},{24,0},{28,4},{1,25},{... | collective-permute-start | bytes 196616 | tf_op jit(solution)/shard_map/ppermute | solution.py:479
  7.0 0.1 collective-permute-start
  7.1 2.0 %prep.1 = (f32[4,256,128]{2,1,0:T(8,128)S(1)}, f32[8,8,128]{2,1,0:T(8,128)S(1)}, f32[12,2,64,128]{3,2,1,0:T(8,128)S(1)}) custom-call(f32[8]{0:T(128)} %gate_ref.1, bf16[4,32,512]{2,1,0:T(8,128)(2,1)} %own_hbm.1, bf16[4,12,8,512]{3,2,1,0:T(8,128)(2,1)} %cot_hbm.1), custom_call_target="tpu_custom_call" | custom-call | flops 1000000000 | bytes 4194304 | tf_op jit(solution)/shard_map/prep/pallas_call | solution.py:489
  9.1 0.0 collective-permute-done.2
  9.2 1.6 %collective-permute-start.3 = (bf16[8,16,512]{2,1,0:T(8,128)(2,1)S(1)}, bf16[8,16,512]{2,1,0:T(8,128)(2,1)S(1)}, u32[]{:S(2)}, u32[]{:S(2)}) collective-permute-start(bf16[8,16,512]{2,1,0:T(8,128)(2,1)S(1)} %pad_maximum_fusion.2.rest_0_), channel_id=1, source_target_pairs={{0,4},{4,0},{8,12},{12,8},{16,20},{20,16},{24,28},{28,24},{1,5},{5... | collective-permute-start | bytes 393224 | tf_op jit(solution)/shard_map/ppermute | solution.py:479
  10.7 0.7 collective-permute-done.1
  11.4 2.1 %collective-permute-done = bf16[4,16,512]{2,1,0:T(8,128)(2,1)S(1)} collective-permute-done((bf16[4,16,512]{2,1,0:T(8,128)(2,1)S(1)}, bf16[4,16,512]{2,1,0:T(8,128)(2,1)S(1)}, u32[]{:S(2)}, u32[]{:S(2)}) %collective-permute-start) | collective-permute-done | bytes 65568 | tf_op jit(solution)/shard_map/ppermute | solution.py:479
  13.5 1.6 %collective-permute-start.4 = (bf16[8,16,512]{2,1,0:T(8,128)(2,1)S(1)}, bf16[8,16,512]{2,1,0:T(8,128)(2,1)S(1)}, u32[]{:S(2)}, u32[]{:S(2)}) collective-permute-start(bf16[8,16,512]{2,1,0:T(8,128)(2,1)S(1)} %pad_maximum_fusion.1.rest_1_), channel_id=1, source_target_pairs={{0,4},{4,0},{8,12},{12,8},{16,20},{20,16},{24,28},{28,24},{1,5},{5... | collective-permute-start | bytes 393224 | tf_op jit(solution)/shard_map/ppermute | solution.py:479
  15.1 0.0 collective-permute-start.5
  15.1 0.5 collective-permute-start.6
  15.6 0.0 collective-permute-done.3.rest_2_
  15.6 0.0 collective-permute-start.7
  15.6 3.3 %collective-permute-done.4.rest_3_ = bf16[8,16,512]{2,1,0:T(8,128)(2,1)S(1)} collective-permute-done((bf16[8,16,512]{2,1,0:T(8,128)(2,1)S(1)}, bf16[8,16,512]{2,1,0:T(8,128)(2,1)S(1)}, u32[]{:S(2)}, u32[]{:S(2)}) %collective-permute-start.4) | collective-permute-done | bytes 131104 | tf_op jit(solution)/shard_map/ppermute | solution.py:479
  18.9 0.0 collective-permute-start.8
  18.9 0.1 constant_dynamic-slice_fusion
  19.0 0.1 copy.15.src_ref
  19.1 0.1 pad_add_fusion.place_ref
  19.2 0.0 collective-permute-done.5.rest_4_
  19.2 1.1 %collective-permute-done.8.rest_7_ = bf16[8,16,512]{2,1,0:T(8,128)(2,1)S(1)} collective-permute-done((bf16[8,16,512]{2,1,0:T(8,128)(2,1)S(1)}, bf16[8,16,512]{2,1,0:T(8,128)(2,1)S(1)}, u32[]{:S(2)}, u32[]{:S(2)}) %collective-permute-start.8) | collective-permute-done | bytes 131104 | tf_op jit(solution)/shard_map/ppermute | solution.py:512
  20.3 1.6 %assemble.1.rows_ref = bf16[1280,512]{1,0:T(8,128)(2,1)S(1)} custom-call(s32[4,10]{1,0:T(4,128)S(1)} %copy.15.src_ref, s32[2]{0:T(128)S(1)} %pad_add_fusion.place_ref, bf16[8,16,512]{2,1,0:T(8,128)(2,1)S(1)} %pad_maximum_fusion.2.rest_0_, bf16[8,16,512]{2,1,0:T(8,128)(2,1)S(1)} %pad_maximum_fusion.1.rest_1_, ...), custom_call_target="tpu_custom_call" | custom-call | tf_op jit(solution)/shard_map/assemble/pallas_call | solution.py:516
  21.8 5.5 %forward_edge.1 = (bf16[12,1280,512]{2,1,0:T(8,128)(2,1)S(1)}, f32[12,320,512]{2,1,0:T(8,128)S(1)}, f32[12,40,512]{2,1,0:T(8,128)S(1)}, f32[12,8,512]{2,1,0:T(8,...) custom-call(f32[8,8,128]{2,1,0:T(8,128)S(1)} %get-tuple-element.34.gates_ref, ...), custom_call_target="tpu_custom_call" | custom-call | tf_op jit(solution)/shard_map/forward_edge/pallas_call | solution.py:544
  27.3 2.1 %collective-permute-start.9 = (f32[3,2,64,128]{3,2,1,0:T(8,128)S(1)}, f32[3,2,64,128]{3,2,1,0:T(8,128)S(1)}, u32[]{:S(2)}, u32[]{:S(2)}) collective-permute-start(f32[3,2,64,128]{3,2,1,0:T(8,128)S(1)} %get-tuple-element.38.rest_3_), channel_id=1, source_target_pairs={{0,1},{1,2},{2,3},{4,5},{5,6},{6,7},{8,9},{9,10},{10,11},{12,13},{... | collective-permute-start | bytes 589832 | tf_op jit(solution)/shard_map/ppermute | solution.py:553
  29.4 1.3 %collective-permute-start.10 = (f32[3,2,64,128]{3,2,1,0:T(8,128)S(1)}, f32[3,2,64,128]{3,2,1,0:T(8,128)S(1)}, u32[]{:S(2)}, u32[]{:S(2)}) collective-permute-start(f32[3,2,64,128]{3,2,1,0:T(8,128)S(1)} %get-tuple-element.39.rest_1_), channel_id=1, source_target_pairs={{1,0},{2,1},{3,2},{5,4},{6,5},{7,6},{9,8},{10,9},{11,10},{13,12},{... | collective-permute-start | bytes 589832 | tf_op jit(solution)/shard_map/ppermute | solution.py:554
  30.7 9.6 %forward_inner.1 = (bf16[12,1280,512]{2,1,0:T(8,128)(2,1)S(1)}, f32[12,320,512]{2,1,0:T(8,128)S(1)}, f32[12,40,512]{2,1,0:T(8,128)S(1)}, f32[12,8,512]{2,1,0:T(8,128)S(1)}, f32[8,2,64,128]{3,2,1,0:T(8,128)S(1)}) custom-call(f32[8,8,128]{2,1,0:T(8,128)S(1)} %get-tuple-element.34.gates_ref, ...), custom_call_target="tpu_custom_call", output_to_operand_aliasing={{0}: (4, {}), {1}: (5, {}), {2}: (6, {}), {3}: (7, {})} | custom-call | flops 5368709120 | bytes 41943040 | tf_op jit(solution)/shard_map/forward_inner/pallas_call | solution.py:556
  40.4 0.0 collective-permute-done.10.rest_4_
  40.4 22.2 %backward.1 = (bf16[4,12,8,512]{3,2,1,0:T(8,128)(2,1)}, f32[32,16,512]{2,1,0:T(8,128)S(1)}, bf16[32,16,512]{2,1,0:T(8,128)(2,1)S(1)}) custom-call(s32[4,10]{1,0:T(4,128)S(1)} %copy.15.src_ref, s32[2]{0:T(128)S(1)} %pad_add_fusion.place_ref, f32[3,8,8]{2,1,0:T(8,128)} %taps_ref.1, f32[8,8,128]{2,1,0:T(8,128)S(1)} %get-tuple-element.34.gates_ref, ...), custom_call_target="tpu_custom_call" | custom-call | tf_op jit(solution)/shard_map/backward/pallas_call | solution.py:574
  62.5 2.1 %collective-permute-start.11 = (bf16[32,16,512]{2,1,0:T(8,128)(2,1)S(1)}, bf16[32,16,512]{2,1,0:T(8,128)(2,1)S(1)}, u32[]{:S(2)}, u32[]{:S(2)}) collective-permute-start(bf16[32,16,512]{2,1,0:T(8,128)(2,1)S(1)} %get-tuple-element.51), channel_id=1, source_target_pairs={{0,1},{1,0},{2,3},{3,2},{4,5},{5,4},{6,7},{7,6},{8,9},{9,8},{10,11... | collective-permute-start | bytes 1572872 | tf_op jit(solution)/shard_map/ppermute | solution.py:605
  64.7 1.5 %collective-permute-done.11.received_ref.after_ref = bf16[32,16,512]{2,1,0:T(8,128)(2,1)S(1)} collective-permute-done((bf16[32,16,512]{2,1,0:T(8,128)(2,1)S(1)}, bf16[32,16,512]{2,1,0:T(8,128)(2,1)S(1)}, u32[]{:S(2)}, u32[]{:S(2)}) %collective-permute-start.11) | collective-permute-done | bytes 524320 | tf_op jit(solution)/shard_map/ppermute | solution.py:605
  66.2 0.1 split.2
  66.3 1.6 %collective-permute-start.12 = (bf16[8,16,512]{2,1,0:T(8,128)(2,1)S(1)}, bf16[8,16,512]{2,1,0:T(8,128)(2,1)S(1)}, u32[]{:S(2)}, u32[]{:S(2)}) collective-permute-start(bf16[8,16,512]{2,1,0:T(8,128)(2,1)S(1)} %get-tuple-element.53), channel_id=1, source_target_pairs={{0,4},{4,0},{8,12},{12,8},{16,20},{20,16},{24,28},{28,24},{1,5},{5... | collective-permute-start | bytes 393224 | tf_op jit(solution)/shard_map/ppermute | solution.py:479
  67.9 4.2 %collective-permute-done.12.received_ref = bf16[8,16,512]{2,1,0:T(8,128)(2,1)S(1)} collective-permute-done((bf16[8,16,512]{2,1,0:T(8,128)(2,1)S(1)}, bf16[8,16,512]{2,1,0:T(8,128)(2,1)S(1)}, u32[]{:S(2)}, u32[]{:S(2)}) %collective-permute-start.12) | collective-permute-done | bytes 131104 | tf_op jit(solution)/shard_map/ppermute | solution.py:479
  72.2 0.1 split.3
  72.2 1.6 %collective-permute-start.13 = (bf16[8,16,512]{2,1,0:T(8,128)(2,1)S(1)}, bf16[8,16,512]{2,1,0:T(8,128)(2,1)S(1)}, u32[]{:S(2)}, u32[]{:S(2)}) collective-permute-start(bf16[8,16,512]{2,1,0:T(8,128)(2,1)S(1)} %get-tuple-element.56), channel_id=1, source_target_pairs={{0,4},{4,0},{8,12},{12,8},{16,20},{20,16},{24,28},{28,24},{1,5},{5... | collective-permute-start | bytes 393224 | tf_op jit(solution)/shard_map/ppermute | solution.py:479
  73.8 0.9 collective-permute-start.14
  74.7 1.3 %collective-permute-start.15 = (bf16[4,16,512]{2,1,0:T(8,128)(2,1)S(1)}, bf16[4,16,512]{2,1,0:T(8,128)(2,1)S(1)}, u32[]{:S(2)}, u32[]{:S(2)}) collective-permute-start(bf16[4,16,512]{2,1,0:T(8,128)(2,1)S(1)} %get-tuple-element.58), channel_id=1, source_target_pairs={{0,24},{4,28},{8,16},{12,20},{16,8},{20,12},{24,0},{28,4},{1,25},{... | collective-permute-start | bytes 196616 | tf_op jit(solution)/shard_map/ppermute | solution.py:479
  76.1 1.2 %collective-permute-done.13.received_ref = bf16[8,16,512]{2,1,0:T(8,128)(2,1)S(1)} collective-permute-done((bf16[8,16,512]{2,1,0:T(8,128)(2,1)S(1)}, bf16[8,16,512]{2,1,0:T(8,128)(2,1)S(1)}, u32[]{:S(2)}, u32[]{:S(2)}) %collective-permute-start.13) | collective-permute-done | bytes 131104 | tf_op jit(solution)/shard_map/ppermute | solution.py:479
  77.3 0.1 collective-permute-start.16
  77.4 3.5 %collective-permute-done.15 = bf16[4,16,512]{2,1,0:T(8,128)(2,1)S(1)} collective-permute-done((bf16[4,16,512]{2,1,0:T(8,128)(2,1)S(1)}, bf16[4,16,512]{2,1,0:T(8,128)(2,1)S(1)}, u32[]{:S(2)}, u32[]{:S(2)}) %collective-permute-start.15) | collective-permute-done | bytes 65568 | tf_op jit(solution)/shard_map/ppermute | solution.py:479
  80.9 0.1 collective-permute-done.14
  81.0 0.8 collective-permute-done.16
  81.8 1.7 %collective-permute-start.17 = (bf16[4,16,512]{2,1,0:T(8,128)(2,1)S(1)}, bf16[4,16,512]{2,1,0:T(8,128)(2,1)S(1)}, u32[]{:S(2)}, u32[]{:S(2)}) collective-permute-start(bf16[4,16,512]{2,1,0:T(8,128)(2,1)S(1)} %add_convert_fusion), channel_id=1, source_target_pairs={{0,2},{1,3},{2,0},{3,1},{4,6},{5,7},{6,4},{7,5},{8,10},{9,11},{10,... | collective-permute-start | bytes 196616 | tf_op jit(solution)/shard_map/ppermute | solution.py:632
  83.5 2.6 %collective-permute-done.17 = bf16[4,16,512]{2,1,0:T(8,128)(2,1)S(1)} collective-permute-done((bf16[4,16,512]{2,1,0:T(8,128)(2,1)S(1)}, bf16[4,16,512]{2,1,0:T(8,128)(2,1)S(1)}, u32[]{:S(2)}, u32[]{:S(2)}) %collective-permute-start.17) | collective-permute-done | bytes 65568 | tf_op jit(solution)/shard_map/ppermute | solution.py:632
  86.1 0.1 collective-permute-start.18
  86.2 1.3 %collective-permute-done.18 = f32[4,16,512]{2,1,0:T(8,128)S(1)} collective-permute-done((f32[4,16,512]{2,1,0:T(8,128)S(1)}, f32[4,16,512]{2,1,0:T(8,128)S(1)}, u32[]{:S(2)}, u32[]{:S(2)}) %collective-permute-start.18) | collective-permute-done | bytes 131104 | tf_op jit(solution)/shard_map/ppermute | solution.py:633
  87.6 0.7 copy.14
  (12 shorter events, 0.2 us)
Async XLA Ops:
  0.6 18.3 %copy-start = (s32[32,10]{0,1:T(8,128)S(1)}, s32[32,10]{0,1:T(8,128)}, u32[]{:S(2)}) copy-start(s32[32,10]{0,1:T(8,128)} %param.7) | copy-start | bytes 3844
  1.5 7.6 %collective-permute-start.2 = (bf16[4,16,512]{2,1,0:T(8,128)(2,1)S(1)}, bf16[4,16,512]{2,1,0:T(8,128)(2,1)S(1)}, u32[]{:S(2)}, u32[]{:S(2)}) collective-permute-start(bf16[4,16,512]{2,1,0:T(8,128)(2,1)S(1)} %dynamic-slice_bitcast_fusion), channel_id=1, source_target_pairs={{0,8},{4,12},{8,0},{12,4},{16,24},{20,28},{24,16},{28,20},{1,9},{5... | collective-permute-start | bytes 196616 | tf_op jit(solution)/shard_map/ppermute | solution.py:479
  4.5 6.9 %collective-permute-start.1 = (bf16[4,16,512]{2,1,0:T(8,128)(2,1)S(1)}, bf16[4,16,512]{2,1,0:T(8,128)(2,1)S(1)}, u32[]{:S(2)}, u32[]{:S(2)}) collective-permute-start(bf16[4,16,512]{2,1,0:T(8,128)(2,1)S(1)} %dynamic-slice_bitcast_fusion), channel_id=1, source_target_pairs={{0,24},{4,28},{8,16},{12,20},{16,8},{20,12},{24,0},{28,4},{1,25},{... | collective-permute-start | bytes 196616 | tf_op jit(solution)/shard_map/ppermute | solution.py:479
  7.0 6.4 %collective-permute-start = (bf16[4,16,512]{2,1,0:T(8,128)(2,1)S(1)}, bf16[4,16,512]{2,1,0:T(8,128)(2,1)S(1)}, u32[]{:S(2)}, u32[]{:S(2)}) collective-permute-start(bf16[4,16,512]{2,1,0:T(8,128)(2,1)S(1)} %dynamic-slice_bitcast_fusion), channel_id=1, source_target_pairs={{0,16},{4,20},{8,24},{12,28},{16,0},{20,4},{24,8},{28,12},{1,17},{... | collective-permute-start | bytes 196616 | tf_op jit(solution)/shard_map/ppermute | solution.py:479
  9.2 6.4 %collective-permute-start.3 = (bf16[8,16,512]{2,1,0:T(8,128)(2,1)S(1)}, bf16[8,16,512]{2,1,0:T(8,128)(2,1)S(1)}, u32[]{:S(2)}, u32[]{:S(2)}) collective-permute-start(bf16[8,16,512]{2,1,0:T(8,128)(2,1)S(1)} %pad_maximum_fusion.2.rest_0_), channel_id=1, source_target_pairs={{0,4},{4,0},{8,12},{12,8},{16,20},{20,16},{24,28},{28,24},{1,5},{5... | collective-permute-start | bytes 393224 | tf_op jit(solution)/shard_map/ppermute | solution.py:479
  13.5 5.4 %collective-permute-start.4 = (bf16[8,16,512]{2,1,0:T(8,128)(2,1)S(1)}, bf16[8,16,512]{2,1,0:T(8,128)(2,1)S(1)}, u32[]{:S(2)}, u32[]{:S(2)}) collective-permute-start(bf16[8,16,512]{2,1,0:T(8,128)(2,1)S(1)} %pad_maximum_fusion.1.rest_1_), channel_id=1, source_target_pairs={{0,4},{4,0},{8,12},{12,8},{16,20},{20,16},{24,28},{28,24},{1,5},{5... | collective-permute-start | bytes 393224 | tf_op jit(solution)/shard_map/ppermute | solution.py:479
  15.1 4.1 %collective-permute-start.5 = (bf16[8,16,512]{2,1,0:T(8,128)(2,1)S(1)}, bf16[8,16,512]{2,1,0:T(8,128)(2,1)S(1)}, u32[]{:S(2)}, u32[]{:S(2)}) collective-permute-start(bf16[8,16,512]{2,1,0:T(8,128)(2,1)S(1)} %pad_maximum_fusion.2.rest_0_), channel_id=1, source_target_pairs={{0,1},{1,0},{2,3},{3,2},{4,5},{5,4},{6,7},{7,6},{8,9},{9,8},{10,11... | collective-permute-start | bytes 393224 | tf_op jit(solution)/shard_map/ppermute | solution.py:512
  15.1 4.1 %collective-permute-start.6 = (bf16[8,16,512]{2,1,0:T(8,128)(2,1)S(1)}, bf16[8,16,512]{2,1,0:T(8,128)(2,1)S(1)}, u32[]{:S(2)}, u32[]{:S(2)}) collective-permute-start(bf16[8,16,512]{2,1,0:T(8,128)(2,1)S(1)} %pad_maximum_fusion.1.rest_1_), channel_id=1, source_target_pairs={{0,1},{1,0},{2,3},{3,2},{4,5},{5,4},{6,7},{7,6},{8,9},{9,8},{10,11... | collective-permute-start | bytes 393224 | tf_op jit(solution)/shard_map/ppermute | solution.py:512
  15.6 3.6 %collective-permute-start.7 = (bf16[8,16,512]{2,1,0:T(8,128)(2,1)S(1)}, bf16[8,16,512]{2,1,0:T(8,128)(2,1)S(1)}, u32[]{:S(2)}, u32[]{:S(2)}) collective-permute-start(bf16[8,16,512]{2,1,0:T(8,128)(2,1)S(1)} %collective-permute-done.3.rest_2_), channel_id=1, source_target_pairs={{0,1},{1,0},{2,3},{3,2},{4,5},{5,4},{6,7},{7,6},{8,9},{9,8},{10,11... | collective-permute-start | bytes 393224 | tf_op jit(solution)/shard_map/ppermute | solution.py:512
  18.9 1.3 %collective-permute-start.8 = (bf16[8,16,512]{2,1,0:T(8,128)(2,1)S(1)}, bf16[8,16,512]{2,1,0:T(8,128)(2,1)S(1)}, u32[]{:S(2)}, u32[]{:S(2)}) collective-permute-start(bf16[8,16,512]{2,1,0:T(8,128)(2,1)S(1)} %collective-permute-done.4.rest_3_), channel_id=1, source_target_pairs={{0,1},{1,0},{2,3},{3,2},{4,5},{5,4},{6,7},{7,6},{8,9},{9,8},{10,11... | collective-permute-start | bytes 393224 | tf_op jit(solution)/shard_map/ppermute | solution.py:512
  27.3 13.0 %collective-permute-start.9 = (f32[3,2,64,128]{3,2,1,0:T(8,128)S(1)}, f32[3,2,64,128]{3,2,1,0:T(8,128)S(1)}, u32[]{:S(2)}, u32[]{:S(2)}) collective-permute-start(f32[3,2,64,128]{3,2,1,0:T(8,128)S(1)} %get-tuple-element.38.rest_3_), channel_id=1, source_target_pairs={{0,1},{1,2},{2,3},{4,5},{5,6},{6,7},{8,9},{9,10},{10,11},{12,13},{... | collective-permute-start | bytes 589832 | tf_op jit(solution)/shard_map/ppermute | solution.py:553
  29.4 11.0 %collective-permute-start.10 = (f32[3,2,64,128]{3,2,1,0:T(8,128)S(1)}, f32[3,2,64,128]{3,2,1,0:T(8,128)S(1)}, u32[]{:S(2)}, u32[]{:S(2)}) collective-permute-start(f32[3,2,64,128]{3,2,1,0:T(8,128)S(1)} %get-tuple-element.39.rest_1_), channel_id=1, source_target_pairs={{1,0},{2,1},{3,2},{5,4},{6,5},{7,6},{9,8},{10,9},{11,10},{13,12},{... | collective-permute-start | bytes 589832 | tf_op jit(solution)/shard_map/ppermute | solution.py:554
  62.5 3.7 %collective-permute-start.11 = (bf16[32,16,512]{2,1,0:T(8,128)(2,1)S(1)}, bf16[32,16,512]{2,1,0:T(8,128)(2,1)S(1)}, u32[]{:S(2)}, u32[]{:S(2)}) collective-permute-start(bf16[32,16,512]{2,1,0:T(8,128)(2,1)S(1)} %get-tuple-element.51), channel_id=1, source_target_pairs={{0,1},{1,0},{2,3},{3,2},{4,5},{5,4},{6,7},{7,6},{8,9},{9,8},{10,11... | collective-permute-start | bytes 1572872 | tf_op jit(solution)/shard_map/ppermute | solution.py:605
  66.3 5.8 %collective-permute-start.12 = (bf16[8,16,512]{2,1,0:T(8,128)(2,1)S(1)}, bf16[8,16,512]{2,1,0:T(8,128)(2,1)S(1)}, u32[]{:S(2)}, u32[]{:S(2)}) collective-permute-start(bf16[8,16,512]{2,1,0:T(8,128)(2,1)S(1)} %get-tuple-element.53), channel_id=1, source_target_pairs={{0,4},{4,0},{8,12},{12,8},{16,20},{20,16},{24,28},{28,24},{1,5},{5... | collective-permute-start | bytes 393224 | tf_op jit(solution)/shard_map/ppermute | solution.py:479
  72.2 5.0 %collective-permute-start.13 = (bf16[8,16,512]{2,1,0:T(8,128)(2,1)S(1)}, bf16[8,16,512]{2,1,0:T(8,128)(2,1)S(1)}, u32[]{:S(2)}, u32[]{:S(2)}) collective-permute-start(bf16[8,16,512]{2,1,0:T(8,128)(2,1)S(1)} %get-tuple-element.56), channel_id=1, source_target_pairs={{0,4},{4,0},{8,12},{12,8},{16,20},{20,16},{24,28},{28,24},{1,5},{5... | collective-permute-start | bytes 393224 | tf_op jit(solution)/shard_map/ppermute | solution.py:479
  73.8 7.2 %collective-permute-start.14 = (bf16[4,16,512]{2,1,0:T(8,128)(2,1)S(1)}, bf16[4,16,512]{2,1,0:T(8,128)(2,1)S(1)}, u32[]{:S(2)}, u32[]{:S(2)}) collective-permute-start(bf16[4,16,512]{2,1,0:T(8,128)(2,1)S(1)} %get-tuple-element.54.after_ref), channel_id=1, source_target_pairs={{0,16},{4,20},{8,24},{12,28},{16,0},{20,4},{24,8},{28,12},{1,17},{... | collective-permute-start | bytes 196616 | tf_op jit(solution)/shard_map/ppermute | solution.py:479
  74.7 6.2 %collective-permute-start.15 = (bf16[4,16,512]{2,1,0:T(8,128)(2,1)S(1)}, bf16[4,16,512]{2,1,0:T(8,128)(2,1)S(1)}, u32[]{:S(2)}, u32[]{:S(2)}) collective-permute-start(bf16[4,16,512]{2,1,0:T(8,128)(2,1)S(1)} %get-tuple-element.58), channel_id=1, source_target_pairs={{0,24},{4,28},{8,16},{12,20},{16,8},{20,12},{24,0},{28,4},{1,25},{... | collective-permute-start | bytes 196616 | tf_op jit(solution)/shard_map/ppermute | solution.py:479
  77.3 4.5 %collective-permute-start.16 = (bf16[4,16,512]{2,1,0:T(8,128)(2,1)S(1)}, bf16[4,16,512]{2,1,0:T(8,128)(2,1)S(1)}, u32[]{:S(2)}, u32[]{:S(2)}) collective-permute-start(bf16[4,16,512]{2,1,0:T(8,128)(2,1)S(1)} %get-tuple-element.59), channel_id=1, source_target_pairs={{0,8},{4,12},{8,0},{12,4},{16,24},{20,28},{24,16},{28,20},{1,9},{5... | collective-permute-start | bytes 196616 | tf_op jit(solution)/shard_map/ppermute | solution.py:479
  81.8 4.3 %collective-permute-start.17 = (bf16[4,16,512]{2,1,0:T(8,128)(2,1)S(1)}, bf16[4,16,512]{2,1,0:T(8,128)(2,1)S(1)}, u32[]{:S(2)}, u32[]{:S(2)}) collective-permute-start(bf16[4,16,512]{2,1,0:T(8,128)(2,1)S(1)} %add_convert_fusion), channel_id=1, source_target_pairs={{0,2},{1,3},{2,0},{3,1},{4,6},{5,7},{6,4},{7,5},{8,10},{9,11},{10,... | collective-permute-start | bytes 196616 | tf_op jit(solution)/shard_map/ppermute | solution.py:632
  86.1 1.4 %collective-permute-start.18 = (f32[4,16,512]{2,1,0:T(8,128)S(1)}, f32[4,16,512]{2,1,0:T(8,128)S(1)}, u32[]{:S(2)}, u32[]{:S(2)}) collective-permute-start(f32[4,16,512]{2,1,0:T(8,128)S(1)} %convert_add_fusion), channel_id=1, source_target_pairs={{0,1},{1,0},{2,3},{3,2},{4,5},{5,4},{6,7},{7,6},{8,9},{9,8},{10,11... | collective-permute-start | bytes 393224 | tf_op jit(solution)/shard_map/ppermute | solution.py:633

commit v7 on v6

--- a/solution.py
+++ b/solution.py
@@ -43,8 +43,10 @@
 
 
 def prep_kernel(
-    gate_ref, own_hbm, cot_hbm, refx_ref, gates_ref, cot_out, own_ref, cot_ref, sems
+    gate_ref, own_hbm, cot_hbm, w_hbm, refx_ref, gates_ref, cot_out, w_ref, own_ref, cot_ref, sems
 ):
+    weights = pltpu.make_async_copy(w_hbm, w_ref, sems.at[2])
+    weights.start()
     copies = [
         pltpu.make_async_copy(own_hbm, own_ref, sems.at[0]),
         pltpu.make_async_copy(cot_hbm, cot_ref, sems.at[1]),
@@ -68,6 +70,7 @@
         return carry
 
     lax.fori_loop(0, cot_out.shape[0], pack_one, 0)
+    weights.wait()
 
 
 def position(view, own_index, local_views, view_count):
@@ -111,7 +114,6 @@
     warped_ref, corr_ref, sig_ref, rden_ref = saved
     pairs = sig_ref.shape[1]
     tiles = pairs // SUB
-    inner = pl.ds((tile % 2) * LANE, LANE)
     lanes = pl.ds(tile * LANE, LANE)
     logits = None
     for g in range(G):
@@ -119,7 +121,7 @@
         for j in range(0, GC, 2):
             c = g * GC + j
             span = pl.ds(c * pairs, 2 * pairs)
-            both = chunk[span, inner]
+            both = chunk[span, lanes]
             warped_ref[plane, span, lanes] = both.astype(jnp.bfloat16)
             both = both.reshape(2, tiles, SUB, LANE)
             for i in range(2):
@@ -143,50 +145,36 @@
     return costs
 
 
-def weight_copy(w_ref, held, sems, plane, slot):
-    return pltpu.make_async_copy(w_ref.at[plane], held.at[slot], sems.at[slot])
-
-
 def forward_body(count, plane_of, gates_ref, rows_ref, refx_ref, w_ref, saved, cost_ref, scratch):
-    held, sems, *chunks = scratch
     low = low_half()
 
-    def matmul(index, slot):
-        chunks[index][...] = lax.dot_general(
-            rows_ref[...],
-            held[slot, pl.ds(index * 2 * LANE, 2 * LANE), :],
-            NT,
-            preferred_element_type=jnp.float32,
+    def matmul(chunk, at):
+        chunk[...] = lax.dot_general(
+            rows_ref[...], w_ref[plane_of(at)], NT, preferred_element_type=jnp.float32
         )
 
-    def vector(index, at):
-        costs = [
-            forward_vector(
-                gates_ref, refx_ref, chunks[index], 2 * index + half, plane_of(at), saved
-            )
-            for half in range(2)
-        ]
-        for g in range(G):
-            cost_ref[at, index, pl.ds(g * SUB, SUB), :] = jnp.where(low, costs[0][g], costs[1][g])
-
-    weight_copy(w_ref, held, sems, plane_of(0), 0).start()
-
-    def one(step, carry):
-        slot = lax.rem(step, 2)
-
-        @pl.when(step + 1 < count)
-        def _():
-            weight_copy(w_ref, held, sems, plane_of(step + 1), 1 - slot).start()
-
-        weight_copy(w_ref, held, sems, plane_of(step), slot).wait()
-        matmul(0, slot)
-        vector(1, jnp.maximum(step - 1, 0))
-        matmul(1, slot)
-        vector(0, step)
+    def vector(chunk, at):
+        plane = plane_of(at)
+        for index in range(2):
+            costs = [
+                forward_vector(gates_ref, refx_ref, chunk, 2 * index + half, plane, saved)
+                for half in range(2)
+            ]
+            for g in range(G):
+                cost_ref[at, index, pl.ds(g * SUB, SUB), :] = jnp.where(
+                    low, costs[0][g], costs[1][g]
+                )
+
+    def two_planes(turn, carry):
+        first = 2 * turn
+        matmul(scratch[0], first)
+        vector(scratch[1], jnp.maximum(first - 1, 0))
+        matmul(scratch[1], first + 1)
+        vector(scratch[0], first)
         return carry
 
-    lax.fori_loop(0, count, one, 0)
-    vector(1, count - 1)
+    lax.fori_loop(0, count // 2, two_planes, 0)
+    vector(scratch[1], count - 1)
 
 
 def edge_plane(planes, index):
@@ -358,17 +346,14 @@
                         corr_grad * warped[i], axis=0
                     )
 
-    def matmul(rows, slot, index):
-        product = jnp.dot(
-            rows[...],
-            held[slot, :, pl.ds(index * 2 * LANE, 2 * LANE)],
-            preferred_element_type=jnp.float32,
-        )
-        for half in range(2):
-            acc[2 * index + half] += product[:, half * LANE : (half + 1) * LANE]
+    def matmul(rows, slot):
+        product = jnp.dot(rows[...], held[slot], preferred_element_type=jnp.float32)
+        for tile in range(lane_tiles):
+            acc[tile] += product[:, tile * LANE : (tile + 1) * LANE]
 
     def fetch(plane):
-        return weight_copy(w_ref, held, sems, plane, lax.rem(plane, 4))
+        slot = lax.rem(plane, 4)
+        return pltpu.make_async_copy(w_ref.at[plane], held.at[slot], sems.at[slot])
 
     fetch(0).start()
     fetch(1).start()
@@ -379,25 +364,21 @@
     depth_conv(taps_ref, *halo_refs, regular_ref, cost, grad_ref, slope, smooth)
 
     def two_planes(turn, carry):
-        first = 2 * turn
         for offset, rows, before in ((0, rows_a, rows_b), (1, rows_b, rows_a)):
-            plane = first + offset
+            plane = 2 * turn + offset
             fetch(plane).wait()
 
             @pl.when(plane + 2 < count)
             def _():
                 fetch(plane + 2).start()
 
-            slot = lax.rem(plane + 3, 4)
+            matmul(before, lax.rem(plane + 3, 4))
             for tile in range(lane_tiles):
-                if tile % 2 == 0:
-                    matmul(before, slot, tile // 2)
                 vector(plane, tile, rows)
         return carry
 
     lax.fori_loop(0, count // 2, two_planes, 0)
-    for index in range(lane_tiles // 2):
-        matmul(rows_b, (count - 1) % 4, index)
+    matmul(rows_b, (count - 1) % 4)
     own_index = place_ref[0]
     parity = place_ref[1]
     blocks = keep_ref.shape[1] // SUB
@@ -485,19 +466,19 @@
     packed = (pixels // (2 * LANE), G * SUB, LANE)
     hbm = pl.BlockSpec(memory_space=pltpu.HBM)
     anywhere = pl.BlockSpec(memory_space=pl.ANY)
-    weights = pltpu.with_memory_space_constraint(warp_weights, pltpu.HBM)
-    refx, gates, cot = pl.pallas_call(
+    refx, gates, cot, weights = pl.pallas_call(
         prep_kernel,
         out_shape=(
             shape((pixels // LANE, channels * SUB, LANE), f32),
             shape((G, SUB, LANE), f32),
             shape((planes,) + packed, f32),
+            pltpu.VMEM(warp_weights.shape, bf16),
         ),
-        in_specs=[SMEM(), hbm, hbm],
+        in_specs=[SMEM(), hbm, hbm, hbm],
         scratch_shapes=[
             pltpu.VMEM(features.shape, bf16),
             pltpu.VMEM(cotangent.shape, bf16),
-            pltpu.SemaphoreType.DMA((2,)),
+            pltpu.SemaphoreType.DMA((3,)),
         ],
         compiler_params=params(),
         cost_estimate=pl.CostEstimate(flops=10**9, bytes_accessed=4 * MIB, transcendentals=0),
@@ -506,6 +487,7 @@
         pltpu.with_memory_space_constraint(view_gate, pltpu.HBM),
         pltpu.with_memory_space_constraint(features, pltpu.HBM),
         pltpu.with_memory_space_constraint(cotangent, pltpu.HBM),
+        pltpu.with_memory_space_constraint(warp_weights, pltpu.HBM),
     )
     far_even, refx, gates, cot = lax.optimization_barrier((far_even, refx, gates, cot))
     maps = [near_even, far_even, over_view(near_even, 1), over_view(far_even, 1)]
@@ -533,18 +515,14 @@
     )
     on_chip = functools.partial(pltpu.with_memory_space_constraint, memory_space=pltpu.VMEM)
     vmem = pl.BlockSpec(memory_space=pltpu.VMEM)
-    scratch = [
-        pltpu.VMEM((2, pixels, pixels), bf16),
-        pltpu.SemaphoreType.DMA((2,)),
-        pltpu.VMEM((channels * pairs, 2 * LANE), f32),
-        pltpu.VMEM((channels * pairs, 2 * LANE), f32),
-    ]
+    scratch = [pltpu.VMEM((channels * pairs, pixels), f32)] * 2
     load = (3,) + packed
     rows, refx, gates, cot = [on_chip(item) for item in (rows, refx, gates, cot)]
+    weights = on_chip(weights)
     *edge_saved, up_load, down_load = pl.pallas_call(
         edge_kernel,
         out_shape=saved + (shape(load, f32),) * 2,
-        in_specs=[vmem] * 3 + [hbm, vmem],
+        in_specs=[vmem] * 5,
         out_specs=(vmem,) * 6,
         scratch_shapes=[pltpu.VMEM((4,) + packed, f32)] + scratch,
         compiler_params=params(8),
@@ -556,7 +534,7 @@
     *all_saved, inner_cost = pl.pallas_call(
         inner_kernel,
         out_shape=saved + (pltpu.VMEM((inner_count,) + packed, f32),),
-        in_specs=[vmem] * 3 + [hbm] + [anywhere] * 4,
+        in_specs=[vmem] * 4 + [anywhere] * 4,
         out_specs=(vmem,) * 5,
         scratch_shapes=scratch,
         input_output_aliases={4 + i: i for i in range(4)},
@@ -597,7 +575,7 @@
         pltpu.with_memory_space_constraint(depth_kernel, pltpu.HBM),
         gates,
         refx,
-        weights,
+        pltpu.with_memory_space_constraint(warp_weights, pltpu.HBM),
         *halo,
         *[on_chip(item) for item in all_saved],
     )

time: 89 us -> 92.8 us (1.043)
  local copies, waits for them, and re-layouts: 1.75 us -> 7.15 us
  waiting for transfers between devices: 22.4 us -> 19.5 us
  starting transfers between devices: 22.1 us -> 24.1 us
    unnamed x3 -> x9, local copies, waits for them, and re-layouts: 0.1 us -> 5.51 us
    ppermute x10, waiting for transfers between devices: 15.8 us -> 13 us  [over_view(): return lax.ppermute(array, 'view', [(i, i ^ k) for i in range(view_count)])]
    pallas_call x1, Pallas kernels: 1.99 us -> 3.78 us  [shards(): pl.pallas_call(prep_kernel, out_shape=(shape((pixels // LANE, channels *...]
    ppermute x10, starting transfers between devices: 14.3 us -> 16 us  [over_view(): return lax.ppermute(array, 'view', [(i, i ^ k) for i in range(view_count)])]
    pallas_call x1, Pallas kernels: 9.64 us -> 8.5 us  [shards(): pl.pallas_call(inner_kernel, out_shape=saved + (pltpu.VMEM((inner_count,)...]
    pallas_call x1, Pallas kernels: 5.49 us -> 4.49 us  [shards(): pl.pallas_call(edge_kernel, out_shape=saved + (shape(load, f32),) * 2, in...]
  transfers between devices with their start and end apart: 19 -> 19, of which waited for: 12 -> 9; matrix products, arithmetic and copies ran while one was open for 0% -> 0% of each run, Pallas kernels for 13% -> 13%
where the time goes in v7:
time: 92.8 us; the launch traced here: 92.4 us
  Pallas kernels  40.7 us (44%)
  starting transfers between devices  24.1 us (26%)
  waiting for transfers between devices  19.5 us (21%)
  local copies, waits for them, and re-layouts  7.15 us (8%)
    pallas_call x1, Pallas kernels, shards(): pl.pallas_call(backward_kernel, out_shape=(shape(cotangent.shape, bf16),...  22.2 us
    ppermute x10, starting transfers between devices, over_view(): return lax.ppermute(array, 'view', [(i, i ^ k) for i in range(view_count)])  16 us
    ppermute x10, waiting for transfers between devices, over_view(): return lax.ppermute(array, 'view', [(i, i ^ k) for i in range(view_count)])  13 us
    pallas_call x1, Pallas kernels, shards(): pl.pallas_call(inner_kernel, out_shape=saved + (pltpu.VMEM((inner_count,)...  8.5 us
    unnamed x9, local copies, waits for them, and re-layouts  5.51 us
    pallas_call x1, Pallas kernels, shards(): pl.pallas_call(edge_kernel, out_shape=saved + (shape(load, f32),) * 2, in...  4.49 us
    pallas_call x1, Pallas kernels, shards(): pl.pallas_call(prep_kernel, out_shape=(shape((pixels // LANE, channels *...  3.78 us
    ppermute x1, waiting for transfers between devices, shards(): lax.ppermute(rounded, 'plane', far).astype(f32)  2.51 us
  transfers between devices with their start and end apart: 19, of which 9 were waited for; matrix products, arithmetic and copies ran while one was open for 0% of the time, Pallas kernels for 13%

profile of v7, /device:TPU:0, one launch (start us, length us, event | category | flops | bytes accessed | tf_op | source)
XLA Modules:
  0.0 92.4 jit_solution(14057457091675068020)
XLA Ops:
  0.6 0.0 copy-start
  0.7 0.8 dynamic-slice_bitcast_fusion
  1.5 3.0 %collective-permute-start.2 = (bf16[4,16,512]{2,1,0:T(8,128)(2,1)S(1)}, bf16[4,16,512]{2,1,0:T(8,128)(2,1)S(1)}, u32[]{:S(2)}, u32[]{:S(2)}) collective-permute-start(bf16[4,16,512]{2,1,0:T(8,128)(2,1)S(1)} %dynamic-slice_bitcast_fusion), channel_id=1, source_target_pairs={{0,8},{4,12},{8,0},{12,4},{16,24},{20,28},{24,16},{28,20},{1,9},{5... | collective-permute-start | bytes 196616 | tf_op jit(solution)/shard_map/ppermute | solution.py:460
  4.5 2.5 %collective-permute-start.1 = (bf16[4,16,512]{2,1,0:T(8,128)(2,1)S(1)}, bf16[4,16,512]{2,1,0:T(8,128)(2,1)S(1)}, u32[]{:S(2)}, u32[]{:S(2)}) collective-permute-start(bf16[4,16,512]{2,1,0:T(8,128)(2,1)S(1)} %dynamic-slice_bitcast_fusion), channel_id=1, source_target_pairs={{0,24},{4,28},{8,16},{12,20},{16,8},{20,12},{24,0},{28,4},{1,25},{... | collective-permute-start | bytes 196616 | tf_op jit(solution)/shard_map/ppermute | solution.py:460
  7.0 0.1 collective-permute-start
  7.1 3.8 %prep.1 = (f32[4,256,128]{2,1,0:T(8,128)S(1)}, f32[8,8,128]{2,1,0:T(8,128)S(1)}, f32[12,2,64,128]{3,2,1,0:T(8,128)S(1)}, bf16[12,512,512]{2,1,0:T(8,128)(2,1)S(1)}) custom-call(f32[8]{0:T(128)} %gate_ref.1, bf16[4,32,512]{2,1,0:T(8,128)(2,1)} %own_hbm.1, bf16[4,12,8,512]{3,2,1,0:T(8,128)(2,1)} %cot_hbm.1, bf16[12,512,512]{2,1,0:T(8,128)(2,1)} %w_ref.1), custom_call_target="tpu_custom_call" | custom-call | flops 1000000000 | bytes 4194304 | tf_op jit(solution)/shard_map/prep/pallas_call | solution.py:469
  10.9 2.6 %copy-done.1 = bf16[12,512,512]{2,1,0:T(8,128)(2,1)} copy-done((bf16[12,512,512]{2,1,0:T(8,128)(2,1)}, bf16[12,512,512]{2,1,0:T(8,128)(2,1)S(1)}, u32[]{:S(2)}) %copy-start.1) | copy-done | bytes 6291480
  13.5 0.0 collective-permute-done.2
  13.6 1.6 %collective-permute-start.3 = (bf16[8,16,512]{2,1,0:T(8,128)(2,1)S(1)}, bf16[8,16,512]{2,1,0:T(8,128)(2,1)S(1)}, u32[]{:S(2)}, u32[]{:S(2)}) collective-permute-start(bf16[8,16,512]{2,1,0:T(8,128)(2,1)S(1)} %pad_maximum_fusion.2.rest_0_), channel_id=1, source_target_pairs={{0,4},{4,0},{8,12},{12,8},{16,20},{20,16},{24,28},{28,24},{1,5},{5... | collective-permute-start | bytes 393224 | tf_op jit(solution)/shard_map/ppermute | solution.py:460
  15.2 0.0 collective-permute-done.1
  15.2 0.6 collective-permute-start.4
  15.8 0.0 collective-permute-start.5
  15.8 0.5 collective-permute-start.6
  16.3 3.5 %collective-permute-done.3.rest_2_ = bf16[8,16,512]{2,1,0:T(8,128)(2,1)S(1)} collective-permute-done((bf16[8,16,512]{2,1,0:T(8,128)(2,1)S(1)}, bf16[8,16,512]{2,1,0:T(8,128)(2,1)S(1)}, u32[]{:S(2)}, u32[]{:S(2)}) %collective-permute-start.3) | collective-permute-done | bytes 131104 | tf_op jit(solution)/shard_map/ppermute | solution.py:460
  19.7 0.0 collective-permute-start.7
  19.7 1.4 %collective-permute-done.4.rest_3_ = bf16[8,16,512]{2,1,0:T(8,128)(2,1)S(1)} collective-permute-done((bf16[8,16,512]{2,1,0:T(8,128)(2,1)S(1)}, bf16[8,16,512]{2,1,0:T(8,128)(2,1)S(1)}, u32[]{:S(2)}, u32[]{:S(2)}) %collective-permute-start.4) | collective-permute-done | bytes 131104 | tf_op jit(solution)/shard_map/ppermute | solution.py:460
  21.1 0.1 constant_dynamic-slice_fusion
  21.2 0.1 copy.15.src_ref
  21.3 0.1 pad_add_fusion.place_ref
  21.4 0.0 collective-permute-done.6.rest_5_
  21.4 0.0 collective-permute-done.7.rest_6_
  21.4 1.1 %collective-permute-done.8.rest_7_ = bf16[8,16,512]{2,1,0:T(8,128)(2,1)S(1)} collective-permute-done((bf16[8,16,512]{2,1,0:T(8,128)(2,1)S(1)}, bf16[8,16,512]{2,1,0:T(8,128)(2,1)S(1)}, u32[]{:S(2)}, u32[]{:S(2)}) %collective-permute-start.8) | collective-permute-done | bytes 131104 | tf_op jit(solution)/shard_map/ppermute | solution.py:494
  22.5 1.6 %assemble.1.rows_ref = bf16[1280,512]{1,0:T(8,128)(2,1)S(1)} custom-call(s32[4,10]{1,0:T(4,128)S(1)} %copy.15.src_ref, s32[2]{0:T(128)S(1)} %pad_add_fusion.place_ref, bf16[8,16,512]{2,1,0:T(8,128)(2,1)S(1)} %pad_maximum_fusion.2.rest_0_, bf16[8,16,512]{2,1,0:T(8,128)(2,1)S(1)} %pad_maximum_fusion.1.rest_1_, ...), custom_call_target="tpu_custom_call" | custom-call | tf_op jit(solution)/shard_map/assemble/pallas_call | solution.py:498
  24.1 2.8 %copy-done.2 = bf16[12,512,512]{2,1,0:T(8,128)(2,1)S(1)} copy-done((bf16[12,512,512]{2,1,0:T(8,128)(2,1)S(1)}, bf16[12,512,512]{2,1,0:T(8,128)(2,1)}, u32[]{:S(2)}) %copy-start.2) | copy-done | bytes 6291480
  26.8 4.5 %forward_edge.1 = (bf16[12,1280,512]{2,1,0:T(8,128)(2,1)S(1)}, f32[12,320,512]{2,1,0:T(8,128)S(1)}, f32[12,40,512]{2,1,0:T(8,128)S(1)}, f32[12,8,512]{2,1,0:T(8,...) custom-call(f32[8,8,128]{2,1,0:T(8,128)S(1)} %get-tuple-element.35.gates_ref, ...), custom_call_target="tpu_custom_call" | custom-call | tf_op jit(solution)/shard_map/forward_edge/pallas_call | solution.py:522
  31.3 2.1 %collective-permute-start.9 = (f32[3,2,64,128]{3,2,1,0:T(8,128)S(1)}, f32[3,2,64,128]{3,2,1,0:T(8,128)S(1)}, u32[]{:S(2)}, u32[]{:S(2)}) collective-permute-start(f32[3,2,64,128]{3,2,1,0:T(8,128)S(1)} %get-tuple-element.40.rest_3_), channel_id=1, source_target_pairs={{0,1},{1,2},{2,3},{4,5},{5,6},{6,7},{8,9},{9,10},{10,11},{12,13},{... | collective-permute-start | bytes 589832 | tf_op jit(solution)/shard_map/ppermute | solution.py:531
  33.4 1.5 %collective-permute-start.10 = (f32[3,2,64,128]{3,2,1,0:T(8,128)S(1)}, f32[3,2,64,128]{3,2,1,0:T(8,128)S(1)}, u32[]{:S(2)}, u32[]{:S(2)}) collective-permute-start(f32[3,2,64,128]{3,2,1,0:T(8,128)S(1)} %get-tuple-element.41.rest_1_), channel_id=1, source_target_pairs={{1,0},{2,1},{3,2},{5,4},{6,5},{7,6},{9,8},{10,9},{11,10},{13,12},{... | collective-permute-start | bytes 589832 | tf_op jit(solution)/shard_map/ppermute | solution.py:532
  34.9 8.5 %forward_inner.1 = (bf16[12,1280,512]{2,1,0:T(8,128)(2,1)S(1)}, f32[12,320,512]{2,1,0:T(8,128)S(1)}, f32[12,40,512]{2,1,0:T(8,128)S(1)}, f32[12,8,512]{2,1,0:T(8,128)S(1)}, f32[8,2,64,128]{3,2,1,0:T(8,128)S(1)}) custom-call(f32[8,8,128]{2,1,0:T(8,128)S(1)} %get-tuple-element.35.gates_ref, ...), custom_call_target="tpu_custom_call", output_to_operand_aliasing={{0}: (4, {}), {1}: (5, {}), {2}: (6, {}), {3}: (7, {})} | custom-call | flops 5368709120 | bytes 41943040 | tf_op jit(solution)/shard_map/forward_inner/pallas_call | solution.py:534
  43.4 0.0 collective-permute-done.10.rest_4_
  43.4 22.2 %backward.1 = (bf16[4,12,8,512]{3,2,1,0:T(8,128)(2,1)}, f32[32,16,512]{2,1,0:T(8,128)S(1)}, bf16[32,16,512]{2,1,0:T(8,128)(2,1)S(1)}) custom-call(s32[4,10]{1,0:T(4,128)S(1)} %copy.15.src_ref, s32[2]{0:T(128)S(1)} %pad_add_fusion.place_ref, f32[3,8,8]{2,1,0:T(8,128)} %taps_ref.1, f32[8,8,128]{2,1,0:T(8,128)S(1)} %get-tuple-element.35.gates_ref, ...), custom_call_target="tpu_custom_call" | custom-call | tf_op jit(solution)/shard_map/backward/pallas_call | solution.py:552
  65.6 2.1 %collective-permute-start.11 = (bf16[32,16,512]{2,1,0:T(8,128)(2,1)S(1)}, bf16[32,16,512]{2,1,0:T(8,128)(2,1)S(1)}, u32[]{:S(2)}, u32[]{:S(2)}) collective-permute-start(bf16[32,16,512]{2,1,0:T(8,128)(2,1)S(1)} %get-tuple-element.53), channel_id=1, source_target_pairs={{0,1},{1,0},{2,3},{3,2},{4,5},{5,4},{6,7},{7,6},{8,9},{9,8},{10,11... | collective-permute-start | bytes 1572872 | tf_op jit(solution)/shard_map/ppermute | solution.py:583
  67.8 1.5 %collective-permute-done.11.received_ref.after_ref = bf16[32,16,512]{2,1,0:T(8,128)(2,1)S(1)} collective-permute-done((bf16[32,16,512]{2,1,0:T(8,128)(2,1)S(1)}, bf16[32,16,512]{2,1,0:T(8,128)(2,1)S(1)}, u32[]{:S(2)}, u32[]{:S(2)}) %collective-permute-start.11) | collective-permute-done | bytes 524320 | tf_op jit(solution)/shard_map/ppermute | solution.py:583
  69.3 0.1 split.2
  69.4 1.6 %collective-permute-start.12 = (bf16[8,16,512]{2,1,0:T(8,128)(2,1)S(1)}, bf16[8,16,512]{2,1,0:T(8,128)(2,1)S(1)}, u32[]{:S(2)}, u32[]{:S(2)}) collective-permute-start(bf16[8,16,512]{2,1,0:T(8,128)(2,1)S(1)} %get-tuple-element.55), channel_id=1, source_target_pairs={{0,4},{4,0},{8,12},{12,8},{16,20},{20,16},{24,28},{28,24},{1,5},{5... | collective-permute-start | bytes 393224 | tf_op jit(solution)/shard_map/ppermute | solution.py:460
  71.0 4.2 %collective-permute-done.12.received_ref = bf16[8,16,512]{2,1,0:T(8,128)(2,1)S(1)} collective-permute-done((bf16[8,16,512]{2,1,0:T(8,128)(2,1)S(1)}, bf16[8,16,512]{2,1,0:T(8,128)(2,1)S(1)}, u32[]{:S(2)}, u32[]{:S(2)}) %collective-permute-start.12) | collective-permute-done | bytes 131104 | tf_op jit(solution)/shard_map/ppermute | solution.py:460
  75.3 0.1 split.3
  75.3 1.6 %collective-permute-start.13 = (bf16[8,16,512]{2,1,0:T(8,128)(2,1)S(1)}, bf16[8,16,512]{2,1,0:T(8,128)(2,1)S(1)}, u32[]{:S(2)}, u32[]{:S(2)}) collective-permute-start(bf16[8,16,512]{2,1,0:T(8,128)(2,1)S(1)} %get-tuple-element.58), channel_id=1, source_target_pairs={{0,4},{4,0},{8,12},{12,8},{16,20},{20,16},{24,28},{28,24},{1,5},{5... | collective-permute-start | bytes 393224 | tf_op jit(solution)/shard_map/ppermute | solution.py:460
  76.9 2.5 %collective-permute-start.14 = (bf16[4,16,512]{2,1,0:T(8,128)(2,1)S(1)}, bf16[4,16,512]{2,1,0:T(8,128)(2,1)S(1)}, u32[]{:S(2)}, u32[]{:S(2)}) collective-permute-start(bf16[4,16,512]{2,1,0:T(8,128)(2,1)S(1)} %get-tuple-element.56.after_ref), channel_id=1, source_target_pairs={{0,16},{4,20},{8,24},{12,28},{16,0},{20,4},{24,8},{28,12},{1,17},{... | collective-permute-start | bytes 196616 | tf_op jit(solution)/shard_map/ppermute | solution.py:460
  79.4 1.3 %collective-permute-start.15 = (bf16[4,16,512]{2,1,0:T(8,128)(2,1)S(1)}, bf16[4,16,512]{2,1,0:T(8,128)(2,1)S(1)}, u32[]{:S(2)}, u32[]{:S(2)}) collective-permute-start(bf16[4,16,512]{2,1,0:T(8,128)(2,1)S(1)} %get-tuple-element.60), channel_id=1, source_target_pairs={{0,24},{4,28},{8,16},{12,20},{16,8},{20,12},{24,0},{28,4},{1,25},{... | collective-permute-start | bytes 196616 | tf_op jit(solution)/shard_map/ppermute | solution.py:460
  80.8 1.1 %collective-permute-start.16 = (bf16[4,16,512]{2,1,0:T(8,128)(2,1)S(1)}, bf16[4,16,512]{2,1,0:T(8,128)(2,1)S(1)}, u32[]{:S(2)}, u32[]{:S(2)}) collective-permute-start(bf16[4,16,512]{2,1,0:T(8,128)(2,1)S(1)} %get-tuple-element.61), channel_id=1, source_target_pairs={{0,8},{4,12},{8,0},{12,4},{16,24},{20,28},{24,16},{28,20},{1,9},{5... | collective-permute-start | bytes 196616 | tf_op jit(solution)/shard_map/ppermute | solution.py:460
  82.0 3.6 %collective-permute-done.15 = bf16[4,16,512]{2,1,0:T(8,128)(2,1)S(1)} collective-permute-done((bf16[4,16,512]{2,1,0:T(8,128)(2,1)S(1)}, bf16[4,16,512]{2,1,0:T(8,128)(2,1)S(1)}, u32[]{:S(2)}, u32[]{:S(2)}) %collective-permute-start.15) | collective-permute-done | bytes 65568 | tf_op jit(solution)/shard_map/ppermute | solution.py:460
  85.6 0.0 collective-permute-done.14
  85.6 0.2 collective-permute-done.16
  85.9 1.8 %collective-permute-start.17 = (bf16[4,16,512]{2,1,0:T(8,128)(2,1)S(1)}, bf16[4,16,512]{2,1,0:T(8,128)(2,1)S(1)}, u32[]{:S(2)}, u32[]{:S(2)}) collective-permute-start(bf16[4,16,512]{2,1,0:T(8,128)(2,1)S(1)} %add_convert_fusion), channel_id=1, source_target_pairs={{0,2},{1,3},{2,0},{3,1},{4,6},{5,7},{6,4},{7,5},{8,10},{9,11},{10,... | collective-permute-start | bytes 196616 | tf_op jit(solution)/shard_map/ppermute | solution.py:610
  87.7 2.5 %collective-permute-done.17 = bf16[4,16,512]{2,1,0:T(8,128)(2,1)S(1)} collective-permute-done((bf16[4,16,512]{2,1,0:T(8,128)(2,1)S(1)}, bf16[4,16,512]{2,1,0:T(8,128)(2,1)S(1)}, u32[]{:S(2)}, u32[]{:S(2)}) %collective-permute-start.17) | collective-permute-done | bytes 65568 | tf_op jit(solution)/shard_map/ppermute | solution.py:610
  90.2 0.1 collective-permute-start.18
  90.3 1.3 %collective-permute-done.18 = f32[4,16,512]{2,1,0:T(8,128)S(1)} collective-permute-done((f32[4,16,512]{2,1,0:T(8,128)S(1)}, f32[4,16,512]{2,1,0:T(8,128)S(1)}, u32[]{:S(2)}, u32[]{:S(2)}) %collective-permute-start.18) | collective-permute-done | bytes 131104 | tf_op jit(solution)/shard_map/ppermute | solution.py:611
  91.7 0.7 copy.14
  (18 shorter events, 0.2 us)
Async XLA Ops:
  0.6 20.5 %copy-start = (s32[32,10]{0,1:T(8,128)S(1)}, s32[32,10]{0,1:T(8,128)}, u32[]{:S(2)}) copy-start(s32[32,10]{0,1:T(8,128)} %param.7) | copy-start | bytes 3844
  1.5 12.0 %collective-permute-start.2 = (bf16[4,16,512]{2,1,0:T(8,128)(2,1)S(1)}, bf16[4,16,512]{2,1,0:T(8,128)(2,1)S(1)}, u32[]{:S(2)}, u32[]{:S(2)}) collective-permute-start(bf16[4,16,512]{2,1,0:T(8,128)(2,1)S(1)} %dynamic-slice_bitcast_fusion), channel_id=1, source_target_pairs={{0,8},{4,12},{8,0},{12,4},{16,24},{20,28},{24,16},{28,20},{1,9},{5... | collective-permute-start | bytes 196616 | tf_op jit(solution)/shard_map/ppermute | solution.py:460
  4.5 10.6 %collective-permute-start.1 = (bf16[4,16,512]{2,1,0:T(8,128)(2,1)S(1)}, bf16[4,16,512]{2,1,0:T(8,128)(2,1)S(1)}, u32[]{:S(2)}, u32[]{:S(2)}) collective-permute-start(bf16[4,16,512]{2,1,0:T(8,128)(2,1)S(1)} %dynamic-slice_bitcast_fusion), channel_id=1, source_target_pairs={{0,24},{4,28},{8,16},{12,20},{16,8},{20,12},{24,0},{28,4},{1,25},{... | collective-permute-start | bytes 196616 | tf_op jit(solution)/shard_map/ppermute | solution.py:460
  7.0 8.1 %collective-permute-start = (bf16[4,16,512]{2,1,0:T(8,128)(2,1)S(1)}, bf16[4,16,512]{2,1,0:T(8,128)(2,1)S(1)}, u32[]{:S(2)}, u32[]{:S(2)}) collective-permute-start(bf16[4,16,512]{2,1,0:T(8,128)(2,1)S(1)} %dynamic-slice_bitcast_fusion), channel_id=1, source_target_pairs={{0,16},{4,20},{8,24},{12,28},{16,0},{20,4},{24,8},{28,12},{1,17},{... | collective-permute-start | bytes 196616 | tf_op jit(solution)/shard_map/ppermute | solution.py:460
  10.9 2.6 %copy-start.1 = (bf16[12,512,512]{2,1,0:T(8,128)(2,1)}, bf16[12,512,512]{2,1,0:T(8,128)(2,1)S(1)}, u32[]{:S(2)}) copy-start(bf16[12,512,512]{2,1,0:T(8,128)(2,1)S(1)} %get-tuple-element.38.w_ref) | copy-start | bytes 18874372
  13.6 6.1 %collective-permute-start.3 = (bf16[8,16,512]{2,1,0:T(8,128)(2,1)S(1)}, bf16[8,16,512]{2,1,0:T(8,128)(2,1)S(1)}, u32[]{:S(2)}, u32[]{:S(2)}) collective-permute-start(bf16[8,16,512]{2,1,0:T(8,128)(2,1)S(1)} %pad_maximum_fusion.2.rest_0_), channel_id=1, source_target_pairs={{0,4},{4,0},{8,12},{12,8},{16,20},{20,16},{24,28},{28,24},{1,5},{5... | collective-permute-start | bytes 393224 | tf_op jit(solution)/shard_map/ppermute | solution.py:460
  15.2 5.9 %collective-permute-start.4 = (bf16[8,16,512]{2,1,0:T(8,128)(2,1)S(1)}, bf16[8,16,512]{2,1,0:T(8,128)(2,1)S(1)}, u32[]{:S(2)}, u32[]{:S(2)}) collective-permute-start(bf16[8,16,512]{2,1,0:T(8,128)(2,1)S(1)} %pad_maximum_fusion.1.rest_1_), channel_id=1, source_target_pairs={{0,4},{4,0},{8,12},{12,8},{16,20},{20,16},{24,28},{28,24},{1,5},{5... | collective-permute-start | bytes 393224 | tf_op jit(solution)/shard_map/ppermute | solution.py:460
  15.8 5.6 %collective-permute-start.5 = (bf16[8,16,512]{2,1,0:T(8,128)(2,1)S(1)}, bf16[8,16,512]{2,1,0:T(8,128)(2,1)S(1)}, u32[]{:S(2)}, u32[]{:S(2)}) collective-permute-start(bf16[8,16,512]{2,1,0:T(8,128)(2,1)S(1)} %pad_maximum_fusion.2.rest_0_), channel_id=1, source_target_pairs={{0,1},{1,0},{2,3},{3,2},{4,5},{5,4},{6,7},{7,6},{8,9},{9,8},{10,11... | collective-permute-start | bytes 393224 | tf_op jit(solution)/shard_map/ppermute | solution.py:494
  15.8 5.6 %collective-permute-start.6 = (bf16[8,16,512]{2,1,0:T(8,128)(2,1)S(1)}, bf16[8,16,512]{2,1,0:T(8,128)(2,1)S(1)}, u32[]{:S(2)}, u32[]{:S(2)}) collective-permute-start(bf16[8,16,512]{2,1,0:T(8,128)(2,1)S(1)} %pad_maximum_fusion.1.rest_1_), channel_id=1, source_target_pairs={{0,1},{1,0},{2,3},{3,2},{4,5},{5,4},{6,7},{7,6},{8,9},{9,8},{10,11... | collective-permute-start | bytes 393224 | tf_op jit(solution)/shard_map/ppermute | solution.py:494
  19.7 1.7 %collective-permute-start.7 = (bf16[8,16,512]{2,1,0:T(8,128)(2,1)S(1)}, bf16[8,16,512]{2,1,0:T(8,128)(2,1)S(1)}, u32[]{:S(2)}, u32[]{:S(2)}) collective-permute-start(bf16[8,16,512]{2,1,0:T(8,128)(2,1)S(1)} %collective-permute-done.3.rest_2_), channel_id=1, source_target_pairs={{0,1},{1,0},{2,3},{3,2},{4,5},{5,4},{6,7},{7,6},{8,9},{9,8},{10,11... | collective-permute-start | bytes 393224 | tf_op jit(solution)/shard_map/ppermute | solution.py:494
  21.1 1.3 %collective-permute-start.8 = (bf16[8,16,512]{2,1,0:T(8,128)(2,1)S(1)}, bf16[8,16,512]{2,1,0:T(8,128)(2,1)S(1)}, u32[]{:S(2)}, u32[]{:S(2)}) collective-permute-start(bf16[8,16,512]{2,1,0:T(8,128)(2,1)S(1)} %collective-permute-done.4.rest_3_), channel_id=1, source_target_pairs={{0,1},{1,0},{2,3},{3,2},{4,5},{5,4},{6,7},{7,6},{8,9},{9,8},{10,11... | collective-permute-start | bytes 393224 | tf_op jit(solution)/shard_map/ppermute | solution.py:494
  24.0 2.8 %copy-start.2 = (bf16[12,512,512]{2,1,0:T(8,128)(2,1)S(1)}, bf16[12,512,512]{2,1,0:T(8,128)(2,1)}, u32[]{:S(2)}) copy-start(bf16[12,512,512]{2,1,0:T(8,128)(2,1)} %copy-done.1) | copy-start | bytes 18874372
  26.8 8.1 %copy-start.3 = (bf16[12,512,512]{2,1,0:T(8,128)(2,1)S(1)}, bf16[12,512,512]{2,1,0:T(8,128)(2,1)}, u32[]{:S(2)}) copy-start(bf16[12,512,512]{2,1,0:T(8,128)(2,1)} %copy-done.1) | copy-start | bytes 18874372
  31.3 12.1 %collective-permute-start.9 = (f32[3,2,64,128]{3,2,1,0:T(8,128)S(1)}, f32[3,2,64,128]{3,2,1,0:T(8,128)S(1)}, u32[]{:S(2)}, u32[]{:S(2)}) collective-permute-start(f32[3,2,64,128]{3,2,1,0:T(8,128)S(1)} %get-tuple-element.40.rest_3_), channel_id=1, source_target_pairs={{0,1},{1,2},{2,3},{4,5},{5,6},{6,7},{8,9},{9,10},{10,11},{12,13},{... | collective-permute-start | bytes 589832 | tf_op jit(solution)/shard_map/ppermute | solution.py:531
  33.4 10.0 %collective-permute-start.10 = (f32[3,2,64,128]{3,2,1,0:T(8,128)S(1)}, f32[3,2,64,128]{3,2,1,0:T(8,128)S(1)}, u32[]{:S(2)}, u32[]{:S(2)}) collective-permute-start(f32[3,2,64,128]{3,2,1,0:T(8,128)S(1)} %get-tuple-element.41.rest_1_), channel_id=1, source_target_pairs={{1,0},{2,1},{3,2},{5,4},{6,5},{7,6},{9,8},{10,9},{11,10},{13,12},{... | collective-permute-start | bytes 589832 | tf_op jit(solution)/shard_map/ppermute | solution.py:532
  65.6 3.7 %collective-permute-start.11 = (bf16[32,16,512]{2,1,0:T(8,128)(2,1)S(1)}, bf16[32,16,512]{2,1,0:T(8,128)(2,1)S(1)}, u32[]{:S(2)}, u32[]{:S(2)}) collective-permute-start(bf16[32,16,512]{2,1,0:T(8,128)(2,1)S(1)} %get-tuple-element.53), channel_id=1, source_target_pairs={{0,1},{1,0},{2,3},{3,2},{4,5},{5,4},{6,7},{7,6},{8,9},{9,8},{10,11... | collective-permute-start | bytes 1572872 | tf_op jit(solution)/shard_map/ppermute | solution.py:583
  69.4 5.8 %collective-permute-start.12 = (bf16[8,16,512]{2,1,0:T(8,128)(2,1)S(1)}, bf16[8,16,512]{2,1,0:T(8,128)(2,1)S(1)}, u32[]{:S(2)}, u32[]{:S(2)}) collective-permute-start(bf16[8,16,512]{2,1,0:T(8,128)(2,1)S(1)} %get-tuple-element.55), channel_id=1, source_target_pairs={{0,4},{4,0},{8,12},{12,8},{16,20},{20,16},{24,28},{28,24},{1,5},{5... | collective-permute-start | bytes 393224 | tf_op jit(solution)/shard_map/ppermute | solution.py:460
  75.3 5.5 %collective-permute-start.13 = (bf16[8,16,512]{2,1,0:T(8,128)(2,1)S(1)}, bf16[8,16,512]{2,1,0:T(8,128)(2,1)S(1)}, u32[]{:S(2)}, u32[]{:S(2)}) collective-permute-start(bf16[8,16,512]{2,1,0:T(8,128)(2,1)S(1)} %get-tuple-element.58), channel_id=1, source_target_pairs={{0,4},{4,0},{8,12},{12,8},{16,20},{20,16},{24,28},{28,24},{1,5},{5... | collective-permute-start | bytes 393224 | tf_op jit(solution)/shard_map/ppermute | solution.py:460
  76.9 8.7 %collective-permute-start.14 = (bf16[4,16,512]{2,1,0:T(8,128)(2,1)S(1)}, bf16[4,16,512]{2,1,0:T(8,128)(2,1)S(1)}, u32[]{:S(2)}, u32[]{:S(2)}) collective-permute-start(bf16[4,16,512]{2,1,0:T(8,128)(2,1)S(1)} %get-tuple-element.56.after_ref), channel_id=1, source_target_pairs={{0,16},{4,20},{8,24},{12,28},{16,0},{20,4},{24,8},{28,12},{1,17},{... | collective-permute-start | bytes 196616 | tf_op jit(solution)/shard_map/ppermute | solution.py:460
  79.4 6.2 %collective-permute-start.15 = (bf16[4,16,512]{2,1,0:T(8,128)(2,1)S(1)}, bf16[4,16,512]{2,1,0:T(8,128)(2,1)S(1)}, u32[]{:S(2)}, u32[]{:S(2)}) collective-permute-start(bf16[4,16,512]{2,1,0:T(8,128)(2,1)S(1)} %get-tuple-element.60), channel_id=1, source_target_pairs={{0,24},{4,28},{8,16},{12,20},{16,8},{20,12},{24,0},{28,4},{1,25},{... | collective-permute-start | bytes 196616 | tf_op jit(solution)/shard_map/ppermute | solution.py:460
  80.8 5.0 %collective-permute-start.16 = (bf16[4,16,512]{2,1,0:T(8,128)(2,1)S(1)}, bf16[4,16,512]{2,1,0:T(8,128)(2,1)S(1)}, u32[]{:S(2)}, u32[]{:S(2)}) collective-permute-start(bf16[4,16,512]{2,1,0:T(8,128)(2,1)S(1)} %get-tuple-element.61), channel_id=1, source_target_pairs={{0,8},{4,12},{8,0},{12,4},{16,24},{20,28},{24,16},{28,20},{1,9},{5... | collective-permute-start | bytes 196616 | tf_op jit(solution)/shard_map/ppermute | solution.py:460
  85.9 4.3 %collective-permute-start.17 = (bf16[4,16,512]{2,1,0:T(8,128)(2,1)S(1)}, bf16[4,16,512]{2,1,0:T(8,128)(2,1)S(1)}, u32[]{:S(2)}, u32[]{:S(2)}) collective-permute-start(bf16[4,16,512]{2,1,0:T(8,128)(2,1)S(1)} %add_convert_fusion), channel_id=1, source_target_pairs={{0,2},{1,3},{2,0},{3,1},{4,6},{5,7},{6,4},{7,5},{8,10},{9,11},{10,... | collective-permute-start | bytes 196616 | tf_op jit(solution)/shard_map/ppermute | solution.py:610
  90.2 1.4 %collective-permute-start.18 = (f32[4,16,512]{2,1,0:T(8,128)S(1)}, f32[4,16,512]{2,1,0:T(8,128)S(1)}, u32[]{:S(2)}, u32[]{:S(2)}) collective-permute-start(f32[4,16,512]{2,1,0:T(8,128)S(1)} %convert_add_fusion), channel_id=1, source_target_pairs={{0,1},{1,0},{2,3},{3,2},{4,5},{5,4},{6,7},{7,6},{8,9},{9,8},{10,11... | collective-permute-start | bytes 393224 | tf_op jit(solution)/shard_map/ppermute | solution.py:611

commit v8 on v7

--- a/solution.py
+++ b/solution.py
@@ -43,10 +43,8 @@
 
 
 def prep_kernel(
-    gate_ref, own_hbm, cot_hbm, w_hbm, refx_ref, gates_ref, cot_out, w_ref, own_ref, cot_ref, sems
+    gate_ref, own_hbm, cot_hbm, refx_ref, gates_ref, cot_out, own_ref, cot_ref, sems
 ):
-    weights = pltpu.make_async_copy(w_hbm, w_ref, sems.at[2])
-    weights.start()
     copies = [
         pltpu.make_async_copy(own_hbm, own_ref, sems.at[0]),
         pltpu.make_async_copy(cot_hbm, cot_ref, sems.at[1]),
@@ -70,7 +68,6 @@
         return carry
 
     lax.fori_loop(0, cot_out.shape[0], pack_one, 0)
-    weights.wait()
 
 
 def position(view, own_index, local_views, view_count):
@@ -79,8 +76,7 @@
     return place * local_views + view % local_views
 
 
-def assemble_kernel(src_ref, place_ref, *rest):
-    *map_refs, rows_ref, maps, scratch = rest
+def assemble(src_ref, place_ref, map_refs, rows_ref, maps, scratch):
     local_views, per_view = src_ref.shape
     tiles = scratch.shape[0]
     pairs = local_views * per_view
@@ -145,19 +141,27 @@
     return costs
 
 
+def weight_copy(w_ref, plane, held, sems, slot):
+    return pltpu.make_async_copy(w_ref.at[plane], held.at[slot], sems.at[slot])
+
+
 def forward_body(count, plane_of, gates_ref, rows_ref, refx_ref, w_ref, saved, cost_ref, scratch):
+    held, sems, *chunks = scratch
     low = low_half()
 
-    def matmul(chunk, at):
-        chunk[...] = lax.dot_general(
-            rows_ref[...], w_ref[plane_of(at)], NT, preferred_element_type=jnp.float32
+    def fetch(at, slot):
+        return weight_copy(w_ref, plane_of(jnp.minimum(at, count - 1)), held, sems, slot)
+
+    def matmul(slot):
+        chunks[slot][...] = lax.dot_general(
+            rows_ref[...], held[slot], NT, preferred_element_type=jnp.float32
         )
 
-    def vector(chunk, at):
+    def vector(slot, at):
         plane = plane_of(at)
         for index in range(2):
             costs = [
-                forward_vector(gates_ref, refx_ref, chunk, 2 * index + half, plane, saved)
+                forward_vector(gates_ref, refx_ref, chunks[slot], 2 * index + half, plane, saved)
                 for half in range(2)
             ]
             for g in range(G):
@@ -167,23 +171,35 @@
 
     def two_planes(turn, carry):
         first = 2 * turn
-        matmul(scratch[0], first)
-        vector(scratch[1], jnp.maximum(first - 1, 0))
-        matmul(scratch[1], first + 1)
-        vector(scratch[0], first)
+        for slot in range(2):
+            fetch(first + slot, slot).wait()
+            matmul(slot)
+            fetch(first + slot + 2, slot).start()
+            vector(1 - slot, jnp.maximum(first + slot - 1, 0))
         return carry
 
     lax.fori_loop(0, count // 2, two_planes, 0)
-    vector(scratch[1], count - 1)
+    vector(1, count - 1)
+    for slot in range(2):
+        fetch(count - 1, slot).wait()
 
 
 def edge_plane(planes, index):
     return jnp.where(index < 2, index, planes - 4 + index)
 
 
-def edge_kernel(gates_ref, rows_ref, refx_ref, w_ref, cot_ref, *rest):
-    up_ref, down_ref, cost, *scratch = rest[4:]
+def edge_kernel(src_ref, place_ref, gates_ref, refx_ref, w_ref, cot_ref, *rest):
+    map_refs = rest[:8]
+    saved = rest[8:12]
+    up_ref, down_ref, rows_ref, next_ref = rest[12:16]
+    maps, gathered, cost, next_sem, *scratch = rest[16:]
+    held, sems, *_ = scratch
     planes = w_ref.shape[0]
+    weight_copy(w_ref, 0, held, sems, 0).start()
+    weight_copy(w_ref, 1, held, sems, 1).start()
+    following = pltpu.make_async_copy(w_ref.at[2], next_ref, next_sem)
+    following.start()
+    assemble(src_ref, place_ref, map_refs, rows_ref, maps, gathered)
     forward_body(
         4,
         functools.partial(edge_plane, planes),
@@ -191,7 +207,7 @@
         rows_ref,
         refx_ref,
         w_ref,
-        rest[:4],
+        saved,
         cost,
         scratch,
     )
@@ -199,10 +215,15 @@
     up_ref[0:2] = cost[2:4]
     down_ref[2] = cot_ref[0]
     up_ref[2] = cot_ref[planes - 1]
-
-
-def inner_kernel(gates_ref, rows_ref, refx_ref, w_ref, *rest):
+    following.wait()
+
+
+def inner_kernel(gates_ref, rows_ref, refx_ref, w_ref, next_ref, *rest):
     cost_ref, *scratch = rest[8:]
+    held, sems, *_ = scratch
+    weight_copy(w_ref, 3, held, sems, 1).start()
+    first = pltpu.make_async_copy(next_ref, held.at[0], sems.at[0])
+    first.start()
     forward_body(
         cost_ref.shape[0],
         lambda index: index + 2,
@@ -292,17 +313,18 @@
     halo_refs = rest[:6]
     warped_ref, corr_ref, sig_ref, rden_ref = rest[6:10]
     regular_ref, keep_ref, send_ref = rest[10:13]
-    cost, grad_ref, slope, smooth, rows_a, rows_b, acc, dref, held, sems, dense = rest[13:]
+    cost, grad_ref, slope, smooth, rows, acc, dref, held, sems, dense = rest[13:]
     count = w_ref.shape[0]
     pairs = sig_ref.shape[1]
     tiles = pairs // SUB
     lane_tiles = dref.shape[0]
+    pixels = sig_ref.shape[2]
     local_views = src_ref.shape[0]
-    channels = G * GC
     low = low_half()
 
-    def vector(plane, tile, target):
+    def vector(plane, tile, offset):
         lanes = pl.ds(tile * LANE, LANE)
+        target = pl.ds(offset * pixels + tile * LANE, LANE)
         pack = tile // 2
         half = tile % 2
         rden = rden_ref[plane, :, lanes]
@@ -310,10 +332,10 @@
         num_grads = []
         mixed = None
         for g in range(G):
-            rows = pl.ds(g * SUB, SUB)
-            grad = grad_ref[plane, pack, rows, :]
+            group = pl.ds(g * SUB, SUB)
+            grad = grad_ref[plane, pack, group, :]
             num_grads.append(spread(grad, half, low) * rden)
-            part = grad * cost[plane + 2, pack, rows, :]
+            part = grad * cost[plane + 2, pack, group, :]
             mixed = part if mixed is None else mixed + part
         vis_grad = -(spread(mixed, half, low) * rden)[None]
         for g in range(G):
@@ -335,7 +357,7 @@
                     ],
                     axis=0,
                 )
-                target[span, lanes] = both.astype(jnp.bfloat16)
+                rows[span, target] = both.astype(jnp.bfloat16)
                 warped = (
                     warped_ref[plane, span, lanes]
                     .astype(jnp.float32)
@@ -346,39 +368,44 @@
                         corr_grad * warped[i], axis=0
                     )
 
-    def matmul(rows, slot):
-        product = jnp.dot(rows[...], held[slot], preferred_element_type=jnp.float32)
+    turns = count // 2
+
+    def fetch(turn):
+        slot = lax.rem(turn, 2)
+        first = 2 * jnp.minimum(turn, turns - 1)
+        return [
+            pltpu.make_async_copy(
+                w_ref.at[first + offset],
+                held.at[slot, pl.ds(offset * pixels, pixels)],
+                sems.at[slot, offset],
+            )
+            for offset in range(2)
+        ]
+
+    for copy in fetch(0):
+        copy.start()
+    acc[...] = jnp.zeros_like(acc)
+    dref[...] = jnp.zeros_like(dref)
+    depth_conv(taps_ref, *halo_refs, regular_ref, cost, grad_ref, slope, smooth)
+
+    def two_planes(turn, carry):
+        for copy in fetch(turn + 1):
+            copy.start()
+        for copy in fetch(turn):
+            copy.wait()
+        for offset in range(2):
+            for tile in range(lane_tiles):
+                vector(2 * turn + offset, tile, offset)
+        product = jnp.dot(
+            rows[...], held[lax.rem(turn, 2)], preferred_element_type=jnp.float32
+        )
         for tile in range(lane_tiles):
             acc[tile] += product[:, tile * LANE : (tile + 1) * LANE]
-
-    def fetch(plane):
-        slot = lax.rem(plane, 4)
-        return pltpu.make_async_copy(w_ref.at[plane], held.at[slot], sems.at[slot])
-
-    fetch(0).start()
-    fetch(1).start()
-    acc[...] = jnp.zeros_like(acc)
-    dref[...] = jnp.zeros_like(dref)
-    rows_b[...] = jnp.zeros_like(rows_b)
-    held[3] = jnp.zeros_like(held[3])
-    depth_conv(taps_ref, *halo_refs, regular_ref, cost, grad_ref, slope, smooth)
-
-    def two_planes(turn, carry):
-        for offset, rows, before in ((0, rows_a, rows_b), (1, rows_b, rows_a)):
-            plane = 2 * turn + offset
-            fetch(plane).wait()
-
-            @pl.when(plane + 2 < count)
-            def _():
-                fetch(plane + 2).start()
-
-            matmul(before, lax.rem(plane + 3, 4))
-            for tile in range(lane_tiles):
-                vector(plane, tile, rows)
         return carry
 
-    lax.fori_loop(0, count // 2, two_planes, 0)
-    matmul(rows_b, (count - 1) % 4)
+    lax.fori_loop(0, turns, two_planes, 0)
+    for copy in fetch(turns):
+        copy.wait()
     own_index = place_ref[0]
     parity = place_ref[1]
     blocks = keep_ref.shape[1] // SUB
@@ -466,28 +493,27 @@
     packed = (pixels // (2 * LANE), G * SUB, LANE)
     hbm = pl.BlockSpec(memory_space=pltpu.HBM)
     anywhere = pl.BlockSpec(memory_space=pl.ANY)
-    refx, gates, cot, weights = pl.pallas_call(
+    weights = pltpu.with_memory_space_constraint(warp_weights, pltpu.HBM)
+    refx, gates, cot = pl.pallas_call(
         prep_kernel,
         out_shape=(
             shape((pixels // LANE, channels * SUB, LANE), f32),
             shape((G, SUB, LANE), f32),
             shape((planes,) + packed, f32),
-            pltpu.VMEM(warp_weights.shape, bf16),
         ),
-        in_specs=[SMEM(), hbm, hbm, hbm],
+        in_specs=[SMEM(), hbm, hbm],
         scratch_shapes=[
             pltpu.VMEM(features.shape, bf16),
             pltpu.VMEM(cotangent.shape, bf16),
-            pltpu.SemaphoreType.DMA((3,)),
+            pltpu.SemaphoreType.DMA((2,)),
         ],
-        compiler_params=params(),
+        compiler_params=params(4),
         cost_estimate=pl.CostEstimate(flops=10**9, bytes_accessed=4 * MIB, transcendentals=0),
         name="prep",
     )(
         pltpu.with_memory_space_constraint(view_gate, pltpu.HBM),
         pltpu.with_memory_space_constraint(features, pltpu.HBM),
         pltpu.with_memory_space_constraint(cotangent, pltpu.HBM),
-        pltpu.with_memory_space_constraint(warp_weights, pltpu.HBM),
     )
     far_even, refx, gates, cot = lax.optimization_barrier((far_even, refx, gates, cot))
     maps = [near_even, far_even, over_view(near_even, 1), over_view(far_even, 1)]
@@ -495,18 +521,6 @@
 
     src_own = lax.dynamic_slice_in_dim(sources, own_index * local_views, local_views, 0)
     place = jnp.stack([own_index, parity]).astype(jnp.int32)
-    rows = pl.pallas_call(
-        assemble_kernel,
-        out_shape=shape((channels * pairs, pixels), bf16),
-        in_specs=[SMEM(), SMEM()] + [pl.BlockSpec()] * len(maps),
-        scratch_shapes=[
-            pltpu.VMEM((2, all_views, channels // 2, pixels), bf16),
-            pltpu.VMEM((pixels // LANE, channels * pairs, LANE), f32),
-        ],
-        compiler_params=params(24),
-        name="assemble",
-    )(src_own, place, *maps)
-
     saved = (
         pltpu.VMEM((planes, channels * pairs, pixels), bf16),
         pltpu.VMEM((planes, G * pairs, pixels), f32),
@@ -515,37 +529,53 @@
     )
     on_chip = functools.partial(pltpu.with_memory_space_constraint, memory_space=pltpu.VMEM)
     vmem = pl.BlockSpec(memory_space=pltpu.VMEM)
-    scratch = [pltpu.VMEM((channels * pairs, pixels), f32)] * 2
+    scratch = [
+        pltpu.VMEM((2, pixels, pixels), bf16),
+        pltpu.SemaphoreType.DMA((2,)),
+        pltpu.VMEM((channels * pairs, pixels), f32),
+        pltpu.VMEM((channels * pairs, pixels), f32),
+    ]
     load = (3,) + packed
-    rows, refx, gates, cot = [on_chip(item) for item in (rows, refx, gates, cot)]
-    weights = on_chip(weights)
-    *edge_saved, up_load, down_load = pl.pallas_call(
+    refx, gates, cot = [on_chip(item) for item in (refx, gates, cot)]
+    *edge_saved, up_load, down_load, rows, following = pl.pallas_call(
         edge_kernel,
-        out_shape=saved + (shape(load, f32),) * 2,
-        in_specs=[vmem] * 5,
-        out_specs=(vmem,) * 6,
-        scratch_shapes=[pltpu.VMEM((4,) + packed, f32)] + scratch,
-        compiler_params=params(8),
+        out_shape=saved
+        + (shape(load, f32),) * 2
+        + (
+            pltpu.VMEM((channels * pairs, pixels), bf16),
+            pltpu.VMEM((pixels, pixels), bf16),
+        ),
+        in_specs=[SMEM()] * 2 + [vmem] * 2 + [hbm, vmem] + [vmem] * len(maps),
+        out_specs=(vmem,) * 8,
+        scratch_shapes=[
+            pltpu.VMEM((2, all_views, channels // 2, pixels), bf16),
+            pltpu.VMEM((pixels // LANE, channels * pairs, LANE), f32),
+            pltpu.VMEM((4,) + packed, f32),
+            pltpu.SemaphoreType.DMA,
+        ]
+        + scratch,
+        compiler_params=params(12 + 4 * all_views * channels * pixels // MIB),
         name="forward_edge",
-    )(gates, rows, refx, weights, cot)
+    )(src_own, place, gates, refx, weights, cot, *maps)
+    rows, following = on_chip(rows), on_chip(following)
     below = lax.ppermute(up_load, "plane", up)
     above = lax.ppermute(down_load, "plane", down)
     inner_count = planes - 4
     *all_saved, inner_cost = pl.pallas_call(
         inner_kernel,
         out_shape=saved + (pltpu.VMEM((inner_count,) + packed, f32),),
-        in_specs=[vmem] * 4 + [anywhere] * 4,
+        in_specs=[vmem] * 3 + [hbm, vmem] + [anywhere] * 4,
         out_specs=(vmem,) * 5,
         scratch_shapes=scratch,
-        input_output_aliases={4 + i: i for i in range(4)},
-        compiler_params=params(8),
+        input_output_aliases={5 + i: i for i in range(4)},
+        compiler_params=params(9),
         cost_estimate=pl.CostEstimate(
             flops=2 * channels * pairs * pixels * pixels * inner_count,
             bytes_accessed=40 * MIB,
             transcendentals=0,
         ),
         name="forward_inner",
-    )(gates, rows, refx, weights, *[on_chip(item) for item in edge_saved])
+    )(gates, rows, refx, weights, following, *[on_chip(item) for item in edge_saved])
 
     halo = (below, down_load, inner_cost, up_load, above, cot)
     returned = (all_views, channels // 2, pixels)
@@ -559,12 +589,11 @@
             pltpu.VMEM((planes,) + packed, f32),
             pltpu.VMEM((planes + 2,) + packed, f32),
             pltpu.VMEM((planes + 2,) + packed, f32),
-            pltpu.VMEM((channels * pairs, pixels), bf16),
-            pltpu.VMEM((channels * pairs, pixels), bf16),
+            pltpu.VMEM((channels * pairs, 2 * pixels), bf16),
             pltpu.VMEM((pixels // LANE, channels * pairs, LANE), f32),
             pltpu.VMEM((pixels // LANE, channels * SUB, LANE), f32),
-            pltpu.VMEM((4, pixels, pixels), bf16),
-            pltpu.SemaphoreType.DMA((4,)),
+            pltpu.VMEM((2, 2 * pixels, pixels), bf16),
+            pltpu.SemaphoreType.DMA((2, 2)),
             pltpu.VMEM(returned, f32),
         ],
         compiler_params=params(14 + 5 * all_views * channels * pixels // MIB),
@@ -575,7 +604,7 @@
         pltpu.with_memory_space_constraint(depth_kernel, pltpu.HBM),
         gates,
         refx,
-        pltpu.with_memory_space_constraint(warp_weights, pltpu.HBM),
+        weights,
         *halo,
         *[on_chip(item) for item in all_saved],
     )

time: 92.8 us -> 83.8 us (0.903)
  local copies, waits for them, and re-layouts: 7.15 us -> 1.75 us
  Pallas kernels: 40.7 us -> 36.1 us
  waiting for transfers between devices: 19.5 us -> 22.5 us
  starting transfers between devices: 24.1 us -> 22.1 us
    unnamed x9 -> x3, local copies, waits for them, and re-layouts: 5.51 us -> 0.1 us
    pallas_call x1, Pallas kernels: 22.2 us -> 18.7 us  [shards(): pl.pallas_call(backward_kernel, out_shape=(shape(cotangent.shape, bf16),...]
    ppermute x10, waiting for transfers between devices: 13 us -> 15.9 us  [over_view(): return lax.ppermute(array, 'view', [(i, i ^ k) for i in range(view_count)])]
    pallas_call x1, Pallas kernels: 3.78 us -> 1.99 us  [shards(): pl.pallas_call(prep_kernel, out_shape=(shape((pixels // LANE, channels *...]
    ppermute x10, starting transfers between devices: 16 us -> 14.3 us  [over_view(): return lax.ppermute(array, 'view', [(i, i ^ k) for i in range(view_count)])]
    pallas_call x2 -> x1, Pallas kernels: 6.06 us -> 6.34 us  [shards(): pl.pallas_call(edge_kernel, out_shape=saved + (shape(load, f32),) * 2 + (...]
  transfers between devices with their start and end apart: 19 -> 19, of which waited for: 9 -> 12; matrix products, arithmetic and copies ran while one was open for 0% -> 0% of each run, Pallas kernels for 13% -> 13%
where the time goes in v8:
time: 83.8 us; the launch traced here: 83.4 us
  Pallas kernels  36.1 us (43%)
  waiting for transfers between devices  22.5 us (27%)
  starting transfers between devices  22.1 us (26%)
  local copies, waits for them, and re-layouts  1.75 us (2%)
    pallas_call x1, Pallas kernels, shards(): pl.pallas_call(backward_kernel, out_shape=(shape(cotangent.shape, bf16),...  18.7 us
    ppermute x10, waiting for transfers between devices, over_view(): return lax.ppermute(array, 'view', [(i, i ^ k) for i in range(view_count)])  15.9 us
    ppermute x10, starting transfers between devices, over_view(): return lax.ppermute(array, 'view', [(i, i ^ k) for i in range(view_count)])  14.3 us
    pallas_call x1, Pallas kernels, shards(): pl.pallas_call(inner_kernel, out_shape=saved + (pltpu.VMEM((inner_count,)...  8.84 us
    pallas_call x1, Pallas kernels, shards(): pl.pallas_call(edge_kernel, out_shape=saved + (shape(load, f32),) * 2 + (...  6.34 us
    ppermute x1, waiting for transfers between devices, shards(): lax.ppermute(rounded, 'plane', far).astype(f32)  2.63 us
    ppermute x1, starting transfers between devices, shards(): received = lax.ppermute(send, 'plane', near)  2.15 us
    ppermute x1, starting transfers between devices, shards(): below = lax.ppermute(up_load, 'plane', up)  2.06 us
  transfers between devices with their start and end apart: 19, of which 12 were waited for; matrix products, arithmetic and copies ran while one was open for 0% of the time, Pallas kernels for 13%

profile of v8, /device:TPU:0, one launch (start us, length us, event | category | flops | bytes accessed | tf_op | source)
XLA Modules:
  0.0 83.4 jit_solution(10396934933759123639)
XLA Ops:
  0.6 0.0 copy-start
  0.7 0.8 %dynamic-slice_bitcast_fusion = bf16[4,16,512]{2,1,0:T(8,128)(2,1)S(1)} fusion(bf16[4,2,2,8,512]{4,3,2,1,0:T(8,128)(2,1)} %bitcast.13, s32[]{:T(128)S(6)} %select_n.28), kind=kLoop, calls=%fused_computation.7 | loop fusion | bytes 131076 | tf_op jit(solution)/shard_map/reshape | solution.py:482
  1.5 3.0 %collective-permute-start.2 = (bf16[4,16,512]{2,1,0:T(8,128)(2,1)S(1)}, bf16[4,16,512]{2,1,0:T(8,128)(2,1)S(1)}, u32[]{:S(2)}, u32[]{:S(2)}) collective-permute-start(bf16[4,16,512]{2,1,0:T(8,128)(2,1)S(1)} %dynamic-slice_bitcast_fusion), channel_id=1, source_target_pairs={{0,8},{4,12},{8,0},{12,4},{16,24},{20,28},{24,16},{28,20},{1,9},{5... | collective-permute-start | bytes 196616 | tf_op jit(solution)/shard_map/ppermute | solution.py:487
  4.5 2.5 %collective-permute-start.1 = (bf16[4,16,512]{2,1,0:T(8,128)(2,1)S(1)}, bf16[4,16,512]{2,1,0:T(8,128)(2,1)S(1)}, u32[]{:S(2)}, u32[]{:S(2)}) collective-permute-start(bf16[4,16,512]{2,1,0:T(8,128)(2,1)S(1)} %dynamic-slice_bitcast_fusion), channel_id=1, source_target_pairs={{0,24},{4,28},{8,16},{12,20},{16,8},{20,12},{24,0},{28,4},{1,25},{... | collective-permute-start | bytes 196616 | tf_op jit(solution)/shard_map/ppermute | solution.py:487
  7.0 0.1 collective-permute-start
  7.1 2.0 %prep.1 = (f32[4,256,128]{2,1,0:T(8,128)S(1)}, f32[8,8,128]{2,1,0:T(8,128)S(1)}, f32[12,2,64,128]{3,2,1,0:T(8,128)S(1)}) custom-call(f32[8]{0:T(128)} %gate_ref.1, bf16[4,32,512]{2,1,0:T(8,128)(2,1)} %own_hbm.1, bf16[4,12,8,512]{3,2,1,0:T(8,128)(2,1)} %cot_hbm.1), custom_call_target="tpu_custom_call" | custom-call | flops 1000000000 | bytes 4194304 | tf_op jit(solution)/shard_map/prep/pallas_call | solution.py:497
  9.1 0.0 collective-permute-done.2
  9.2 1.6 %collective-permute-start.3 = (bf16[8,16,512]{2,1,0:T(8,128)(2,1)S(1)}, bf16[8,16,512]{2,1,0:T(8,128)(2,1)S(1)}, u32[]{:S(2)}, u32[]{:S(2)}) collective-permute-start(bf16[8,16,512]{2,1,0:T(8,128)(2,1)S(1)} %pad_maximum_fusion.2.rest_0_), channel_id=1, source_target_pairs={{0,4},{4,0},{8,12},{12,8},{16,20},{20,16},{24,28},{28,24},{1,5},{5... | collective-permute-start | bytes 393224 | tf_op jit(solution)/shard_map/ppermute | solution.py:487
  10.7 0.7 collective-permute-done.1
  11.4 2.1 %collective-permute-done = bf16[4,16,512]{2,1,0:T(8,128)(2,1)S(1)} collective-permute-done((bf16[4,16,512]{2,1,0:T(8,128)(2,1)S(1)}, bf16[4,16,512]{2,1,0:T(8,128)(2,1)S(1)}, u32[]{:S(2)}, u32[]{:S(2)}) %collective-permute-start) | collective-permute-done | bytes 65568 | tf_op jit(solution)/shard_map/ppermute | solution.py:487
  13.5 1.6 %collective-permute-start.4 = (bf16[8,16,512]{2,1,0:T(8,128)(2,1)S(1)}, bf16[8,16,512]{2,1,0:T(8,128)(2,1)S(1)}, u32[]{:S(2)}, u32[]{:S(2)}) collective-permute-start(bf16[8,16,512]{2,1,0:T(8,128)(2,1)S(1)} %pad_maximum_fusion.1.rest_1_), channel_id=1, source_target_pairs={{0,4},{4,0},{8,12},{12,8},{16,20},{20,16},{24,28},{28,24},{1,5},{5... | collective-permute-start | bytes 393224 | tf_op jit(solution)/shard_map/ppermute | solution.py:487
  15.1 0.0 collective-permute-start.5
  15.1 0.5 collective-permute-start.6
  15.6 0.0 collective-permute-done.3.rest_2_
  15.6 0.0 collective-permute-start.7
  15.6 3.3 %collective-permute-done.4.rest_3_ = bf16[8,16,512]{2,1,0:T(8,128)(2,1)S(1)} collective-permute-done((bf16[8,16,512]{2,1,0:T(8,128)(2,1)S(1)}, bf16[8,16,512]{2,1,0:T(8,128)(2,1)S(1)}, u32[]{:S(2)}, u32[]{:S(2)}) %collective-permute-start.4) | collective-permute-done | bytes 131104 | tf_op jit(solution)/shard_map/ppermute | solution.py:487
  18.9 0.0 collective-permute-start.8
  18.9 0.1 constant_dynamic-slice_fusion
  19.0 0.1 copy.15.src_ref
  19.1 0.1 pad_add_fusion.place_ref
  19.2 0.0 collective-permute-done.5.rest_4_
  19.2 0.0 collective-permute-done.6.rest_5_
  19.2 1.1 %collective-permute-done.8.rest_7_ = bf16[8,16,512]{2,1,0:T(8,128)(2,1)S(1)} collective-permute-done((bf16[8,16,512]{2,1,0:T(8,128)(2,1)S(1)}, bf16[8,16,512]{2,1,0:T(8,128)(2,1)S(1)}, u32[]{:S(2)}, u32[]{:S(2)}) %collective-permute-start.8) | collective-permute-done | bytes 131104 | tf_op jit(solution)/shard_map/ppermute | solution.py:520
  20.3 6.3 %forward_edge.1 = (bf16[12,1280,512]{2,1,0:T(8,128)(2,1)S(1)}, f32[12,320,512]{2,1,0:T(8,128)S(1)}, f32[12,40,512]{2,1,0:T(8,128)S(1)}, f32[12,8,512]{2,1,0:T(8,...) custom-call(s32[4,10]{1,0:T(4,128)S(1)} %copy.15.src_ref, ...), custom_call_target="tpu_custom_call" | custom-call | tf_op jit(solution)/shard_map/forward_edge/pallas_call | solution.py:540
  26.6 2.1 %collective-permute-start.9 = (f32[3,2,64,128]{3,2,1,0:T(8,128)S(1)}, f32[3,2,64,128]{3,2,1,0:T(8,128)S(1)}, u32[]{:S(2)}, u32[]{:S(2)}) collective-permute-start(f32[3,2,64,128]{3,2,1,0:T(8,128)S(1)} %get-tuple-element.40.rest_3_), channel_id=1, source_target_pairs={{0,1},{1,2},{2,3},{4,5},{5,6},{6,7},{8,9},{9,10},{10,11},{12,13},{... | collective-permute-start | bytes 589832 | tf_op jit(solution)/shard_map/ppermute | solution.py:561
  28.7 1.3 %collective-permute-start.10 = (f32[3,2,64,128]{3,2,1,0:T(8,128)S(1)}, f32[3,2,64,128]{3,2,1,0:T(8,128)S(1)}, u32[]{:S(2)}, u32[]{:S(2)}) collective-permute-start(f32[3,2,64,128]{3,2,1,0:T(8,128)S(1)} %get-tuple-element.41.rest_1_), channel_id=1, source_target_pairs={{1,0},{2,1},{3,2},{5,4},{6,5},{7,6},{9,8},{10,9},{11,10},{13,12},{... | collective-permute-start | bytes 589832 | tf_op jit(solution)/shard_map/ppermute | solution.py:562
  30.0 8.8 %forward_inner.1 = (bf16[12,1280,512]{2,1,0:T(8,128)(2,1)S(1)}, f32[12,320,512]{2,1,0:T(8,128)S(1)}, f32[12,40,512]{2,1,0:T(8,128)S(1)}, f32[12,8,512]{2,1,0:T(8,128)S(1)}, f32[8,2,64,128]{3,2,1,0:T(8,128)S(1)}) custom-call(f32[8,8,128]{2,1,0:T(8,128)S(1)} %get-tuple-element.36.gates_ref, ...), custom_call_target="tpu_custom_call", output_to_operand_aliasing={{0}: (5, {}), {1}: (6, {}), {2}: (7, {}), {3}: (8, {})} | custom-call | flops 5368709120 | bytes 41943040 | tf_op jit(solution)/shard_map/forward_inner/pallas_call | solution.py:564
  38.8 0.0 collective-permute-done.9.rest_0_
  38.9 18.7 %backward.1 = (bf16[4,12,8,512]{3,2,1,0:T(8,128)(2,1)}, f32[32,16,512]{2,1,0:T(8,128)S(1)}, bf16[32,16,512]{2,1,0:T(8,128)(2,1)S(1)}) custom-call(s32[4,10]{1,0:T(4,128)S(1)} %copy.15.src_ref, s32[2]{0:T(128)S(1)} %pad_add_fusion.place_ref, f32[3,8,8]{2,1,0:T(8,128)} %taps_ref.1, f32[8,8,128]{2,1,0:T(8,128)S(1)} %get-tuple-element.36.gates_ref, ...), custom_call_target="tpu_custom_call" | custom-call | tf_op jit(solution)/shard_map/backward/pallas_call | solution.py:582
  57.6 2.1 %collective-permute-start.11 = (bf16[32,16,512]{2,1,0:T(8,128)(2,1)S(1)}, bf16[32,16,512]{2,1,0:T(8,128)(2,1)S(1)}, u32[]{:S(2)}, u32[]{:S(2)}) collective-permute-start(bf16[32,16,512]{2,1,0:T(8,128)(2,1)S(1)} %get-tuple-element.55), channel_id=1, source_target_pairs={{0,1},{1,0},{2,3},{3,2},{4,5},{5,4},{6,7},{7,6},{8,9},{9,8},{10,11... | collective-permute-start | bytes 1572872 | tf_op jit(solution)/shard_map/ppermute | solution.py:612
  59.7 1.5 %collective-permute-done.11.received_ref.after_ref = bf16[32,16,512]{2,1,0:T(8,128)(2,1)S(1)} collective-permute-done((bf16[32,16,512]{2,1,0:T(8,128)(2,1)S(1)}, bf16[32,16,512]{2,1,0:T(8,128)(2,1)S(1)}, u32[]{:S(2)}, u32[]{:S(2)}) %collective-permute-start.11) | collective-permute-done | bytes 524320 | tf_op jit(solution)/shard_map/ppermute | solution.py:612
  61.3 0.1 split.2
  61.3 1.6 %collective-permute-start.12 = (bf16[8,16,512]{2,1,0:T(8,128)(2,1)S(1)}, bf16[8,16,512]{2,1,0:T(8,128)(2,1)S(1)}, u32[]{:S(2)}, u32[]{:S(2)}) collective-permute-start(bf16[8,16,512]{2,1,0:T(8,128)(2,1)S(1)} %get-tuple-element.57), channel_id=1, source_target_pairs={{0,4},{4,0},{8,12},{12,8},{16,20},{20,16},{24,28},{28,24},{1,5},{5... | collective-permute-start | bytes 393224 | tf_op jit(solution)/shard_map/ppermute | solution.py:487
  62.9 4.2 %collective-permute-done.12.received_ref = bf16[8,16,512]{2,1,0:T(8,128)(2,1)S(1)} collective-permute-done((bf16[8,16,512]{2,1,0:T(8,128)(2,1)S(1)}, bf16[8,16,512]{2,1,0:T(8,128)(2,1)S(1)}, u32[]{:S(2)}, u32[]{:S(2)}) %collective-permute-start.12) | collective-permute-done | bytes 131104 | tf_op jit(solution)/shard_map/ppermute | solution.py:487
  67.2 0.1 split.3
  67.3 1.6 %collective-permute-start.13 = (bf16[8,16,512]{2,1,0:T(8,128)(2,1)S(1)}, bf16[8,16,512]{2,1,0:T(8,128)(2,1)S(1)}, u32[]{:S(2)}, u32[]{:S(2)}) collective-permute-start(bf16[8,16,512]{2,1,0:T(8,128)(2,1)S(1)} %get-tuple-element.60), channel_id=1, source_target_pairs={{0,4},{4,0},{8,12},{12,8},{16,20},{20,16},{24,28},{28,24},{1,5},{5... | collective-permute-start | bytes 393224 | tf_op jit(solution)/shard_map/ppermute | solution.py:487
  68.9 0.9 %collective-permute-start.14 = (bf16[4,16,512]{2,1,0:T(8,128)(2,1)S(1)}, bf16[4,16,512]{2,1,0:T(8,128)(2,1)S(1)}, u32[]{:S(2)}, u32[]{:S(2)}) collective-permute-start(bf16[4,16,512]{2,1,0:T(8,128)(2,1)S(1)} %get-tuple-element.58.after_ref), channel_id=1, source_target_pairs={{0,16},{4,20},{8,24},{12,28},{16,0},{20,4},{24,8},{28,12},{1,17},{... | collective-permute-start | bytes 196616 | tf_op jit(solution)/shard_map/ppermute | solution.py:487
  69.8 1.3 %collective-permute-start.15 = (bf16[4,16,512]{2,1,0:T(8,128)(2,1)S(1)}, bf16[4,16,512]{2,1,0:T(8,128)(2,1)S(1)}, u32[]{:S(2)}, u32[]{:S(2)}) collective-permute-start(bf16[4,16,512]{2,1,0:T(8,128)(2,1)S(1)} %get-tuple-element.62), channel_id=1, source_target_pairs={{0,24},{4,28},{8,16},{12,20},{16,8},{20,12},{24,0},{28,4},{1,25},{... | collective-permute-start | bytes 196616 | tf_op jit(solution)/shard_map/ppermute | solution.py:487
  71.1 1.2 %collective-permute-done.13.received_ref = bf16[8,16,512]{2,1,0:T(8,128)(2,1)S(1)} collective-permute-done((bf16[8,16,512]{2,1,0:T(8,128)(2,1)S(1)}, bf16[8,16,512]{2,1,0:T(8,128)(2,1)S(1)}, u32[]{:S(2)}, u32[]{:S(2)}) %collective-permute-start.13) | collective-permute-done | bytes 131104 | tf_op jit(solution)/shard_map/ppermute | solution.py:487
  72.3 0.1 collective-permute-start.16
  72.5 3.5 %collective-permute-done.15 = bf16[4,16,512]{2,1,0:T(8,128)(2,1)S(1)} collective-permute-done((bf16[4,16,512]{2,1,0:T(8,128)(2,1)S(1)}, bf16[4,16,512]{2,1,0:T(8,128)(2,1)S(1)}, u32[]{:S(2)}, u32[]{:S(2)}) %collective-permute-start.15) | collective-permute-done | bytes 65568 | tf_op jit(solution)/shard_map/ppermute | solution.py:487
  76.0 0.1 collective-permute-done.14
  76.0 0.8 collective-permute-done.16
  76.8 1.7 %collective-permute-start.17 = (bf16[4,16,512]{2,1,0:T(8,128)(2,1)S(1)}, bf16[4,16,512]{2,1,0:T(8,128)(2,1)S(1)}, u32[]{:S(2)}, u32[]{:S(2)}) collective-permute-start(bf16[4,16,512]{2,1,0:T(8,128)(2,1)S(1)} %add_convert_fusion), channel_id=1, source_target_pairs={{0,2},{1,3},{2,0},{3,1},{4,6},{5,7},{6,4},{7,5},{8,10},{9,11},{10,... | collective-permute-start | bytes 196616 | tf_op jit(solution)/shard_map/ppermute | solution.py:639
  78.5 2.6 %collective-permute-done.17 = bf16[4,16,512]{2,1,0:T(8,128)(2,1)S(1)} collective-permute-done((bf16[4,16,512]{2,1,0:T(8,128)(2,1)S(1)}, bf16[4,16,512]{2,1,0:T(8,128)(2,1)S(1)}, u32[]{:S(2)}, u32[]{:S(2)}) %collective-permute-start.17) | collective-permute-done | bytes 65568 | tf_op jit(solution)/shard_map/ppermute | solution.py:639
  81.2 0.1 collective-permute-start.18
  81.3 1.3 %collective-permute-done.18 = f32[4,16,512]{2,1,0:T(8,128)S(1)} collective-permute-done((f32[4,16,512]{2,1,0:T(8,128)S(1)}, f32[4,16,512]{2,1,0:T(8,128)S(1)}, u32[]{:S(2)}, u32[]{:S(2)}) %collective-permute-start.18) | collective-permute-done | bytes 131104 | tf_op jit(solution)/shard_map/ppermute | solution.py:640
  82.7 0.7 copy.14
  (11 shorter events, 0.2 us)
Async XLA Ops:
  0.6 18.3 %copy-start = (s32[32,10]{0,1:T(8,128)S(1)}, s32[32,10]{0,1:T(8,128)}, u32[]{:S(2)}) copy-start(s32[32,10]{0,1:T(8,128)} %param.7) | copy-start | bytes 3844
  1.5 7.6 %collective-permute-start.2 = (bf16[4,16,512]{2,1,0:T(8,128)(2,1)S(1)}, bf16[4,16,512]{2,1,0:T(8,128)(2,1)S(1)}, u32[]{:S(2)}, u32[]{:S(2)}) collective-permute-start(bf16[4,16,512]{2,1,0:T(8,128)(2,1)S(1)} %dynamic-slice_bitcast_fusion), channel_id=1, source_target_pairs={{0,8},{4,12},{8,0},{12,4},{16,24},{20,28},{24,16},{28,20},{1,9},{5... | collective-permute-start | bytes 196616 | tf_op jit(solution)/shard_map/ppermute | solution.py:487
  4.5 6.9 %collective-permute-start.1 = (bf16[4,16,512]{2,1,0:T(8,128)(2,1)S(1)}, bf16[4,16,512]{2,1,0:T(8,128)(2,1)S(1)}, u32[]{:S(2)}, u32[]{:S(2)}) collective-permute-start(bf16[4,16,512]{2,1,0:T(8,128)(2,1)S(1)} %dynamic-slice_bitcast_fusion), channel_id=1, source_target_pairs={{0,24},{4,28},{8,16},{12,20},{16,8},{20,12},{24,0},{28,4},{1,25},{... | collective-permute-start | bytes 196616 | tf_op jit(solution)/shard_map/ppermute | solution.py:487
  7.0 6.4 %collective-permute-start = (bf16[4,16,512]{2,1,0:T(8,128)(2,1)S(1)}, bf16[4,16,512]{2,1,0:T(8,128)(2,1)S(1)}, u32[]{:S(2)}, u32[]{:S(2)}) collective-permute-start(bf16[4,16,512]{2,1,0:T(8,128)(2,1)S(1)} %dynamic-slice_bitcast_fusion), channel_id=1, source_target_pairs={{0,16},{4,20},{8,24},{12,28},{16,0},{20,4},{24,8},{28,12},{1,17},{... | collective-permute-start | bytes 196616 | tf_op jit(solution)/shard_map/ppermute | solution.py:487
  9.2 6.4 %collective-permute-start.3 = (bf16[8,16,512]{2,1,0:T(8,128)(2,1)S(1)}, bf16[8,16,512]{2,1,0:T(8,128)(2,1)S(1)}, u32[]{:S(2)}, u32[]{:S(2)}) collective-permute-start(bf16[8,16,512]{2,1,0:T(8,128)(2,1)S(1)} %pad_maximum_fusion.2.rest_0_), channel_id=1, source_target_pairs={{0,4},{4,0},{8,12},{12,8},{16,20},{20,16},{24,28},{28,24},{1,5},{5... | collective-permute-start | bytes 393224 | tf_op jit(solution)/shard_map/ppermute | solution.py:487
  13.5 5.4 %collective-permute-start.4 = (bf16[8,16,512]{2,1,0:T(8,128)(2,1)S(1)}, bf16[8,16,512]{2,1,0:T(8,128)(2,1)S(1)}, u32[]{:S(2)}, u32[]{:S(2)}) collective-permute-start(bf16[8,16,512]{2,1,0:T(8,128)(2,1)S(1)} %pad_maximum_fusion.1.rest_1_), channel_id=1, source_target_pairs={{0,4},{4,0},{8,12},{12,8},{16,20},{20,16},{24,28},{28,24},{1,5},{5... | collective-permute-start | bytes 393224 | tf_op jit(solution)/shard_map/ppermute | solution.py:487
  15.1 4.1 %collective-permute-start.5 = (bf16[8,16,512]{2,1,0:T(8,128)(2,1)S(1)}, bf16[8,16,512]{2,1,0:T(8,128)(2,1)S(1)}, u32[]{:S(2)}, u32[]{:S(2)}) collective-permute-start(bf16[8,16,512]{2,1,0:T(8,128)(2,1)S(1)} %pad_maximum_fusion.2.rest_0_), channel_id=1, source_target_pairs={{0,1},{1,0},{2,3},{3,2},{4,5},{5,4},{6,7},{7,6},{8,9},{9,8},{10,11... | collective-permute-start | bytes 393224 | tf_op jit(solution)/shard_map/ppermute | solution.py:520
  15.1 4.1 %collective-permute-start.6 = (bf16[8,16,512]{2,1,0:T(8,128)(2,1)S(1)}, bf16[8,16,512]{2,1,0:T(8,128)(2,1)S(1)}, u32[]{:S(2)}, u32[]{:S(2)}) collective-permute-start(bf16[8,16,512]{2,1,0:T(8,128)(2,1)S(1)} %pad_maximum_fusion.1.rest_1_), channel_id=1, source_target_pairs={{0,1},{1,0},{2,3},{3,2},{4,5},{5,4},{6,7},{7,6},{8,9},{9,8},{10,11... | collective-permute-start | bytes 393224 | tf_op jit(solution)/shard_map/ppermute | solution.py:520
  15.6 3.6 %collective-permute-start.7 = (bf16[8,16,512]{2,1,0:T(8,128)(2,1)S(1)}, bf16[8,16,512]{2,1,0:T(8,128)(2,1)S(1)}, u32[]{:S(2)}, u32[]{:S(2)}) collective-permute-start(bf16[8,16,512]{2,1,0:T(8,128)(2,1)S(1)} %collective-permute-done.3.rest_2_), channel_id=1, source_target_pairs={{0,1},{1,0},{2,3},{3,2},{4,5},{5,4},{6,7},{7,6},{8,9},{9,8},{10,11... | collective-permute-start | bytes 393224 | tf_op jit(solution)/shard_map/ppermute | solution.py:520
  18.9 1.3 %collective-permute-start.8 = (bf16[8,16,512]{2,1,0:T(8,128)(2,1)S(1)}, bf16[8,16,512]{2,1,0:T(8,128)(2,1)S(1)}, u32[]{:S(2)}, u32[]{:S(2)}) collective-permute-start(bf16[8,16,512]{2,1,0:T(8,128)(2,1)S(1)} %collective-permute-done.4.rest_3_), channel_id=1, source_target_pairs={{0,1},{1,0},{2,3},{3,2},{4,5},{5,4},{6,7},{7,6},{8,9},{9,8},{10,11... | collective-permute-start | bytes 393224 | tf_op jit(solution)/shard_map/ppermute | solution.py:520
  26.6 12.2 %collective-permute-start.9 = (f32[3,2,64,128]{3,2,1,0:T(8,128)S(1)}, f32[3,2,64,128]{3,2,1,0:T(8,128)S(1)}, u32[]{:S(2)}, u32[]{:S(2)}) collective-permute-start(f32[3,2,64,128]{3,2,1,0:T(8,128)S(1)} %get-tuple-element.40.rest_3_), channel_id=1, source_target_pairs={{0,1},{1,2},{2,3},{4,5},{5,6},{6,7},{8,9},{9,10},{10,11},{12,13},{... | collective-permute-start | bytes 589832 | tf_op jit(solution)/shard_map/ppermute | solution.py:561
  28.7 10.2 %collective-permute-start.10 = (f32[3,2,64,128]{3,2,1,0:T(8,128)S(1)}, f32[3,2,64,128]{3,2,1,0:T(8,128)S(1)}, u32[]{:S(2)}, u32[]{:S(2)}) collective-permute-start(f32[3,2,64,128]{3,2,1,0:T(8,128)S(1)} %get-tuple-element.41.rest_1_), channel_id=1, source_target_pairs={{1,0},{2,1},{3,2},{5,4},{6,5},{7,6},{9,8},{10,9},{11,10},{13,12},{... | collective-permute-start | bytes 589832 | tf_op jit(solution)/shard_map/ppermute | solution.py:562
  57.6 3.7 %collective-permute-start.11 = (bf16[32,16,512]{2,1,0:T(8,128)(2,1)S(1)}, bf16[32,16,512]{2,1,0:T(8,128)(2,1)S(1)}, u32[]{:S(2)}, u32[]{:S(2)}) collective-permute-start(bf16[32,16,512]{2,1,0:T(8,128)(2,1)S(1)} %get-tuple-element.55), channel_id=1, source_target_pairs={{0,1},{1,0},{2,3},{3,2},{4,5},{5,4},{6,7},{7,6},{8,9},{9,8},{10,11... | collective-permute-start | bytes 1572872 | tf_op jit(solution)/shard_map/ppermute | solution.py:612
  61.3 5.8 %collective-permute-start.12 = (bf16[8,16,512]{2,1,0:T(8,128)(2,1)S(1)}, bf16[8,16,512]{2,1,0:T(8,128)(2,1)S(1)}, u32[]{:S(2)}, u32[]{:S(2)}) collective-permute-start(bf16[8,16,512]{2,1,0:T(8,128)(2,1)S(1)} %get-tuple-element.57), channel_id=1, source_target_pairs={{0,4},{4,0},{8,12},{12,8},{16,20},{20,16},{24,28},{28,24},{1,5},{5... | collective-permute-start | bytes 393224 | tf_op jit(solution)/shard_map/ppermute | solution.py:487
  67.3 5.0 %collective-permute-start.13 = (bf16[8,16,512]{2,1,0:T(8,128)(2,1)S(1)}, bf16[8,16,512]{2,1,0:T(8,128)(2,1)S(1)}, u32[]{:S(2)}, u32[]{:S(2)}) collective-permute-start(bf16[8,16,512]{2,1,0:T(8,128)(2,1)S(1)} %get-tuple-element.60), channel_id=1, source_target_pairs={{0,4},{4,0},{8,12},{12,8},{16,20},{20,16},{24,28},{28,24},{1,5},{5... | collective-permute-start | bytes 393224 | tf_op jit(solution)/shard_map/ppermute | solution.py:487
  68.9 7.2 %collective-permute-start.14 = (bf16[4,16,512]{2,1,0:T(8,128)(2,1)S(1)}, bf16[4,16,512]{2,1,0:T(8,128)(2,1)S(1)}, u32[]{:S(2)}, u32[]{:S(2)}) collective-permute-start(bf16[4,16,512]{2,1,0:T(8,128)(2,1)S(1)} %get-tuple-element.58.after_ref), channel_id=1, source_target_pairs={{0,16},{4,20},{8,24},{12,28},{16,0},{20,4},{24,8},{28,12},{1,17},{... | collective-permute-start | bytes 196616 | tf_op jit(solution)/shard_map/ppermute | solution.py:487
  69.8 6.2 %collective-permute-start.15 = (bf16[4,16,512]{2,1,0:T(8,128)(2,1)S(1)}, bf16[4,16,512]{2,1,0:T(8,128)(2,1)S(1)}, u32[]{:S(2)}, u32[]{:S(2)}) collective-permute-start(bf16[4,16,512]{2,1,0:T(8,128)(2,1)S(1)} %get-tuple-element.62), channel_id=1, source_target_pairs={{0,24},{4,28},{8,16},{12,20},{16,8},{20,12},{24,0},{28,4},{1,25},{... | collective-permute-start | bytes 196616 | tf_op jit(solution)/shard_map/ppermute | solution.py:487
  72.3 4.5 %collective-permute-start.16 = (bf16[4,16,512]{2,1,0:T(8,128)(2,1)S(1)}, bf16[4,16,512]{2,1,0:T(8,128)(2,1)S(1)}, u32[]{:S(2)}, u32[]{:S(2)}) collective-permute-start(bf16[4,16,512]{2,1,0:T(8,128)(2,1)S(1)} %get-tuple-element.63), channel_id=1, source_target_pairs={{0,8},{4,12},{8,0},{12,4},{16,24},{20,28},{24,16},{28,20},{1,9},{5... | collective-permute-start | bytes 196616 | tf_op jit(solution)/shard_map/ppermute | solution.py:487
  76.8 4.3 %collective-permute-start.17 = (bf16[4,16,512]{2,1,0:T(8,128)(2,1)S(1)}, bf16[4,16,512]{2,1,0:T(8,128)(2,1)S(1)}, u32[]{:S(2)}, u32[]{:S(2)}) collective-permute-start(bf16[4,16,512]{2,1,0:T(8,128)(2,1)S(1)} %add_convert_fusion), channel_id=1, source_target_pairs={{0,2},{1,3},{2,0},{3,1},{4,6},{5,7},{6,4},{7,5},{8,10},{9,11},{10,... | collective-permute-start | bytes 196616 | tf_op jit(solution)/shard_map/ppermute | solution.py:639
  81.2 1.4 %collective-permute-start.18 = (f32[4,16,512]{2,1,0:T(8,128)S(1)}, f32[4,16,512]{2,1,0:T(8,128)S(1)}, u32[]{:S(2)}, u32[]{:S(2)}) collective-permute-start(f32[4,16,512]{2,1,0:T(8,128)S(1)} %convert_add_fusion), channel_id=1, source_target_pairs={{0,1},{1,0},{2,3},{3,2},{4,5},{5,4},{6,7},{7,6},{8,9},{9,8},{10,11... | collective-permute-start | bytes 393224 | tf_op jit(solution)/shard_map/ppermute | solution.py:640

commit v9 on v8

--- a/solution.py
+++ b/solution.py
@@ -313,7 +313,7 @@
     halo_refs = rest[:6]
     warped_ref, corr_ref, sig_ref, rden_ref = rest[6:10]
     regular_ref, keep_ref, send_ref = rest[10:13]
-    cost, grad_ref, slope, smooth, rows, acc, dref, held, sems, dense = rest[13:]
+    cost, grad_ref, slope, smooth, rows, acc, column, dref, held, sems, dense = rest[13:]
     count = w_ref.shape[0]
     pairs = sig_ref.shape[1]
     tiles = pairs // SUB
@@ -324,7 +324,7 @@
 
     def vector(plane, tile, offset):
         lanes = pl.ds(tile * LANE, LANE)
-        target = pl.ds(offset * pixels + tile * LANE, LANE)
+        target = pl.ds(pl.multiple_of(offset * pixels + tile * LANE, LANE), LANE)
         pack = tile // 2
         half = tile % 2
         rden = rden_ref[plane, :, lanes]
@@ -368,51 +368,49 @@
                         corr_grad * warped[i], axis=0
                     )
 
-    turns = count // 2
-
-    def fetch(turn):
-        slot = lax.rem(turn, 2)
-        first = 2 * jnp.minimum(turn, turns - 1)
-        return [
-            pltpu.make_async_copy(
-                w_ref.at[first + offset],
-                held.at[slot, pl.ds(offset * pixels, pixels)],
-                sems.at[slot, offset],
-            )
-            for offset in range(2)
-        ]
-
-    for copy in fetch(0):
-        copy.start()
+    group = rows.shape[1] // pixels
+
+    def fetch(turn, offset):
+        return pltpu.make_async_copy(
+            w_ref.at[turn * group + offset],
+            held.at[pl.ds(offset * pixels, pixels)],
+            sems.at[offset],
+        )
+
     acc[...] = jnp.zeros_like(acc)
     dref[...] = jnp.zeros_like(dref)
     depth_conv(taps_ref, *halo_refs, regular_ref, cost, grad_ref, slope, smooth)
 
-    def two_planes(turn, carry):
-        for copy in fetch(turn + 1):
-            copy.start()
-        for copy in fetch(turn):
-            copy.wait()
-        for offset in range(2):
+    def one_turn(turn, carry):
+        for offset in range(group):
+            fetch(turn, offset).start()
+
+        def one_plane(offset, carry):
             for tile in range(lane_tiles):
-                vector(2 * turn + offset, tile, offset)
-        product = jnp.dot(
-            rows[...], held[lax.rem(turn, 2)], preferred_element_type=jnp.float32
-        )
-        for tile in range(lane_tiles):
-            acc[tile] += product[:, tile * LANE : (tile + 1) * LANE]
+                vector(turn * group + offset, tile, offset)
+            return carry
+
+        lax.fori_loop(0, group, one_plane, 0)
+        for offset in range(group):
+            fetch(turn, offset).wait()
+        for first in range(0, pixels, 2 * LANE):
+            lanes = pl.ds(first, 2 * LANE)
+            acc[:, lanes] += jnp.dot(
+                rows[...], held[:, lanes], preferred_element_type=jnp.float32
+            )
         return carry
 
-    lax.fori_loop(0, turns, two_planes, 0)
-    for copy in fetch(turns):
-        copy.wait()
+    lax.fori_loop(0, count // group, one_turn, 0)
     own_index = place_ref[0]
     parity = place_ref[1]
     blocks = keep_ref.shape[1] // SUB
-    for target, held_side in ((dense, 1 - parity), (keep_ref, parity)):
+    sides = ((dense, 1 - parity), (keep_ref, parity))
+    for target, held_side in sides:
         target[...] = jnp.zeros_like(target)
-        for tile in range(lane_tiles):
-            lanes = pl.ds(tile * LANE, LANE)
+    for tile in range(lane_tiles):
+        lanes = pl.ds(tile * LANE, LANE)
+        column[...] = acc[:, lanes]
+        for target, held_side in sides:
             for block in range(blocks):
                 channel = (2 * block + held_side) * SUB
                 part = pl.ds(block * SUB, SUB)
@@ -423,15 +421,11 @@
                         value = dref[tile, pl.ds(first, SUB, stride=SUB), :]
                         total = value if total is None else total + value
                     target[view, part, lanes] = total
-        for pair in range(pairs):
-            view = src_ref[pair % local_views, pair // local_views]
-            slot = position(view, own_index, local_views, dense.shape[0] // local_views)
-            for block in range(blocks):
-                first = (2 * block + held_side) * (SUB * pairs) + pair
-                part = pl.ds(block * SUB, SUB)
-                for tile in range(lane_tiles):
-                    target[slot, part, pl.ds(tile * LANE, LANE)] += acc[
-                        tile, pl.ds(first, SUB, stride=pairs), :
+                for pair in range(pairs):
+                    view = src_ref[pair % local_views, pair // local_views]
+                    slot = position(view, own_index, local_views, dense.shape[0] // local_views)
+                    target[slot, part, lanes] += column[
+                        pl.ds(channel * pairs + pair, SUB, stride=pairs), :
                     ]
     send_ref[...] = dense[...].astype(jnp.bfloat16)
 
@@ -453,6 +447,14 @@
         out_ref[...] = (even_ref[span] + received_ref[span].astype(jnp.float32)).astype(
             out_ref.dtype
         )
+
+
+def join_kernel(place_ref, mine_ref, other_ref, out_ref):
+    parity = place_ref[1]
+    for ref, side in ((mine_ref, parity), (other_ref, 1 - parity)):
+        for block in range(ref.shape[1] // SUB):
+            first = pl.multiple_of((2 * block + side) * SUB, SUB)
+            out_ref[:, pl.ds(first, SUB), :] = ref[:, block * SUB : (block + 1) * SUB, :]
 
 
 SMEM = functools.partial(pl.BlockSpec, memory_space=pltpu.SMEM)
@@ -579,6 +581,7 @@
 
     halo = (below, down_load, inner_cost, up_load, above, cot)
     returned = (all_views, channels // 2, pixels)
+    group = max(size for size in (4, 2, 1) if planes % size == 0)
     regular, keep, send = pl.pallas_call(
         backward_kernel,
         out_shape=(shape(cotangent.shape, bf16), shape(returned, f32), shape(returned, bf16)),
@@ -589,14 +592,15 @@
             pltpu.VMEM((planes,) + packed, f32),
             pltpu.VMEM((planes + 2,) + packed, f32),
             pltpu.VMEM((planes + 2,) + packed, f32),
-            pltpu.VMEM((channels * pairs, 2 * pixels), bf16),
-            pltpu.VMEM((pixels // LANE, channels * pairs, LANE), f32),
+            pltpu.VMEM((channels * pairs, group * pixels), bf16),
+            pltpu.VMEM((channels * pairs, pixels), f32),
+            pltpu.VMEM((channels * pairs, LANE), f32),
             pltpu.VMEM((pixels // LANE, channels * SUB, LANE), f32),
-            pltpu.VMEM((2, 2 * pixels, pixels), bf16),
-            pltpu.SemaphoreType.DMA((2, 2)),
+            pltpu.VMEM((group * pixels, pixels), bf16),
+            pltpu.SemaphoreType.DMA((group,)),
             pltpu.VMEM(returned, f32),
         ],
-        compiler_params=params(14 + 5 * all_views * channels * pixels // MIB),
+        compiler_params=params(16 + 9 * all_views * channels * pixels // MIB),
         name="backward",
     )(
         src_own,
@@ -638,10 +642,13 @@
     rounded = total.astype(bf16)
     total = rounded.astype(f32) + lax.ppermute(rounded, "plane", far).astype(f32)
     other = lax.ppermute(total, "plane", near)
-    cut = (local_views, blocks, 1, share, pixels)
-    first = jnp.where(parity == 0, total, other).reshape(cut)
-    second = jnp.where(parity == 0, other, total).reshape(cut)
-    feature_grads = jnp.concatenate([first, second], axis=2).reshape(features.shape)
+    feature_grads = pl.pallas_call(
+        join_kernel,
+        out_shape=shape(features.shape, f32),
+        in_specs=[SMEM(), vmem, vmem],
+        compiler_params=params(4),
+        name="join",
+    )(place, total, other)
     return (regular, feature_grads)
 
 

time: 83.8 us -> 116 us (1.38)
  local copies, waits for them, and re-layouts: 1.75 us -> 18.3 us
  Pallas kernels: 36.1 us -> 51.8 us
    unnamed x3 -> x11, local copies, waits for them, and re-layouts: 0.1 us -> 17.4 us
    pallas_call x1, Pallas kernels: 18.7 us -> 33.2 us  [shards(): pl.pallas_call(backward_kernel, out_shape=(shape(cotangent.shape, bf16),...]
    pallas_call x0 -> x1, Pallas kernels: none -> 1.26 us  [shards(): pl.pallas_call(join_kernel, out_shape=shape(features.shape, f32), in_spec...]
  transfers between devices with their start and end apart: 19 -> 19, of which waited for: 12 -> 12; matrix products, arithmetic and copies ran while one was open for 0% -> 0% of each run, Pallas kernels for 13% -> 9%
where the time goes in v9:
time: 116 us
  Pallas kernels  51.8 us (45%)
  waiting for transfers between devices  22.4 us (19%)
  starting transfers between devices  22.1 us (19%)
  local copies, waits for them, and re-layouts  18.3 us (16%)
    pallas_call x1, Pallas kernels, shards(): pl.pallas_call(backward_kernel, out_shape=(shape(cotangent.shape, bf16),...  33.2 us
    unnamed x11, local copies, waits for them, and re-layouts  17.4 us
    ppermute x10, waiting for transfers between devices, over_view(): return lax.ppermute(array, 'view', [(i, i ^ k) for i in range(view_count)])  15.8 us
    ppermute x10, starting transfers between devices, over_view(): return lax.ppermute(array, 'view', [(i, i ^ k) for i in range(view_count)])  14.3 us
    pallas_call x1, Pallas kernels, shards(): pl.pallas_call(inner_kernel, out_shape=saved + (pltpu.VMEM((inner_count,)...  8.84 us
    pallas_call x1, Pallas kernels, shards(): pl.pallas_call(edge_kernel, out_shape=saved + (shape(load, f32),) * 2 + (...  6.33 us
    ppermute x1, waiting for transfers between devices, shards(): lax.ppermute(rounded, 'plane', far).astype(f32)  2.63 us
  transfers between devices with their start and end apart: 19, of which 12 were waited for; matrix products, arithmetic and copies ran while one was open for 0% of the time, Pallas kernels for 9%

profile of v9, /device:TPU:0, one launch (start us, length us, event | category | flops | bytes accessed | tf_op | source)
XLA Modules:
  0.0 115.6 jit_solution(18035420235259337589)
XLA Ops:
  0.6 0.0 copy-start
  0.7 0.8 dynamic-slice_bitcast_fusion
  1.5 3.0 %collective-permute-start.2 = (bf16[4,16,512]{2,1,0:T(8,128)(2,1)S(1)}, bf16[4,16,512]{2,1,0:T(8,128)(2,1)S(1)}, u32[]{:S(2)}, u32[]{:S(2)}) collective-permute-start(bf16[4,16,512]{2,1,0:T(8,128)(2,1)S(1)} %dynamic-slice_bitcast_fusion), channel_id=1, source_target_pairs={{0,8},{4,12},{8,0},{12,4},{16,24},{20,28},{24,16},{28,20},{1,9},{5... | collective-permute-start | bytes 196616 | tf_op jit(solution)/shard_map/ppermute | solution.py:489
  4.5 2.5 %collective-permute-start.1 = (bf16[4,16,512]{2,1,0:T(8,128)(2,1)S(1)}, bf16[4,16,512]{2,1,0:T(8,128)(2,1)S(1)}, u32[]{:S(2)}, u32[]{:S(2)}) collective-permute-start(bf16[4,16,512]{2,1,0:T(8,128)(2,1)S(1)} %dynamic-slice_bitcast_fusion), channel_id=1, source_target_pairs={{0,24},{4,28},{8,16},{12,20},{16,8},{20,12},{24,0},{28,4},{1,25},{... | collective-permute-start | bytes 196616 | tf_op jit(solution)/shard_map/ppermute | solution.py:489
  7.0 0.1 collective-permute-start
  7.1 2.0 %prep.1 = (f32[4,256,128]{2,1,0:T(8,128)S(1)}, f32[8,8,128]{2,1,0:T(8,128)S(1)}, f32[12,2,64,128]{3,2,1,0:T(8,128)S(1)}) custom-call(f32[8]{0:T(128)} %gate_ref.1, bf16[4,32,512]{2,1,0:T(8,128)(2,1)} %own_hbm.1, bf16[4,12,8,512]{3,2,1,0:T(8,128)(2,1)} %cot_hbm.1), custom_call_target="tpu_custom_call" | custom-call | flops 1000000000 | bytes 4194304 | tf_op jit(solution)/shard_map/prep/pallas_call | solution.py:499
  9.1 0.0 collective-permute-done.2
  9.2 1.6 %collective-permute-start.3 = (bf16[8,16,512]{2,1,0:T(8,128)(2,1)S(1)}, bf16[8,16,512]{2,1,0:T(8,128)(2,1)S(1)}, u32[]{:S(2)}, u32[]{:S(2)}) collective-permute-start(bf16[8,16,512]{2,1,0:T(8,128)(2,1)S(1)} %pad_maximum_fusion.1.rest_0_), channel_id=1, source_target_pairs={{0,4},{4,0},{8,12},{12,8},{16,20},{20,16},{24,28},{28,24},{1,5},{5... | collective-permute-start | bytes 393224 | tf_op jit(solution)/shard_map/ppermute | solution.py:489
  10.7 0.7 collective-permute-done.1
  11.4 2.1 %collective-permute-done = bf16[4,16,512]{2,1,0:T(8,128)(2,1)S(1)} collective-permute-done((bf16[4,16,512]{2,1,0:T(8,128)(2,1)S(1)}, bf16[4,16,512]{2,1,0:T(8,128)(2,1)S(1)}, u32[]{:S(2)}, u32[]{:S(2)}) %collective-permute-start) | collective-permute-done | bytes 65568 | tf_op jit(solution)/shard_map/ppermute | solution.py:489
  13.5 1.6 %collective-permute-start.4 = (bf16[8,16,512]{2,1,0:T(8,128)(2,1)S(1)}, bf16[8,16,512]{2,1,0:T(8,128)(2,1)S(1)}, u32[]{:S(2)}, u32[]{:S(2)}) collective-permute-start(bf16[8,16,512]{2,1,0:T(8,128)(2,1)S(1)} %pad_maximum_fusion.rest_1_), channel_id=1, source_target_pairs={{0,4},{4,0},{8,12},{12,8},{16,20},{20,16},{24,28},{28,24},{1,5},{5... | collective-permute-start | bytes 393224 | tf_op jit(solution)/shard_map/ppermute | solution.py:489
  15.1 0.5 collective-permute-start.6
  15.6 0.0 collective-permute-done.3.rest_2_
  15.6 0.0 collective-permute-start.7
  15.6 3.3 %collective-permute-done.4.rest_3_ = bf16[8,16,512]{2,1,0:T(8,128)(2,1)S(1)} collective-permute-done((bf16[8,16,512]{2,1,0:T(8,128)(2,1)S(1)}, bf16[8,16,512]{2,1,0:T(8,128)(2,1)S(1)}, u32[]{:S(2)}, u32[]{:S(2)}) %collective-permute-start.4) | collective-permute-done | bytes 131104 | tf_op jit(solution)/shard_map/ppermute | solution.py:489
  18.9 0.1 constant_dynamic-slice_fusion
  19.0 0.1 copy.14.src_ref
  19.1 0.1 pad_add_fusion.place_ref
  19.2 0.0 collective-permute-done.7.rest_6_
  19.2 1.1 collective-permute-done.8.rest_7_
  20.3 6.3 %forward_edge.1 = (bf16[12,1280,512]{2,1,0:T(8,128)(2,1)S(1)}, f32[12,320,512]{2,1,0:T(8,128)S(1)}, f32[12,40,512]{2,1,0:T(8,128)S(1)}, f32[12,8,512]{2,1,0:T(8,...) custom-call(s32[4,10]{1,0:T(4,128)S(1)} %copy.14.src_ref, ...), custom_call_target="tpu_custom_call" | custom-call | tf_op jit(solution)/shard_map/forward_edge/pallas_call | solution.py:542
  26.6 2.1 %collective-permute-start.9 = (f32[3,2,64,128]{3,2,1,0:T(8,128)S(1)}, f32[3,2,64,128]{3,2,1,0:T(8,128)S(1)}, u32[]{:S(2)}, u32[]{:S(2)}) collective-permute-start(f32[3,2,64,128]{3,2,1,0:T(8,128)S(1)} %get-tuple-element.40.rest_3_), channel_id=1, source_target_pairs={{0,1},{1,2},{2,3},{4,5},{5,6},{6,7},{8,9},{9,10},{10,11},{12,13},{... | collective-permute-start | bytes 589832 | tf_op jit(solution)/shard_map/ppermute | solution.py:563
  28.7 1.3 %collective-permute-start.10 = (f32[3,2,64,128]{3,2,1,0:T(8,128)S(1)}, f32[3,2,64,128]{3,2,1,0:T(8,128)S(1)}, u32[]{:S(2)}, u32[]{:S(2)}) collective-permute-start(f32[3,2,64,128]{3,2,1,0:T(8,128)S(1)} %get-tuple-element.41.rest_1_), channel_id=1, source_target_pairs={{1,0},{2,1},{3,2},{5,4},{6,5},{7,6},{9,8},{10,9},{11,10},{13,12},{... | collective-permute-start | bytes 589832 | tf_op jit(solution)/shard_map/ppermute | solution.py:564
  30.0 8.8 %forward_inner.1 = (bf16[12,1280,512]{2,1,0:T(8,128)(2,1)S(1)}, f32[12,320,512]{2,1,0:T(8,128)S(1)}, f32[12,40,512]{2,1,0:T(8,128)S(1)}, f32[12,8,512]{2,1,0:T(8,128)S(1)}, f32[8,2,64,128]{3,2,1,0:T(8,128)S(1)}) custom-call(f32[8,8,128]{2,1,0:T(8,128)S(1)} %get-tuple-element.36.gates_ref, ...), custom_call_target="tpu_custom_call", output_to_operand_aliasing={{0}: (5, {}), {1}: (6, {}), {2}: (7, {}), {3}: (8, {})} | custom-call | flops 5368709120 | bytes 41943040 | tf_op jit(solution)/shard_map/forward_inner/pallas_call | solution.py:566
  38.8 5.5 %copy-done.1 = bf16[12,1280,512]{2,1,0:T(8,128)(2,1)} copy-done((bf16[12,1280,512]{2,1,0:T(8,128)(2,1)}, bf16[12,1280,512]{2,1,0:T(8,128)(2,1)S(1)}, u32[]{:S(2)}) %copy-start.1) | copy-done | bytes 15728664
  44.3 3.1 %copy-done.3 = f32[12,320,512]{2,1,0:T(8,128)} copy-done((f32[12,320,512]{2,1,0:T(8,128)}, f32[12,320,512]{2,1,0:T(8,128)S(1)}, u32[]{:S(2)}) %copy-start.3) | copy-done | bytes 7864344
  47.4 5.5 %copy-done.2 = bf16[12,1280,512]{2,1,0:T(8,128)(2,1)S(1)} copy-done((bf16[12,1280,512]{2,1,0:T(8,128)(2,1)S(1)}, bf16[12,1280,512]{2,1,0:T(8,128)(2,1)}, u32[]{:S(2)}) %copy-start.2) | copy-done | bytes 15728664
  52.9 3.2 %copy-done.4 = f32[12,320,512]{2,1,0:T(8,128)S(1)} copy-done((f32[12,320,512]{2,1,0:T(8,128)S(1)}, f32[12,320,512]{2,1,0:T(8,128)}, u32[]{:S(2)}) %copy-start.4) | copy-done | bytes 7864344
  56.1 33.2 %backward.1 = (bf16[4,12,8,512]{3,2,1,0:T(8,128)(2,1)}, f32[32,16,512]{2,1,0:T(8,128)S(1)}, bf16[32,16,512]{2,1,0:T(8,128)(2,1)S(1)}) custom-call(s32[4,10]{1,0:T(4,128)S(1)} %copy.14.src_ref, s32[2]{0:T(128)S(1)} %pad_add_fusion.place_ref, f32[3,8,8]{2,1,0:T(8,128)} %taps_ref.1, f32[8,8,128]{2,1,0:T(8,128)S(1)} %get-tuple-element.36.gates_ref, ...), custom_call_target="tpu_custom_call" | custom-call | tf_op jit(solution)/shard_map/backward/pallas_call | solution.py:585
  89.3 2.1 %collective-permute-start.11 = (bf16[32,16,512]{2,1,0:T(8,128)(2,1)S(1)}, bf16[32,16,512]{2,1,0:T(8,128)(2,1)S(1)}, u32[]{:S(2)}, u32[]{:S(2)}) collective-permute-start(bf16[32,16,512]{2,1,0:T(8,128)(2,1)S(1)} %get-tuple-element.55), channel_id=1, source_target_pairs={{0,1},{1,0},{2,3},{3,2},{4,5},{5,4},{6,7},{7,6},{8,9},{9,8},{10,11... | collective-permute-start | bytes 1572872 | tf_op jit(solution)/shard_map/ppermute | solution.py:616
  91.4 1.5 %collective-permute-done.11.received_ref.after_ref = bf16[32,16,512]{2,1,0:T(8,128)(2,1)S(1)} collective-permute-done((bf16[32,16,512]{2,1,0:T(8,128)(2,1)S(1)}, bf16[32,16,512]{2,1,0:T(8,128)(2,1)S(1)}, u32[]{:S(2)}, u32[]{:S(2)}) %collective-permute-start.11) | collective-permute-done | bytes 524320 | tf_op jit(solution)/shard_map/ppermute | solution.py:616
  93.0 0.1 split.2
  93.1 1.6 %collective-permute-start.12 = (bf16[8,16,512]{2,1,0:T(8,128)(2,1)S(1)}, bf16[8,16,512]{2,1,0:T(8,128)(2,1)S(1)}, u32[]{:S(2)}, u32[]{:S(2)}) collective-permute-start(bf16[8,16,512]{2,1,0:T(8,128)(2,1)S(1)} %get-tuple-element.57), channel_id=1, source_target_pairs={{0,4},{4,0},{8,12},{12,8},{16,20},{20,16},{24,28},{28,24},{1,5},{5... | collective-permute-start | bytes 393224 | tf_op jit(solution)/shard_map/ppermute | solution.py:489
  94.7 4.2 %collective-permute-done.12.received_ref = bf16[8,16,512]{2,1,0:T(8,128)(2,1)S(1)} collective-permute-done((bf16[8,16,512]{2,1,0:T(8,128)(2,1)S(1)}, bf16[8,16,512]{2,1,0:T(8,128)(2,1)S(1)}, u32[]{:S(2)}, u32[]{:S(2)}) %collective-permute-start.12) | collective-permute-done | bytes 131104 | tf_op jit(solution)/shard_map/ppermute | solution.py:489
  98.9 0.1 split.3
  99.0 1.6 %collective-permute-start.13 = (bf16[8,16,512]{2,1,0:T(8,128)(2,1)S(1)}, bf16[8,16,512]{2,1,0:T(8,128)(2,1)S(1)}, u32[]{:S(2)}, u32[]{:S(2)}) collective-permute-start(bf16[8,16,512]{2,1,0:T(8,128)(2,1)S(1)} %get-tuple-element.60), channel_id=1, source_target_pairs={{0,4},{4,0},{8,12},{12,8},{16,20},{20,16},{24,28},{28,24},{1,5},{5... | collective-permute-start | bytes 393224 | tf_op jit(solution)/shard_map/ppermute | solution.py:489
  100.6 0.9 collective-permute-start.14
  101.5 1.3 %collective-permute-start.15 = (bf16[4,16,512]{2,1,0:T(8,128)(2,1)S(1)}, bf16[4,16,512]{2,1,0:T(8,128)(2,1)S(1)}, u32[]{:S(2)}, u32[]{:S(2)}) collective-permute-start(bf16[4,16,512]{2,1,0:T(8,128)(2,1)S(1)} %get-tuple-element.62), channel_id=1, source_target_pairs={{0,24},{4,28},{8,16},{12,20},{16,8},{20,12},{24,0},{28,4},{1,25},{... | collective-permute-start | bytes 196616 | tf_op jit(solution)/shard_map/ppermute | solution.py:489
  102.8 1.2 %collective-permute-done.13.received_ref = bf16[8,16,512]{2,1,0:T(8,128)(2,1)S(1)} collective-permute-done((bf16[8,16,512]{2,1,0:T(8,128)(2,1)S(1)}, bf16[8,16,512]{2,1,0:T(8,128)(2,1)S(1)}, u32[]{:S(2)}, u32[]{:S(2)}) %collective-permute-start.13) | collective-permute-done | bytes 131104 | tf_op jit(solution)/shard_map/ppermute | solution.py:489
  104.1 0.1 collective-permute-start.16
  104.2 3.5 %collective-permute-done.15 = bf16[4,16,512]{2,1,0:T(8,128)(2,1)S(1)} collective-permute-done((bf16[4,16,512]{2,1,0:T(8,128)(2,1)S(1)}, bf16[4,16,512]{2,1,0:T(8,128)(2,1)S(1)}, u32[]{:S(2)}, u32[]{:S(2)}) %collective-permute-start.15) | collective-permute-done | bytes 65568 | tf_op jit(solution)/shard_map/ppermute | solution.py:489
  107.7 0.1 collective-permute-done.14
  107.7 0.8 collective-permute-done.16
  108.6 1.7 %collective-permute-start.17 = (bf16[4,16,512]{2,1,0:T(8,128)(2,1)S(1)}, bf16[4,16,512]{2,1,0:T(8,128)(2,1)S(1)}, u32[]{:S(2)}, u32[]{:S(2)}) collective-permute-start(bf16[4,16,512]{2,1,0:T(8,128)(2,1)S(1)} %add_convert_fusion), channel_id=1, source_target_pairs={{0,2},{1,3},{2,0},{3,1},{4,6},{5,7},{6,4},{7,5},{8,10},{9,11},{10,... | collective-permute-start | bytes 196616 | tf_op jit(solution)/shard_map/ppermute | solution.py:643
  110.3 2.6 %collective-permute-done.17 = bf16[4,16,512]{2,1,0:T(8,128)(2,1)S(1)} collective-permute-done((bf16[4,16,512]{2,1,0:T(8,128)(2,1)S(1)}, bf16[4,16,512]{2,1,0:T(8,128)(2,1)S(1)}, u32[]{:S(2)}, u32[]{:S(2)}) %collective-permute-start.17) | collective-permute-done | bytes 65568 | tf_op jit(solution)/shard_map/ppermute | solution.py:643
  112.9 0.1 collective-permute-start.18
  113.0 1.3 %collective-permute-done.18.other_ref = f32[4,16,512]{2,1,0:T(8,128)S(1)} collective-permute-done((f32[4,16,512]{2,1,0:T(8,128)S(1)}, f32[4,16,512]{2,1,0:T(8,128)S(1)}, u32[]{:S(2)}, u32[]{:S(2)}) %collective-permute-start.18) | collective-permute-done | bytes 131104 | tf_op jit(solution)/shard_map/ppermute | solution.py:644
  114.3 1.3 %join.1 = f32[4,32,512]{2,1,0:T(8,128)} custom-call(s32[2]{0:T(128)S(1)} %pad_add_fusion.place_ref, f32[4,16,512]{2,1,0:T(8,128)S(1)} %convert_add_fusion.mine_ref, f32[4,16,512]{2,1,0:T(8,128)S(1)} %collective-permute-done.18.other_ref), custom_call_target="tpu_custom_call" | custom-call | tf_op jit(solution)/shard_map/join/pallas_call | solution.py:645
  (17 shorter events, 0.2 us)
Async XLA Ops:
  0.6 18.3 %copy-start = (s32[32,10]{0,1:T(8,128)S(1)}, s32[32,10]{0,1:T(8,128)}, u32[]{:S(2)}) copy-start(s32[32,10]{0,1:T(8,128)} %param.7) | copy-start | bytes 3844
  1.5 7.6 %collective-permute-start.2 = (bf16[4,16,512]{2,1,0:T(8,128)(2,1)S(1)}, bf16[4,16,512]{2,1,0:T(8,128)(2,1)S(1)}, u32[]{:S(2)}, u32[]{:S(2)}) collective-permute-start(bf16[4,16,512]{2,1,0:T(8,128)(2,1)S(1)} %dynamic-slice_bitcast_fusion), channel_id=1, source_target_pairs={{0,8},{4,12},{8,0},{12,4},{16,24},{20,28},{24,16},{28,20},{1,9},{5... | collective-permute-start | bytes 196616 | tf_op jit(solution)/shard_map/ppermute | solution.py:489
  4.5 6.9 %collective-permute-start.1 = (bf16[4,16,512]{2,1,0:T(8,128)(2,1)S(1)}, bf16[4,16,512]{2,1,0:T(8,128)(2,1)S(1)}, u32[]{:S(2)}, u32[]{:S(2)}) collective-permute-start(bf16[4,16,512]{2,1,0:T(8,128)(2,1)S(1)} %dynamic-slice_bitcast_fusion), channel_id=1, source_target_pairs={{0,24},{4,28},{8,16},{12,20},{16,8},{20,12},{24,0},{28,4},{1,25},{... | collective-permute-start | bytes 196616 | tf_op jit(solution)/shard_map/ppermute | solution.py:489
  7.0 6.4 %collective-permute-start = (bf16[4,16,512]{2,1,0:T(8,128)(2,1)S(1)}, bf16[4,16,512]{2,1,0:T(8,128)(2,1)S(1)}, u32[]{:S(2)}, u32[]{:S(2)}) collective-permute-start(bf16[4,16,512]{2,1,0:T(8,128)(2,1)S(1)} %dynamic-slice_bitcast_fusion), channel_id=1, source_target_pairs={{0,16},{4,20},{8,24},{12,28},{16,0},{20,4},{24,8},{28,12},{1,17},{... | collective-permute-start | bytes 196616 | tf_op jit(solution)/shard_map/ppermute | solution.py:489
  9.2 6.4 %collective-permute-start.3 = (bf16[8,16,512]{2,1,0:T(8,128)(2,1)S(1)}, bf16[8,16,512]{2,1,0:T(8,128)(2,1)S(1)}, u32[]{:S(2)}, u32[]{:S(2)}) collective-permute-start(bf16[8,16,512]{2,1,0:T(8,128)(2,1)S(1)} %pad_maximum_fusion.1.rest_0_), channel_id=1, source_target_pairs={{0,4},{4,0},{8,12},{12,8},{16,20},{20,16},{24,28},{28,24},{1,5},{5... | collective-permute-start | bytes 393224 | tf_op jit(solution)/shard_map/ppermute | solution.py:489
  13.5 5.4 %collective-permute-start.4 = (bf16[8,16,512]{2,1,0:T(8,128)(2,1)S(1)}, bf16[8,16,512]{2,1,0:T(8,128)(2,1)S(1)}, u32[]{:S(2)}, u32[]{:S(2)}) collective-permute-start(bf16[8,16,512]{2,1,0:T(8,128)(2,1)S(1)} %pad_maximum_fusion.rest_1_), channel_id=1, source_target_pairs={{0,4},{4,0},{8,12},{12,8},{16,20},{20,16},{24,28},{28,24},{1,5},{5... | collective-permute-start | bytes 393224 | tf_op jit(solution)/shard_map/ppermute | solution.py:489
  15.1 4.1 %collective-permute-start.5 = (bf16[8,16,512]{2,1,0:T(8,128)(2,1)S(1)}, bf16[8,16,512]{2,1,0:T(8,128)(2,1)S(1)}, u32[]{:S(2)}, u32[]{:S(2)}) collective-permute-start(bf16[8,16,512]{2,1,0:T(8,128)(2,1)S(1)} %pad_maximum_fusion.1.rest_0_), channel_id=1, source_target_pairs={{0,1},{1,0},{2,3},{3,2},{4,5},{5,4},{6,7},{7,6},{8,9},{9,8},{10,11... | collective-permute-start | bytes 393224 | tf_op jit(solution)/shard_map/ppermute | solution.py:522
  15.1 4.1 %collective-permute-start.6 = (bf16[8,16,512]{2,1,0:T(8,128)(2,1)S(1)}, bf16[8,16,512]{2,1,0:T(8,128)(2,1)S(1)}, u32[]{:S(2)}, u32[]{:S(2)}) collective-permute-start(bf16[8,16,512]{2,1,0:T(8,128)(2,1)S(1)} %pad_maximum_fusion.rest_1_), channel_id=1, source_target_pairs={{0,1},{1,0},{2,3},{3,2},{4,5},{5,4},{6,7},{7,6},{8,9},{9,8},{10,11... | collective-permute-start | bytes 393224 | tf_op jit(solution)/shard_map/ppermute | solution.py:522
  15.6 3.6 %collective-permute-start.7 = (bf16[8,16,512]{2,1,0:T(8,128)(2,1)S(1)}, bf16[8,16,512]{2,1,0:T(8,128)(2,1)S(1)}, u32[]{:S(2)}, u32[]{:S(2)}) collective-permute-start(bf16[8,16,512]{2,1,0:T(8,128)(2,1)S(1)} %collective-permute-done.3.rest_2_), channel_id=1, source_target_pairs={{0,1},{1,0},{2,3},{3,2},{4,5},{5,4},{6,7},{7,6},{8,9},{9,8},{10,11... | collective-permute-start | bytes 393224 | tf_op jit(solution)/shard_map/ppermute | solution.py:522
  18.9 1.3 %collective-permute-start.8 = (bf16[8,16,512]{2,1,0:T(8,128)(2,1)S(1)}, bf16[8,16,512]{2,1,0:T(8,128)(2,1)S(1)}, u32[]{:S(2)}, u32[]{:S(2)}) collective-permute-start(bf16[8,16,512]{2,1,0:T(8,128)(2,1)S(1)} %collective-permute-done.4.rest_3_), channel_id=1, source_target_pairs={{0,1},{1,0},{2,3},{3,2},{4,5},{5,4},{6,7},{7,6},{8,9},{9,8},{10,11... | collective-permute-start | bytes 393224 | tf_op jit(solution)/shard_map/ppermute | solution.py:522
  26.6 20.8 %collective-permute-start.9 = (f32[3,2,64,128]{3,2,1,0:T(8,128)S(1)}, f32[3,2,64,128]{3,2,1,0:T(8,128)S(1)}, u32[]{:S(2)}, u32[]{:S(2)}) collective-permute-start(f32[3,2,64,128]{3,2,1,0:T(8,128)S(1)} %get-tuple-element.40.rest_3_), channel_id=1, source_target_pairs={{0,1},{1,2},{2,3},{4,5},{5,6},{6,7},{8,9},{9,10},{10,11},{12,13},{... | collective-permute-start | bytes 589832 | tf_op jit(solution)/shard_map/ppermute | solution.py:563
  28.7 18.7 %collective-permute-start.10 = (f32[3,2,64,128]{3,2,1,0:T(8,128)S(1)}, f32[3,2,64,128]{3,2,1,0:T(8,128)S(1)}, u32[]{:S(2)}, u32[]{:S(2)}) collective-permute-start(f32[3,2,64,128]{3,2,1,0:T(8,128)S(1)} %get-tuple-element.41.rest_1_), channel_id=1, source_target_pairs={{1,0},{2,1},{3,2},{5,4},{6,5},{7,6},{9,8},{10,9},{11,10},{13,12},{... | collective-permute-start | bytes 589832 | tf_op jit(solution)/shard_map/ppermute | solution.py:564
  38.8 5.5 %copy-start.1 = (bf16[12,1280,512]{2,1,0:T(8,128)(2,1)}, bf16[12,1280,512]{2,1,0:T(8,128)(2,1)S(1)}, u32[]{:S(2)}) copy-start(bf16[12,1280,512]{2,1,0:T(8,128)(2,1)S(1)} %get-tuple-element.49.rest_6_) | copy-start | bytes 47185924
  44.3 3.1 %copy-start.3 = (f32[12,320,512]{2,1,0:T(8,128)}, f32[12,320,512]{2,1,0:T(8,128)S(1)}, u32[]{:S(2)}) copy-start(f32[12,320,512]{2,1,0:T(8,128)S(1)} %get-tuple-element.50.rest_7_) | copy-start | bytes 23592964
  47.4 5.5 %copy-start.2 = (bf16[12,1280,512]{2,1,0:T(8,128)(2,1)S(1)}, bf16[12,1280,512]{2,1,0:T(8,128)(2,1)}, u32[]{:S(2)}) copy-start(bf16[12,1280,512]{2,1,0:T(8,128)(2,1)} %copy-done.1) | copy-start | bytes 47185924
  52.9 3.2 %copy-start.4 = (f32[12,320,512]{2,1,0:T(8,128)S(1)}, f32[12,320,512]{2,1,0:T(8,128)}, u32[]{:S(2)}) copy-start(f32[12,320,512]{2,1,0:T(8,128)} %copy-done.3) | copy-start | bytes 23592964
  89.3 3.7 %collective-permute-start.11 = (bf16[32,16,512]{2,1,0:T(8,128)(2,1)S(1)}, bf16[32,16,512]{2,1,0:T(8,128)(2,1)S(1)}, u32[]{:S(2)}, u32[]{:S(2)}) collective-permute-start(bf16[32,16,512]{2,1,0:T(8,128)(2,1)S(1)} %get-tuple-element.55), channel_id=1, source_target_pairs={{0,1},{1,0},{2,3},{3,2},{4,5},{5,4},{6,7},{7,6},{8,9},{9,8},{10,11... | collective-permute-start | bytes 1572872 | tf_op jit(solution)/shard_map/ppermute | solution.py:616
  93.1 5.8 %collective-permute-start.12 = (bf16[8,16,512]{2,1,0:T(8,128)(2,1)S(1)}, bf16[8,16,512]{2,1,0:T(8,128)(2,1)S(1)}, u32[]{:S(2)}, u32[]{:S(2)}) collective-permute-start(bf16[8,16,512]{2,1,0:T(8,128)(2,1)S(1)} %get-tuple-element.57), channel_id=1, source_target_pairs={{0,4},{4,0},{8,12},{12,8},{16,20},{20,16},{24,28},{28,24},{1,5},{5... | collective-permute-start | bytes 393224 | tf_op jit(solution)/shard_map/ppermute | solution.py:489
  99.0 5.0 %collective-permute-start.13 = (bf16[8,16,512]{2,1,0:T(8,128)(2,1)S(1)}, bf16[8,16,512]{2,1,0:T(8,128)(2,1)S(1)}, u32[]{:S(2)}, u32[]{:S(2)}) collective-permute-start(bf16[8,16,512]{2,1,0:T(8,128)(2,1)S(1)} %get-tuple-element.60), channel_id=1, source_target_pairs={{0,4},{4,0},{8,12},{12,8},{16,20},{20,16},{24,28},{28,24},{1,5},{5... | collective-permute-start | bytes 393224 | tf_op jit(solution)/shard_map/ppermute | solution.py:489
  100.6 7.2 %collective-permute-start.14 = (bf16[4,16,512]{2,1,0:T(8,128)(2,1)S(1)}, bf16[4,16,512]{2,1,0:T(8,128)(2,1)S(1)}, u32[]{:S(2)}, u32[]{:S(2)}) collective-permute-start(bf16[4,16,512]{2,1,0:T(8,128)(2,1)S(1)} %get-tuple-element.58.after_ref), channel_id=1, source_target_pairs={{0,16},{4,20},{8,24},{12,28},{16,0},{20,4},{24,8},{28,12},{1,17},{... | collective-permute-start | bytes 196616 | tf_op jit(solution)/shard_map/ppermute | solution.py:489
  101.5 6.2 %collective-permute-start.15 = (bf16[4,16,512]{2,1,0:T(8,128)(2,1)S(1)}, bf16[4,16,512]{2,1,0:T(8,128)(2,1)S(1)}, u32[]{:S(2)}, u32[]{:S(2)}) collective-permute-start(bf16[4,16,512]{2,1,0:T(8,128)(2,1)S(1)} %get-tuple-element.62), channel_id=1, source_target_pairs={{0,24},{4,28},{8,16},{12,20},{16,8},{20,12},{24,0},{28,4},{1,25},{... | collective-permute-start | bytes 196616 | tf_op jit(solution)/shard_map/ppermute | solution.py:489
  104.1 4.5 %collective-permute-start.16 = (bf16[4,16,512]{2,1,0:T(8,128)(2,1)S(1)}, bf16[4,16,512]{2,1,0:T(8,128)(2,1)S(1)}, u32[]{:S(2)}, u32[]{:S(2)}) collective-permute-start(bf16[4,16,512]{2,1,0:T(8,128)(2,1)S(1)} %get-tuple-element.63), channel_id=1, source_target_pairs={{0,8},{4,12},{8,0},{12,4},{16,24},{20,28},{24,16},{28,20},{1,9},{5... | collective-permute-start | bytes 196616 | tf_op jit(solution)/shard_map/ppermute | solution.py:489
  108.6 4.3 %collective-permute-start.17 = (bf16[4,16,512]{2,1,0:T(8,128)(2,1)S(1)}, bf16[4,16,512]{2,1,0:T(8,128)(2,1)S(1)}, u32[]{:S(2)}, u32[]{:S(2)}) collective-permute-start(bf16[4,16,512]{2,1,0:T(8,128)(2,1)S(1)} %add_convert_fusion), channel_id=1, source_target_pairs={{0,2},{1,3},{2,0},{3,1},{4,6},{5,7},{6,4},{7,5},{8,10},{9,11},{10,... | collective-permute-start | bytes 196616 | tf_op jit(solution)/shard_map/ppermute | solution.py:643
  112.9 1.4 %collective-permute-start.18 = (f32[4,16,512]{2,1,0:T(8,128)S(1)}, f32[4,16,512]{2,1,0:T(8,128)S(1)}, u32[]{:S(2)}, u32[]{:S(2)}) collective-permute-start(f32[4,16,512]{2,1,0:T(8,128)S(1)} %convert_add_fusion.mine_ref), channel_id=1, source_target_pairs={{0,1},{1,0},{2,3},{3,2},{4,5},{5,4},{6,7},{7,6},{8,9},{9,8},{10,11... | collective-permute-start | bytes 393224 | tf_op jit(solution)/shard_map/ppermute | solution.py:644

commit v10 on v9

--- a/solution.py
+++ b/solution.py
@@ -247,12 +247,10 @@
     cot_ref,
     regular_ref,
     cost,
-    grad_ref,
     slope,
     smooth,
 ):
-    planes = grad_ref.shape[0]
-    local_views, _, groups, pixels = regular_ref.shape
+    local_views, planes, groups, pixels = regular_ref.shape
     cost[0:2] = below_ref[0:2]
     cost[2:4] = down_ref[0:2]
     cost[4:planes] = inner_ref[...]
@@ -284,7 +282,13 @@
             sig = jax.nn.sigmoid(pre)
             both = pl.ds(plane, 2)
             slope[both, :, rows, :] = slope[both, :, rows, :] * (sig * (1.0 + pre * (1.0 - sig)))
-            smooth[both, :, rows, :] = pre * sig
+            smooth[:, :, rows, :] = pre * sig
+        for view in range(local_views):
+            for tile in range(pixels // LANE):
+                first = (tile % 2) * local_views + view
+                for i, at in ((1, jnp.minimum(plane, planes - 1)), (0, jnp.abs(plane - 1))):
+                    kept = smooth[i, tile // 2, pl.ds(first, groups, stride=SUB), :]
+                    regular_ref[view, at, :, pl.ds(tile * LANE, LANE)] = kept.astype(jnp.bfloat16)
         return carry
 
     lax.fori_loop(0, (planes + 2) // 2, forward_planes, 0)
@@ -296,14 +300,7 @@
             lambda k, g, o: taps_ref[k, o, g],
         )
         for g in range(G):
-            grad_ref[pl.ds(plane, 2), :, pl.ds(g * SUB, SUB), :] = grads[g]
-        for view in range(local_views):
-            for tile in range(pixels // LANE):
-                first = (tile % 2) * local_views + view
-                for i in range(2):
-                    regular_ref[view, plane + i, :, pl.ds(tile * LANE, LANE)] = smooth[
-                        plane + i + 1, tile // 2, pl.ds(first, groups, stride=SUB), :
-                    ].astype(jnp.bfloat16)
+            slope[pl.ds(plane, 2), :, pl.ds(g * SUB, SUB), :] = grads[g]
         return carry
 
     lax.fori_loop(0, planes // 2, backward_planes, 0)
@@ -313,7 +310,7 @@
     halo_refs = rest[:6]
     warped_ref, corr_ref, sig_ref, rden_ref = rest[6:10]
     regular_ref, keep_ref, send_ref = rest[10:13]
-    cost, grad_ref, slope, smooth, rows, acc, column, dref, held, sems, dense = rest[13:]
+    cost, grad_ref, smooth, rows, acc, dref, held, sems, dense = rest[13:]
     count = w_ref.shape[0]
     pairs = sig_ref.shape[1]
     tiles = pairs // SUB
@@ -324,7 +321,7 @@
 
     def vector(plane, tile, offset):
         lanes = pl.ds(tile * LANE, LANE)
-        target = pl.ds(pl.multiple_of(offset * pixels + tile * LANE, LANE), LANE)
+        target = pl.ds(offset * pixels + tile * LANE, LANE)
         pack = tile // 2
         half = tile % 2
         rden = rden_ref[plane, :, lanes]
@@ -379,38 +376,29 @@
 
     acc[...] = jnp.zeros_like(acc)
     dref[...] = jnp.zeros_like(dref)
-    depth_conv(taps_ref, *halo_refs, regular_ref, cost, grad_ref, slope, smooth)
+    depth_conv(taps_ref, *halo_refs, regular_ref, cost, grad_ref, smooth)
 
     def one_turn(turn, carry):
         for offset in range(group):
             fetch(turn, offset).start()
-
-        def one_plane(offset, carry):
+        for offset in range(group):
             for tile in range(lane_tiles):
                 vector(turn * group + offset, tile, offset)
-            return carry
-
-        lax.fori_loop(0, group, one_plane, 0)
         for offset in range(group):
             fetch(turn, offset).wait()
-        for first in range(0, pixels, 2 * LANE):
-            lanes = pl.ds(first, 2 * LANE)
-            acc[:, lanes] += jnp.dot(
-                rows[...], held[:, lanes], preferred_element_type=jnp.float32
-            )
+        product = jnp.dot(rows[...], held[...], preferred_element_type=jnp.float32)
+        for tile in range(lane_tiles):
+            acc[tile] += product[:, tile * LANE : (tile + 1) * LANE]
         return carry
 
     lax.fori_loop(0, count // group, one_turn, 0)
     own_index = place_ref[0]
     parity = place_ref[1]
     blocks = keep_ref.shape[1] // SUB
-    sides = ((dense, 1 - parity), (keep_ref, parity))
-    for target, held_side in sides:
+    for target, held_side in ((dense, 1 - parity), (keep_ref, parity)):
         target[...] = jnp.zeros_like(target)
-    for tile in range(lane_tiles):
-        lanes = pl.ds(tile * LANE, LANE)
-        column[...] = acc[:, lanes]
-        for target, held_side in sides:
+        for tile in range(lane_tiles):
+            lanes = pl.ds(tile * LANE, LANE)
             for block in range(blocks):
                 channel = (2 * block + held_side) * SUB
                 part = pl.ds(block * SUB, SUB)
@@ -421,11 +409,15 @@
                         value = dref[tile, pl.ds(first, SUB, stride=SUB), :]
                         total = value if total is None else total + value
                     target[view, part, lanes] = total
-                for pair in range(pairs):
-                    view = src_ref[pair % local_views, pair // local_views]
-                    slot = position(view, own_index, local_views, dense.shape[0] // local_views)
-                    target[slot, part, lanes] += column[
-                        pl.ds(channel * pairs + pair, SUB, stride=pairs), :
+        for pair in range(pairs):
+            view = src_ref[pair % local_views, pair // local_views]
+            slot = position(view, own_index, local_views, dense.shape[0] // local_views)
+            for block in range(blocks):
+                first = (2 * block + held_side) * (SUB * pairs) + pair
+                part = pl.ds(block * SUB, SUB)
+                for tile in range(lane_tiles):
+                    target[slot, part, pl.ds(tile * LANE, LANE)] += acc[
+                        tile, pl.ds(first, SUB, stride=pairs), :
                     ]
     send_ref[...] = dense[...].astype(jnp.bfloat16)
 
@@ -581,7 +573,7 @@
 
     halo = (below, down_load, inner_cost, up_load, above, cot)
     returned = (all_views, channels // 2, pixels)
-    group = max(size for size in (4, 2, 1) if planes % size == 0)
+    group = max(size for size in (3, 2, 1) if planes % size == 0)
     regular, keep, send = pl.pallas_call(
         backward_kernel,
         out_shape=(shape(cotangent.shape, bf16), shape(returned, f32), shape(returned, bf16)),
@@ -589,18 +581,16 @@
         out_specs=(vmem,) * 3,
         scratch_shapes=[
             pltpu.VMEM((planes + 4,) + packed, f32),
-            pltpu.VMEM((planes,) + packed, f32),
             pltpu.VMEM((planes + 2,) + packed, f32),
-            pltpu.VMEM((planes + 2,) + packed, f32),
+            pltpu.VMEM((2,) + packed, f32),
             pltpu.VMEM((channels * pairs, group * pixels), bf16),
-            pltpu.VMEM((channels * pairs, pixels), f32),
-            pltpu.VMEM((channels * pairs, LANE), f32),
+            pltpu.VMEM((pixels // LANE, channels * pairs, LANE), f32),
             pltpu.VMEM((pixels // LANE, channels * SUB, LANE), f32),
             pltpu.VMEM((group * pixels, pixels), bf16),
             pltpu.SemaphoreType.DMA((group,)),
             pltpu.VMEM(returned, f32),
         ],
-        compiler_params=params(16 + 9 * all_views * channels * pixels // MIB),
+        compiler_params=params(14 + 5 * all_views * channels * pixels // MIB),
         name="backward",
     )(
         src_own,

time: 116 us -> 88.7 us (0.76)
  local copies, waits for them, and re-layouts: 18.3 us -> 1.02 us
  Pallas kernels: 51.8 us -> 41.6 us
    unnamed x11 -> x3, local copies, waits for them, and re-layouts: 17.4 us -> 0.1 us
    pallas_call x1, Pallas kernels: 33.2 us -> 23 us  [shards(): pl.pallas_call(backward_kernel, out_shape=(shape(cotangent.shape, bf16),...]
  transfers between devices with their start and end apart: 19 -> 19, of which waited for: 12 -> 12; matrix products, arithmetic and copies ran while one was open for 0% -> 0% of each run, Pallas kernels for 9% -> 12%
where the time goes in v10:
time: 88.7 us; the launch traced here: 88.3 us
  Pallas kernels  41.6 us (47%)
  waiting for transfers between devices  22.4 us (25%)
  starting transfers between devices  22.3 us (25%)
  local copies, waits for them, and re-layouts  1.02 us (1%)
    pallas_call x1, Pallas kernels, shards(): pl.pallas_call(backward_kernel, out_shape=(shape(cotangent.shape, bf16),...  23 us
    ppermute x10, waiting for transfers between devices, over_view(): return lax.ppermute(array, 'view', [(i, i ^ k) for i in range(view_count)])  15.8 us
    ppermute x10, starting transfers between devices, over_view(): return lax.ppermute(array, 'view', [(i, i ^ k) for i in range(view_count)])  14.3 us
    pallas_call x1, Pallas kernels, shards(): pl.pallas_call(inner_kernel, out_shape=saved + (pltpu.VMEM((inner_count,)...  8.85 us
    pallas_call x1, Pallas kernels, shards(): pl.pallas_call(edge_kernel, out_shape=saved + (shape(load, f32),) * 2 + (...  6.33 us
    ppermute x1, waiting for transfers between devices, shards(): lax.ppermute(rounded, 'plane', far).astype(f32)  2.63 us
    ppermute x1, starting transfers between devices, shards(): received = lax.ppermute(send, 'plane', near)  2.15 us
    ppermute x1, starting transfers between devices, shards(): below = lax.ppermute(up_load, 'plane', up)  2.06 us
  transfers between devices with their start and end apart: 19, of which 12 were waited for; matrix products, arithmetic and copies ran while one was open for 0% of the time, Pallas kernels for 12%

profile of v10, /device:TPU:0, one launch (start us, length us, event | category | flops | bytes accessed | tf_op | source)
XLA Modules:
  0.0 88.3 jit_solution(2918914402227938911)
XLA Ops:
  0.6 0.0 copy-start
  0.7 0.8 dynamic-slice_bitcast_fusion
  1.5 3.0 %collective-permute-start.2 = (bf16[4,16,512]{2,1,0:T(8,128)(2,1)S(1)}, bf16[4,16,512]{2,1,0:T(8,128)(2,1)S(1)}, u32[]{:S(2)}, u32[]{:S(2)}) collective-permute-start(bf16[4,16,512]{2,1,0:T(8,128)(2,1)S(1)} %dynamic-slice_bitcast_fusion), channel_id=1, source_target_pairs={{0,8},{4,12},{8,0},{12,4},{16,24},{20,28},{24,16},{28,20},{1,9},{5... | collective-permute-start | bytes 196616 | tf_op jit(solution)/shard_map/ppermute | solution.py:481
  4.5 2.5 %collective-permute-start.1 = (bf16[4,16,512]{2,1,0:T(8,128)(2,1)S(1)}, bf16[4,16,512]{2,1,0:T(8,128)(2,1)S(1)}, u32[]{:S(2)}, u32[]{:S(2)}) collective-permute-start(bf16[4,16,512]{2,1,0:T(8,128)(2,1)S(1)} %dynamic-slice_bitcast_fusion), channel_id=1, source_target_pairs={{0,24},{4,28},{8,16},{12,20},{16,8},{20,12},{24,0},{28,4},{1,25},{... | collective-permute-start | bytes 196616 | tf_op jit(solution)/shard_map/ppermute | solution.py:481
  7.0 0.1 collective-permute-start
  7.1 2.0 %prep.1 = (f32[4,256,128]{2,1,0:T(8,128)S(1)}, f32[8,8,128]{2,1,0:T(8,128)S(1)}, f32[12,2,64,128]{3,2,1,0:T(8,128)S(1)}) custom-call(f32[8]{0:T(128)} %gate_ref.1, bf16[4,32,512]{2,1,0:T(8,128)(2,1)} %own_hbm.1, bf16[4,12,8,512]{3,2,1,0:T(8,128)(2,1)} %cot_hbm.1), custom_call_target="tpu_custom_call" | custom-call | flops 1000000000 | bytes 4194304 | tf_op jit(solution)/shard_map/prep/pallas_call | solution.py:491
  9.1 0.0 collective-permute-done.2
  9.2 1.6 %collective-permute-start.3 = (bf16[8,16,512]{2,1,0:T(8,128)(2,1)S(1)}, bf16[8,16,512]{2,1,0:T(8,128)(2,1)S(1)}, u32[]{:S(2)}, u32[]{:S(2)}) collective-permute-start(bf16[8,16,512]{2,1,0:T(8,128)(2,1)S(1)} %pad_maximum_fusion.1.rest_0_), channel_id=1, source_target_pairs={{0,4},{4,0},{8,12},{12,8},{16,20},{20,16},{24,28},{28,24},{1,5},{5... | collective-permute-start | bytes 393224 | tf_op jit(solution)/shard_map/ppermute | solution.py:481
  10.7 0.7 collective-permute-done.1
  11.4 2.1 %collective-permute-done = bf16[4,16,512]{2,1,0:T(8,128)(2,1)S(1)} collective-permute-done((bf16[4,16,512]{2,1,0:T(8,128)(2,1)S(1)}, bf16[4,16,512]{2,1,0:T(8,128)(2,1)S(1)}, u32[]{:S(2)}, u32[]{:S(2)}) %collective-permute-start) | collective-permute-done | bytes 65568 | tf_op jit(solution)/shard_map/ppermute | solution.py:481
  13.5 1.6 %collective-permute-start.4 = (bf16[8,16,512]{2,1,0:T(8,128)(2,1)S(1)}, bf16[8,16,512]{2,1,0:T(8,128)(2,1)S(1)}, u32[]{:S(2)}, u32[]{:S(2)}) collective-permute-start(bf16[8,16,512]{2,1,0:T(8,128)(2,1)S(1)} %pad_maximum_fusion.rest_1_), channel_id=1, source_target_pairs={{0,4},{4,0},{8,12},{12,8},{16,20},{20,16},{24,28},{28,24},{1,5},{5... | collective-permute-start | bytes 393224 | tf_op jit(solution)/shard_map/ppermute | solution.py:481
  15.1 0.0 collective-permute-start.5
  15.1 0.5 collective-permute-start.6
  15.6 0.0 collective-permute-done.3.rest_2_
  15.6 0.0 collective-permute-start.7
  15.6 3.3 %collective-permute-done.4.rest_3_ = bf16[8,16,512]{2,1,0:T(8,128)(2,1)S(1)} collective-permute-done((bf16[8,16,512]{2,1,0:T(8,128)(2,1)S(1)}, bf16[8,16,512]{2,1,0:T(8,128)(2,1)S(1)}, u32[]{:S(2)}, u32[]{:S(2)}) %collective-permute-start.4) | collective-permute-done | bytes 131104 | tf_op jit(solution)/shard_map/ppermute | solution.py:481
  18.9 0.0 collective-permute-start.8
  18.9 0.1 constant_dynamic-slice_fusion
  19.0 0.1 copy.14.src_ref
  19.1 0.1 pad_add_fusion.place_ref
  19.2 0.0 collective-permute-done.6.rest_5_
  19.2 0.0 collective-permute-done.7.rest_6_
  19.2 1.1 %collective-permute-done.8.rest_7_ = bf16[8,16,512]{2,1,0:T(8,128)(2,1)S(1)} collective-permute-done((bf16[8,16,512]{2,1,0:T(8,128)(2,1)S(1)}, bf16[8,16,512]{2,1,0:T(8,128)(2,1)S(1)}, u32[]{:S(2)}, u32[]{:S(2)}) %collective-permute-start.8) | collective-permute-done | bytes 131104 | tf_op jit(solution)/shard_map/ppermute | solution.py:514
  20.3 6.3 %forward_edge.1 = (bf16[12,1280,512]{2,1,0:T(8,128)(2,1)S(1)}, f32[12,320,512]{2,1,0:T(8,128)S(1)}, f32[12,40,512]{2,1,0:T(8,128)S(1)}, f32[12,8,512]{2,1,0:T(8,...) custom-call(s32[4,10]{1,0:T(4,128)S(1)} %copy.14.src_ref, ...), custom_call_target="tpu_custom_call" | custom-call | tf_op jit(solution)/shard_map/forward_edge/pallas_call | solution.py:534
  26.6 2.1 %collective-permute-start.9 = (f32[3,2,64,128]{3,2,1,0:T(8,128)S(1)}, f32[3,2,64,128]{3,2,1,0:T(8,128)S(1)}, u32[]{:S(2)}, u32[]{:S(2)}) collective-permute-start(f32[3,2,64,128]{3,2,1,0:T(8,128)S(1)} %get-tuple-element.40.rest_3_), channel_id=1, source_target_pairs={{0,1},{1,2},{2,3},{4,5},{5,6},{6,7},{8,9},{9,10},{10,11},{12,13},{... | collective-permute-start | bytes 589832 | tf_op jit(solution)/shard_map/ppermute | solution.py:555
  28.7 1.5 %collective-permute-start.10 = (f32[3,2,64,128]{3,2,1,0:T(8,128)S(1)}, f32[3,2,64,128]{3,2,1,0:T(8,128)S(1)}, u32[]{:S(2)}, u32[]{:S(2)}) collective-permute-start(f32[3,2,64,128]{3,2,1,0:T(8,128)S(1)} %get-tuple-element.41.rest_1_), channel_id=1, source_target_pairs={{1,0},{2,1},{3,2},{5,4},{6,5},{7,6},{9,8},{10,9},{11,10},{13,12},{... | collective-permute-start | bytes 589832 | tf_op jit(solution)/shard_map/ppermute | solution.py:556
  30.2 8.8 %forward_inner.1 = (bf16[12,1280,512]{2,1,0:T(8,128)(2,1)S(1)}, f32[12,320,512]{2,1,0:T(8,128)S(1)}, f32[12,40,512]{2,1,0:T(8,128)S(1)}, f32[12,8,512]{2,1,0:T(8,128)S(1)}, f32[8,2,64,128]{3,2,1,0:T(8,128)S(1)}) custom-call(f32[8,8,128]{2,1,0:T(8,128)S(1)} %get-tuple-element.36.gates_ref, ...), custom_call_target="tpu_custom_call", output_to_operand_aliasing={{0}: (5, {}), {1}: (6, {}), {2}: (7, {}), {3}: (8, {})} | custom-call | flops 5368709120 | bytes 41943040 | tf_op jit(solution)/shard_map/forward_inner/pallas_call | solution.py:558
  39.0 0.0 collective-permute-done.10.rest_4_
  39.0 23.0 %backward.1 = (bf16[4,12,8,512]{3,2,1,0:T(8,128)(2,1)}, f32[32,16,512]{2,1,0:T(8,128)S(1)}, bf16[32,16,512]{2,1,0:T(8,128)(2,1)S(1)}) custom-call(s32[4,10]{1,0:T(4,128)S(1)} %copy.14.src_ref, s32[2]{0:T(128)S(1)} %pad_add_fusion.place_ref, f32[3,8,8]{2,1,0:T(8,128)} %taps_ref.1, f32[8,8,128]{2,1,0:T(8,128)S(1)} %get-tuple-element.36.gates_ref, ...), custom_call_target="tpu_custom_call" | custom-call | tf_op jit(solution)/shard_map/backward/pallas_call | solution.py:577
  62.0 2.1 %collective-permute-start.11 = (bf16[32,16,512]{2,1,0:T(8,128)(2,1)S(1)}, bf16[32,16,512]{2,1,0:T(8,128)(2,1)S(1)}, u32[]{:S(2)}, u32[]{:S(2)}) collective-permute-start(bf16[32,16,512]{2,1,0:T(8,128)(2,1)S(1)} %get-tuple-element.55), channel_id=1, source_target_pairs={{0,1},{1,0},{2,3},{3,2},{4,5},{5,4},{6,7},{7,6},{8,9},{9,8},{10,11... | collective-permute-start | bytes 1572872 | tf_op jit(solution)/shard_map/ppermute | solution.py:606
  64.2 1.5 %collective-permute-done.11.received_ref.after_ref = bf16[32,16,512]{2,1,0:T(8,128)(2,1)S(1)} collective-permute-done((bf16[32,16,512]{2,1,0:T(8,128)(2,1)S(1)}, bf16[32,16,512]{2,1,0:T(8,128)(2,1)S(1)}, u32[]{:S(2)}, u32[]{:S(2)}) %collective-permute-start.11) | collective-permute-done | bytes 524320 | tf_op jit(solution)/shard_map/ppermute | solution.py:606
  65.7 0.1 split.2
  65.8 1.6 %collective-permute-start.12 = (bf16[8,16,512]{2,1,0:T(8,128)(2,1)S(1)}, bf16[8,16,512]{2,1,0:T(8,128)(2,1)S(1)}, u32[]{:S(2)}, u32[]{:S(2)}) collective-permute-start(bf16[8,16,512]{2,1,0:T(8,128)(2,1)S(1)} %get-tuple-element.57), channel_id=1, source_target_pairs={{0,4},{4,0},{8,12},{12,8},{16,20},{20,16},{24,28},{28,24},{1,5},{5... | collective-permute-start | bytes 393224 | tf_op jit(solution)/shard_map/ppermute | solution.py:481
  67.4 4.2 %collective-permute-done.12.received_ref = bf16[8,16,512]{2,1,0:T(8,128)(2,1)S(1)} collective-permute-done((bf16[8,16,512]{2,1,0:T(8,128)(2,1)S(1)}, bf16[8,16,512]{2,1,0:T(8,128)(2,1)S(1)}, u32[]{:S(2)}, u32[]{:S(2)}) %collective-permute-start.12) | collective-permute-done | bytes 131104 | tf_op jit(solution)/shard_map/ppermute | solution.py:481
  71.7 0.1 split.3
  71.7 1.6 %collective-permute-start.13 = (bf16[8,16,512]{2,1,0:T(8,128)(2,1)S(1)}, bf16[8,16,512]{2,1,0:T(8,128)(2,1)S(1)}, u32[]{:S(2)}, u32[]{:S(2)}) collective-permute-start(bf16[8,16,512]{2,1,0:T(8,128)(2,1)S(1)} %get-tuple-element.60), channel_id=1, source_target_pairs={{0,4},{4,0},{8,12},{12,8},{16,20},{20,16},{24,28},{28,24},{1,5},{5... | collective-permute-start | bytes 393224 | tf_op jit(solution)/shard_map/ppermute | solution.py:481
  73.3 0.9 collective-permute-start.14
  74.2 1.4 %collective-permute-start.15 = (bf16[4,16,512]{2,1,0:T(8,128)(2,1)S(1)}, bf16[4,16,512]{2,1,0:T(8,128)(2,1)S(1)}, u32[]{:S(2)}, u32[]{:S(2)}) collective-permute-start(bf16[4,16,512]{2,1,0:T(8,128)(2,1)S(1)} %get-tuple-element.62), channel_id=1, source_target_pairs={{0,24},{4,28},{8,16},{12,20},{16,8},{20,12},{24,0},{28,4},{1,25},{... | collective-permute-start | bytes 196616 | tf_op jit(solution)/shard_map/ppermute | solution.py:481
  75.6 1.2 %collective-permute-done.13.received_ref = bf16[8,16,512]{2,1,0:T(8,128)(2,1)S(1)} collective-permute-done((bf16[8,16,512]{2,1,0:T(8,128)(2,1)S(1)}, bf16[8,16,512]{2,1,0:T(8,128)(2,1)S(1)}, u32[]{:S(2)}, u32[]{:S(2)}) %collective-permute-start.13) | collective-permute-done | bytes 131104 | tf_op jit(solution)/shard_map/ppermute | solution.py:481
  76.8 0.1 collective-permute-start.16
  76.9 3.5 %collective-permute-done.15 = bf16[4,16,512]{2,1,0:T(8,128)(2,1)S(1)} collective-permute-done((bf16[4,16,512]{2,1,0:T(8,128)(2,1)S(1)}, bf16[4,16,512]{2,1,0:T(8,128)(2,1)S(1)}, u32[]{:S(2)}, u32[]{:S(2)}) %collective-permute-start.15) | collective-permute-done | bytes 65568 | tf_op jit(solution)/shard_map/ppermute | solution.py:481
  80.4 0.1 collective-permute-done.14
  80.5 0.8 collective-permute-done.16
  81.3 1.7 %collective-permute-start.17 = (bf16[4,16,512]{2,1,0:T(8,128)(2,1)S(1)}, bf16[4,16,512]{2,1,0:T(8,128)(2,1)S(1)}, u32[]{:S(2)}, u32[]{:S(2)}) collective-permute-start(bf16[4,16,512]{2,1,0:T(8,128)(2,1)S(1)} %add_convert_fusion), channel_id=1, source_target_pairs={{0,2},{1,3},{2,0},{3,1},{4,6},{5,7},{6,4},{7,5},{8,10},{9,11},{10,... | collective-permute-start | bytes 196616 | tf_op jit(solution)/shard_map/ppermute | solution.py:633
  83.0 2.6 %collective-permute-done.17 = bf16[4,16,512]{2,1,0:T(8,128)(2,1)S(1)} collective-permute-done((bf16[4,16,512]{2,1,0:T(8,128)(2,1)S(1)}, bf16[4,16,512]{2,1,0:T(8,128)(2,1)S(1)}, u32[]{:S(2)}, u32[]{:S(2)}) %collective-permute-start.17) | collective-permute-done | bytes 65568 | tf_op jit(solution)/shard_map/ppermute | solution.py:633
  85.6 0.1 collective-permute-start.18
  85.7 1.3 %collective-permute-done.18.other_ref = f32[4,16,512]{2,1,0:T(8,128)S(1)} collective-permute-done((f32[4,16,512]{2,1,0:T(8,128)S(1)}, f32[4,16,512]{2,1,0:T(8,128)S(1)}, u32[]{:S(2)}, u32[]{:S(2)}) %collective-permute-start.18) | collective-permute-done | bytes 131104 | tf_op jit(solution)/shard_map/ppermute | solution.py:634
  87.1 1.3 %join.1 = f32[4,32,512]{2,1,0:T(8,128)} custom-call(s32[2]{0:T(128)S(1)} %pad_add_fusion.place_ref, f32[4,16,512]{2,1,0:T(8,128)S(1)} %convert_add_fusion.mine_ref, f32[4,16,512]{2,1,0:T(8,128)S(1)} %collective-permute-done.18.other_ref), custom_call_target="tpu_custom_call" | custom-call | tf_op jit(solution)/shard_map/join/pallas_call | solution.py:635
  (9 shorter events, 0.1 us)
Async XLA Ops:
  0.6 18.3 %copy-start = (s32[32,10]{0,1:T(8,128)S(1)}, s32[32,10]{0,1:T(8,128)}, u32[]{:S(2)}) copy-start(s32[32,10]{0,1:T(8,128)} %param.7) | copy-start | bytes 3844
  1.5 7.6 %collective-permute-start.2 = (bf16[4,16,512]{2,1,0:T(8,128)(2,1)S(1)}, bf16[4,16,512]{2,1,0:T(8,128)(2,1)S(1)}, u32[]{:S(2)}, u32[]{:S(2)}) collective-permute-start(bf16[4,16,512]{2,1,0:T(8,128)(2,1)S(1)} %dynamic-slice_bitcast_fusion), channel_id=1, source_target_pairs={{0,8},{4,12},{8,0},{12,4},{16,24},{20,28},{24,16},{28,20},{1,9},{5... | collective-permute-start | bytes 196616 | tf_op jit(solution)/shard_map/ppermute | solution.py:481
  4.5 6.9 %collective-permute-start.1 = (bf16[4,16,512]{2,1,0:T(8,128)(2,1)S(1)}, bf16[4,16,512]{2,1,0:T(8,128)(2,1)S(1)}, u32[]{:S(2)}, u32[]{:S(2)}) collective-permute-start(bf16[4,16,512]{2,1,0:T(8,128)(2,1)S(1)} %dynamic-slice_bitcast_fusion), channel_id=1, source_target_pairs={{0,24},{4,28},{8,16},{12,20},{16,8},{20,12},{24,0},{28,4},{1,25},{... | collective-permute-start | bytes 196616 | tf_op jit(solution)/shard_map/ppermute | solution.py:481
  7.0 6.4 %collective-permute-start = (bf16[4,16,512]{2,1,0:T(8,128)(2,1)S(1)}, bf16[4,16,512]{2,1,0:T(8,128)(2,1)S(1)}, u32[]{:S(2)}, u32[]{:S(2)}) collective-permute-start(bf16[4,16,512]{2,1,0:T(8,128)(2,1)S(1)} %dynamic-slice_bitcast_fusion), channel_id=1, source_target_pairs={{0,16},{4,20},{8,24},{12,28},{16,0},{20,4},{24,8},{28,12},{1,17},{... | collective-permute-start | bytes 196616 | tf_op jit(solution)/shard_map/ppermute | solution.py:481
  9.2 6.4 %collective-permute-start.3 = (bf16[8,16,512]{2,1,0:T(8,128)(2,1)S(1)}, bf16[8,16,512]{2,1,0:T(8,128)(2,1)S(1)}, u32[]{:S(2)}, u32[]{:S(2)}) collective-permute-start(bf16[8,16,512]{2,1,0:T(8,128)(2,1)S(1)} %pad_maximum_fusion.1.rest_0_), channel_id=1, source_target_pairs={{0,4},{4,0},{8,12},{12,8},{16,20},{20,16},{24,28},{28,24},{1,5},{5... | collective-permute-start | bytes 393224 | tf_op jit(solution)/shard_map/ppermute | solution.py:481
  13.5 5.4 %collective-permute-start.4 = (bf16[8,16,512]{2,1,0:T(8,128)(2,1)S(1)}, bf16[8,16,512]{2,1,0:T(8,128)(2,1)S(1)}, u32[]{:S(2)}, u32[]{:S(2)}) collective-permute-start(bf16[8,16,512]{2,1,0:T(8,128)(2,1)S(1)} %pad_maximum_fusion.rest_1_), channel_id=1, source_target_pairs={{0,4},{4,0},{8,12},{12,8},{16,20},{20,16},{24,28},{28,24},{1,5},{5... | collective-permute-start | bytes 393224 | tf_op jit(solution)/shard_map/ppermute | solution.py:481
  15.1 4.1 %collective-permute-start.5 = (bf16[8,16,512]{2,1,0:T(8,128)(2,1)S(1)}, bf16[8,16,512]{2,1,0:T(8,128)(2,1)S(1)}, u32[]{:S(2)}, u32[]{:S(2)}) collective-permute-start(bf16[8,16,512]{2,1,0:T(8,128)(2,1)S(1)} %pad_maximum_fusion.1.rest_0_), channel_id=1, source_target_pairs={{0,1},{1,0},{2,3},{3,2},{4,5},{5,4},{6,7},{7,6},{8,9},{9,8},{10,11... | collective-permute-start | bytes 393224 | tf_op jit(solution)/shard_map/ppermute | solution.py:514
  15.1 4.1 %collective-permute-start.6 = (bf16[8,16,512]{2,1,0:T(8,128)(2,1)S(1)}, bf16[8,16,512]{2,1,0:T(8,128)(2,1)S(1)}, u32[]{:S(2)}, u32[]{:S(2)}) collective-permute-start(bf16[8,16,512]{2,1,0:T(8,128)(2,1)S(1)} %pad_maximum_fusion.rest_1_), channel_id=1, source_target_pairs={{0,1},{1,0},{2,3},{3,2},{4,5},{5,4},{6,7},{7,6},{8,9},{9,8},{10,11... | collective-permute-start | bytes 393224 | tf_op jit(solution)/shard_map/ppermute | solution.py:514
  15.6 3.6 %collective-permute-start.7 = (bf16[8,16,512]{2,1,0:T(8,128)(2,1)S(1)}, bf16[8,16,512]{2,1,0:T(8,128)(2,1)S(1)}, u32[]{:S(2)}, u32[]{:S(2)}) collective-permute-start(bf16[8,16,512]{2,1,0:T(8,128)(2,1)S(1)} %collective-permute-done.3.rest_2_), channel_id=1, source_target_pairs={{0,1},{1,0},{2,3},{3,2},{4,5},{5,4},{6,7},{7,6},{8,9},{9,8},{10,11... | collective-permute-start | bytes 393224 | tf_op jit(solution)/shard_map/ppermute | solution.py:514
  18.9 1.3 %collective-permute-start.8 = (bf16[8,16,512]{2,1,0:T(8,128)(2,1)S(1)}, bf16[8,16,512]{2,1,0:T(8,128)(2,1)S(1)}, u32[]{:S(2)}, u32[]{:S(2)}) collective-permute-start(bf16[8,16,512]{2,1,0:T(8,128)(2,1)S(1)} %collective-permute-done.4.rest_3_), channel_id=1, source_target_pairs={{0,1},{1,0},{2,3},{3,2},{4,5},{5,4},{6,7},{7,6},{8,9},{9,8},{10,11... | collective-permute-start | bytes 393224 | tf_op jit(solution)/shard_map/ppermute | solution.py:514
  26.6 12.4 %collective-permute-start.9 = (f32[3,2,64,128]{3,2,1,0:T(8,128)S(1)}, f32[3,2,64,128]{3,2,1,0:T(8,128)S(1)}, u32[]{:S(2)}, u32[]{:S(2)}) collective-permute-start(f32[3,2,64,128]{3,2,1,0:T(8,128)S(1)} %get-tuple-element.40.rest_3_), channel_id=1, source_target_pairs={{0,1},{1,2},{2,3},{4,5},{5,6},{6,7},{8,9},{9,10},{10,11},{12,13},{... | collective-permute-start | bytes 589832 | tf_op jit(solution)/shard_map/ppermute | solution.py:555
  28.7 10.3 %collective-permute-start.10 = (f32[3,2,64,128]{3,2,1,0:T(8,128)S(1)}, f32[3,2,64,128]{3,2,1,0:T(8,128)S(1)}, u32[]{:S(2)}, u32[]{:S(2)}) collective-permute-start(f32[3,2,64,128]{3,2,1,0:T(8,128)S(1)} %get-tuple-element.41.rest_1_), channel_id=1, source_target_pairs={{1,0},{2,1},{3,2},{5,4},{6,5},{7,6},{9,8},{10,9},{11,10},{13,12},{... | collective-permute-start | bytes 589832 | tf_op jit(solution)/shard_map/ppermute | solution.py:556
  62.0 3.7 %collective-permute-start.11 = (bf16[32,16,512]{2,1,0:T(8,128)(2,1)S(1)}, bf16[32,16,512]{2,1,0:T(8,128)(2,1)S(1)}, u32[]{:S(2)}, u32[]{:S(2)}) collective-permute-start(bf16[32,16,512]{2,1,0:T(8,128)(2,1)S(1)} %get-tuple-element.55), channel_id=1, source_target_pairs={{0,1},{1,0},{2,3},{3,2},{4,5},{5,4},{6,7},{7,6},{8,9},{9,8},{10,11... | collective-permute-start | bytes 1572872 | tf_op jit(solution)/shard_map/ppermute | solution.py:606
  65.8 5.8 %collective-permute-start.12 = (bf16[8,16,512]{2,1,0:T(8,128)(2,1)S(1)}, bf16[8,16,512]{2,1,0:T(8,128)(2,1)S(1)}, u32[]{:S(2)}, u32[]{:S(2)}) collective-permute-start(bf16[8,16,512]{2,1,0:T(8,128)(2,1)S(1)} %get-tuple-element.57), channel_id=1, source_target_pairs={{0,4},{4,0},{8,12},{12,8},{16,20},{20,16},{24,28},{28,24},{1,5},{5... | collective-permute-start | bytes 393224 | tf_op jit(solution)/shard_map/ppermute | solution.py:481
  71.7 5.0 %collective-permute-start.13 = (bf16[8,16,512]{2,1,0:T(8,128)(2,1)S(1)}, bf16[8,16,512]{2,1,0:T(8,128)(2,1)S(1)}, u32[]{:S(2)}, u32[]{:S(2)}) collective-permute-start(bf16[8,16,512]{2,1,0:T(8,128)(2,1)S(1)} %get-tuple-element.60), channel_id=1, source_target_pairs={{0,4},{4,0},{8,12},{12,8},{16,20},{20,16},{24,28},{28,24},{1,5},{5... | collective-permute-start | bytes 393224 | tf_op jit(solution)/shard_map/ppermute | solution.py:481
  73.3 7.1 %collective-permute-start.14 = (bf16[4,16,512]{2,1,0:T(8,128)(2,1)S(1)}, bf16[4,16,512]{2,1,0:T(8,128)(2,1)S(1)}, u32[]{:S(2)}, u32[]{:S(2)}) collective-permute-start(bf16[4,16,512]{2,1,0:T(8,128)(2,1)S(1)} %get-tuple-element.58.after_ref), channel_id=1, source_target_pairs={{0,16},{4,20},{8,24},{12,28},{16,0},{20,4},{24,8},{28,12},{1,17},{... | collective-permute-start | bytes 196616 | tf_op jit(solution)/shard_map/ppermute | solution.py:481
  74.2 6.2 %collective-permute-start.15 = (bf16[4,16,512]{2,1,0:T(8,128)(2,1)S(1)}, bf16[4,16,512]{2,1,0:T(8,128)(2,1)S(1)}, u32[]{:S(2)}, u32[]{:S(2)}) collective-permute-start(bf16[4,16,512]{2,1,0:T(8,128)(2,1)S(1)} %get-tuple-element.62), channel_id=1, source_target_pairs={{0,24},{4,28},{8,16},{12,20},{16,8},{20,12},{24,0},{28,4},{1,25},{... | collective-permute-start | bytes 196616 | tf_op jit(solution)/shard_map/ppermute | solution.py:481
  76.8 4.5 %collective-permute-start.16 = (bf16[4,16,512]{2,1,0:T(8,128)(2,1)S(1)}, bf16[4,16,512]{2,1,0:T(8,128)(2,1)S(1)}, u32[]{:S(2)}, u32[]{:S(2)}) collective-permute-start(bf16[4,16,512]{2,1,0:T(8,128)(2,1)S(1)} %get-tuple-element.63), channel_id=1, source_target_pairs={{0,8},{4,12},{8,0},{12,4},{16,24},{20,28},{24,16},{28,20},{1,9},{5... | collective-permute-start | bytes 196616 | tf_op jit(solution)/shard_map/ppermute | solution.py:481
  81.3 4.3 %collective-permute-start.17 = (bf16[4,16,512]{2,1,0:T(8,128)(2,1)S(1)}, bf16[4,16,512]{2,1,0:T(8,128)(2,1)S(1)}, u32[]{:S(2)}, u32[]{:S(2)}) collective-permute-start(bf16[4,16,512]{2,1,0:T(8,128)(2,1)S(1)} %add_convert_fusion), channel_id=1, source_target_pairs={{0,2},{1,3},{2,0},{3,1},{4,6},{5,7},{6,4},{7,5},{8,10},{9,11},{10,... | collective-permute-start | bytes 196616 | tf_op jit(solution)/shard_map/ppermute | solution.py:633
  85.6 1.4 %collective-permute-start.18 = (f32[4,16,512]{2,1,0:T(8,128)S(1)}, f32[4,16,512]{2,1,0:T(8,128)S(1)}, u32[]{:S(2)}, u32[]{:S(2)}) collective-permute-start(f32[4,16,512]{2,1,0:T(8,128)S(1)} %convert_add_fusion.mine_ref), channel_id=1, source_target_pairs={{0,1},{1,0},{2,3},{3,2},{4,5},{5,4},{6,7},{7,6},{8,9},{9,8},{10,11... | collective-permute-start | bytes 393224 | tf_op jit(solution)/shard_map/ppermute | solution.py:634

commit v11 on v8

--- a/solution.py
+++ b/solution.py
@@ -247,12 +247,10 @@
     cot_ref,
     regular_ref,
     cost,
-    grad_ref,
     slope,
     smooth,
 ):
-    planes = grad_ref.shape[0]
-    local_views, _, groups, pixels = regular_ref.shape
+    local_views, planes, groups, pixels = regular_ref.shape
     cost[0:2] = below_ref[0:2]
     cost[2:4] = down_ref[0:2]
     cost[4:planes] = inner_ref[...]
@@ -284,7 +282,13 @@
             sig = jax.nn.sigmoid(pre)
             both = pl.ds(plane, 2)
             slope[both, :, rows, :] = slope[both, :, rows, :] * (sig * (1.0 + pre * (1.0 - sig)))
-            smooth[both, :, rows, :] = pre * sig
+            smooth[:, :, rows, :] = pre * sig
+        for view in range(local_views):
+            for tile in range(pixels // LANE):
+                first = (tile % 2) * local_views + view
+                for i, at in ((1, jnp.minimum(plane, planes - 1)), (0, jnp.abs(plane - 1))):
+                    kept = smooth[i, tile // 2, pl.ds(first, groups, stride=SUB), :]
+                    regular_ref[view, at, :, pl.ds(tile * LANE, LANE)] = kept.astype(jnp.bfloat16)
         return carry
 
     lax.fori_loop(0, (planes + 2) // 2, forward_planes, 0)
@@ -296,14 +300,7 @@
             lambda k, g, o: taps_ref[k, o, g],
         )
         for g in range(G):
-            grad_ref[pl.ds(plane, 2), :, pl.ds(g * SUB, SUB), :] = grads[g]
-        for view in range(local_views):
-            for tile in range(pixels // LANE):
-                first = (tile % 2) * local_views + view
-                for i in range(2):
-                    regular_ref[view, plane + i, :, pl.ds(tile * LANE, LANE)] = smooth[
-                        plane + i + 1, tile // 2, pl.ds(first, groups, stride=SUB), :
-                    ].astype(jnp.bfloat16)
+            slope[pl.ds(plane, 2), :, pl.ds(g * SUB, SUB), :] = grads[g]
         return carry
 
     lax.fori_loop(0, planes // 2, backward_planes, 0)
@@ -313,7 +310,7 @@
     halo_refs = rest[:6]
     warped_ref, corr_ref, sig_ref, rden_ref = rest[6:10]
     regular_ref, keep_ref, send_ref = rest[10:13]
-    cost, grad_ref, slope, smooth, rows, acc, dref, held, sems, dense = rest[13:]
+    cost, grad_ref, smooth, rows, acc, dref, held, sems = rest[13:]
     count = w_ref.shape[0]
     pairs = sig_ref.shape[1]
     tiles = pairs // SUB
@@ -322,7 +319,7 @@
     local_views = src_ref.shape[0]
     low = low_half()
 
-    def vector(plane, tile, offset):
+    def vector(plane, tile, offset, side):
         lanes = pl.ds(tile * LANE, LANE)
         target = pl.ds(offset * pixels + tile * LANE, LANE)
         pack = tile // 2
@@ -357,7 +354,7 @@
                     ],
                     axis=0,
                 )
-                rows[span, target] = both.astype(jnp.bfloat16)
+                rows[side, span, target] = both.astype(jnp.bfloat16)
                 warped = (
                     warped_ref[plane, span, lanes]
                     .astype(jnp.float32)
@@ -382,34 +379,40 @@
             for offset in range(2)
         ]
 
+    def matmul(side):
+        product = jnp.dot(rows[side], held[side], preferred_element_type=jnp.float32)
+        for tile in range(lane_tiles):
+            acc[tile] += product[:, tile * LANE : (tile + 1) * LANE]
+
     for copy in fetch(0):
         copy.start()
     acc[...] = jnp.zeros_like(acc)
     dref[...] = jnp.zeros_like(dref)
-    depth_conv(taps_ref, *halo_refs, regular_ref, cost, grad_ref, slope, smooth)
+    rows[1] = jnp.zeros_like(rows[1])
+    held[1] = jnp.zeros_like(held[1])
+    depth_conv(taps_ref, *halo_refs, regular_ref, cost, grad_ref, smooth)
 
     def two_planes(turn, carry):
+        side = lax.rem(turn, 2)
+        matmul(1 - side)
         for copy in fetch(turn + 1):
             copy.start()
+        for offset in range(2):
+            for tile in range(lane_tiles):
+                vector(2 * turn + offset, tile, offset, side)
         for copy in fetch(turn):
             copy.wait()
-        for offset in range(2):
-            for tile in range(lane_tiles):
-                vector(2 * turn + offset, tile, offset)
-        product = jnp.dot(
-            rows[...], held[lax.rem(turn, 2)], preferred_element_type=jnp.float32
-        )
-        for tile in range(lane_tiles):
-            acc[tile] += product[:, tile * LANE : (tile + 1) * LANE]
         return carry
 
     lax.fori_loop(0, turns, two_planes, 0)
+    matmul((turns - 1) % 2)
     for copy in fetch(turns):
         copy.wait()
     own_index = place_ref[0]
     parity = place_ref[1]
     blocks = keep_ref.shape[1] // SUB
-    for target, held_side in ((dense, 1 - parity), (keep_ref, parity)):
+    target = keep_ref
+    for held_side in (1 - parity, parity):
         target[...] = jnp.zeros_like(target)
         for tile in range(lane_tiles):
             lanes = pl.ds(tile * LANE, LANE)
@@ -425,7 +428,7 @@
                     target[view, part, lanes] = total
         for pair in range(pairs):
             view = src_ref[pair % local_views, pair // local_views]
-            slot = position(view, own_index, local_views, dense.shape[0] // local_views)
+            slot = position(view, own_index, local_views, keep_ref.shape[0] // local_views)
             for block in range(blocks):
                 first = (2 * block + held_side) * (SUB * pairs) + pair
                 part = pl.ds(block * SUB, SUB)
@@ -433,7 +436,8 @@
                     target[slot, part, pl.ds(tile * LANE, LANE)] += acc[
                         tile, pl.ds(first, SUB, stride=pairs), :
                     ]
-    send_ref[...] = dense[...].astype(jnp.bfloat16)
+        if held_side is not parity:
+            send_ref[...] = target[...].astype(jnp.bfloat16)
 
 
 def split_kernel(first, keep_ref, received_ref, after_ref, even_ref, send_ref):
@@ -586,17 +590,15 @@
         out_specs=(vmem,) * 3,
         scratch_shapes=[
             pltpu.VMEM((planes + 4,) + packed, f32),
-            pltpu.VMEM((planes,) + packed, f32),
             pltpu.VMEM((planes + 2,) + packed, f32),
-            pltpu.VMEM((planes + 2,) + packed, f32),
-            pltpu.VMEM((channels * pairs, 2 * pixels), bf16),
+            pltpu.VMEM((2,) + packed, f32),
+            pltpu.VMEM((2, channels * pairs, 2 * pixels), bf16),
             pltpu.VMEM((pixels // LANE, channels * pairs, LANE), f32),
             pltpu.VMEM((pixels // LANE, channels * SUB, LANE), f32),
             pltpu.VMEM((2, 2 * pixels, pixels), bf16),
             pltpu.SemaphoreType.DMA((2, 2)),
-            pltpu.VMEM(returned, f32),
         ],
-        compiler_params=params(14 + 5 * all_views * channels * pixels // MIB),
+        compiler_params=params(16 + 5 * all_views * channels * pixels // MIB),
         name="backward",
     )(
         src_own,
@@ -639,10 +641,9 @@
     total = rounded.astype(f32) + lax.ppermute(rounded, "plane", far).astype(f32)
     other = lax.ppermute(total, "plane", near)
     cut = (local_views, blocks, 1, share, pixels)
-    first = jnp.where(parity == 0, total, other).reshape(cut)
-    second = jnp.where(parity == 0, other, total).reshape(cut)
-    feature_grads = jnp.concatenate([first, second], axis=2).reshape(features.shape)
-    return (regular, feature_grads)
+    is_mine = jnp.arange(2).reshape(1, 1, 2, 1, 1) == parity
+    feature_grads = jnp.where(is_mine, total.reshape(cut), other.reshape(cut))
+    return (regular, feature_grads.reshape(features.shape))
 
 
 def solution(mesh):

time: 83.8 us -> 106 us (1.26)
  local copies, waits for them, and re-layouts: 1.75 us -> 18.5 us
  Pallas kernels: 36.1 us -> 41.1 us
    unnamed x3 -> x11, local copies, waits for them, and re-layouts: 0.1 us -> 17.4 us
    pallas_call x1, Pallas kernels: 18.7 us -> 23.7 us  [shards(): pl.pallas_call(backward_kernel, out_shape=(shape(cotangent.shape, bf16),...]
  transfers between devices with their start and end apart: 19 -> 19, of which waited for: 12 -> 12; matrix products, arithmetic and copies ran while one was open for 0% -> 0% of each run, Pallas kernels for 13% -> 10%
where the time goes in v11:
time: 106 us
  Pallas kernels  41.1 us (39%)
  starting transfers between devices  22.3 us (21%)
  waiting for transfers between devices  22.3 us (21%)
  local copies, waits for them, and re-layouts  18.5 us (17%)
    pallas_call x1, Pallas kernels, shards(): pl.pallas_call(backward_kernel, out_shape=(shape(cotangent.shape, bf16),...  23.7 us
    unnamed x11, local copies, waits for them, and re-layouts  17.4 us
    ppermute x10, waiting for transfers between devices, over_view(): return lax.ppermute(array, 'view', [(i, i ^ k) for i in range(view_count)])  15.8 us
    ppermute x10, starting transfers between devices, over_view(): return lax.ppermute(array, 'view', [(i, i ^ k) for i in range(view_count)])  14.3 us
    pallas_call x1, Pallas kernels, shards(): pl.pallas_call(inner_kernel, out_shape=saved + (pltpu.VMEM((inner_count,)...  8.85 us
    pallas_call x1, Pallas kernels, shards(): pl.pallas_call(edge_kernel, out_shape=saved + (shape(load, f32),) * 2 + (...  6.33 us
    ppermute x1, waiting for transfers between devices, shards(): lax.ppermute(rounded, 'plane', far).astype(f32)  2.63 us
    ppermute x1, starting transfers between devices, shards(): received = lax.ppermute(send, 'plane', near)  2.15 us
  transfers between devices with their start and end apart: 19, of which 12 were waited for; matrix products, arithmetic and copies ran while one was open for 0% of the time, Pallas kernels for 10%

profile of v11, /device:TPU:0, one launch (start us, length us, event | category | flops | bytes accessed | tf_op | source)
XLA Modules:
  0.0 105.8 jit_solution(5624362637179880559)
XLA Ops:
  0.6 0.0 copy-start
  0.7 0.8 dynamic-slice_bitcast_fusion
  1.5 3.0 %collective-permute-start.2 = (bf16[4,16,512]{2,1,0:T(8,128)(2,1)S(1)}, bf16[4,16,512]{2,1,0:T(8,128)(2,1)S(1)}, u32[]{:S(2)}, u32[]{:S(2)}) collective-permute-start(bf16[4,16,512]{2,1,0:T(8,128)(2,1)S(1)} %dynamic-slice_bitcast_fusion), channel_id=1, source_target_pairs={{0,8},{4,12},{8,0},{12,4},{16,24},{20,28},{24,16},{28,20},{1,9},{5... | collective-permute-start | bytes 196616 | tf_op jit(solution)/shard_map/ppermute | solution.py:491
  4.5 2.5 %collective-permute-start.1 = (bf16[4,16,512]{2,1,0:T(8,128)(2,1)S(1)}, bf16[4,16,512]{2,1,0:T(8,128)(2,1)S(1)}, u32[]{:S(2)}, u32[]{:S(2)}) collective-permute-start(bf16[4,16,512]{2,1,0:T(8,128)(2,1)S(1)} %dynamic-slice_bitcast_fusion), channel_id=1, source_target_pairs={{0,24},{4,28},{8,16},{12,20},{16,8},{20,12},{24,0},{28,4},{1,25},{... | collective-permute-start | bytes 196616 | tf_op jit(solution)/shard_map/ppermute | solution.py:491
  7.0 0.1 collective-permute-start
  7.1 2.0 %prep.1 = (f32[4,256,128]{2,1,0:T(8,128)S(1)}, f32[8,8,128]{2,1,0:T(8,128)S(1)}, f32[12,2,64,128]{3,2,1,0:T(8,128)S(1)}) custom-call(f32[8]{0:T(128)} %gate_ref.1, bf16[4,32,512]{2,1,0:T(8,128)(2,1)} %own_hbm.1, bf16[4,12,8,512]{3,2,1,0:T(8,128)(2,1)} %cot_hbm.1), custom_call_target="tpu_custom_call" | custom-call | flops 1000000000 | bytes 4194304 | tf_op jit(solution)/shard_map/prep/pallas_call | solution.py:501
  9.1 0.0 collective-permute-done.2
  9.2 1.6 %collective-permute-start.3 = (bf16[8,16,512]{2,1,0:T(8,128)(2,1)S(1)}, bf16[8,16,512]{2,1,0:T(8,128)(2,1)S(1)}, u32[]{:S(2)}, u32[]{:S(2)}) collective-permute-start(bf16[8,16,512]{2,1,0:T(8,128)(2,1)S(1)} %pad_maximum_fusion.1.rest_0_), channel_id=1, source_target_pairs={{0,4},{4,0},{8,12},{12,8},{16,20},{20,16},{24,28},{28,24},{1,5},{5... | collective-permute-start | bytes 393224 | tf_op jit(solution)/shard_map/ppermute | solution.py:491
  10.7 0.7 collective-permute-done.1
  11.4 2.1 %collective-permute-done = bf16[4,16,512]{2,1,0:T(8,128)(2,1)S(1)} collective-permute-done((bf16[4,16,512]{2,1,0:T(8,128)(2,1)S(1)}, bf16[4,16,512]{2,1,0:T(8,128)(2,1)S(1)}, u32[]{:S(2)}, u32[]{:S(2)}) %collective-permute-start) | collective-permute-done | bytes 65568 | tf_op jit(solution)/shard_map/ppermute | solution.py:491
  13.5 1.6 %collective-permute-start.4 = (bf16[8,16,512]{2,1,0:T(8,128)(2,1)S(1)}, bf16[8,16,512]{2,1,0:T(8,128)(2,1)S(1)}, u32[]{:S(2)}, u32[]{:S(2)}) collective-permute-start(bf16[8,16,512]{2,1,0:T(8,128)(2,1)S(1)} %pad_maximum_fusion.rest_1_), channel_id=1, source_target_pairs={{0,4},{4,0},{8,12},{12,8},{16,20},{20,16},{24,28},{28,24},{1,5},{5... | collective-permute-start | bytes 393224 | tf_op jit(solution)/shard_map/ppermute | solution.py:491
  15.1 0.5 collective-permute-start.6
  15.6 0.0 collective-permute-start.7
  15.6 3.3 %collective-permute-done.4.rest_3_ = bf16[8,16,512]{2,1,0:T(8,128)(2,1)S(1)} collective-permute-done((bf16[8,16,512]{2,1,0:T(8,128)(2,1)S(1)}, bf16[8,16,512]{2,1,0:T(8,128)(2,1)S(1)}, u32[]{:S(2)}, u32[]{:S(2)}) %collective-permute-start.4) | collective-permute-done | bytes 131104 | tf_op jit(solution)/shard_map/ppermute | solution.py:491
  18.9 0.1 constant_dynamic-slice_fusion
  19.0 0.1 copy.14.src_ref
  19.1 0.1 pad_add_fusion.place_ref
  19.2 1.1 %collective-permute-done.8.rest_7_ = bf16[8,16,512]{2,1,0:T(8,128)(2,1)S(1)} collective-permute-done((bf16[8,16,512]{2,1,0:T(8,128)(2,1)S(1)}, bf16[8,16,512]{2,1,0:T(8,128)(2,1)S(1)}, u32[]{:S(2)}, u32[]{:S(2)}) %collective-permute-start.8) | collective-permute-done | bytes 131104 | tf_op jit(solution)/shard_map/ppermute | solution.py:524
  20.3 6.3 %forward_edge.1 = (bf16[12,1280,512]{2,1,0:T(8,128)(2,1)S(1)}, f32[12,320,512]{2,1,0:T(8,128)S(1)}, f32[12,40,512]{2,1,0:T(8,128)S(1)}, f32[12,8,512]{2,1,0:T(8,...) custom-call(s32[4,10]{1,0:T(4,128)S(1)} %copy.14.src_ref, ...), custom_call_target="tpu_custom_call" | custom-call | tf_op jit(solution)/shard_map/forward_edge/pallas_call | solution.py:544
  26.6 2.1 %collective-permute-start.9 = (f32[3,2,64,128]{3,2,1,0:T(8,128)S(1)}, f32[3,2,64,128]{3,2,1,0:T(8,128)S(1)}, u32[]{:S(2)}, u32[]{:S(2)}) collective-permute-start(f32[3,2,64,128]{3,2,1,0:T(8,128)S(1)} %get-tuple-element.40.rest_3_), channel_id=1, source_target_pairs={{0,1},{1,2},{2,3},{4,5},{5,6},{6,7},{8,9},{9,10},{10,11},{12,13},{... | collective-permute-start | bytes 589832 | tf_op jit(solution)/shard_map/ppermute | solution.py:565
  28.7 1.5 %collective-permute-start.10 = (f32[3,2,64,128]{3,2,1,0:T(8,128)S(1)}, f32[3,2,64,128]{3,2,1,0:T(8,128)S(1)}, u32[]{:S(2)}, u32[]{:S(2)}) collective-permute-start(f32[3,2,64,128]{3,2,1,0:T(8,128)S(1)} %get-tuple-element.41.rest_1_), channel_id=1, source_target_pairs={{1,0},{2,1},{3,2},{5,4},{6,5},{7,6},{9,8},{10,9},{11,10},{13,12},{... | collective-permute-start | bytes 589832 | tf_op jit(solution)/shard_map/ppermute | solution.py:566
  30.2 8.8 %forward_inner.1 = (bf16[12,1280,512]{2,1,0:T(8,128)(2,1)S(1)}, f32[12,320,512]{2,1,0:T(8,128)S(1)}, f32[12,40,512]{2,1,0:T(8,128)S(1)}, f32[12,8,512]{2,1,0:T(8,128)S(1)}, f32[8,2,64,128]{3,2,1,0:T(8,128)S(1)}) custom-call(f32[8,8,128]{2,1,0:T(8,128)S(1)} %get-tuple-element.36.gates_ref, ...), custom_call_target="tpu_custom_call", output_to_operand_aliasing={{0}: (5, {}), {1}: (6, {}), {2}: (7, {}), {3}: (8, {})} | custom-call | flops 5368709120 | bytes 41943040 | tf_op jit(solution)/shard_map/forward_inner/pallas_call | solution.py:568
  39.0 5.4 %copy-done.1 = bf16[12,1280,512]{2,1,0:T(8,128)(2,1)} copy-done((bf16[12,1280,512]{2,1,0:T(8,128)(2,1)}, bf16[12,1280,512]{2,1,0:T(8,128)(2,1)S(1)}, u32[]{:S(2)}) %copy-start.1) | copy-done | bytes 15728664
  44.5 3.1 %copy-done.3 = f32[12,320,512]{2,1,0:T(8,128)} copy-done((f32[12,320,512]{2,1,0:T(8,128)}, f32[12,320,512]{2,1,0:T(8,128)S(1)}, u32[]{:S(2)}) %copy-start.3) | copy-done | bytes 7864344
  47.6 5.5 %copy-done.2 = bf16[12,1280,512]{2,1,0:T(8,128)(2,1)S(1)} copy-done((bf16[12,1280,512]{2,1,0:T(8,128)(2,1)S(1)}, bf16[12,1280,512]{2,1,0:T(8,128)(2,1)}, u32[]{:S(2)}) %copy-start.2) | copy-done | bytes 15728664
  53.1 3.2 %copy-done.4 = f32[12,320,512]{2,1,0:T(8,128)S(1)} copy-done((f32[12,320,512]{2,1,0:T(8,128)S(1)}, f32[12,320,512]{2,1,0:T(8,128)}, u32[]{:S(2)}) %copy-start.4) | copy-done | bytes 7864344
  56.3 23.7 %backward.1 = (bf16[4,12,8,512]{3,2,1,0:T(8,128)(2,1)}, f32[32,16,512]{2,1,0:T(8,128)S(1)}, bf16[32,16,512]{2,1,0:T(8,128)(2,1)S(1)}) custom-call(s32[4,10]{1,0:T(4,128)S(1)} %copy.14.src_ref, s32[2]{0:T(128)S(1)} %pad_add_fusion.place_ref, f32[3,8,8]{2,1,0:T(8,128)} %taps_ref.1, f32[8,8,128]{2,1,0:T(8,128)S(1)} %get-tuple-element.36.gates_ref, ...), custom_call_target="tpu_custom_call" | custom-call | tf_op jit(solution)/shard_map/backward/pallas_call | solution.py:586
  80.0 2.1 %collective-permute-start.11 = (bf16[32,16,512]{2,1,0:T(8,128)(2,1)S(1)}, bf16[32,16,512]{2,1,0:T(8,128)(2,1)S(1)}, u32[]{:S(2)}, u32[]{:S(2)}) collective-permute-start(bf16[32,16,512]{2,1,0:T(8,128)(2,1)S(1)} %get-tuple-element.55), channel_id=1, source_target_pairs={{0,1},{1,0},{2,3},{3,2},{4,5},{5,4},{6,7},{7,6},{8,9},{9,8},{10,11... | collective-permute-start | bytes 1572872 | tf_op jit(solution)/shard_map/ppermute | solution.py:614
  82.2 1.5 %collective-permute-done.11.received_ref.after_ref = bf16[32,16,512]{2,1,0:T(8,128)(2,1)S(1)} collective-permute-done((bf16[32,16,512]{2,1,0:T(8,128)(2,1)S(1)}, bf16[32,16,512]{2,1,0:T(8,128)(2,1)S(1)}, u32[]{:S(2)}, u32[]{:S(2)}) %collective-permute-start.11) | collective-permute-done | bytes 524320 | tf_op jit(solution)/shard_map/ppermute | solution.py:614
  83.7 0.1 split.2
  83.8 1.6 %collective-permute-start.12 = (bf16[8,16,512]{2,1,0:T(8,128)(2,1)S(1)}, bf16[8,16,512]{2,1,0:T(8,128)(2,1)S(1)}, u32[]{:S(2)}, u32[]{:S(2)}) collective-permute-start(bf16[8,16,512]{2,1,0:T(8,128)(2,1)S(1)} %get-tuple-element.57), channel_id=1, source_target_pairs={{0,4},{4,0},{8,12},{12,8},{16,20},{20,16},{24,28},{28,24},{1,5},{5... | collective-permute-start | bytes 393224 | tf_op jit(solution)/shard_map/ppermute | solution.py:491
  85.4 4.2 %collective-permute-done.12.received_ref = bf16[8,16,512]{2,1,0:T(8,128)(2,1)S(1)} collective-permute-done((bf16[8,16,512]{2,1,0:T(8,128)(2,1)S(1)}, bf16[8,16,512]{2,1,0:T(8,128)(2,1)S(1)}, u32[]{:S(2)}, u32[]{:S(2)}) %collective-permute-start.12) | collective-permute-done | bytes 131104 | tf_op jit(solution)/shard_map/ppermute | solution.py:491
  89.6 0.1 split.3
  89.7 1.6 %collective-permute-start.13 = (bf16[8,16,512]{2,1,0:T(8,128)(2,1)S(1)}, bf16[8,16,512]{2,1,0:T(8,128)(2,1)S(1)}, u32[]{:S(2)}, u32[]{:S(2)}) collective-permute-start(bf16[8,16,512]{2,1,0:T(8,128)(2,1)S(1)} %get-tuple-element.60), channel_id=1, source_target_pairs={{0,4},{4,0},{8,12},{12,8},{16,20},{20,16},{24,28},{28,24},{1,5},{5... | collective-permute-start | bytes 393224 | tf_op jit(solution)/shard_map/ppermute | solution.py:491
  91.3 0.9 collective-permute-start.14
  92.2 1.4 %collective-permute-start.15 = (bf16[4,16,512]{2,1,0:T(8,128)(2,1)S(1)}, bf16[4,16,512]{2,1,0:T(8,128)(2,1)S(1)}, u32[]{:S(2)}, u32[]{:S(2)}) collective-permute-start(bf16[4,16,512]{2,1,0:T(8,128)(2,1)S(1)} %get-tuple-element.62), channel_id=1, source_target_pairs={{0,24},{4,28},{8,16},{12,20},{16,8},{20,12},{24,0},{28,4},{1,25},{... | collective-permute-start | bytes 196616 | tf_op jit(solution)/shard_map/ppermute | solution.py:491
  93.5 1.2 %collective-permute-done.13.received_ref = bf16[8,16,512]{2,1,0:T(8,128)(2,1)S(1)} collective-permute-done((bf16[8,16,512]{2,1,0:T(8,128)(2,1)S(1)}, bf16[8,16,512]{2,1,0:T(8,128)(2,1)S(1)}, u32[]{:S(2)}, u32[]{:S(2)}) %collective-permute-start.13) | collective-permute-done | bytes 131104 | tf_op jit(solution)/shard_map/ppermute | solution.py:491
  94.8 0.1 collective-permute-start.16
  94.9 3.5 %collective-permute-done.15 = bf16[4,16,512]{2,1,0:T(8,128)(2,1)S(1)} collective-permute-done((bf16[4,16,512]{2,1,0:T(8,128)(2,1)S(1)}, bf16[4,16,512]{2,1,0:T(8,128)(2,1)S(1)}, u32[]{:S(2)}, u32[]{:S(2)}) %collective-permute-start.15) | collective-permute-done | bytes 65568 | tf_op jit(solution)/shard_map/ppermute | solution.py:491
  98.4 0.1 collective-permute-done.14
  98.5 0.8 collective-permute-done.16
  99.3 1.7 %collective-permute-start.17 = (bf16[4,16,512]{2,1,0:T(8,128)(2,1)S(1)}, bf16[4,16,512]{2,1,0:T(8,128)(2,1)S(1)}, u32[]{:S(2)}, u32[]{:S(2)}) collective-permute-start(bf16[4,16,512]{2,1,0:T(8,128)(2,1)S(1)} %add_convert_fusion), channel_id=1, source_target_pairs={{0,2},{1,3},{2,0},{3,1},{4,6},{5,7},{6,4},{7,5},{8,10},{9,11},{10,... | collective-permute-start | bytes 196616 | tf_op jit(solution)/shard_map/ppermute | solution.py:641
  101.0 2.6 %collective-permute-done.17 = bf16[4,16,512]{2,1,0:T(8,128)(2,1)S(1)} collective-permute-done((bf16[4,16,512]{2,1,0:T(8,128)(2,1)S(1)}, bf16[4,16,512]{2,1,0:T(8,128)(2,1)S(1)}, u32[]{:S(2)}, u32[]{:S(2)}) %collective-permute-start.17) | collective-permute-done | bytes 65568 | tf_op jit(solution)/shard_map/ppermute | solution.py:641
  103.6 0.1 collective-permute-start.18
  103.7 0.1 broadcast_in_dim.36
  103.8 0.1 broadcast_in_dim.37
  103.9 1.2 %collective-permute-done.18 = f32[4,16,512]{2,1,0:T(8,128)S(1)} collective-permute-done((f32[4,16,512]{2,1,0:T(8,128)S(1)}, f32[4,16,512]{2,1,0:T(8,128)S(1)}, u32[]{:S(2)}, u32[]{:S(2)}) %collective-permute-start.18) | collective-permute-done | bytes 131104 | tf_op jit(solution)/shard_map/ppermute | solution.py:642
  105.0 0.8 bitcast_select_fusion
  (20 shorter events, 0.2 us)
Async XLA Ops:
  0.6 18.3 %copy-start = (s32[32,10]{0,1:T(8,128)S(1)}, s32[32,10]{0,1:T(8,128)}, u32[]{:S(2)}) copy-start(s32[32,10]{0,1:T(8,128)} %param.7) | copy-start | bytes 3844
  1.5 7.6 %collective-permute-start.2 = (bf16[4,16,512]{2,1,0:T(8,128)(2,1)S(1)}, bf16[4,16,512]{2,1,0:T(8,128)(2,1)S(1)}, u32[]{:S(2)}, u32[]{:S(2)}) collective-permute-start(bf16[4,16,512]{2,1,0:T(8,128)(2,1)S(1)} %dynamic-slice_bitcast_fusion), channel_id=1, source_target_pairs={{0,8},{4,12},{8,0},{12,4},{16,24},{20,28},{24,16},{28,20},{1,9},{5... | collective-permute-start | bytes 196616 | tf_op jit(solution)/shard_map/ppermute | solution.py:491
  4.5 6.9 %collective-permute-start.1 = (bf16[4,16,512]{2,1,0:T(8,128)(2,1)S(1)}, bf16[4,16,512]{2,1,0:T(8,128)(2,1)S(1)}, u32[]{:S(2)}, u32[]{:S(2)}) collective-permute-start(bf16[4,16,512]{2,1,0:T(8,128)(2,1)S(1)} %dynamic-slice_bitcast_fusion), channel_id=1, source_target_pairs={{0,24},{4,28},{8,16},{12,20},{16,8},{20,12},{24,0},{28,4},{1,25},{... | collective-permute-start | bytes 196616 | tf_op jit(solution)/shard_map/ppermute | solution.py:491
  7.0 6.4 %collective-permute-start = (bf16[4,16,512]{2,1,0:T(8,128)(2,1)S(1)}, bf16[4,16,512]{2,1,0:T(8,128)(2,1)S(1)}, u32[]{:S(2)}, u32[]{:S(2)}) collective-permute-start(bf16[4,16,512]{2,1,0:T(8,128)(2,1)S(1)} %dynamic-slice_bitcast_fusion), channel_id=1, source_target_pairs={{0,16},{4,20},{8,24},{12,28},{16,0},{20,4},{24,8},{28,12},{1,17},{... | collective-permute-start | bytes 196616 | tf_op jit(solution)/shard_map/ppermute | solution.py:491
  9.2 6.4 %collective-permute-start.3 = (bf16[8,16,512]{2,1,0:T(8,128)(2,1)S(1)}, bf16[8,16,512]{2,1,0:T(8,128)(2,1)S(1)}, u32[]{:S(2)}, u32[]{:S(2)}) collective-permute-start(bf16[8,16,512]{2,1,0:T(8,128)(2,1)S(1)} %pad_maximum_fusion.1.rest_0_), channel_id=1, source_target_pairs={{0,4},{4,0},{8,12},{12,8},{16,20},{20,16},{24,28},{28,24},{1,5},{5... | collective-permute-start | bytes 393224 | tf_op jit(solution)/shard_map/ppermute | solution.py:491
  13.5 5.4 %collective-permute-start.4 = (bf16[8,16,512]{2,1,0:T(8,128)(2,1)S(1)}, bf16[8,16,512]{2,1,0:T(8,128)(2,1)S(1)}, u32[]{:S(2)}, u32[]{:S(2)}) collective-permute-start(bf16[8,16,512]{2,1,0:T(8,128)(2,1)S(1)} %pad_maximum_fusion.rest_1_), channel_id=1, source_target_pairs={{0,4},{4,0},{8,12},{12,8},{16,20},{20,16},{24,28},{28,24},{1,5},{5... | collective-permute-start | bytes 393224 | tf_op jit(solution)/shard_map/ppermute | solution.py:491
  15.1 4.1 %collective-permute-start.5 = (bf16[8,16,512]{2,1,0:T(8,128)(2,1)S(1)}, bf16[8,16,512]{2,1,0:T(8,128)(2,1)S(1)}, u32[]{:S(2)}, u32[]{:S(2)}) collective-permute-start(bf16[8,16,512]{2,1,0:T(8,128)(2,1)S(1)} %pad_maximum_fusion.1.rest_0_), channel_id=1, source_target_pairs={{0,1},{1,0},{2,3},{3,2},{4,5},{5,4},{6,7},{7,6},{8,9},{9,8},{10,11... | collective-permute-start | bytes 393224 | tf_op jit(solution)/shard_map/ppermute | solution.py:524
  15.1 4.1 %collective-permute-start.6 = (bf16[8,16,512]{2,1,0:T(8,128)(2,1)S(1)}, bf16[8,16,512]{2,1,0:T(8,128)(2,1)S(1)}, u32[]{:S(2)}, u32[]{:S(2)}) collective-permute-start(bf16[8,16,512]{2,1,0:T(8,128)(2,1)S(1)} %pad_maximum_fusion.rest_1_), channel_id=1, source_target_pairs={{0,1},{1,0},{2,3},{3,2},{4,5},{5,4},{6,7},{7,6},{8,9},{9,8},{10,11... | collective-permute-start | bytes 393224 | tf_op jit(solution)/shard_map/ppermute | solution.py:524
  15.6 3.6 %collective-permute-start.7 = (bf16[8,16,512]{2,1,0:T(8,128)(2,1)S(1)}, bf16[8,16,512]{2,1,0:T(8,128)(2,1)S(1)}, u32[]{:S(2)}, u32[]{:S(2)}) collective-permute-start(bf16[8,16,512]{2,1,0:T(8,128)(2,1)S(1)} %collective-permute-done.3.rest_2_), channel_id=1, source_target_pairs={{0,1},{1,0},{2,3},{3,2},{4,5},{5,4},{6,7},{7,6},{8,9},{9,8},{10,11... | collective-permute-start | bytes 393224 | tf_op jit(solution)/shard_map/ppermute | solution.py:524
  18.9 1.3 %collective-permute-start.8 = (bf16[8,16,512]{2,1,0:T(8,128)(2,1)S(1)}, bf16[8,16,512]{2,1,0:T(8,128)(2,1)S(1)}, u32[]{:S(2)}, u32[]{:S(2)}) collective-permute-start(bf16[8,16,512]{2,1,0:T(8,128)(2,1)S(1)} %collective-permute-done.4.rest_3_), channel_id=1, source_target_pairs={{0,1},{1,0},{2,3},{3,2},{4,5},{5,4},{6,7},{7,6},{8,9},{9,8},{10,11... | collective-permute-start | bytes 393224 | tf_op jit(solution)/shard_map/ppermute | solution.py:524
  26.6 21.0 %collective-permute-start.9 = (f32[3,2,64,128]{3,2,1,0:T(8,128)S(1)}, f32[3,2,64,128]{3,2,1,0:T(8,128)S(1)}, u32[]{:S(2)}, u32[]{:S(2)}) collective-permute-start(f32[3,2,64,128]{3,2,1,0:T(8,128)S(1)} %get-tuple-element.40.rest_3_), channel_id=1, source_target_pairs={{0,1},{1,2},{2,3},{4,5},{5,6},{6,7},{8,9},{9,10},{10,11},{12,13},{... | collective-permute-start | bytes 589832 | tf_op jit(solution)/shard_map/ppermute | solution.py:565
  28.7 18.9 %collective-permute-start.10 = (f32[3,2,64,128]{3,2,1,0:T(8,128)S(1)}, f32[3,2,64,128]{3,2,1,0:T(8,128)S(1)}, u32[]{:S(2)}, u32[]{:S(2)}) collective-permute-start(f32[3,2,64,128]{3,2,1,0:T(8,128)S(1)} %get-tuple-element.41.rest_1_), channel_id=1, source_target_pairs={{1,0},{2,1},{3,2},{5,4},{6,5},{7,6},{9,8},{10,9},{11,10},{13,12},{... | collective-permute-start | bytes 589832 | tf_op jit(solution)/shard_map/ppermute | solution.py:566
  39.0 5.5 %copy-start.1 = (bf16[12,1280,512]{2,1,0:T(8,128)(2,1)}, bf16[12,1280,512]{2,1,0:T(8,128)(2,1)S(1)}, u32[]{:S(2)}) copy-start(bf16[12,1280,512]{2,1,0:T(8,128)(2,1)S(1)} %get-tuple-element.49.rest_6_) | copy-start | bytes 47185924
  44.5 3.1 %copy-start.3 = (f32[12,320,512]{2,1,0:T(8,128)}, f32[12,320,512]{2,1,0:T(8,128)S(1)}, u32[]{:S(2)}) copy-start(f32[12,320,512]{2,1,0:T(8,128)S(1)} %get-tuple-element.50.rest_7_) | copy-start | bytes 23592964
  47.6 5.5 %copy-start.2 = (bf16[12,1280,512]{2,1,0:T(8,128)(2,1)S(1)}, bf16[12,1280,512]{2,1,0:T(8,128)(2,1)}, u32[]{:S(2)}) copy-start(bf16[12,1280,512]{2,1,0:T(8,128)(2,1)} %copy-done.1) | copy-start | bytes 47185924
  53.1 3.2 %copy-start.4 = (f32[12,320,512]{2,1,0:T(8,128)S(1)}, f32[12,320,512]{2,1,0:T(8,128)}, u32[]{:S(2)}) copy-start(f32[12,320,512]{2,1,0:T(8,128)} %copy-done.3) | copy-start | bytes 23592964
  80.0 3.7 %collective-permute-start.11 = (bf16[32,16,512]{2,1,0:T(8,128)(2,1)S(1)}, bf16[32,16,512]{2,1,0:T(8,128)(2,1)S(1)}, u32[]{:S(2)}, u32[]{:S(2)}) collective-permute-start(bf16[32,16,512]{2,1,0:T(8,128)(2,1)S(1)} %get-tuple-element.55), channel_id=1, source_target_pairs={{0,1},{1,0},{2,3},{3,2},{4,5},{5,4},{6,7},{7,6},{8,9},{9,8},{10,11... | collective-permute-start | bytes 1572872 | tf_op jit(solution)/shard_map/ppermute | solution.py:614
  83.8 5.8 %collective-permute-start.12 = (bf16[8,16,512]{2,1,0:T(8,128)(2,1)S(1)}, bf16[8,16,512]{2,1,0:T(8,128)(2,1)S(1)}, u32[]{:S(2)}, u32[]{:S(2)}) collective-permute-start(bf16[8,16,512]{2,1,0:T(8,128)(2,1)S(1)} %get-tuple-element.57), channel_id=1, source_target_pairs={{0,4},{4,0},{8,12},{12,8},{16,20},{20,16},{24,28},{28,24},{1,5},{5... | collective-permute-start | bytes 393224 | tf_op jit(solution)/shard_map/ppermute | solution.py:491
  89.7 5.0 %collective-permute-start.13 = (bf16[8,16,512]{2,1,0:T(8,128)(2,1)S(1)}, bf16[8,16,512]{2,1,0:T(8,128)(2,1)S(1)}, u32[]{:S(2)}, u32[]{:S(2)}) collective-permute-start(bf16[8,16,512]{2,1,0:T(8,128)(2,1)S(1)} %get-tuple-element.60), channel_id=1, source_target_pairs={{0,4},{4,0},{8,12},{12,8},{16,20},{20,16},{24,28},{28,24},{1,5},{5... | collective-permute-start | bytes 393224 | tf_op jit(solution)/shard_map/ppermute | solution.py:491
  91.3 7.1 %collective-permute-start.14 = (bf16[4,16,512]{2,1,0:T(8,128)(2,1)S(1)}, bf16[4,16,512]{2,1,0:T(8,128)(2,1)S(1)}, u32[]{:S(2)}, u32[]{:S(2)}) collective-permute-start(bf16[4,16,512]{2,1,0:T(8,128)(2,1)S(1)} %get-tuple-element.58.after_ref), channel_id=1, source_target_pairs={{0,16},{4,20},{8,24},{12,28},{16,0},{20,4},{24,8},{28,12},{1,17},{... | collective-permute-start | bytes 196616 | tf_op jit(solution)/shard_map/ppermute | solution.py:491
  92.2 6.2 %collective-permute-start.15 = (bf16[4,16,512]{2,1,0:T(8,128)(2,1)S(1)}, bf16[4,16,512]{2,1,0:T(8,128)(2,1)S(1)}, u32[]{:S(2)}, u32[]{:S(2)}) collective-permute-start(bf16[4,16,512]{2,1,0:T(8,128)(2,1)S(1)} %get-tuple-element.62), channel_id=1, source_target_pairs={{0,24},{4,28},{8,16},{12,20},{16,8},{20,12},{24,0},{28,4},{1,25},{... | collective-permute-start | bytes 196616 | tf_op jit(solution)/shard_map/ppermute | solution.py:491
  94.8 4.5 %collective-permute-start.16 = (bf16[4,16,512]{2,1,0:T(8,128)(2,1)S(1)}, bf16[4,16,512]{2,1,0:T(8,128)(2,1)S(1)}, u32[]{:S(2)}, u32[]{:S(2)}) collective-permute-start(bf16[4,16,512]{2,1,0:T(8,128)(2,1)S(1)} %get-tuple-element.63), channel_id=1, source_target_pairs={{0,8},{4,12},{8,0},{12,4},{16,24},{20,28},{24,16},{28,20},{1,9},{5... | collective-permute-start | bytes 196616 | tf_op jit(solution)/shard_map/ppermute | solution.py:491
  99.3 4.3 %collective-permute-start.17 = (bf16[4,16,512]{2,1,0:T(8,128)(2,1)S(1)}, bf16[4,16,512]{2,1,0:T(8,128)(2,1)S(1)}, u32[]{:S(2)}, u32[]{:S(2)}) collective-permute-start(bf16[4,16,512]{2,1,0:T(8,128)(2,1)S(1)} %add_convert_fusion), channel_id=1, source_target_pairs={{0,2},{1,3},{2,0},{3,1},{4,6},{5,7},{6,4},{7,5},{8,10},{9,11},{10,... | collective-permute-start | bytes 196616 | tf_op jit(solution)/shard_map/ppermute | solution.py:641
  103.6 1.4 %collective-permute-start.18 = (f32[4,16,512]{2,1,0:T(8,128)S(1)}, f32[4,16,512]{2,1,0:T(8,128)S(1)}, u32[]{:S(2)}, u32[]{:S(2)}) collective-permute-start(f32[4,16,512]{2,1,0:T(8,128)S(1)} %get-tuple-element.65), channel_id=1, source_target_pairs={{0,1},{1,0},{2,3},{3,2},{4,5},{5,4},{6,7},{7,6},{8,9},{9,8},{10,11... | collective-permute-start | bytes 393224 | tf_op jit(solution)/shard_map/ppermute | solution.py:642

commit v12 on v10

--- a/solution.py
+++ b/solution.py
@@ -247,10 +247,12 @@
     cot_ref,
     regular_ref,
     cost,
+    grad_ref,
     slope,
     smooth,
 ):
-    local_views, planes, groups, pixels = regular_ref.shape
+    planes = grad_ref.shape[0]
+    local_views, _, groups, pixels = regular_ref.shape
     cost[0:2] = below_ref[0:2]
     cost[2:4] = down_ref[0:2]
     cost[4:planes] = inner_ref[...]
@@ -282,13 +284,7 @@
             sig = jax.nn.sigmoid(pre)
             both = pl.ds(plane, 2)
             slope[both, :, rows, :] = slope[both, :, rows, :] * (sig * (1.0 + pre * (1.0 - sig)))
-            smooth[:, :, rows, :] = pre * sig
-        for view in range(local_views):
-            for tile in range(pixels // LANE):
-                first = (tile % 2) * local_views + view
-                for i, at in ((1, jnp.minimum(plane, planes - 1)), (0, jnp.abs(plane - 1))):
-                    kept = smooth[i, tile // 2, pl.ds(first, groups, stride=SUB), :]
-                    regular_ref[view, at, :, pl.ds(tile * LANE, LANE)] = kept.astype(jnp.bfloat16)
+            smooth[both, :, rows, :] = pre * sig
         return carry
 
     lax.fori_loop(0, (planes + 2) // 2, forward_planes, 0)
@@ -300,7 +296,14 @@
             lambda k, g, o: taps_ref[k, o, g],
         )
         for g in range(G):
-            slope[pl.ds(plane, 2), :, pl.ds(g * SUB, SUB), :] = grads[g]
+            grad_ref[pl.ds(plane, 2), :, pl.ds(g * SUB, SUB), :] = grads[g]
+        for view in range(local_views):
+            for tile in range(pixels // LANE):
+                first = (tile % 2) * local_views + view
+                for i in range(2):
+                    regular_ref[view, plane + i, :, pl.ds(tile * LANE, LANE)] = smooth[
+                        plane + i + 1, tile // 2, pl.ds(first, groups, stride=SUB), :
+                    ].astype(jnp.bfloat16)
         return carry
 
     lax.fori_loop(0, planes // 2, backward_planes, 0)
@@ -310,7 +313,7 @@
     halo_refs = rest[:6]
     warped_ref, corr_ref, sig_ref, rden_ref = rest[6:10]
     regular_ref, keep_ref, send_ref = rest[10:13]
-    cost, grad_ref, smooth, rows, acc, dref, held, sems, dense = rest[13:]
+    cost, grad_ref, slope, smooth, rows, acc, dref, held, sems = rest[13:]
     count = w_ref.shape[0]
     pairs = sig_ref.shape[1]
     tiles = pairs // SUB
@@ -376,7 +379,7 @@
 
     acc[...] = jnp.zeros_like(acc)
     dref[...] = jnp.zeros_like(dref)
-    depth_conv(taps_ref, *halo_refs, regular_ref, cost, grad_ref, smooth)
+    depth_conv(taps_ref, *halo_refs, regular_ref, cost, grad_ref, slope, smooth)
 
     def one_turn(turn, carry):
         for offset in range(group):
@@ -395,7 +398,8 @@
     own_index = place_ref[0]
     parity = place_ref[1]
     blocks = keep_ref.shape[1] // SUB
-    for target, held_side in ((dense, 1 - parity), (keep_ref, parity)):
+    target = keep_ref
+    for held_side in (1 - parity, parity):
         target[...] = jnp.zeros_like(target)
         for tile in range(lane_tiles):
             lanes = pl.ds(tile * LANE, LANE)
@@ -411,7 +415,7 @@
                     target[view, part, lanes] = total
         for pair in range(pairs):
             view = src_ref[pair % local_views, pair // local_views]
-            slot = position(view, own_index, local_views, dense.shape[0] // local_views)
+            slot = position(view, own_index, local_views, keep_ref.shape[0] // local_views)
             for block in range(blocks):
                 first = (2 * block + held_side) * (SUB * pairs) + pair
                 part = pl.ds(block * SUB, SUB)
@@ -419,7 +423,8 @@
                     target[slot, part, pl.ds(tile * LANE, LANE)] += acc[
                         tile, pl.ds(first, SUB, stride=pairs), :
                     ]
-    send_ref[...] = dense[...].astype(jnp.bfloat16)
+        if held_side is not parity:
+            send_ref[...] = target[...].astype(jnp.bfloat16)
 
 
 def split_kernel(first, keep_ref, received_ref, after_ref, even_ref, send_ref):
@@ -439,14 +444,6 @@
         out_ref[...] = (even_ref[span] + received_ref[span].astype(jnp.float32)).astype(
             out_ref.dtype
         )
-
-
-def join_kernel(place_ref, mine_ref, other_ref, out_ref):
-    parity = place_ref[1]
-    for ref, side in ((mine_ref, parity), (other_ref, 1 - parity)):
-        for block in range(ref.shape[1] // SUB):
-            first = pl.multiple_of((2 * block + side) * SUB, SUB)
-            out_ref[:, pl.ds(first, SUB), :] = ref[:, block * SUB : (block + 1) * SUB, :]
 
 
 SMEM = functools.partial(pl.BlockSpec, memory_space=pltpu.SMEM)
@@ -581,14 +578,14 @@
         out_specs=(vmem,) * 3,
         scratch_shapes=[
             pltpu.VMEM((planes + 4,) + packed, f32),
+            pltpu.VMEM((planes,) + packed, f32),
             pltpu.VMEM((planes + 2,) + packed, f32),
-            pltpu.VMEM((2,) + packed, f32),
+            pltpu.VMEM((planes + 2,) + packed, f32),
             pltpu.VMEM((channels * pairs, group * pixels), bf16),
             pltpu.VMEM((pixels // LANE, channels * pairs, LANE), f32),
             pltpu.VMEM((pixels // LANE, channels * SUB, LANE), f32),
             pltpu.VMEM((group * pixels, pixels), bf16),
             pltpu.SemaphoreType.DMA((group,)),
-            pltpu.VMEM(returned, f32),
         ],
         compiler_params=params(14 + 5 * all_views * channels * pixels // MIB),
         name="backward",
@@ -632,13 +629,10 @@
     rounded = total.astype(bf16)
     total = rounded.astype(f32) + lax.ppermute(rounded, "plane", far).astype(f32)
     other = lax.ppermute(total, "plane", near)
-    feature_grads = pl.pallas_call(
-        join_kernel,
-        out_shape=shape(features.shape, f32),
-        in_specs=[SMEM(), vmem, vmem],
-        compiler_params=params(4),
-        name="join",
-    )(place, total, other)
+    cut = (local_views, blocks, 1, share, pixels)
+    first = jnp.where(parity == 0, total, other).reshape(cut)
+    second = jnp.where(parity == 0, other, total).reshape(cut)
+    feature_grads = jnp.concatenate([first, second], axis=2).reshape(features.shape)
     return (regular, feature_grads)
 
 

time: 88.7 us -> 88.3 us (level)
  Pallas kernels: 41.6 us -> 40.4 us
    pallas_call x1 -> x0, Pallas kernels: 1.26 us -> none  [shards(): pl.pallas_call(join_kernel, out_shape=shape(features.shape, f32), in_spec...]
where the time goes in v12:
time: 88.3 us; the launch traced here: 87.9 us
  Pallas kernels  40.4 us (46%)
  waiting for transfers between devices  22.4 us (25%)
  starting transfers between devices  22.3 us (25%)
  local copies, waits for them, and re-layouts  1.75 us (2%)
    pallas_call x1, Pallas kernels, shards(): pl.pallas_call(backward_kernel, out_shape=(shape(cotangent.shape, bf16),...  23 us
    ppermute x10, waiting for transfers between devices, over_view(): return lax.ppermute(array, 'view', [(i, i ^ k) for i in range(view_count)])  15.8 us
    ppermute x10, starting transfers between devices, over_view(): return lax.ppermute(array, 'view', [(i, i ^ k) for i in range(view_count)])  14.3 us
    pallas_call x1, Pallas kernels, shards(): pl.pallas_call(inner_kernel, out_shape=saved + (pltpu.VMEM((inner_count,)...  8.85 us
    pallas_call x1, Pallas kernels, shards(): pl.pallas_call(edge_kernel, out_shape=saved + (shape(load, f32),) * 2 + (...  6.33 us
    ppermute x1, waiting for transfers between devices, shards(): lax.ppermute(rounded, 'plane', far).astype(f32)  2.63 us
    ppermute x1, starting transfers between devices, shards(): received = lax.ppermute(send, 'plane', near)  2.15 us
    ppermute x1, starting transfers between devices, shards(): below = lax.ppermute(up_load, 'plane', up)  2.06 us
  transfers between devices with their start and end apart: 19, of which 12 were waited for; matrix products, arithmetic and copies ran while one was open for 0% of the time, Pallas kernels for 12%

profile of v12, /device:TPU:0, one launch (start us, length us, event | category | flops | bytes accessed | tf_op | source)
XLA Modules:
  0.0 87.9 jit_solution(1506360382907759353)
XLA Ops:
  0.6 0.0 copy-start
  0.7 0.8 dynamic-slice_bitcast_fusion
  1.5 3.0 %collective-permute-start.2 = (bf16[4,16,512]{2,1,0:T(8,128)(2,1)S(1)}, bf16[4,16,512]{2,1,0:T(8,128)(2,1)S(1)}, u32[]{:S(2)}, u32[]{:S(2)}) collective-permute-start(bf16[4,16,512]{2,1,0:T(8,128)(2,1)S(1)} %dynamic-slice_bitcast_fusion), channel_id=1, source_target_pairs={{0,8},{4,12},{8,0},{12,4},{16,24},{20,28},{24,16},{28,20},{1,9},{5... | collective-permute-start | bytes 196616 | tf_op jit(solution)/shard_map/ppermute | solution.py:478
  4.5 2.5 %collective-permute-start.1 = (bf16[4,16,512]{2,1,0:T(8,128)(2,1)S(1)}, bf16[4,16,512]{2,1,0:T(8,128)(2,1)S(1)}, u32[]{:S(2)}, u32[]{:S(2)}) collective-permute-start(bf16[4,16,512]{2,1,0:T(8,128)(2,1)S(1)} %dynamic-slice_bitcast_fusion), channel_id=1, source_target_pairs={{0,24},{4,28},{8,16},{12,20},{16,8},{20,12},{24,0},{28,4},{1,25},{... | collective-permute-start | bytes 196616 | tf_op jit(solution)/shard_map/ppermute | solution.py:478
  7.0 0.1 collective-permute-start
  7.1 2.0 %prep.1 = (f32[4,256,128]{2,1,0:T(8,128)S(1)}, f32[8,8,128]{2,1,0:T(8,128)S(1)}, f32[12,2,64,128]{3,2,1,0:T(8,128)S(1)}) custom-call(f32[8]{0:T(128)} %gate_ref.1, bf16[4,32,512]{2,1,0:T(8,128)(2,1)} %own_hbm.1, bf16[4,12,8,512]{3,2,1,0:T(8,128)(2,1)} %cot_hbm.1), custom_call_target="tpu_custom_call" | custom-call | flops 1000000000 | bytes 4194304 | tf_op jit(solution)/shard_map/prep/pallas_call | solution.py:488
  9.1 0.0 collective-permute-done.2
  9.2 1.6 %collective-permute-start.3 = (bf16[8,16,512]{2,1,0:T(8,128)(2,1)S(1)}, bf16[8,16,512]{2,1,0:T(8,128)(2,1)S(1)}, u32[]{:S(2)}, u32[]{:S(2)}) collective-permute-start(bf16[8,16,512]{2,1,0:T(8,128)(2,1)S(1)} %pad_maximum_fusion.2.rest_0_), channel_id=1, source_target_pairs={{0,4},{4,0},{8,12},{12,8},{16,20},{20,16},{24,28},{28,24},{1,5},{5... | collective-permute-start | bytes 393224 | tf_op jit(solution)/shard_map/ppermute | solution.py:478
  10.7 0.7 collective-permute-done.1
  11.4 2.1 %collective-permute-done = bf16[4,16,512]{2,1,0:T(8,128)(2,1)S(1)} collective-permute-done((bf16[4,16,512]{2,1,0:T(8,128)(2,1)S(1)}, bf16[4,16,512]{2,1,0:T(8,128)(2,1)S(1)}, u32[]{:S(2)}, u32[]{:S(2)}) %collective-permute-start) | collective-permute-done | bytes 65568 | tf_op jit(solution)/shard_map/ppermute | solution.py:478
  13.5 1.6 %collective-permute-start.4 = (bf16[8,16,512]{2,1,0:T(8,128)(2,1)S(1)}, bf16[8,16,512]{2,1,0:T(8,128)(2,1)S(1)}, u32[]{:S(2)}, u32[]{:S(2)}) collective-permute-start(bf16[8,16,512]{2,1,0:T(8,128)(2,1)S(1)} %pad_maximum_fusion.1.rest_1_), channel_id=1, source_target_pairs={{0,4},{4,0},{8,12},{12,8},{16,20},{20,16},{24,28},{28,24},{1,5},{5... | collective-permute-start | bytes 393224 | tf_op jit(solution)/shard_map/ppermute | solution.py:478
  15.1 0.0 collective-permute-start.5
  15.1 0.5 collective-permute-start.6
  15.6 0.0 collective-permute-done.3.rest_2_
  15.6 0.0 collective-permute-start.7
  15.6 3.3 %collective-permute-done.4.rest_3_ = bf16[8,16,512]{2,1,0:T(8,128)(2,1)S(1)} collective-permute-done((bf16[8,16,512]{2,1,0:T(8,128)(2,1)S(1)}, bf16[8,16,512]{2,1,0:T(8,128)(2,1)S(1)}, u32[]{:S(2)}, u32[]{:S(2)}) %collective-permute-start.4) | collective-permute-done | bytes 131104 | tf_op jit(solution)/shard_map/ppermute | solution.py:478
  18.9 0.0 collective-permute-start.8
  18.9 0.1 constant_dynamic-slice_fusion
  19.0 0.1 copy.15.src_ref
  19.1 0.1 pad_add_fusion.place_ref
  19.2 0.0 collective-permute-done.6.rest_5_
  19.2 0.0 collective-permute-done.7.rest_6_
  19.2 1.1 %collective-permute-done.8.rest_7_ = bf16[8,16,512]{2,1,0:T(8,128)(2,1)S(1)} collective-permute-done((bf16[8,16,512]{2,1,0:T(8,128)(2,1)S(1)}, bf16[8,16,512]{2,1,0:T(8,128)(2,1)S(1)}, u32[]{:S(2)}, u32[]{:S(2)}) %collective-permute-start.8) | collective-permute-done | bytes 131104 | tf_op jit(solution)/shard_map/ppermute | solution.py:511
  20.3 6.3 %forward_edge.1 = (bf16[12,1280,512]{2,1,0:T(8,128)(2,1)S(1)}, f32[12,320,512]{2,1,0:T(8,128)S(1)}, f32[12,40,512]{2,1,0:T(8,128)S(1)}, f32[12,8,512]{2,1,0:T(8,...) custom-call(s32[4,10]{1,0:T(4,128)S(1)} %copy.15.src_ref, ...), custom_call_target="tpu_custom_call" | custom-call | tf_op jit(solution)/shard_map/forward_edge/pallas_call | solution.py:531
  26.6 2.1 %collective-permute-start.9 = (f32[3,2,64,128]{3,2,1,0:T(8,128)S(1)}, f32[3,2,64,128]{3,2,1,0:T(8,128)S(1)}, u32[]{:S(2)}, u32[]{:S(2)}) collective-permute-start(f32[3,2,64,128]{3,2,1,0:T(8,128)S(1)} %get-tuple-element.40.rest_3_), channel_id=1, source_target_pairs={{0,1},{1,2},{2,3},{4,5},{5,6},{6,7},{8,9},{9,10},{10,11},{12,13},{... | collective-permute-start | bytes 589832 | tf_op jit(solution)/shard_map/ppermute | solution.py:552
  28.7 1.5 %collective-permute-start.10 = (f32[3,2,64,128]{3,2,1,0:T(8,128)S(1)}, f32[3,2,64,128]{3,2,1,0:T(8,128)S(1)}, u32[]{:S(2)}, u32[]{:S(2)}) collective-permute-start(f32[3,2,64,128]{3,2,1,0:T(8,128)S(1)} %get-tuple-element.41.rest_1_), channel_id=1, source_target_pairs={{1,0},{2,1},{3,2},{5,4},{6,5},{7,6},{9,8},{10,9},{11,10},{13,12},{... | collective-permute-start | bytes 589832 | tf_op jit(solution)/shard_map/ppermute | solution.py:553
  30.2 8.8 %forward_inner.1 = (bf16[12,1280,512]{2,1,0:T(8,128)(2,1)S(1)}, f32[12,320,512]{2,1,0:T(8,128)S(1)}, f32[12,40,512]{2,1,0:T(8,128)S(1)}, f32[12,8,512]{2,1,0:T(8,128)S(1)}, f32[8,2,64,128]{3,2,1,0:T(8,128)S(1)}) custom-call(f32[8,8,128]{2,1,0:T(8,128)S(1)} %get-tuple-element.36.gates_ref, ...), custom_call_target="tpu_custom_call", output_to_operand_aliasing={{0}: (5, {}), {1}: (6, {}), {2}: (7, {}), {3}: (8, {})} | custom-call | flops 5368709120 | bytes 41943040 | tf_op jit(solution)/shard_map/forward_inner/pallas_call | solution.py:555
  39.0 0.0 collective-permute-done.10.rest_4_
  39.0 23.0 %backward.1 = (bf16[4,12,8,512]{3,2,1,0:T(8,128)(2,1)}, f32[32,16,512]{2,1,0:T(8,128)S(1)}, bf16[32,16,512]{2,1,0:T(8,128)(2,1)S(1)}) custom-call(s32[4,10]{1,0:T(4,128)S(1)} %copy.15.src_ref, s32[2]{0:T(128)S(1)} %pad_add_fusion.place_ref, f32[3,8,8]{2,1,0:T(8,128)} %taps_ref.1, f32[8,8,128]{2,1,0:T(8,128)S(1)} %get-tuple-element.36.gates_ref, ...), custom_call_target="tpu_custom_call" | custom-call | tf_op jit(solution)/shard_map/backward/pallas_call | solution.py:574
  62.1 2.1 %collective-permute-start.11 = (bf16[32,16,512]{2,1,0:T(8,128)(2,1)S(1)}, bf16[32,16,512]{2,1,0:T(8,128)(2,1)S(1)}, u32[]{:S(2)}, u32[]{:S(2)}) collective-permute-start(bf16[32,16,512]{2,1,0:T(8,128)(2,1)S(1)} %get-tuple-element.55), channel_id=1, source_target_pairs={{0,1},{1,0},{2,3},{3,2},{4,5},{5,4},{6,7},{7,6},{8,9},{9,8},{10,11... | collective-permute-start | bytes 1572872 | tf_op jit(solution)/shard_map/ppermute | solution.py:603
  64.2 1.5 %collective-permute-done.11.received_ref.after_ref = bf16[32,16,512]{2,1,0:T(8,128)(2,1)S(1)} collective-permute-done((bf16[32,16,512]{2,1,0:T(8,128)(2,1)S(1)}, bf16[32,16,512]{2,1,0:T(8,128)(2,1)S(1)}, u32[]{:S(2)}, u32[]{:S(2)}) %collective-permute-start.11) | collective-permute-done | bytes 524320 | tf_op jit(solution)/shard_map/ppermute | solution.py:603
  65.8 0.1 split.2
  65.9 1.6 %collective-permute-start.12 = (bf16[8,16,512]{2,1,0:T(8,128)(2,1)S(1)}, bf16[8,16,512]{2,1,0:T(8,128)(2,1)S(1)}, u32[]{:S(2)}, u32[]{:S(2)}) collective-permute-start(bf16[8,16,512]{2,1,0:T(8,128)(2,1)S(1)} %get-tuple-element.57), channel_id=1, source_target_pairs={{0,4},{4,0},{8,12},{12,8},{16,20},{20,16},{24,28},{28,24},{1,5},{5... | collective-permute-start | bytes 393224 | tf_op jit(solution)/shard_map/ppermute | solution.py:478
  67.5 4.2 %collective-permute-done.12.received_ref = bf16[8,16,512]{2,1,0:T(8,128)(2,1)S(1)} collective-permute-done((bf16[8,16,512]{2,1,0:T(8,128)(2,1)S(1)}, bf16[8,16,512]{2,1,0:T(8,128)(2,1)S(1)}, u32[]{:S(2)}, u32[]{:S(2)}) %collective-permute-start.12) | collective-permute-done | bytes 131104 | tf_op jit(solution)/shard_map/ppermute | solution.py:478
  71.7 0.1 split.3
  71.8 1.6 %collective-permute-start.13 = (bf16[8,16,512]{2,1,0:T(8,128)(2,1)S(1)}, bf16[8,16,512]{2,1,0:T(8,128)(2,1)S(1)}, u32[]{:S(2)}, u32[]{:S(2)}) collective-permute-start(bf16[8,16,512]{2,1,0:T(8,128)(2,1)S(1)} %get-tuple-element.60), channel_id=1, source_target_pairs={{0,4},{4,0},{8,12},{12,8},{16,20},{20,16},{24,28},{28,24},{1,5},{5... | collective-permute-start | bytes 393224 | tf_op jit(solution)/shard_map/ppermute | solution.py:478
  73.4 0.9 collective-permute-start.14
  74.3 1.4 %collective-permute-start.15 = (bf16[4,16,512]{2,1,0:T(8,128)(2,1)S(1)}, bf16[4,16,512]{2,1,0:T(8,128)(2,1)S(1)}, u32[]{:S(2)}, u32[]{:S(2)}) collective-permute-start(bf16[4,16,512]{2,1,0:T(8,128)(2,1)S(1)} %get-tuple-element.62), channel_id=1, source_target_pairs={{0,24},{4,28},{8,16},{12,20},{16,8},{20,12},{24,0},{28,4},{1,25},{... | collective-permute-start | bytes 196616 | tf_op jit(solution)/shard_map/ppermute | solution.py:478
  75.6 1.2 %collective-permute-done.13.received_ref = bf16[8,16,512]{2,1,0:T(8,128)(2,1)S(1)} collective-permute-done((bf16[8,16,512]{2,1,0:T(8,128)(2,1)S(1)}, bf16[8,16,512]{2,1,0:T(8,128)(2,1)S(1)}, u32[]{:S(2)}, u32[]{:S(2)}) %collective-permute-start.13) | collective-permute-done | bytes 131104 | tf_op jit(solution)/shard_map/ppermute | solution.py:478
  76.9 0.1 collective-permute-start.16
  77.0 3.5 %collective-permute-done.15 = bf16[4,16,512]{2,1,0:T(8,128)(2,1)S(1)} collective-permute-done((bf16[4,16,512]{2,1,0:T(8,128)(2,1)S(1)}, bf16[4,16,512]{2,1,0:T(8,128)(2,1)S(1)}, u32[]{:S(2)}, u32[]{:S(2)}) %collective-permute-start.15) | collective-permute-done | bytes 65568 | tf_op jit(solution)/shard_map/ppermute | solution.py:478
  80.5 0.1 collective-permute-done.14
  80.5 0.8 collective-permute-done.16
  81.3 1.7 %collective-permute-start.17 = (bf16[4,16,512]{2,1,0:T(8,128)(2,1)S(1)}, bf16[4,16,512]{2,1,0:T(8,128)(2,1)S(1)}, u32[]{:S(2)}, u32[]{:S(2)}) collective-permute-start(bf16[4,16,512]{2,1,0:T(8,128)(2,1)S(1)} %add_convert_fusion), channel_id=1, source_target_pairs={{0,2},{1,3},{2,0},{3,1},{4,6},{5,7},{6,4},{7,5},{8,10},{9,11},{10,... | collective-permute-start | bytes 196616 | tf_op jit(solution)/shard_map/ppermute | solution.py:630
  83.1 2.6 %collective-permute-done.17 = bf16[4,16,512]{2,1,0:T(8,128)(2,1)S(1)} collective-permute-done((bf16[4,16,512]{2,1,0:T(8,128)(2,1)S(1)}, bf16[4,16,512]{2,1,0:T(8,128)(2,1)S(1)}, u32[]{:S(2)}, u32[]{:S(2)}) %collective-permute-start.17) | collective-permute-done | bytes 65568 | tf_op jit(solution)/shard_map/ppermute | solution.py:630
  85.7 0.1 collective-permute-start.18
  85.8 1.3 %collective-permute-done.18 = f32[4,16,512]{2,1,0:T(8,128)S(1)} collective-permute-done((f32[4,16,512]{2,1,0:T(8,128)S(1)}, f32[4,16,512]{2,1,0:T(8,128)S(1)}, u32[]{:S(2)}, u32[]{:S(2)}) %collective-permute-start.18) | collective-permute-done | bytes 131104 | tf_op jit(solution)/shard_map/ppermute | solution.py:631
  87.2 0.7 copy.14
  (11 shorter events, 0.2 us)
Async XLA Ops:
  0.6 18.3 %copy-start = (s32[32,10]{0,1:T(8,128)S(1)}, s32[32,10]{0,1:T(8,128)}, u32[]{:S(2)}) copy-start(s32[32,10]{0,1:T(8,128)} %param.7) | copy-start | bytes 3844
  1.5 7.6 %collective-permute-start.2 = (bf16[4,16,512]{2,1,0:T(8,128)(2,1)S(1)}, bf16[4,16,512]{2,1,0:T(8,128)(2,1)S(1)}, u32[]{:S(2)}, u32[]{:S(2)}) collective-permute-start(bf16[4,16,512]{2,1,0:T(8,128)(2,1)S(1)} %dynamic-slice_bitcast_fusion), channel_id=1, source_target_pairs={{0,8},{4,12},{8,0},{12,4},{16,24},{20,28},{24,16},{28,20},{1,9},{5... | collective-permute-start | bytes 196616 | tf_op jit(solution)/shard_map/ppermute | solution.py:478
  4.5 6.9 %collective-permute-start.1 = (bf16[4,16,512]{2,1,0:T(8,128)(2,1)S(1)}, bf16[4,16,512]{2,1,0:T(8,128)(2,1)S(1)}, u32[]{:S(2)}, u32[]{:S(2)}) collective-permute-start(bf16[4,16,512]{2,1,0:T(8,128)(2,1)S(1)} %dynamic-slice_bitcast_fusion), channel_id=1, source_target_pairs={{0,24},{4,28},{8,16},{12,20},{16,8},{20,12},{24,0},{28,4},{1,25},{... | collective-permute-start | bytes 196616 | tf_op jit(solution)/shard_map/ppermute | solution.py:478
  7.0 6.4 %collective-permute-start = (bf16[4,16,512]{2,1,0:T(8,128)(2,1)S(1)}, bf16[4,16,512]{2,1,0:T(8,128)(2,1)S(1)}, u32[]{:S(2)}, u32[]{:S(2)}) collective-permute-start(bf16[4,16,512]{2,1,0:T(8,128)(2,1)S(1)} %dynamic-slice_bitcast_fusion), channel_id=1, source_target_pairs={{0,16},{4,20},{8,24},{12,28},{16,0},{20,4},{24,8},{28,12},{1,17},{... | collective-permute-start | bytes 196616 | tf_op jit(solution)/shard_map/ppermute | solution.py:478
  9.2 6.4 %collective-permute-start.3 = (bf16[8,16,512]{2,1,0:T(8,128)(2,1)S(1)}, bf16[8,16,512]{2,1,0:T(8,128)(2,1)S(1)}, u32[]{:S(2)}, u32[]{:S(2)}) collective-permute-start(bf16[8,16,512]{2,1,0:T(8,128)(2,1)S(1)} %pad_maximum_fusion.2.rest_0_), channel_id=1, source_target_pairs={{0,4},{4,0},{8,12},{12,8},{16,20},{20,16},{24,28},{28,24},{1,5},{5... | collective-permute-start | bytes 393224 | tf_op jit(solution)/shard_map/ppermute | solution.py:478
  13.5 5.4 %collective-permute-start.4 = (bf16[8,16,512]{2,1,0:T(8,128)(2,1)S(1)}, bf16[8,16,512]{2,1,0:T(8,128)(2,1)S(1)}, u32[]{:S(2)}, u32[]{:S(2)}) collective-permute-start(bf16[8,16,512]{2,1,0:T(8,128)(2,1)S(1)} %pad_maximum_fusion.1.rest_1_), channel_id=1, source_target_pairs={{0,4},{4,0},{8,12},{12,8},{16,20},{20,16},{24,28},{28,24},{1,5},{5... | collective-permute-start | bytes 393224 | tf_op jit(solution)/shard_map/ppermute | solution.py:478
  15.1 4.1 %collective-permute-start.5 = (bf16[8,16,512]{2,1,0:T(8,128)(2,1)S(1)}, bf16[8,16,512]{2,1,0:T(8,128)(2,1)S(1)}, u32[]{:S(2)}, u32[]{:S(2)}) collective-permute-start(bf16[8,16,512]{2,1,0:T(8,128)(2,1)S(1)} %pad_maximum_fusion.2.rest_0_), channel_id=1, source_target_pairs={{0,1},{1,0},{2,3},{3,2},{4,5},{5,4},{6,7},{7,6},{8,9},{9,8},{10,11... | collective-permute-start | bytes 393224 | tf_op jit(solution)/shard_map/ppermute | solution.py:511
  15.1 4.1 %collective-permute-start.6 = (bf16[8,16,512]{2,1,0:T(8,128)(2,1)S(1)}, bf16[8,16,512]{2,1,0:T(8,128)(2,1)S(1)}, u32[]{:S(2)}, u32[]{:S(2)}) collective-permute-start(bf16[8,16,512]{2,1,0:T(8,128)(2,1)S(1)} %pad_maximum_fusion.1.rest_1_), channel_id=1, source_target_pairs={{0,1},{1,0},{2,3},{3,2},{4,5},{5,4},{6,7},{7,6},{8,9},{9,8},{10,11... | collective-permute-start | bytes 393224 | tf_op jit(solution)/shard_map/ppermute | solution.py:511
  15.6 3.6 %collective-permute-start.7 = (bf16[8,16,512]{2,1,0:T(8,128)(2,1)S(1)}, bf16[8,16,512]{2,1,0:T(8,128)(2,1)S(1)}, u32[]{:S(2)}, u32[]{:S(2)}) collective-permute-start(bf16[8,16,512]{2,1,0:T(8,128)(2,1)S(1)} %collective-permute-done.3.rest_2_), channel_id=1, source_target_pairs={{0,1},{1,0},{2,3},{3,2},{4,5},{5,4},{6,7},{7,6},{8,9},{9,8},{10,11... | collective-permute-start | bytes 393224 | tf_op jit(solution)/shard_map/ppermute | solution.py:511
  18.9 1.3 %collective-permute-start.8 = (bf16[8,16,512]{2,1,0:T(8,128)(2,1)S(1)}, bf16[8,16,512]{2,1,0:T(8,128)(2,1)S(1)}, u32[]{:S(2)}, u32[]{:S(2)}) collective-permute-start(bf16[8,16,512]{2,1,0:T(8,128)(2,1)S(1)} %collective-permute-done.4.rest_3_), channel_id=1, source_target_pairs={{0,1},{1,0},{2,3},{3,2},{4,5},{5,4},{6,7},{7,6},{8,9},{9,8},{10,11... | collective-permute-start | bytes 393224 | tf_op jit(solution)/shard_map/ppermute | solution.py:511
  26.6 12.4 %collective-permute-start.9 = (f32[3,2,64,128]{3,2,1,0:T(8,128)S(1)}, f32[3,2,64,128]{3,2,1,0:T(8,128)S(1)}, u32[]{:S(2)}, u32[]{:S(2)}) collective-permute-start(f32[3,2,64,128]{3,2,1,0:T(8,128)S(1)} %get-tuple-element.40.rest_3_), channel_id=1, source_target_pairs={{0,1},{1,2},{2,3},{4,5},{5,6},{6,7},{8,9},{9,10},{10,11},{12,13},{... | collective-permute-start | bytes 589832 | tf_op jit(solution)/shard_map/ppermute | solution.py:552
  28.7 10.3 %collective-permute-start.10 = (f32[3,2,64,128]{3,2,1,0:T(8,128)S(1)}, f32[3,2,64,128]{3,2,1,0:T(8,128)S(1)}, u32[]{:S(2)}, u32[]{:S(2)}) collective-permute-start(f32[3,2,64,128]{3,2,1,0:T(8,128)S(1)} %get-tuple-element.41.rest_1_), channel_id=1, source_target_pairs={{1,0},{2,1},{3,2},{5,4},{6,5},{7,6},{9,8},{10,9},{11,10},{13,12},{... | collective-permute-start | bytes 589832 | tf_op jit(solution)/shard_map/ppermute | solution.py:553
  62.1 3.7 %collective-permute-start.11 = (bf16[32,16,512]{2,1,0:T(8,128)(2,1)S(1)}, bf16[32,16,512]{2,1,0:T(8,128)(2,1)S(1)}, u32[]{:S(2)}, u32[]{:S(2)}) collective-permute-start(bf16[32,16,512]{2,1,0:T(8,128)(2,1)S(1)} %get-tuple-element.55), channel_id=1, source_target_pairs={{0,1},{1,0},{2,3},{3,2},{4,5},{5,4},{6,7},{7,6},{8,9},{9,8},{10,11... | collective-permute-start | bytes 1572872 | tf_op jit(solution)/shard_map/ppermute | solution.py:603
  65.9 5.8 %collective-permute-start.12 = (bf16[8,16,512]{2,1,0:T(8,128)(2,1)S(1)}, bf16[8,16,512]{2,1,0:T(8,128)(2,1)S(1)}, u32[]{:S(2)}, u32[]{:S(2)}) collective-permute-start(bf16[8,16,512]{2,1,0:T(8,128)(2,1)S(1)} %get-tuple-element.57), channel_id=1, source_target_pairs={{0,4},{4,0},{8,12},{12,8},{16,20},{20,16},{24,28},{28,24},{1,5},{5... | collective-permute-start | bytes 393224 | tf_op jit(solution)/shard_map/ppermute | solution.py:478
  71.8 5.0 %collective-permute-start.13 = (bf16[8,16,512]{2,1,0:T(8,128)(2,1)S(1)}, bf16[8,16,512]{2,1,0:T(8,128)(2,1)S(1)}, u32[]{:S(2)}, u32[]{:S(2)}) collective-permute-start(bf16[8,16,512]{2,1,0:T(8,128)(2,1)S(1)} %get-tuple-element.60), channel_id=1, source_target_pairs={{0,4},{4,0},{8,12},{12,8},{16,20},{20,16},{24,28},{28,24},{1,5},{5... | collective-permute-start | bytes 393224 | tf_op jit(solution)/shard_map/ppermute | solution.py:478
  73.4 7.1 %collective-permute-start.14 = (bf16[4,16,512]{2,1,0:T(8,128)(2,1)S(1)}, bf16[4,16,512]{2,1,0:T(8,128)(2,1)S(1)}, u32[]{:S(2)}, u32[]{:S(2)}) collective-permute-start(bf16[4,16,512]{2,1,0:T(8,128)(2,1)S(1)} %get-tuple-element.58.after_ref), channel_id=1, source_target_pairs={{0,16},{4,20},{8,24},{12,28},{16,0},{20,4},{24,8},{28,12},{1,17},{... | collective-permute-start | bytes 196616 | tf_op jit(solution)/shard_map/ppermute | solution.py:478
  74.3 6.2 %collective-permute-start.15 = (bf16[4,16,512]{2,1,0:T(8,128)(2,1)S(1)}, bf16[4,16,512]{2,1,0:T(8,128)(2,1)S(1)}, u32[]{:S(2)}, u32[]{:S(2)}) collective-permute-start(bf16[4,16,512]{2,1,0:T(8,128)(2,1)S(1)} %get-tuple-element.62), channel_id=1, source_target_pairs={{0,24},{4,28},{8,16},{12,20},{16,8},{20,12},{24,0},{28,4},{1,25},{... | collective-permute-start | bytes 196616 | tf_op jit(solution)/shard_map/ppermute | solution.py:478
  76.9 4.5 %collective-permute-start.16 = (bf16[4,16,512]{2,1,0:T(8,128)(2,1)S(1)}, bf16[4,16,512]{2,1,0:T(8,128)(2,1)S(1)}, u32[]{:S(2)}, u32[]{:S(2)}) collective-permute-start(bf16[4,16,512]{2,1,0:T(8,128)(2,1)S(1)} %get-tuple-element.63), channel_id=1, source_target_pairs={{0,8},{4,12},{8,0},{12,4},{16,24},{20,28},{24,16},{28,20},{1,9},{5... | collective-permute-start | bytes 196616 | tf_op jit(solution)/shard_map/ppermute | solution.py:478
  81.3 4.3 %collective-permute-start.17 = (bf16[4,16,512]{2,1,0:T(8,128)(2,1)S(1)}, bf16[4,16,512]{2,1,0:T(8,128)(2,1)S(1)}, u32[]{:S(2)}, u32[]{:S(2)}) collective-permute-start(bf16[4,16,512]{2,1,0:T(8,128)(2,1)S(1)} %add_convert_fusion), channel_id=1, source_target_pairs={{0,2},{1,3},{2,0},{3,1},{4,6},{5,7},{6,4},{7,5},{8,10},{9,11},{10,... | collective-permute-start | bytes 196616 | tf_op jit(solution)/shard_map/ppermute | solution.py:630
  85.7 1.4 %collective-permute-start.18 = (f32[4,16,512]{2,1,0:T(8,128)S(1)}, f32[4,16,512]{2,1,0:T(8,128)S(1)}, u32[]{:S(2)}, u32[]{:S(2)}) collective-permute-start(f32[4,16,512]{2,1,0:T(8,128)S(1)} %convert_add_fusion), channel_id=1, source_target_pairs={{0,1},{1,0},{2,3},{3,2},{4,5},{5,4},{6,7},{7,6},{8,9},{9,8},{10,11... | collective-permute-start | bytes 393224 | tf_op jit(solution)/shard_map/ppermute | solution.py:631
